TPU v7x, 32 devices: a whole 2x2x4 slice. The times are simulated.
32 devices in a mesh: dp: 2 (over y), expert: 16 (over z, x, core).
Axes of the slice: x: 2, y: 2, z: 4, core: 2. Of those that a mesh axis runs over, the one named last changes fastest.
Arguments:
- tokens: bfloat16 [1024, 4096], P('expert', 'dp'), may hold values from -6 to 6
- expert_ids: int32 [1024, 8], P('expert'), may hold values from 0 to 15, all different within a row; in each aligned block of 64 rows (0 to 63, 64 to 127, ...) at most 64 rows name the same one
- gate_weights: float32 [1024, 8], P('expert'), may hold values from 0.05 to 1
- gate_proj: bfloat16 [16, 4096, 1536], P('expert', 'dp'), may hold values from -0.09375 to 0.09375
- up_proj: bfloat16 [16, 4096, 1536], P('expert', 'dp'), may hold values from -0.09375 to 0.09375
- down_proj: bfloat16 [16, 1536, 4096], P('expert', None, 'dp'), may hold values from -0.15625 to 0.15625
Outputs:
- combined: bfloat16 [1024, 4096], P('expert', 'dp')
Inputs may be any that keep to these rules, and one draw needn't show every extreme that they name: `expert_ids`: each row names 8 different experts. Among the 64 rows of one device (one aligned block), no expert is named by more than 64 rows, and in every draw some expert is named by exactly 64 rows of some block.
All inputs are finite; a program needn't handle non-finite values.
Results may differ from a plain program's by a relative error of at most 0.029.
Values may be sent and summed in bfloat16 or wider, within the bound.
No kernel may reach another device: no remote copies, remote signals or barrier semaphores. Data moves between devices by JAX's collectives and lax.ppermute only.
A program may use at most 64 MiB of HBM per device.

v0:
```python
import jax
import jax.numpy as jnp
from jax import lax
from jax.sharding import PartitionSpec as P


def block_places(block_ids, expert_count, capacity):
    tok_count, top_count = block_ids.shape
    flat_ids = block_ids.reshape(tok_count * top_count)
    matches = (flat_ids[:, None] == jnp.arange(expert_count, dtype=jnp.int32)[None, :]).astype(
        jnp.int32
    )
    earlier = jnp.cumsum(matches, axis=0) - matches
    slot_index = jnp.sum(earlier * matches, axis=1)
    return (flat_ids * capacity + slot_index).reshape(tok_count, top_count)


def body(tokens, expert_ids, gate_weights, gate_proj, up_proj, down_proj):
    tok_count, top_count = expert_ids.shape
    row_width = tokens.shape[1]
    sources = lax.axis_size("expert")
    capacity = 2 * tok_count * top_count // sources
    positions = jnp.arange(sources * capacity, dtype=jnp.int32)
    places = block_places(expert_ids, sources, capacity)
    matches = places[:, :, None] == positions[None, None, :]
    weighting = jnp.sum(jnp.where(matches, gate_weights[:, :, None], 0.0), axis=1)
    chosen = jnp.any(matches, axis=1).astype(jnp.bfloat16)
    outgoing = lax.dot_general(
        chosen, tokens, (((0,), (0,)), ((), ())), preferred_element_type=jnp.float32
    ).astype(jnp.bfloat16)
    incoming = lax.all_to_all(
        outgoing.reshape(sources, capacity, row_width),
        "expert",
        split_axis=0,
        concat_axis=0,
        tiled=True,
    )
    expert_rows = incoming.reshape(sources * capacity, row_width)
    gate_part = jnp.dot(expert_rows, gate_proj[0], preferred_element_type=jnp.float32)
    up_part = jnp.dot(expert_rows, up_proj[0], preferred_element_type=jnp.float32)
    gate_sum, up_sum = (
        lax.psum(gate_part.astype(jnp.bfloat16), "dp").astype(jnp.float32),
        lax.psum(up_part.astype(jnp.bfloat16), "dp").astype(jnp.float32),
    )
    hidden = (jax.nn.silu(gate_sum) * up_sum).astype(jnp.bfloat16)
    expert_out = jnp.dot(hidden, down_proj[0], preferred_element_type=jnp.float32).astype(
        jnp.bfloat16
    )
    returned = lax.all_to_all(
        expert_out.reshape(sources, capacity, row_width),
        "expert",
        split_axis=0,
        concat_axis=0,
        tiled=True,
    )
    returned_flat = returned.reshape(sources * capacity, row_width)
    weight_high = weighting.astype(jnp.bfloat16)
    weight_low = (weighting - weight_high.astype(jnp.float32)).astype(jnp.bfloat16)
    combined = jnp.dot(weight_high, returned_flat, preferred_element_type=jnp.float32)
    combined = combined + jnp.dot(weight_low, returned_flat, preferred_element_type=jnp.float32)
    return combined.astype(jnp.bfloat16)


def solution(mesh):
    placed = (
        P("expert", "dp"),
        P("expert", None),
        P("expert", None),
        P("expert", "dp", None),
        P("expert", "dp", None),
        P("expert", None, "dp"),
    )
    return jax.shard_map(
        body, mesh=mesh, in_specs=placed, out_specs=P("expert", "dp"), check_vma=False
    )
```

profile of v0, /device:TPU:8, one launch (start us, length us, event | category | flops | bytes accessed | tf_op | source)
XLA Modules:
  0.0 404.0 jit_solution(10712476980029509893)
XLA Ops:
  6.5 0.0 copy-start
  6.5 0.0 all-reduce.3.cloned.1.call-start
  6.5 0.8 copy.21
  7.4 0.1 eq.42
  7.4 0.1 eq.38
  7.5 1.2 reduce-window.6
  8.7 0.2 slice_reduce_fusion
  9.0 0.1 fusion.29
  9.1 0.1 reduce_sum.21
  9.2 0.1 copy.24
  9.2 0.7 multiply_add_fusion
  9.9 0.1 copy.25
  10.0 0.7 fusion.23
  10.7 0.0 copy-done
  10.7 0.0 slice-start
  10.7 1.3 convolution_convert_fusion
  12.0 0.0 slice-start.1
  12.1 0.0 slice-start.2
  12.1 98.6 %all_to_all.10 = bf16[16,64,2048]{2,1,0:T(8,128)(2,1)S(1)} all-to-all(bf16[16,64,2048]{2,1,0:T(8,128)(2,1)S(1)} %bitcast.44), channel_id=1, replica_groups=mesh['dp'=2,'expert'=16] {'expert'}, dimensions={0} | all-to-all | bytes 8388608 | tf_op jit(solution)/shard_map/all_to_all | solution.py:31
  110.7 0.0 slice-done
  110.7 8.1 %fusion.11 = bf16[1024,1536]{1,0:T(8,128)(2,1)} fusion(bf16[1024,2048]{1,0:T(8,128)(2,1)S(1)} %bitcast.46, bf16[1,2048,1536]{2,1,0:T(8,128)(2,1)S(1)} %bitcast.49), kind=kOutput, calls=%fused_computation.13 | convolution fusion | flops 6444023808 | bytes 13631488 | tf_op jit(solution)/shard_map/dot_general | solution.py:39
  118.8 0.0 slice-done.3
  118.8 8.1 %fusion.14 = bf16[1024,1536]{1,0:T(8,128)(2,1)} fusion(bf16[1024,2048]{1,0:T(8,128)(2,1)S(1)} %bitcast.47, bf16[1,2048,1536]{2,1,0:T(8,128)(2,1)S(1)} %bitcast.51), kind=kOutput, calls=%fused_computation.14 | convolution fusion | flops 6444023808 | bytes 13631488 | tf_op jit(solution)/shard_map/dot_general | solution.py:40
  126.9 0.0 all-reduce.3.cloned.1.call-update
  127.0 153.9 %all-reduce.3.cloned.1.call-done = (bf16[1024,1536]{1,0:T(8,128)(2,1)}, bf16[1024,1536]{1,0:T(8,128)(2,1)}) async-done(((bf16[1024,1536]{1,0:T(8,128)(2,1)}, bf16[1024,1536]{1,0:T(8,128)(2,1)}), (bf16[1024,1536]{1,0:T(8,128)(2,1)}, bf16[1024,1536]{1,0:T(8,128)(2,1)})) %all-reduce.3.cloned.1.call-update) | async-done | bytes 6291472 | tf_op jit(solution)/shard_map/psum | solution.py:43
  280.8 12.5 %fusion.17 = bf16[1024,2048]{1,0:T(8,128)(2,1)} fusion(bf16[1,1536,2048]{2,1,0:T(8,128)(2,1)} %param.11, bf16[1024,1536]{1,0:T(8,128)(2,1)} %get-tuple-element.5, bf16[1024,1536]{1,0:T(8,128)(2,1)} %get-tuple-element.6), kind=kOutput, calls=%fused_computation.15 | convolution fusion | flops 6457131008 | bytes 16777216 | tf_op jit(solution)/shard_map/dot_general | solution.py:46
  293.3 6.2 %all-to-all-start.1 = ((bf16[16,64,2048]{2,1,0:T(8,128)(2,1)}), bf16[16,64,2048]{2,1,0:T(8,128)(2,1)}, u32[]{:S(2)}, u32[]{:S(2)}) async-start(bf16[16,64,2048]{2,1,0:T(8,128)(2,1)} %bitcast.45), calls=%async_computation.1 | async-start | bytes 8388608 | tf_op jit(solution)/shard_map/all_to_all | solution.py:49
  299.5 0.1 copy.26
  299.6 0.7 select_reduce_fusion
  300.3 90.0 %all-to-all-done.1 = bf16[16,64,2048]{2,1,0:T(8,128)(2,1)} async-done(((bf16[16,64,2048]{2,1,0:T(8,128)(2,1)}), bf16[16,64,2048]{2,1,0:T(8,128)(2,1)}, u32[]{:S(2)}, u32[]{:S(2)}) %all-to-all-start.1) | async-done | bytes 4194336 | tf_op jit(solution)/shard_map/all_to_all | solution.py:49
  390.4 3.0 fusion.25
  393.4 3.8 fusion.22
  (10 shorter events, 0.1 us)
Async XLA Ops:
  6.5 4.2 %copy-start = (bf16[64,2048]{1,0:T(8,128)(2,1)S(1)}, bf16[64,2048]{1,0:T(8,128)(2,1)}, u32[]{:S(2)}) copy-start(bf16[64,2048]{1,0:T(8,128)(2,1)} %param.6) | copy-start | bytes 786436
  6.5 274.3 %all-reduce.3.cloned.1.call-start = ((), (), s32[]{:S(2)}) async-start(), calls=%async_computation.2 | async-start | bytes 12582912 | tf_op jit(solution)/shard_map/psum | solution.py:43
  10.7 100.0 %slice-start = ((s8[6291456]{0:T(1024)(128)(4,1)}), s8[4194304]{0:T(1024)(128)(4,1)S(1)}, s32[]{:S(2)}) async-start(s8[6291456]{0:T(1024)(128)(4,1)} %bitcast.48), calls=%async_computation.3 | async-start | bytes 8388608
  12.0 98.7 %slice-start.1 = ((s8[6291456]{0:T(1024)(128)(4,1)}), s8[2097152]{0:T(1024)(128)(4,1)S(1)}, s32[]{:S(2)}) async-start(s8[6291456]{0:T(1024)(128)(4,1)} %bitcast.48), calls=%async_computation.4 | async-start | bytes 4194304
  12.1 106.7 %slice-start.2 = ((s8[6291456]{0:T(1024)(128)(4,1)}), s8[4194304]{0:T(1024)(128)(4,1)S(1)}, s32[]{:S(2)}) async-start(s8[6291456]{0:T(1024)(128)(4,1)} %bitcast.50), calls=%async_computation.5 | async-start | bytes 8388608
  110.7 8.1 %slice-start.3 = ((s8[6291456]{0:T(1024)(128)(4,1)}), s8[2097152]{0:T(1024)(128)(4,1)S(1)}, s32[]{:S(2)}) async-start(s8[6291456]{0:T(1024)(128)(4,1)} %bitcast.50), calls=%async_computation.6 | async-start | bytes 4194304
  293.3 6.2 %copy-start.1 = (f32[64,8]{0,1:T(8,128)S(1)}, f32[64,8]{0,1:T(8,128)}, u32[]{:S(2)}) copy-start(f32[64,8]{0,1:T(8,128)} %param.8) | copy-start | bytes 6148
  293.3 97.0 %all-to-all-start.1 = ((bf16[16,64,2048]{2,1,0:T(8,128)(2,1)}), bf16[16,64,2048]{2,1,0:T(8,128)(2,1)}, u32[]{:S(2)}, u32[]{:S(2)}) async-start(bf16[16,64,2048]{2,1,0:T(8,128)(2,1)} %bitcast.45), calls=%async_computation.1 | async-start | bytes 8388608 | tf_op jit(solution)/shard_map/all_to_all | solution.py:49
Sparse Core Ops, SparseCore 0:
  127.1 153.6 all-reduce.2
where the time goes:
time: 406 us; the launch traced here: 404 us
  waiting for transfers between devices  244 us (60%)
  blocking collectives  98.6 us (24%)
  matrix products  36.8 us (9%)
  between operations  13.5 us (3%)
  starting transfers between devices  6.2 us (2%)
    psum x1, waiting for transfers between devices, body(): lax.psum(up_part.astype(jnp.bfloat16), 'dp').astype(jnp.float32)  154 us
    all_to_all x1, blocking collectives, body(): lax.all_to_all(outgoing.reshape(sources, capacity, row_width), 'expert',...  98.6 us
    all_to_all x1, waiting for transfers between devices, body(): lax.all_to_all(expert_out.reshape(sources, capacity, row_width), 'expert'...  90 us
    dot_general x1, matrix products, body(): jnp.dot(hidden, down_proj[0], preferred_element_type=jnp.float32)  12.5 us
    dot_general x1, matrix products, body(): jnp.dot(expert_rows, up_proj[0], preferred_element_type=jnp.float32)  8.14 us
  transfers between devices with their start and end apart: 2, of which 2 were waited for; matrix products, arithmetic and copies ran while one was open for 0% of the time, Pallas kernels for 0%

commit v1 on v0

--- a/solution.py
+++ b/solution.py
@@ -15,7 +15,7 @@
     return (flat_ids * capacity + slot_index).reshape(tok_count, top_count)
 
 
-def body(tokens, expert_ids, gate_weights, gate_proj, up_proj, down_proj):
+def dispatch_body(tokens, expert_ids, gate_weights, gate_proj, up_proj, down_proj):
     tok_count, top_count = expert_ids.shape
     row_width = tokens.shape[1]
     sources = lax.axis_size("expert")
@@ -61,6 +61,93 @@
     return combined.astype(jnp.bfloat16)
 
 
+def gather_body(tokens, expert_ids, gate_weights, gate_proj, up_proj, down_proj):
+    rows = tokens.shape[0]
+    sources = lax.axis_size("expert")
+    half = gate_proj.shape[2] // 2
+    me = lax.axis_index("expert")
+    low = lax.axis_index("dp") == 0
+    gate, up, down = gate_proj[0], up_proj[0], down_proj[0]
+
+    def swap(value, r):
+        return lax.ppermute(value, "expert", [(i, i ^ r) for i in range(sources)])
+
+    def cross(value):
+        return lax.ppermute(value, "dp", [(0, 1), (1, 0)])
+
+    names = jnp.arange(sources, dtype=jnp.int32)
+    own_weights = jnp.sum(
+        jnp.where(expert_ids[:, :, None] == names, gate_weights[:, :, None], 0.0), axis=1
+    )
+    all_weights = lax.all_gather(own_weights, "expert", axis=0)
+    my_weights = jnp.sum(jnp.where(names == me, all_weights, 0.0), axis=2)
+
+    held = {0: tokens}
+    for r in range(4, sources, 4):
+        held[r] = swap(tokens, r)
+    for r in range(0, sources, 4):
+        held[r + 2] = swap(held[r], 2)
+    for r in range(0, sources, 4):
+        pair = swap(jnp.concatenate([held[r], held[r + 2]]), 1)
+        held[r + 1], held[r + 3] = pair[:rows], pair[rows:]
+
+    def partials(blocks):
+        chunk = jnp.concatenate([held[r] for r in blocks])
+        gate_part = jnp.dot(chunk, gate, preferred_element_type=jnp.float32)
+        up_part = jnp.dot(chunk, up, preferred_element_type=jnp.float32)
+        kept, sent = [], []
+        for part in (gate_part, up_part):
+            first, second = part[:, :half], part[:, half:]
+            kept.append(jnp.where(low, first, second))
+            sent.append(jnp.where(low, second, first).astype(jnp.bfloat16))
+        return kept, cross(jnp.concatenate(sent, axis=1))
+
+    def hidden_half(kept, arrived):
+        gate_sum = kept[0] + arrived[:, :half].astype(jnp.float32)
+        up_sum = kept[1] + arrived[:, half:].astype(jnp.float32)
+        return (jax.nn.silu(gate_sum) * up_sum).astype(jnp.bfloat16)
+
+    def outputs(blocks, mine, other):
+        hidden = jnp.concatenate(
+            [jnp.where(low, mine, other), jnp.where(low, other, mine)], axis=1
+        )
+        out = jnp.dot(hidden, down, preferred_element_type=jnp.float32)
+        return {
+            r: out[i * rows : (i + 1) * rows]
+            * lax.dynamic_index_in_dim(my_weights, me ^ r, 0, keepdims=False)[:, None]
+            for i, r in enumerate(blocks)
+        }
+
+    chunks = [[0], [4, 5]]
+    chunks += [[r, r + 1, r + 2, r + 3] for r in range(8, sources, 4)]
+    chunks += [[6, 7], [2, 3], [1]]
+
+    added = {}
+    for blocks in chunks:
+        kept, arrived = partials(blocks)
+        mine = hidden_half(kept, arrived)
+        other = cross(mine)
+        added.update(outputs(blocks, mine, other))
+
+    def send(value, r):
+        return swap(value.astype(jnp.bfloat16), r).astype(jnp.float32)
+
+    for blocks in chunks:
+        odd = [r for r in blocks if r % 2 == 1]
+        if not odd:
+            continue
+        arrived = send(jnp.concatenate([added[r] for r in odd]), 1)
+        for i, r in enumerate(odd):
+            added[r - 1] = added[r - 1] + arrived[i * rows : (i + 1) * rows]
+    total = None
+    for r in list(range(8, sources, 4)) + [4, 0]:
+        part = added[r] + send(added[r + 2], 2)
+        if r > 0:
+            part = send(part, r)
+        total = part if total is None else total + part
+    return total.astype(jnp.bfloat16)
+
+
 def solution(mesh):
     placed = (
         P("expert", "dp"),
@@ -70,6 +157,15 @@
         P("expert", "dp", None),
         P("expert", None, "dp"),
     )
+
+    def body(tokens, expert_ids, gate_weights, gate_proj, up_proj, down_proj):
+        tok_count, top_count = expert_ids.shape
+        sources = lax.axis_size("expert")
+        whole_blocks = 2 * tok_count * top_count >= sources * tok_count
+        paired = lax.axis_size("dp") == 2 and sources >= 8 and sources & (sources - 1) == 0
+        plan = gather_body if whole_blocks and paired else dispatch_body
+        return plan(tokens, expert_ids, gate_weights, gate_proj, up_proj, down_proj)
+
     return jax.shard_map(
         body, mesh=mesh, in_specs=placed, out_specs=P("expert", "dp"), check_vma=False
     )

time: 406 us -> 225 us (0.55)
  waiting for transfers between devices: 244 us -> 114 us
  blocking collectives: 98.6 us -> 22.5 us
  starting transfers between devices: 6.2 us -> 34.7 us
  between operations: 13.5 us -> 0.89 us
  other arithmetic: 3.4 us -> 8.97 us
    psum x1 -> x0, waiting for transfers between devices: 154 us -> none  [body(): lax.psum(up_part.astype(jnp.bfloat16), 'dp').astype(jnp.float32)]
    ppermute x0 -> x38, waiting for transfers between devices: none -> 114 us  [the longest x14 64.1 us: cross(): return lax.ppermute(value, 'dp', [(0, 1), (1, 0)])]
    all_to_all x1 -> x0, blocking collectives: 98.6 us -> none  [body(): lax.all_to_all(outgoing.reshape(sources, capacity, row_width), 'expert',...]
    all_to_all x1 -> x0, waiting for transfers between devices: 90 us -> none  [body(): lax.all_to_all(expert_out.reshape(sources, capacity, row_width), 'expert'...]
    ppermute x0 -> x38, starting transfers between devices: none -> 34.7 us  [the longest x24 17.8 us: swap(): return lax.ppermute(value, 'expert', [(i, i ^ r) for i in range(sources)])]
    all_gather x0 -> x1, blocking collectives: none -> 22.5 us  [gather_body(): all_weights = lax.all_gather(own_weights, 'expert', axis=0)]
    all_to_all x1 -> x0, starting transfers between devices: 6.2 us -> none  [body(): lax.all_to_all(expert_out.reshape(sources, capacity, row_width), 'expert'...]
    convert_element_type x1 -> x26, other arithmetic: 0.01 us -> 4.39 us  [the longest x7 2.34 us: hidden_half(): return (jax.nn.silu(gate_sum) * up_sum).astype(jnp.bfloat16)]
  transfers between devices with their start and end apart: 2 -> 38, of which waited for: 2 -> 14; matrix products, arithmetic and copies ran while one was open for 0% -> 21% of each run, Pallas kernels for 0% -> 0%
where the time goes in v1:
time: 225 us; the launch traced here: 222 us
  waiting for transfers between devices  114 us (51%)
  matrix products  40 us (18%)
  starting transfers between devices  34.7 us (15%)
  blocking collectives  22.5 us (10%)
  other arithmetic  8.97 us (4%)
    ppermute x14, waiting for transfers between devices, cross(): return lax.ppermute(value, 'dp', [(0, 1), (1, 0)])  64.1 us
    ppermute x24, waiting for transfers between devices, swap(): return lax.ppermute(value, 'expert', [(i, i ^ r) for i in range(sources)])  49.8 us
    all_gather x1, blocking collectives, gather_body(): all_weights = lax.all_gather(own_weights, 'expert', axis=0)  22.5 us
    dot_general x7, matrix products, partials(): up_part = jnp.dot(chunk, up, preferred_element_type=jnp.float32)  18.2 us
    ppermute x24, starting transfers between devices, swap(): return lax.ppermute(value, 'expert', [(i, i ^ r) for i in range(sources)])  17.8 us
    ppermute x14, starting transfers between devices, cross(): return lax.ppermute(value, 'dp', [(0, 1), (1, 0)])  16.9 us
    dot_general x7, matrix products, partials(): gate_part = jnp.dot(chunk, gate, preferred_element_type=jnp.float32)  11.9 us
    dot_general x7, matrix products, outputs(): out = jnp.dot(hidden, down, preferred_element_type=jnp.float32)  9.94 us
  transfers between devices with their start and end apart: 38, of which 14 were waited for; matrix products, arithmetic and copies ran while one was open for 21% of the time, Pallas kernels for 0%

profile of v1, /device:TPU:8, one launch (start us, length us, event | category | flops | bytes accessed | tf_op | source)
XLA Modules:
  0.0 221.7 jit_solution(16956216457271444716)
XLA Ops:
  0.0 3.1 %collective-permute-start.8 = (bf16[64,2048]{1,0:T(8,128)(2,1)}, bf16[64,2048]{1,0:T(8,128)(2,1)}, u32[]{:S(2)}, u32[]{:S(2)}) collective-permute-start(bf16[64,2048]{1,0:T(8,128)(2,1)} %param.6), channel_id=1, source_target_pairs={{0,12},{1,13},{2,14},{3,15},{4,8},{5,9},{6,10},{7,11},{8,4},{9,5},... | collective-permute-start | bytes 786440 | tf_op jit(solution)/shard_map/ppermute | solution.py:73
  5.9 4.2 %fusion.18 = f32[64,1536]{1,0:T(8,128)S(1)} fusion(bf16[64,2048]{1,0:T(8,128)(2,1)} %param.6, bf16[1,2048,1536]{2,1,0:T(8,128)(2,1)} %param.10), kind=kOutput, calls=%fused_computation.18 | convolution fusion | flops 402653184 | bytes 6946816 | tf_op jit(solution)/shard_map/dot_general | solution.py:97
  14.1 22.5 %all-gather.1 = f32[16,64,16]{1,2,0:T(8,128)S(1)} all-gather(f32[1,64,16]{1,2,0:T(8,128)S(1)} %bitcast.98), channel_id=2, replica_groups=mesh['dp'=2,'expert'=16] {'expert'}, dimensions={0}, use_global_device_ids=true | all-gather | bytes 69632 | tf_op jit(solution)/shard_map/all_gather | solution.py:82
  36.8 1.9 collective-permute-start.17
  39.7 1.6 collective-permute-start.28
  42.6 1.9 collective-permute-start.1
  46.1 5.5 %collective-permute-done.9 = bf16[64,2048]{1,0:T(8,128)(2,1)S(1)} collective-permute-done((bf16[64,2048]{1,0:T(8,128)(2,1)}, bf16[64,2048]{1,0:T(8,128)(2,1)S(1)}, u32[]{:S(2)}, u32[]{:S(2)}) %collective-permute-start.9) | collective-permute-done | bytes 262176 | tf_op jit(solution)/shard_map/ppermute | solution.py:73
  52.7 4.0 %collective-permute-done.1 = bf16[64,2048]{1,0:T(8,128)(2,1)S(1)} collective-permute-done((bf16[64,2048]{1,0:T(8,128)(2,1)}, bf16[64,2048]{1,0:T(8,128)(2,1)S(1)}, u32[]{:S(2)}, u32[]{:S(2)}) %collective-permute-start.1) | collective-permute-done | bytes 262176 | tf_op jit(solution)/shard_map/ppermute | solution.py:73
  57.8 4.1 %fusion.16 = f32[64,1536]{1,0:T(8,128)S(1)} fusion(bf16[1,2048,1536]{2,1,0:T(8,128)(2,1)} %param.10, bf16[128,2048]{1,0:T(8,128)(2,1)S(1)} %collective-permute-done.30), kind=kOutput, calls=%fused_computation.16 | convolution fusion | flops 402653184 | bytes 6946816 | tf_op jit(solution)/shard_map/dot_general | solution.py:97
  63.2 1.6 collective-permute-start.31
  64.8 2.0 fusion.14
  66.8 1.9 fusion.28
  68.9 1.8 collective-permute-done.31
  77.3 1.6 collective-permute-start.19
  78.9 2.8 %fusion.24 = f32[256,1536]{1,0:T(8,128)S(1)} fusion(bf16[1,2048,1536]{2,1,0:T(8,128)(2,1)S(1)} %bitcast.95, bf16[64,2048]{1,0:T(8,128)(2,1)S(1)} %get-tuple-element.16, bf16[64,2048]{1,0:T(8,128)(2,1)S(1)} %collective-permute-done.9, bf16[64,2048]{1,0:T(8,128)(2,1)S(1)} %get-tuple-element.15, bf16[64,2048]{1,0:T(8,128)(2,1)} %collective-permute-done.8), kind=kOutput, calls=%fused_computation.24 | convolution fusion | flops 1614807040 | bytes 8912896 | tf_op jit(solution)/shard_map/dot_general | solution.py:97
  81.7 2.7 %fusion.38 = f32[256,1536]{1,0:T(8,128)S(1)} fusion(bf16[1,2048,1536]{2,1,0:T(8,128)(2,1)S(1)} %bitcast.97, bf16[64,2048]{1,0:T(8,128)(2,1)S(1)} %get-tuple-element.16, bf16[64,2048]{1,0:T(8,128)(2,1)S(1)} %collective-permute-done.9, bf16[64,2048]{1,0:T(8,128)(2,1)S(1)} %get-tuple-element.15, bf16[64,2048]{1,0:T(8,128)(2,1)} %collective-permute-done.8), kind=kOutput, calls=%fused_computation.38 | convolution fusion | flops 1614807040 | bytes 8912896 | tf_op jit(solution)/shard_map/dot_general | solution.py:96
  85.3 3.1 %fusion.26 = f32[256,1536]{1,0:T(8,128)S(1)} fusion(bf16[1,2048,1536]{2,1,0:T(8,128)(2,1)S(1)} %bitcast.95, bf16[64,2048]{1,0:T(8,128)(2,1)S(1)} %get-tuple-element.14, bf16[64,2048]{1,0:T(8,128)(2,1)S(1)} %collective-permute-done.1, bf16[64,2048]{1,0:T(8,128)(2,1)S(1)} %get-tuple-element.13, bf16[64,2048]{1,0:T(8,128)(2,1)} %collective-permute-done), kind=kOutput, calls=%fused_computation.26 | convolution fusion | flops 1614807040 | bytes 8912896 | tf_op jit(solution)/shard_map/dot_general | solution.py:97
  88.4 2.9 %fusion.40 = f32[256,1536]{1,0:T(8,128)S(1)} fusion(bf16[1,2048,1536]{2,1,0:T(8,128)(2,1)S(1)} %bitcast.97, bf16[64,2048]{1,0:T(8,128)(2,1)S(1)} %get-tuple-element.14, bf16[64,2048]{1,0:T(8,128)(2,1)S(1)} %collective-permute-done.1, bf16[64,2048]{1,0:T(8,128)(2,1)S(1)} %get-tuple-element.13, bf16[64,2048]{1,0:T(8,128)(2,1)} %collective-permute-done), kind=kOutput, calls=%fused_computation.40 | convolution fusion | flops 1614807040 | bytes 8912896 | tf_op jit(solution)/shard_map/dot_general | solution.py:96
  91.5 1.6 collective-permute-start.11
  95.1 26.5 %collective-permute-done.35 = bf16[128,768]{1,0:T(8,128)(2,1)S(1)} collective-permute-done((bf16[128,768]{1,0:T(8,128)(2,1)S(1)}, bf16[128,768]{1,0:T(8,128)(2,1)S(1)}, u32[]{:S(2)}, u32[]{:S(2)}) %collective-permute-start.35) | collective-permute-done | bytes 196640 | tf_op jit(solution)/shard_map/ppermute | solution.py:76
  125.3 18.9 %collective-permute-done.23 = bf16[128,768]{1,0:T(8,128)(2,1)S(1)} collective-permute-done((bf16[128,768]{1,0:T(8,128)(2,1)S(1)}, bf16[128,768]{1,0:T(8,128)(2,1)S(1)}, u32[]{:S(2)}, u32[]{:S(2)}) %collective-permute-start.23) | collective-permute-done | bytes 196640 | tf_op jit(solution)/shard_map/ppermute | solution.py:76
  146.9 3.0 %collective-permute-done.20 = bf16[128,768]{1,0:T(8,128)(2,1)S(1)} collective-permute-done((bf16[128,768]{1,0:T(8,128)(2,1)S(1)}, bf16[128,768]{1,0:T(8,128)(2,1)S(1)}, u32[]{:S(2)}, u32[]{:S(2)}) %collective-permute-start.20) | collective-permute-done | bytes 196640 | tf_op jit(solution)/shard_map/ppermute | solution.py:76
  154.9 9.3 %collective-permute-done.12 = bf16[256,768]{1,0:T(8,128)(2,1)S(1)} collective-permute-done((bf16[256,768]{1,0:T(8,128)(2,1)S(1)}, bf16[256,768]{1,0:T(8,128)(2,1)S(1)}, u32[]{:S(2)}, u32[]{:S(2)}) %collective-permute-start.12) | collective-permute-done | bytes 393248 | tf_op jit(solution)/shard_map/ppermute | solution.py:76
  165.8 1.8 fusion.10
  167.8 4.5 %collective-permute-done.4 = bf16[256,768]{1,0:T(8,128)(2,1)S(1)} collective-permute-done((bf16[256,768]{1,0:T(8,128)(2,1)S(1)}, bf16[256,768]{1,0:T(8,128)(2,1)S(1)}, u32[]{:S(2)}, u32[]{:S(2)}) %collective-permute-start.4) | collective-permute-done | bytes 393248 | tf_op jit(solution)/shard_map/ppermute | solution.py:76
  172.3 1.8 fusion.12
  174.3 1.6 collective-permute-start.37
  178.5 10.2 %collective-permute-done.14 = bf16[64,2048]{1,0:T(8,128)(2,1)S(1)} collective-permute-done((bf16[64,2048]{1,0:T(8,128)(2,1)S(1)}, bf16[64,2048]{1,0:T(8,128)(2,1)S(1)}, u32[]{:S(2)}, u32[]{:S(2)}) %collective-permute-start.14) | collective-permute-done | bytes 262176 | tf_op jit(solution)/shard_map/ppermute | solution.py:73
  190.4 6.2 %collective-permute-done.6 = bf16[64,2048]{1,0:T(8,128)(2,1)S(1)} collective-permute-done((bf16[64,2048]{1,0:T(8,128)(2,1)S(1)}, bf16[64,2048]{1,0:T(8,128)(2,1)S(1)}, u32[]{:S(2)}, u32[]{:S(2)}) %collective-permute-start.6) | collective-permute-done | bytes 262176 | tf_op jit(solution)/shard_map/ppermute | solution.py:73
  198.4 16.5 %collective-permute-done.15 = bf16[64,2048]{1,0:T(8,128)(2,1)S(1)} collective-permute-done((bf16[64,2048]{1,0:T(8,128)(2,1)S(1)}, bf16[64,2048]{1,0:T(8,128)(2,1)S(1)}, u32[]{:S(2)}, u32[]{:S(2)}) %collective-permute-start.15) | collective-permute-done | bytes 262176 | tf_op jit(solution)/shard_map/ppermute | solution.py:73
  214.9 4.6 %collective-permute-done.7 = bf16[64,2048]{1,0:T(8,128)(2,1)S(1)} collective-permute-done((bf16[64,2048]{1,0:T(8,128)(2,1)S(1)}, bf16[64,2048]{1,0:T(8,128)(2,1)S(1)}, u32[]{:S(2)}, u32[]{:S(2)}) %collective-permute-start.7) | collective-permute-done | bytes 262176 | tf_op jit(solution)/shard_map/ppermute | solution.py:73
  219.5 2.2 add_convert_fusion
  (145 shorter events, 43.0 us)
Async XLA Ops:
  0.0 36.8 %collective-permute-start.16 = (bf16[64,2048]{1,0:T(8,128)(2,1)}, bf16[64,2048]{1,0:T(8,128)(2,1)S(1)}, u32[]{:S(2)}, u32[]{:S(2)}) collective-permute-start(bf16[64,2048]{1,0:T(8,128)(2,1)} %param.6), channel_id=1, source_target_pairs={{0,4},{1,5},{2,6},{3,7},{4,0},{5,1},{6,2},{7,3},{8,12},{9,13},{10,... | collective-permute-start | bytes 786440 | tf_op jit(solution)/shard_map/ppermute | solution.py:73
  0.0 41.3 %collective-permute-start.8 = (bf16[64,2048]{1,0:T(8,128)(2,1)}, bf16[64,2048]{1,0:T(8,128)(2,1)}, u32[]{:S(2)}, u32[]{:S(2)}) collective-permute-start(bf16[64,2048]{1,0:T(8,128)(2,1)} %param.6), channel_id=1, source_target_pairs={{0,12},{1,13},{2,14},{3,15},{4,8},{5,9},{6,10},{7,11},{8,4},{9,5},... | collective-permute-start | bytes 786440 | tf_op jit(solution)/shard_map/ppermute | solution.py:73
  3.2 39.4 %collective-permute-start = (bf16[64,2048]{1,0:T(8,128)(2,1)}, bf16[64,2048]{1,0:T(8,128)(2,1)}, u32[]{:S(2)}, u32[]{:S(2)}) collective-permute-start(bf16[64,2048]{1,0:T(8,128)(2,1)} %param.6), channel_id=1, source_target_pairs={{0,8},{1,9},{2,10},{3,11},{4,12},{5,13},{6,14},{7,15},{8,0},{9,1},... | collective-permute-start | bytes 786440 | tf_op jit(solution)/shard_map/ppermute | solution.py:73
  4.4 37.1 %collective-permute-start.29 = (bf16[64,2048]{1,0:T(8,128)(2,1)}, bf16[64,2048]{1,0:T(8,128)(2,1)}, u32[]{:S(2)}, u32[]{:S(2)}) collective-permute-start(bf16[64,2048]{1,0:T(8,128)(2,1)} %param.6), channel_id=1, source_target_pairs={{0,2},{1,3},{2,0},{3,1},{4,6},{5,7},{6,4},{7,5},{8,10},{9,11},{10,... | collective-permute-start | bytes 786440 | tf_op jit(solution)/shard_map/ppermute | solution.py:73
  12.5 26.2 %collective-permute-start.27 = (bf16[64,1536]{1,0:T(8,128)(2,1)}, bf16[64,1536]{1,0:T(8,128)(2,1)}, u32[]{:S(2)}, u32[]{:S(2)}) collective-permute-start(bf16[64,1536]{1,0:T(8,128)(2,1)} %pad_maximum_fusion.22), channel_id=1, source_target_pairs={{0,16},{16,0},{1,17},{17,1},{2,18},{18,2},{3,19},{19,3},{4,20},{20... | collective-permute-start | bytes 589832 | tf_op jit(solution)/shard_map/ppermute | solution.py:76
  36.8 9.2 %collective-permute-start.17 = (bf16[64,2048]{1,0:T(8,128)(2,1)S(1)}, bf16[64,2048]{1,0:T(8,128)(2,1)S(1)}, u32[]{:S(2)}, u32[]{:S(2)}) collective-permute-start(bf16[64,2048]{1,0:T(8,128)(2,1)S(1)} %collective-permute-done.16), channel_id=1, source_target_pairs={{0,2},{1,3},{2,0},{3,1},{4,6},{5,7},{6,4},{7,5},{8,10},{9,11},{10,... | collective-permute-start | bytes 786440 | tf_op jit(solution)/shard_map/ppermute | solution.py:73
  39.7 158.5 %collective-permute-start.28 = (bf16[64,768]{1,0:T(8,128)(2,1)S(1)}, bf16[64,768]{1,0:T(8,128)(2,1)S(1)}, u32[]{:S(2)}, u32[]{:S(2)}) collective-permute-start(bf16[64,768]{1,0:T(8,128)(2,1)S(1)} %multiply_convert_fusion.6), channel_id=1, source_target_pairs={{0,16},{16,0},{1,17},{17,1},{2,18},{18,2},{3,19},{19,3},{4,20},{20... | collective-permute-start | bytes 294920 | tf_op jit(solution)/shard_map/ppermute | solution.py:76
  41.3 10.3 %collective-permute-start.9 = (bf16[64,2048]{1,0:T(8,128)(2,1)}, bf16[64,2048]{1,0:T(8,128)(2,1)S(1)}, u32[]{:S(2)}, u32[]{:S(2)}) collective-permute-start(bf16[64,2048]{1,0:T(8,128)(2,1)} %collective-permute-done.8), channel_id=1, source_target_pairs={{0,2},{1,3},{2,0},{3,1},{4,6},{5,7},{6,4},{7,5},{8,10},{9,11},{10,... | collective-permute-start | bytes 786440 | tf_op jit(solution)/shard_map/ppermute | solution.py:73
  42.5 15.3 %collective-permute-start.30 = (bf16[128,2048]{1,0:T(8,128)(2,1)S(1)}, bf16[128,2048]{1,0:T(8,128)(2,1)S(1)}, u32[]{:S(2)}, u32[]{:S(2)}) collective-permute-start(bf16[128,2048]{1,0:T(8,128)(2,1)S(1)} %pad_maximum_fusion.11), channel_id=1, source_target_pairs={{0,1},{1,0},{2,3},{3,2},{4,5},{5,4},{6,7},{7,6},{8,9},{9,8},{10,11... | collective-permute-start | bytes 1572872 | tf_op jit(solution)/shard_map/ppermute | solution.py:73
  42.6 14.1 %collective-permute-start.1 = (bf16[64,2048]{1,0:T(8,128)(2,1)}, bf16[64,2048]{1,0:T(8,128)(2,1)S(1)}, u32[]{:S(2)}, u32[]{:S(2)}) collective-permute-start(bf16[64,2048]{1,0:T(8,128)(2,1)} %collective-permute-done), channel_id=1, source_target_pairs={{0,2},{1,3},{2,0},{3,1},{4,6},{5,7},{6,4},{7,5},{8,10},{9,11},{10,... | collective-permute-start | bytes 786440 | tf_op jit(solution)/shard_map/ppermute | solution.py:73
  46.0 26.3 %collective-permute-start.18 = (bf16[128,2048]{1,0:T(8,128)(2,1)S(1)}, bf16[128,2048]{1,0:T(8,128)(2,1)S(1)}, u32[]{:S(2)}, u32[]{:S(2)}) collective-permute-start(bf16[128,2048]{1,0:T(8,128)(2,1)S(1)} %pad_maximum_fusion.4), channel_id=1, source_target_pairs={{0,1},{1,0},{2,3},{3,2},{4,5},{5,4},{6,7},{7,6},{8,9},{9,8},{10,11... | collective-permute-start | bytes 1572872 | tf_op jit(solution)/shard_map/ppermute | solution.py:73
  52.6 24.7 %collective-permute-start.10 = (bf16[128,2048]{1,0:T(8,128)(2,1)S(1)}, bf16[128,2048]{1,0:T(8,128)(2,1)S(1)}, u32[]{:S(2)}, u32[]{:S(2)}) collective-permute-start(bf16[128,2048]{1,0:T(8,128)(2,1)S(1)} %pad_maximum_fusion.8), channel_id=1, source_target_pairs={{0,1},{1,0},{2,3},{3,2},{4,5},{5,4},{6,7},{7,6},{8,9},{9,8},{10,11... | collective-permute-start | bytes 1572872 | tf_op jit(solution)/shard_map/ppermute | solution.py:73
  57.7 26.9 %collective-permute-start.2 = (bf16[128,2048]{1,0:T(8,128)(2,1)S(1)}, bf16[128,2048]{1,0:T(8,128)(2,1)S(1)}, u32[]{:S(2)}, u32[]{:S(2)}) collective-permute-start(bf16[128,2048]{1,0:T(8,128)(2,1)S(1)} %pad_maximum_fusion.6), channel_id=1, source_target_pairs={{0,1},{1,0},{2,3},{3,2},{4,5},{5,4},{6,7},{7,6},{8,9},{9,8},{10,11... | collective-permute-start | bytes 1572872 | tf_op jit(solution)/shard_map/ppermute | solution.py:73
  70.7 22.4 %collective-permute-start.34 = (bf16[128,1536]{1,0:T(8,128)(2,1)S(1)}, bf16[128,1536]{1,0:T(8,128)(2,1)S(1)}, u32[]{:S(2)}, u32[]{:S(2)}) collective-permute-start(bf16[128,1536]{1,0:T(8,128)(2,1)S(1)} %pad_maximum_fusion.15), channel_id=1, source_target_pairs={{0,16},{16,0},{1,17},{17,1},{2,18},{18,2},{3,19},{19,3},{4,20},{20... | collective-permute-start | bytes 1179656 | tf_op jit(solution)/shard_map/ppermute | solution.py:76
  72.3 19.2 %collective-permute-start.32 = (bf16[64,768]{1,0:T(8,128)(2,1)S(1)}, bf16[64,768]{1,0:T(8,128)(2,1)S(1)}, u32[]{:S(2)}, u32[]{:S(2)}) collective-permute-start(bf16[64,768]{1,0:T(8,128)(2,1)S(1)} %multiply_convert_fusion.5), channel_id=1, source_target_pairs={{0,16},{16,0},{1,17},{17,1},{2,18},{18,2},{3,19},{19,3},{4,20},{20... | collective-permute-start | bytes 294920 | tf_op jit(solution)/shard_map/ppermute | solution.py:76
  77.3 47.2 %collective-permute-start.19 = (bf16[128,1536]{1,0:T(8,128)(2,1)S(1)}, bf16[128,1536]{1,0:T(8,128)(2,1)S(1)}, u32[]{:S(2)}, u32[]{:S(2)}) collective-permute-start(bf16[128,1536]{1,0:T(8,128)(2,1)S(1)} %pad_maximum_fusion.13), channel_id=1, source_target_pairs={{0,16},{16,0},{1,17},{17,1},{2,18},{18,2},{3,19},{19,3},{4,20},{20... | collective-permute-start | bytes 1179656 | tf_op jit(solution)/shard_map/ppermute | solution.py:76
  84.6 39.6 %collective-permute-start.22 = (bf16[128,1536]{1,0:T(8,128)(2,1)S(1)}, bf16[128,1536]{1,0:T(8,128)(2,1)S(1)}, u32[]{:S(2)}, u32[]{:S(2)}) collective-permute-start(bf16[128,1536]{1,0:T(8,128)(2,1)S(1)} %pad_maximum_fusion.14), channel_id=1, source_target_pairs={{0,16},{16,0},{1,17},{17,1},{2,18},{18,2},{3,19},{19,3},{4,20},{20... | collective-permute-start | bytes 1179656 | tf_op jit(solution)/shard_map/ppermute | solution.py:76
  91.5 60.3 %collective-permute-start.11 = (bf16[256,1536]{1,0:T(8,128)(2,1)S(1)}, bf16[256,1536]{1,0:T(8,128)(2,1)S(1)}, u32[]{:S(2)}, u32[]{:S(2)}) collective-permute-start(bf16[256,1536]{1,0:T(8,128)(2,1)S(1)} %pad_maximum_fusion.3), channel_id=1, source_target_pairs={{0,16},{16,0},{1,17},{17,1},{2,18},{18,2},{3,19},{19,3},{4,20},{20... | collective-permute-start | bytes 2359304 | tf_op jit(solution)/shard_map/ppermute | solution.py:76
  93.3 28.3 %collective-permute-start.35 = (bf16[128,768]{1,0:T(8,128)(2,1)S(1)}, bf16[128,768]{1,0:T(8,128)(2,1)S(1)}, u32[]{:S(2)}, u32[]{:S(2)}) collective-permute-start(bf16[128,768]{1,0:T(8,128)(2,1)S(1)} %multiply_convert_fusion.2), channel_id=1, source_target_pairs={{0,16},{16,0},{1,17},{17,1},{2,18},{18,2},{3,19},{19,3},{4,20},{20... | collective-permute-start | bytes 589832 | tf_op jit(solution)/shard_map/ppermute | solution.py:76
  121.6 30.6 %collective-permute-start.3 = (bf16[256,1536]{1,0:T(8,128)(2,1)S(1)}, bf16[256,1536]{1,0:T(8,128)(2,1)S(1)}, u32[]{:S(2)}, u32[]{:S(2)}) collective-permute-start(bf16[256,1536]{1,0:T(8,128)(2,1)S(1)} %pad_maximum_fusion.2), channel_id=1, source_target_pairs={{0,16},{16,0},{1,17},{17,1},{2,18},{18,2},{3,19},{19,3},{4,20},{20... | collective-permute-start | bytes 2359304 | tf_op jit(solution)/shard_map/ppermute | solution.py:76
  124.2 25.7 %collective-permute-start.36 = (bf16[64,2048]{1,0:T(8,128)(2,1)S(1)}, bf16[64,2048]{1,0:T(8,128)(2,1)S(1)}, u32[]{:S(2)}, u32[]{:S(2)}) collective-permute-start(bf16[64,2048]{1,0:T(8,128)(2,1)S(1)} %fusion.63), channel_id=1, source_target_pairs={{0,1},{1,0},{2,3},{3,2},{4,5},{5,4},{6,7},{7,6},{8,9},{9,8},{10,11... | collective-permute-start | bytes 786440 | tf_op jit(solution)/shard_map/ppermute | solution.py:73
  124.5 19.7 %collective-permute-start.23 = (bf16[128,768]{1,0:T(8,128)(2,1)S(1)}, bf16[128,768]{1,0:T(8,128)(2,1)S(1)}, u32[]{:S(2)}, u32[]{:S(2)}) collective-permute-start(bf16[128,768]{1,0:T(8,128)(2,1)S(1)} %multiply_convert_fusion.3), channel_id=1, source_target_pairs={{0,16},{16,0},{1,17},{17,1},{2,18},{18,2},{3,19},{19,3},{4,20},{20... | collective-permute-start | bytes 589832 | tf_op jit(solution)/shard_map/ppermute | solution.py:76
  149.9 48.5 %collective-permute-start.33 = (bf16[64,2048]{1,0:T(8,128)(2,1)S(1)}, bf16[64,2048]{1,0:T(8,128)(2,1)S(1)}, u32[]{:S(2)}, u32[]{:S(2)}) collective-permute-start(bf16[64,2048]{1,0:T(8,128)(2,1)S(1)} %fusion.54), channel_id=1, source_target_pairs={{0,1},{1,0},{2,3},{3,2},{4,5},{5,4},{6,7},{7,6},{8,9},{9,8},{10,11... | collective-permute-start | bytes 786440 | tf_op jit(solution)/shard_map/ppermute | solution.py:73
  151.8 22.5 %collective-permute-start.21 = (bf16[64,2048]{1,0:T(8,128)(2,1)S(1)}, bf16[64,2048]{1,0:T(8,128)(2,1)S(1)}, u32[]{:S(2)}, u32[]{:S(2)}) collective-permute-start(bf16[64,2048]{1,0:T(8,128)(2,1)S(1)} %fusion.69), channel_id=1, source_target_pairs={{0,1},{1,0},{2,3},{3,2},{4,5},{5,4},{6,7},{7,6},{8,9},{9,8},{10,11... | collective-permute-start | bytes 786440 | tf_op jit(solution)/shard_map/ppermute | solution.py:73
  152.2 12.0 %collective-permute-start.12 = (bf16[256,768]{1,0:T(8,128)(2,1)S(1)}, bf16[256,768]{1,0:T(8,128)(2,1)S(1)}, u32[]{:S(2)}, u32[]{:S(2)}) collective-permute-start(bf16[256,768]{1,0:T(8,128)(2,1)S(1)} %multiply_convert_fusion), channel_id=1, source_target_pairs={{0,16},{16,0},{1,17},{17,1},{2,18},{18,2},{3,19},{19,3},{4,20},{20... | collective-permute-start | bytes 1179656 | tf_op jit(solution)/shard_map/ppermute | solution.py:76
  154.1 18.1 %collective-permute-start.4 = (bf16[256,768]{1,0:T(8,128)(2,1)S(1)}, bf16[256,768]{1,0:T(8,128)(2,1)S(1)}, u32[]{:S(2)}, u32[]{:S(2)}) collective-permute-start(bf16[256,768]{1,0:T(8,128)(2,1)S(1)} %multiply_convert_fusion.1), channel_id=1, source_target_pairs={{0,16},{16,0},{1,17},{17,1},{2,18},{18,2},{3,19},{19,3},{4,20},{20... | collective-permute-start | bytes 1179656 | tf_op jit(solution)/shard_map/ppermute | solution.py:76
  164.2 11.7 %collective-permute-start.25 = (bf16[64,2048]{1,0:T(8,128)(2,1)S(1)}, bf16[64,2048]{1,0:T(8,128)(2,1)S(1)}, u32[]{:S(2)}, u32[]{:S(2)}) collective-permute-start(bf16[64,2048]{1,0:T(8,128)(2,1)S(1)} %fusion.68), channel_id=1, source_target_pairs={{0,2},{1,3},{2,0},{3,1},{4,6},{5,7},{6,4},{7,5},{8,10},{9,11},{10,... | collective-permute-start | bytes 786440 | tf_op jit(solution)/shard_map/ppermute | solution.py:73
  174.3 24.1 %collective-permute-start.37 = (bf16[64,2048]{1,0:T(8,128)(2,1)S(1)}, bf16[64,2048]{1,0:T(8,128)(2,1)S(1)}, u32[]{:S(2)}, u32[]{:S(2)}) collective-permute-start(bf16[64,2048]{1,0:T(8,128)(2,1)S(1)} %fusion.65), channel_id=1, source_target_pairs={{0,2},{1,3},{2,0},{3,1},{4,6},{5,7},{6,4},{7,5},{8,10},{9,11},{10,... | collective-permute-start | bytes 786440 | tf_op jit(solution)/shard_map/ppermute | solution.py:73
  176.3 22.1 %collective-permute-start.26 = (bf16[64,2048]{1,0:T(8,128)(2,1)S(1)}, bf16[64,2048]{1,0:T(8,128)(2,1)S(1)}, u32[]{:S(2)}, u32[]{:S(2)}) collective-permute-start(bf16[64,2048]{1,0:T(8,128)(2,1)S(1)} %fusion.72), channel_id=1, source_target_pairs={{0,4},{1,5},{2,6},{3,7},{4,0},{5,1},{6,2},{7,3},{8,12},{9,13},{10,... | collective-permute-start | bytes 786440 | tf_op jit(solution)/shard_map/ppermute | solution.py:73
  177.8 10.9 %collective-permute-start.14 = (bf16[64,2048]{1,0:T(8,128)(2,1)S(1)}, bf16[64,2048]{1,0:T(8,128)(2,1)S(1)}, u32[]{:S(2)}, u32[]{:S(2)}) collective-permute-start(bf16[64,2048]{1,0:T(8,128)(2,1)S(1)} %fusion.73), channel_id=1, source_target_pairs={{0,2},{1,3},{2,0},{3,1},{4,6},{5,7},{6,4},{7,5},{8,10},{9,11},{10,... | collective-permute-start | bytes 786440 | tf_op jit(solution)/shard_map/ppermute | solution.py:73
  196.6 18.3 %collective-permute-start.15 = (bf16[64,2048]{1,0:T(8,128)(2,1)S(1)}, bf16[64,2048]{1,0:T(8,128)(2,1)S(1)}, u32[]{:S(2)}, u32[]{:S(2)}) collective-permute-start(bf16[64,2048]{1,0:T(8,128)(2,1)S(1)} %fusion.75), channel_id=1, source_target_pairs={{0,12},{1,13},{2,14},{3,15},{4,8},{5,9},{6,10},{7,11},{8,4},{9,5},... | collective-permute-start | bytes 786440 | tf_op jit(solution)/shard_map/ppermute | solution.py:73
  198.3 21.2 %collective-permute-start.7 = (bf16[64,2048]{1,0:T(8,128)(2,1)S(1)}, bf16[64,2048]{1,0:T(8,128)(2,1)S(1)}, u32[]{:S(2)}, u32[]{:S(2)}) collective-permute-start(bf16[64,2048]{1,0:T(8,128)(2,1)S(1)} %fusion.80), channel_id=1, source_target_pairs={{0,8},{1,9},{2,10},{3,11},{4,12},{5,13},{6,14},{7,15},{8,0},{9,1},... | collective-permute-start | bytes 786440 | tf_op jit(solution)/shard_map/ppermute | solution.py:73
  (16 other events, 159.9 us)

commit v2 on v0

--- a/solution.py
+++ b/solution.py
@@ -1,6 +1,10 @@
+import functools
+
 import jax
 import jax.numpy as jnp
 from jax import lax
+from jax.experimental import pallas as pl
+from jax.experimental.pallas import tpu as pltpu
 from jax.sharding import PartitionSpec as P
 
 
@@ -15,7 +19,7 @@
     return (flat_ids * capacity + slot_index).reshape(tok_count, top_count)
 
 
-def body(tokens, expert_ids, gate_weights, gate_proj, up_proj, down_proj):
+def dispatch_body(tokens, expert_ids, gate_weights, gate_proj, up_proj, down_proj):
     tok_count, top_count = expert_ids.shape
     row_width = tokens.shape[1]
     sources = lax.axis_size("expert")
@@ -61,6 +65,348 @@
     return combined.astype(jnp.bfloat16)
 
 
+LANES = 128
+MIB = 1024 * 1024
+VMEM_LIMIT = 16 * MIB
+TOKEN = jax.ShapeDtypeStruct((8, LANES), jnp.float32)
+HERE = pl.BlockSpec(memory_space=pltpu.VMEM)
+FAR = pl.BlockSpec(memory_space=pltpu.HBM)
+
+
+def call(kernel, inputs, outputs, after, scratch=(), relays=(), room=VMEM_LIMIT):
+    inputs = [v if isinstance(v, tuple) else (v, HERE) for v in inputs]
+    flat = [value for group in relays for value in group]
+    joined = [
+        jax.ShapeDtypeStruct((sum(v.shape[0] for v in group),) + group[0].shape[1:], group[0].dtype)
+        for group in relays
+    ]
+
+    def run(*refs):
+        refs = list(refs)
+        taken = [refs.pop(0) for _ in inputs]
+        carried = [refs.pop(0) for _ in flat]
+        refs.pop(0)
+        made = [refs.pop(0) for _ in outputs]
+        joined_refs = [refs.pop(0) for _ in joined]
+        token_ref = refs.pop(0)
+        token_ref[...] = jnp.zeros(token_ref.shape, token_ref.dtype)
+        for group, out_ref in zip(relays, joined_refs, strict=True):
+            start = 0
+            for _ in group:
+                piece = carried.pop(0)
+                out_ref[start : start + piece.shape[0], :] = piece[...]
+                start += piece.shape[0]
+        if kernel is not None:
+            kernel(*taken, *made, *refs)
+
+    results = pl.pallas_call(
+        run,
+        in_specs=[spec for _, spec in inputs] + [HERE] * len(flat) + [pl.BlockSpec(memory_space=pl.ANY)],
+        out_specs=[HERE] * (len(outputs) + len(joined) + 1),
+        out_shape=list(outputs) + joined + [TOKEN],
+        scratch_shapes=list(scratch),
+        compiler_params=pltpu.CompilerParams(vmem_limit_bytes=room),
+        cost_estimate=pl.CostEstimate(flops=100_000_000_000, bytes_accessed=1, transcendentals=0),
+    )(*[value for value, _ in inputs], *flat, after)
+    return results[:-1], results[-1]
+
+
+def label_kernel(sources, tokens_ref, ids_ref, weights_ref, out_ref):
+    rows, width = tokens_ref.shape
+    out_ref[:, :width] = tokens_ref[...]
+    place = lax.broadcasted_iota(jnp.int32, (LANES, rows), 0)
+    weight = jnp.zeros((LANES, rows), jnp.float32)
+    for k in range(ids_ref.shape[0]):
+        weight += jnp.where(ids_ref[k : k + 1, :] == place % sources, weights_ref[k : k + 1, :], 0.0)
+    high = weight.astype(jnp.bfloat16).astype(jnp.float32)
+    mid = (weight - high).astype(jnp.bfloat16).astype(jnp.float32)
+    low = weight - high - mid
+    term = place // sources
+    picked = jnp.where(term == 0, high, jnp.where(term == 1, mid, jnp.where(term == 2, low, 0.0)))
+    out_ref[:, width:] = jnp.transpose(picked).astype(jnp.bfloat16)
+
+
+def load_kernel(mine, depth, gate_ref, up_ref, *refs):
+    *chunk, held_ref, total_ref, sems = refs
+    half = held_ref.shape[2]
+    owner = lax.axis_index("dp")
+    column = pl.multiple_of((owner if mine else 1 - owner) * half, LANES)
+    steps = held_ref.shape[1] // depth
+    copies = []
+    for n in range(steps):
+        for i, ref in enumerate((gate_ref, up_ref)):
+            copies.append(
+                pltpu.make_async_copy(
+                    ref.at[0, pl.ds(n * depth, depth), pl.ds(column, half)],
+                    held_ref.at[i, pl.ds(n * depth, depth), :],
+                    sems.at[n, i],
+                )
+            )
+            copies[-1].start()
+    for n in range(steps):
+        for i in range(2):
+            copies[2 * n + i].wait()
+            if not chunk:
+                continue
+            tokens_ref, out_ref = chunk
+            rows = tokens_ref.shape[0]
+            part = jnp.dot(
+                tokens_ref[:, n * depth : (n + 1) * depth],
+                held_ref[i, n * depth : (n + 1) * depth, :],
+                preferred_element_type=jnp.float32,
+            )
+            if n > 0:
+                part += total_ref[i]
+            if n < steps - 1:
+                total_ref[i] = part
+            else:
+                out_ref[i * rows : (i + 1) * rows, :] = part.astype(jnp.bfloat16)
+
+
+def collect(piece_refs, width, chunk_ref):
+    start = 0
+    for piece in piece_refs:
+        chunk_ref[start : start + piece.shape[0], :] = piece[:, :width]
+        start += piece.shape[0]
+
+
+def partial_kernel(pieces, riders, tile, *refs):
+    held_ref, *rider_refs, out_ref, chunk_ref = refs[pieces:]
+    rows, width = chunk_ref.shape
+    collect(refs[:pieces], width, chunk_ref)
+    start = 2 * rows
+    for ref in rider_refs:
+        out_ref[start : start + ref.shape[0], :] = ref[...]
+        start += ref.shape[0]
+
+    @pl.loop(0, held_ref.shape[2] // tile)
+    def _(n):
+        here = pl.ds(pl.multiple_of(n * tile, LANES), tile)
+        for i in range(2):
+            part = jnp.dot(chunk_ref[...], held_ref[i, :, here], preferred_element_type=jnp.float32)
+            out_ref[i * rows : (i + 1) * rows, here] = part.astype(jnp.bfloat16)
+
+
+def hidden_kernel(pieces, tile, *refs):
+    held_ref, arrived_ref, out_ref, chunk_ref = refs[pieces:]
+    rows, width = chunk_ref.shape
+    collect(refs[:pieces], width, chunk_ref)
+
+    @pl.loop(0, held_ref.shape[2] // tile)
+    def _(n):
+        here = pl.ds(pl.multiple_of(n * tile, LANES), tile)
+        gate_sum, up_sum = (
+            jnp.dot(chunk_ref[...], held_ref[i, :, here], preferred_element_type=jnp.float32)
+            + arrived_ref[i * rows : (i + 1) * rows, here].astype(jnp.float32)
+            for i in range(2)
+        )
+        out_ref[:, here] = (gate_sum / (1.0 + jnp.exp(-gate_sum)) * up_sum).astype(jnp.bfloat16)
+
+
+def output_kernel(pieces, sources, tile, behind, *refs):
+    mine_ref, other_ref, down_ref = refs[pieces : pieces + 3]
+    *out_refs, weight_ref = refs[pieces + 3 :]
+    start = 0
+    for piece in refs[:pieces]:
+        rows = piece.shape[0]
+        lane = lax.broadcasted_iota(jnp.int32, (rows, LANES), 1)
+        label = piece[:, piece.shape[1] - LANES :].astype(jnp.float32)
+        terms = jnp.where(lane % sources == lax.axis_index("expert"), label, 0.0)
+        weight_ref[start : start + rows, :] = jnp.sum(terms, axis=1, keepdims=True)
+        start += rows
+    count, half = mine_ref.shape
+    other = other_ref[behind : behind + count, :]
+    first = lax.axis_index("dp") * half
+    mine_rows = pl.ds(pl.multiple_of(first, LANES), half)
+    other_rows = pl.ds(pl.multiple_of(half - first, LANES), half)
+
+    @pl.loop(0, down_ref.shape[2] // tile)
+    def _(n):
+        here = pl.ds(pl.multiple_of(n * tile, LANES), tile)
+        out = jnp.dot(mine_ref[...], down_ref[0, mine_rows, here], preferred_element_type=jnp.float32)
+        out += jnp.dot(other, down_ref[0, other_rows, here], preferred_element_type=jnp.float32)
+        out *= weight_ref[...]
+        start = 0
+        for ref in out_refs:
+            ref[:, here] = out[start : start + ref.shape[0]].astype(ref.dtype)
+            start += ref.shape[0]
+
+
+def add_kernel(sums, *refs):
+    inputs = 1 + max(i for terms in sums for i, _ in terms)
+    for terms, out_ref in zip(sums, refs[inputs:], strict=True):
+        rows = out_ref.shape[0]
+        total = None
+        for i, start in terms:
+            value = refs[i][start : start + rows, :].astype(jnp.float32)
+            total = value if total is None else total + value
+        out_ref[...] = total.astype(out_ref.dtype)
+
+
+def gather_body(tokens, expert_ids, gate_weights, gate_proj, up_proj, down_proj):
+    rows, width = tokens.shape
+    sources = lax.axis_size("expert")
+    half = gate_proj.shape[2] // 2
+    tile = 256 if half % 256 == 0 else half
+    out_tile = 512 if width % 512 == 0 else width
+    depth = 512 if width % 512 == 0 else width
+
+    def swap(value, r):
+        return lax.ppermute(value, "expert", [(i, i ^ r) for i in range(sources)])
+
+    def cross(value):
+        return lax.ppermute(value, "dp", [(0, 1), (1, 0)])
+
+    def array(shape, dtype=jnp.bfloat16):
+        return jax.ShapeDtypeStruct(shape, dtype)
+
+    tail = [jnp.zeros(TOKEN.shape, TOKEN.dtype)]
+
+    def step(kernel, inputs, outputs, scratch=(), relays=(), room=VMEM_LIMIT):
+        results, tail[0] = call(kernel, inputs, outputs, tail[0], scratch, relays, room)
+        return results
+
+    def count(pieces):
+        return sum(p.shape[0] for p in pieces)
+
+    def load(mine, chunk, room):
+        made = [array((2 * rows, half))] if chunk else []
+        *sent, held = step(
+            functools.partial(load_kernel, mine, depth),
+            [(gate_proj, FAR), (up_proj, FAR), *chunk],
+            made + [array((2, width, half))],
+            [pltpu.VMEM((2, rows, half), jnp.float32), pltpu.SemaphoreType.DMA((width // depth, 2))],
+            room=room,
+        )
+        return held, *sent
+
+    def partials(pieces, riders=(), relays=()):
+        total = count(pieces)
+        sent, *relayed = step(
+            functools.partial(partial_kernel, len(pieces), len(riders), tile),
+            [*pieces, held_other, *riders],
+            [array((2 * total + count(riders), half))],
+            [pltpu.VMEM((total, width), jnp.bfloat16)],
+            relays,
+        )
+        return cross(sent), *relayed
+
+    def hidden(pieces, arrived, relays=()):
+        total = count(pieces)
+        mine, *relayed = step(
+            functools.partial(hidden_kernel, len(pieces), tile),
+            [*pieces, held_mine, arrived],
+            [array((total, half))],
+            [pltpu.VMEM((total, width), jnp.bfloat16)],
+            relays,
+        )
+        return mine, *relayed
+
+    def outputs(pieces, mine, arrived, behind, even, relays=()):
+        total = count(pieces)
+        made = [array((even, width), jnp.float32)] if even else []
+        made += [array((total - even, width))] if total > even else []
+        results = step(
+            functools.partial(output_kernel, len(pieces), sources, out_tile, behind),
+            [*pieces, mine, arrived, down_proj],
+            made,
+            [pltpu.VMEM((total, 1), jnp.float32)],
+            relays,
+        )
+        kept = results[0] if even else None
+        back = swap(results[len(made) - 1], 1) if total > even else None
+        return kept, back, *results[len(made) :]
+
+    def add(values, *sums, relays=()):
+        return step(
+            functools.partial(add_kernel, [terms for terms, _ in sums]),
+            values,
+            [shape for _, shape in sums],
+            relays=relays,
+        )
+
+    def relay(*groups):
+        return step(None, [], [], relays=[list(g) for g in groups])
+
+    one, two, wide = array((rows, width)), array((2 * rows, width)), array((rows, width), jnp.float32)
+    whole = [(0, 0), (1, 0)]
+
+    held_other, sent = load(False, [tokens], 52 * MIB)
+    y0 = cross(sent)
+    (labelled,) = step(
+        functools.partial(label_kernel, sources),
+        [tokens, expert_ids.T, gate_weights.T],
+        [array((rows, width + LANES))],
+    )
+    b1 = swap(labelled, 1)
+    z4, z8 = swap(labelled, 4), swap(labelled, 8)
+    (held_mine,) = load(True, [], 46 * MIB)
+    (y1,) = partials([b1])
+    (b4,) = relay([z4])
+    b5, x6 = swap(b4, 1), swap(b4, 2)
+    (h0,) = hidden([tokens], y0)
+    p2 = [b4, b5]
+    y2, again = partials(p2, [h0], relays=[[labelled]])
+    z12 = swap(again, 12)
+    (b8,) = relay([z8])
+    x10 = swap(b8, 2)
+    (h1,) = hidden([b1], y1)
+    (b8,) = relay([b8, x10])
+    b9 = swap(b8, 1)
+    b6, again = relay([x6], [labelled])
+    b7 = swap(b6, 1)
+    p3 = [b8, b9]
+    (y3,) = partials(p3, [h1])
+    (b12,) = relay([z12])
+    x14 = swap(b12, 2)
+    h2, again = hidden(p2, y2, relays=[[again]])
+    (b12,) = relay([b12, x14])
+    b13 = swap(b12, 1)
+    c0, _ = outputs([labelled], h0, y2, 4 * rows, rows)
+    p4 = [b12, b13]
+    y4, again = partials(p4, [h2], relays=[[again]])
+    x2 = swap(again, 2)
+    (h3,) = hidden(p3, y3)
+    p5 = [b6, b7]
+    (y5,) = partials(p5, [h3])
+    _, c1 = outputs([b1], h1, y3, 8 * rows, 0)
+    (b2,) = relay([x2])
+    b3 = swap(b2, 1)
+    (total,) = add([c0, c1], (whole, wide))
+    (h4,) = hidden(p4, y4)
+    t4 = cross(h4)
+    c4, c5 = outputs(p2, h2, y4, 8 * rows, rows)
+    p6 = [b2, b3]
+    (y6,) = partials(p6)
+    (sent,) = add([c4, c5], (whole, one))
+    s4 = swap(sent, 4)
+    (h5,) = hidden(p5, y5)
+    t5 = cross(h5)
+    c8, c9 = outputs(p3, h3, y5, 4 * rows, 2 * rows)
+    (total,) = add([total, s4], (whole, wide))
+    kept, sent = add([c8, c9], (whole, wide), ([(0, rows), (1, rows)], one))
+    x10 = swap(sent, 2)
+    c12, c13 = outputs(p4, h4, t4, 0, 2 * rows)
+    (sent,) = add([kept, x10], (whole, one))
+    s8 = swap(sent, 8)
+    kept, sent = add([c12, c13], (whole, wide), ([(0, rows), (1, rows)], one))
+    x14 = swap(sent, 2)
+    (h6,) = hidden(p6, y6)
+    t6 = cross(h6)
+    c6, c7 = outputs(p5, h5, t5, 0, rows)
+    (sent,) = add([kept, x14], (whole, one))
+    s12 = swap(sent, 12)
+    (sent,) = add([c6, c7], (whole, one))
+    s6 = swap(sent, 6)
+    c2, c3 = outputs(p6, h6, t6, 0, rows)
+    (total,) = add([total, s8], (whole, wide))
+    (sent,) = add([c2, c3], (whole, one))
+    s2 = swap(sent, 2)
+    (total,) = add([total, s12, s6], (whole + [(2, 0)], wide))
+    (total,) = add([total, s2], (whole, one))
+    return total
+
+
 def solution(mesh):
     placed = (
         P("expert", "dp"),
@@ -70,6 +416,15 @@
         P("expert", "dp", None),
         P("expert", None, "dp"),
     )
+
+    def body(tokens, expert_ids, gate_weights, gate_proj, up_proj, down_proj):
+        tok_count, top_count = expert_ids.shape
+        sources = lax.axis_size("expert")
+        whole_blocks = 2 * tok_count * top_count >= sources * tok_count
+        paired = lax.axis_size("dp") == 2 and sources == 16
+        plan = gather_body if whole_blocks and paired else dispatch_body
+        return plan(tokens, expert_ids, gate_weights, gate_proj, up_proj, down_proj)
+
     return jax.shard_map(
         body, mesh=mesh, in_specs=placed, out_specs=P("expert", "dp"), check_vma=False
     )

time: 406 us -> 173 us (0.43)
  the two profiles are of different devices: /device:TPU:8 before, /device:TPU:0 now
where the time goes in v2:
time: 173 us; the launch traced here: 172 us
  Pallas kernels  85.4 us (49%)
  waiting for transfers between devices  50.2 us (29%)
  starting transfers between devices  30.5 us (18%)
  local copies, waits for them, and re-layouts  5.56 us (3%)
    pallas_call x42, Pallas kernels, call(): pl.pallas_call(run, in_specs=[spec for _, spec in inputs] + [HERE] * len(...  85.4 us
    ppermute x26, waiting for transfers between devices, swap(): return lax.ppermute(value, 'expert', [(i, i ^ r) for i in range(sources)])  28.5 us
    ppermute x26, starting transfers between devices, swap(): return lax.ppermute(value, 'expert', [(i, i ^ r) for i in range(sources)])  21.9 us
    ppermute x10, waiting for transfers between devices, cross(): return lax.ppermute(value, 'dp', [(0, 1), (1, 0)])  21.7 us
    ppermute x10, starting transfers between devices, cross(): return lax.ppermute(value, 'dp', [(0, 1), (1, 0)])  8.59 us
    unnamed x64, local copies, waits for them, and re-layouts  5.56 us
  transfers between devices with their start and end apart: 36, of which 12 were waited for; matrix products, arithmetic and copies ran while one was open for 0% of the time, Pallas kernels for 45%

profile of v2, /device:TPU:0, one launch (start us, length us, event | category | flops | bytes accessed | tf_op | source)
XLA Modules:
  0.0 172.1 jit_solution(14972104409527608554)
XLA Ops:
  1.0 5.7 %shard_map.64 = (bf16[128,768]{1,0:T(8,128)(2,1)}, bf16[2,2048,768]{2,1,0:T(8,128)(2,1)}, f32[8,128]{1,0:T(8,128)S(1)}) custom-call(bf16[1,2048,1536]{2,1,0:T(8,128)(2,1)} %refs_0_.6, bf16[1,2048,1536]{2,1,0:T(8,128)(2,1)} %refs_1_.3, bf16[64,2048]{1,0:T(8,128)(2,1)S(1)} %copy-done.19, f32[8,128]{1,0:T(8,128)S(1)} %broadcast_in_dim.3.refs_3_), custom_call_target="tpu_custom_call" | custom-call | flops 99999997952 | bytes 1 | tf_op jit(solution)/shard_map/pallas_call | solution.py:102
  7.5 4.0 %collective-permute-start.6 = (bf16[64,2176]{1,0:T(8,128)(2,1)}, bf16[64,2176]{1,0:T(8,128)(2,1)}, u32[]{:S(2)}, u32[]{:S(2)}) collective-permute-start(bf16[64,2176]{1,0:T(8,128)(2,1)} %get-tuple-element.101.refs_4_.refs_1_.refs_0_), channel_id=1, source_target_pairs={{0,8},{1,9},{2,10},{3,11},{4,12},{5,13},{6,14},{7,15},{8,0},{9,1},... | collective-permute-start | bytes 835592 | tf_op jit(solution)/shard_map/ppermute | solution.py:255
  14.7 3.0 %shard_map.66 = (bf16[2,2048,768]{2,1,0:T(8,128)(2,1)S(1)}, f32[8,128]{1,0:T(8,128)S(1)}) custom-call(bf16[1,2048,1536]{2,1,0:T(8,128)(2,1)} %refs_0_.6, bf16[1,2048,1536]{2,1,0:T(8,128)(2,1)} %refs_1_.3, f32[8,128]{1,0:T(8,128)S(1)} %get-tuple-element.102.refs_2_), custom_call_target="tpu_custom_call" | custom-call | flops 99999997952 | bytes 1 | tf_op jit(solution)/shard_map/pallas_call | solution.py:102
  21.5 4.3 %collective-permute-done.1.refs_0_ = bf16[64,2176]{1,0:T(8,128)(2,1)} collective-permute-done((bf16[64,2176]{1,0:T(8,128)(2,1)}, bf16[64,2176]{1,0:T(8,128)(2,1)}, u32[]{:S(2)}, u32[]{:S(2)}) %collective-permute-start.1) | collective-permute-done | bytes 278560 | tf_op jit(solution)/shard_map/ppermute | solution.py:255
  33.1 3.4 %shard_map.70 = (bf16[320,768]{1,0:T(8,128)(2,1)}, bf16[64,2176]{1,0:T(8,128)(2,1)}, f32[8,128]{1,0:T(8,128)S(1)}) custom-call(bf16[64,2176]{1,0:T(8,128)(2,1)} %get-tuple-element.110.refs_0_, bf16[64,2176]{1,0:T(8,128)(2,1)S(1)} %collective-permute-done.3.refs_1_, bf16[2,2048,768]{2,1,0:T(8,128)(2,1)S(1)} %copy-done.23, ...), custom_call_target="tpu_custom_call" | custom-call | flops 99999997952 | bytes 1 | tf_op jit(solution)/shard_map/pallas_call | solution.py:102
  43.5 2.8 %collective-permute-done.7.refs_1_ = bf16[64,2176]{1,0:T(8,128)(2,1)S(1)} collective-permute-done((bf16[64,2176]{1,0:T(8,128)(2,1)S(1)}, bf16[64,2176]{1,0:T(8,128)(2,1)S(1)}, u32[]{:S(2)}, u32[]{:S(2)}) %collective-permute-start.7) | collective-permute-done | bytes 278560 | tf_op jit(solution)/shard_map/ppermute | solution.py:255
  48.8 3.2 %shard_map.75 = (bf16[576,768]{1,0:T(8,128)(2,1)}, f32[8,128]{1,0:T(8,128)S(1)}) custom-call(bf16[128,2176]{1,0:T(8,128)(2,1)S(1)} %get-tuple-element.119.refs_0_, bf16[128,2176]{1,0:T(8,128)(2,1)S(1)} %collective-permute-done.9.refs_1_, bf16[2,2048,768]{2,1,0:T(8,128)(2,1)S(1)} %copy-done.23, bf16[64,768]{1,0:T(8,128)(2,1)S(1)} %get-tuple-element.120.refs_3_.refs_1_, ...), custom_call_target="tpu_custom_call" | custom-call | flops 99999997952 | bytes 1 | tf_op jit(solution)/shard_map/pallas_call | solution.py:102
  54.0 2.6 %shard_map.77 = (bf16[128,768]{1,0:T(8,128)(2,1)S(1)}, bf16[64,2176]{1,0:T(8,128)(2,1)S(1)}, f32[8,128]{1,0:T(8,128)S(1)}) custom-call(bf16[64,2176]{1,0:T(8,128)(2,1)} %get-tuple-element.110.refs_0_, bf16[64,2176]{1,0:T(8,128)(2,1)S(1)} %copy-done.17, bf16[2,2048,768]{2,1,0:T(8,128)(2,1)S(1)} %get-tuple-element.103.refs_1_.refs_2_, ...), custom_call_target="tpu_custom_call" | custom-call | flops 99999997952 | bytes 1 | tf_op jit(solution)/shard_map/pallas_call | solution.py:102
  56.7 5.0 %collective-permute-done.11.refs_1_ = bf16[64,2176]{1,0:T(8,128)(2,1)S(1)} collective-permute-done((bf16[64,2176]{1,0:T(8,128)(2,1)S(1)}, bf16[64,2176]{1,0:T(8,128)(2,1)S(1)}, u32[]{:S(2)}, u32[]{:S(2)}) %collective-permute-start.11) | collective-permute-done | bytes 278560 | tf_op jit(solution)/shard_map/ppermute | solution.py:255
  61.9 2.9 %copy-done = bf16[1,1536,2048]{2,1,0:T(8,128)(2,1)S(1)} copy-done((bf16[1,1536,2048]{2,1,0:T(8,128)(2,1)S(1)}, bf16[1,1536,2048]{2,1,0:T(8,128)(2,1)}, u32[]{:S(2)}) %copy-start) | copy-done | bytes 6291480
  64.7 2.8 %shard_map.79 = (f32[64,2048]{1,0:T(8,128)S(1)}, f32[8,128]{1,0:T(8,128)S(1)}) custom-call(bf16[64,2176]{1,0:T(8,128)(2,1)} %get-tuple-element.101.refs_4_.refs_1_.refs_0_, bf16[64,768]{1,0:T(8,128)(2,1)S(1)} %copy-done.31, bf16[320,768]{1,0:T(8,128)(2,1)} %collective-permute-done.4.refs_3_.refs_2_, bf16[1,1536,2048]{2,1,0:T(8,128)(2,1)S(1)} %copy-done, ...), custom_call_target="tpu_custom_call" | custom-call | flops 99999997952 | bytes 1 | tf_op jit(solution)/shard_map/pallas_call | solution.py:102
  67.6 3.2 %shard_map.80 = (bf16[640,768]{1,0:T(8,128)(2,1)}, bf16[64,2176]{1,0:T(8,128)(2,1)}, f32[8,128]{1,0:T(8,128)S(1)}) custom-call(bf16[128,2176]{1,0:T(8,128)(2,1)S(1)} %get-tuple-element.132.refs_0_, bf16[128,2176]{1,0:T(8,128)(2,1)S(1)} %collective-permute-done.14.refs_1_, bf16[2,2048,768]{2,1,0:T(8,128)(2,1)S(1)} %copy-done.23, ...), custom_call_target="tpu_custom_call" | custom-call | flops 99999997952 | bytes 1 | tf_op jit(solution)/shard_map/pallas_call | solution.py:102
  71.8 4.6 %collective-permute-done.12.refs_3_.refs_2_ = bf16[576,768]{1,0:T(8,128)(2,1)} collective-permute-done((bf16[576,768]{1,0:T(8,128)(2,1)}, bf16[576,768]{1,0:T(8,128)(2,1)}, u32[]{:S(2)}, u32[]{:S(2)}) %collective-permute-start.12) | collective-permute-done | bytes 884768 | tf_op jit(solution)/shard_map/ppermute | solution.py:258
  76.4 3.5 %shard_map.81 = (bf16[256,768]{1,0:T(8,128)(2,1)S(1)}, f32[8,128]{1,0:T(8,128)S(1)}) custom-call(bf16[128,2176]{1,0:T(8,128)(2,1)S(1)} %copy-done.5, bf16[128,2176]{1,0:T(8,128)(2,1)S(1)} %copy-done.8, bf16[2,2048,768]{2,1,0:T(8,128)(2,1)S(1)} %get-tuple-element.103.refs_1_.refs_2_, bf16[576,768]{1,0:T(8,128)(2,1)} %collective-permute-done.12.refs_3_.refs_2_, ...), custom_call_target="tpu_custom_call" | custom-call | flops 99999997952 | bytes 1 | tf_op jit(solution)/shard_map/pallas_call | solution.py:102
  80.0 3.5 %shard_map.82 = (bf16[512,768]{1,0:T(8,128)(2,1)}, f32[8,128]{1,0:T(8,128)S(1)}) custom-call(bf16[64,2176]{1,0:T(8,128)(2,1)} %get-tuple-element.131.refs_0_, bf16[64,2176]{1,0:T(8,128)(2,1)} %collective-permute-done.13.refs_1_, bf16[2,2048,768]{2,1,0:T(8,128)(2,1)S(1)} %copy-done.23, bf16[256,768]{1,0:T(8,128)(2,1)S(1)} %get-tuple-element.137.refs_3_.refs_2_, ...), custom_call_target="tpu_custom_call" | custom-call | flops 99999997952 | bytes 1 | tf_op jit(solution)/shard_map/pallas_call | solution.py:102
  83.6 2.8 %shard_map.83 = (bf16[64,2048]{1,0:T(8,128)(2,1)S(1)}, f32[8,128]{1,0:T(8,128)S(1)}) custom-call(bf16[64,2176]{1,0:T(8,128)(2,1)S(1)} %collective-permute-done.2.refs_0_, bf16[64,768]{1,0:T(8,128)(2,1)S(1)} %copy-done.29, bf16[576,768]{1,0:T(8,128)(2,1)} %collective-permute-done.12.refs_3_.refs_2_, bf16[1,1536,2048]{2,1,0:T(8,128)(2,1)S(1)} %copy-done.1, ...), custom_call_target="tpu_custom_call" | custom-call | flops 99999997952 | bytes 1 | tf_op jit(solution)/shard_map/pallas_call | solution.py:102
  88.9 8.6 %collective-permute-done.17.refs_3_ = bf16[640,768]{1,0:T(8,128)(2,1)} collective-permute-done((bf16[640,768]{1,0:T(8,128)(2,1)}, bf16[640,768]{1,0:T(8,128)(2,1)}, u32[]{:S(2)}, u32[]{:S(2)}) %collective-permute-start.17) | collective-permute-done | bytes 983072 | tf_op jit(solution)/shard_map/ppermute | solution.py:258
  97.5 4.5 %shard_map.86 = (bf16[256,768]{1,0:T(8,128)(2,1)}, f32[8,128]{1,0:T(8,128)S(1)}) custom-call(bf16[128,2176]{1,0:T(8,128)(2,1)S(1)} %copy-done.11, bf16[128,2176]{1,0:T(8,128)(2,1)S(1)} %copy-done.14, bf16[2,2048,768]{2,1,0:T(8,128)(2,1)S(1)} %get-tuple-element.103.refs_1_.refs_2_, bf16[640,768]{1,0:T(8,128)(2,1)} %collective-permute-done.17.refs_3_, ...), custom_call_target="tpu_custom_call" | custom-call | flops 99999997952 | bytes 1 | tf_op jit(solution)/shard_map/pallas_call | solution.py:102
  102.0 3.0 %shard_map.87 = (f32[64,2048]{1,0:T(8,128)S(1)}, bf16[64,2048]{1,0:T(8,128)(2,1)S(1)}, f32[8,128]{1,0:T(8,128)S(1)}) custom-call(bf16[64,2176]{1,0:T(8,128)(2,1)} %get-tuple-element.110.refs_0_, bf16[64,2176]{1,0:T(8,128)(2,1)S(1)} %copy-done.18, bf16[128,768]{1,0:T(8,128)(2,1)S(1)} %copy-done.27, bf16[640,768]{1,0:T(8,128)(2,1)} %collective-permute-done.17.refs_3_, ...), custom_call_target="tpu_custom_call" | custom-call | flops 99999997952 | bytes 1 | tf_op jit(solution)/shard_map/pallas_call | solution.py:102
  105.1 3.2 %shard_map.88 = (bf16[256,768]{1,0:T(8,128)(2,1)}, f32[8,128]{1,0:T(8,128)S(1)}) custom-call(bf16[64,2176]{1,0:T(8,128)(2,1)} %get-tuple-element.150.refs_0_, bf16[64,2176]{1,0:T(8,128)(2,1)} %collective-permute-done.19.refs_1_, bf16[2,2048,768]{2,1,0:T(8,128)(2,1)S(1)} %copy-done.23, f32[8,128]{1,0:T(8,128)S(1)} %get-tuple-element.151.refs_3_), custom_call_target="tpu_custom_call" | custom-call | flops 99999997952 | bytes 1 | tf_op jit(solution)/shard_map/pallas_call | solution.py:102
  110.4 4.0 %collective-permute-done.21.refs_3_ = bf16[512,768]{1,0:T(8,128)(2,1)} collective-permute-done((bf16[512,768]{1,0:T(8,128)(2,1)}, bf16[512,768]{1,0:T(8,128)(2,1)}, u32[]{:S(2)}, u32[]{:S(2)}) %collective-permute-start.21) | collective-permute-done | bytes 786464 | tf_op jit(solution)/shard_map/ppermute | solution.py:258
  114.4 3.6 %shard_map.90 = (bf16[128,768]{1,0:T(8,128)(2,1)}, f32[8,128]{1,0:T(8,128)S(1)}) custom-call(bf16[64,2176]{1,0:T(8,128)(2,1)} %get-tuple-element.131.refs_0_, bf16[64,2176]{1,0:T(8,128)(2,1)} %collective-permute-done.13.refs_1_, bf16[2,2048,768]{2,1,0:T(8,128)(2,1)S(1)} %get-tuple-element.103.refs_1_.refs_2_, ...), custom_call_target="tpu_custom_call" | custom-call | flops 99999997952 | bytes 1 | tf_op jit(solution)/shard_map/pallas_call | solution.py:102
  119.0 3.6 %shard_map.91 = (f32[128,2048]{1,0:T(8,128)S(1)}, bf16[128,2048]{1,0:T(8,128)(2,1)S(1)}, f32[8,128]{1,0:T(8,128)S(1)}) custom-call(bf16[128,2176]{1,0:T(8,128)(2,1)S(1)} %copy-done.6, bf16[128,2176]{1,0:T(8,128)(2,1)S(1)} %copy-done.9, bf16[256,768]{1,0:T(8,128)(2,1)S(1)} %copy-done.25, bf16[512,768]{1,0:T(8,128)(2,1)} %collective-permute-done.21.refs_3_, ...), custom_call_target="tpu_custom_call" | custom-call | flops 99999997952 | bytes 1 | tf_op jit(solution)/shard_map/pallas_call | solution.py:102
  126.6 4.6 %collective-permute-done.24.refs_3_ = bf16[256,768]{1,0:T(8,128)(2,1)} collective-permute-done((bf16[256,768]{1,0:T(8,128)(2,1)}, bf16[256,768]{1,0:T(8,128)(2,1)}, u32[]{:S(2)}, u32[]{:S(2)}) %collective-permute-start.24) | collective-permute-done | bytes 393248 | tf_op jit(solution)/shard_map/ppermute | solution.py:258
  131.2 3.6 %shard_map.94 = (f32[128,2048]{1,0:T(8,128)S(1)}, bf16[128,2048]{1,0:T(8,128)(2,1)S(1)}, f32[8,128]{1,0:T(8,128)S(1)}) custom-call(bf16[128,2176]{1,0:T(8,128)(2,1)S(1)} %copy-done.12, bf16[128,2176]{1,0:T(8,128)(2,1)S(1)} %copy-done.15, bf16[256,768]{1,0:T(8,128)(2,1)} %get-tuple-element.164.refs_2_, bf16[256,768]{1,0:T(8,128)(2,1)} %collective-permute-done.24.refs_3_, ...), custom_call_target="tpu_custom_call" | custom-call | flops 99999997952 | bytes 1 | tf_op jit(solution)/shard_map/pallas_call | solution.py:102
  136.9 3.4 %shard_map.97 = (bf16[128,768]{1,0:T(8,128)(2,1)}, f32[8,128]{1,0:T(8,128)S(1)}) custom-call(bf16[64,2176]{1,0:T(8,128)(2,1)} %get-tuple-element.150.refs_0_, bf16[64,2176]{1,0:T(8,128)(2,1)} %collective-permute-done.19.refs_1_, bf16[2,2048,768]{2,1,0:T(8,128)(2,1)S(1)} %get-tuple-element.103.refs_1_.refs_2_, ...), custom_call_target="tpu_custom_call" | custom-call | flops 99999997952 | bytes 1 | tf_op jit(solution)/shard_map/pallas_call | solution.py:102
  142.9 2.9 %shard_map.98 = (f32[64,2048]{1,0:T(8,128)S(1)}, bf16[64,2048]{1,0:T(8,128)(2,1)S(1)}, f32[8,128]{1,0:T(8,128)S(1)}) custom-call(bf16[64,2176]{1,0:T(8,128)(2,1)} %get-tuple-element.131.refs_0_, bf16[64,2176]{1,0:T(8,128)(2,1)} %collective-permute-done.13.refs_1_, bf16[128,768]{1,0:T(8,128)(2,1)} %get-tuple-element.174.refs_2_, ...), custom_call_target="tpu_custom_call" | custom-call | flops 99999997952 | bytes 1 | tf_op jit(solution)/shard_map/pallas_call | solution.py:102
  145.8 2.9 %collective-permute-done.31.refs_1_ = bf16[64,2048]{1,0:T(8,128)(2,1)S(1)} collective-permute-done((bf16[64,2048]{1,0:T(8,128)(2,1)S(1)}, bf16[64,2048]{1,0:T(8,128)(2,1)S(1)}, u32[]{:S(2)}, u32[]{:S(2)}) %collective-permute-start.31) | collective-permute-done | bytes 262176 | tf_op jit(solution)/shard_map/ppermute | solution.py:255
  150.3 2.8 %shard_map.101 = (f32[64,2048]{1,0:T(8,128)S(1)}, bf16[64,2048]{1,0:T(8,128)(2,1)S(1)}, f32[8,128]{1,0:T(8,128)S(1)}) custom-call(bf16[64,2176]{1,0:T(8,128)(2,1)} %get-tuple-element.150.refs_0_, bf16[64,2176]{1,0:T(8,128)(2,1)} %collective-permute-done.19.refs_1_, bf16[128,768]{1,0:T(8,128)(2,1)} %get-tuple-element.173.refs_2_, ...), custom_call_target="tpu_custom_call" | custom-call | flops 99999997952 | bytes 1 | tf_op jit(solution)/shard_map/pallas_call | solution.py:102
  153.2 3.0 %collective-permute-start.33 = (bf16[64,2048]{1,0:T(8,128)(2,1)}, bf16[64,2048]{1,0:T(8,128)(2,1)}, u32[]{:S(2)}, u32[]{:S(2)}) collective-permute-start(bf16[64,2048]{1,0:T(8,128)(2,1)} %get-tuple-element.186), channel_id=1, source_target_pairs={{0,6},{1,7},{2,4},{3,5},{4,2},{5,3},{6,0},{7,1},{8,14},{9,15},{10,... | collective-permute-start | bytes 786440 | tf_op jit(solution)/shard_map/ppermute | solution.py:255
  159.2 4.3 %collective-permute-done.33.refs_2_ = bf16[64,2048]{1,0:T(8,128)(2,1)} collective-permute-done((bf16[64,2048]{1,0:T(8,128)(2,1)}, bf16[64,2048]{1,0:T(8,128)(2,1)}, u32[]{:S(2)}, u32[]{:S(2)}) %collective-permute-start.33) | collective-permute-done | bytes 262176 | tf_op jit(solution)/shard_map/ppermute | solution.py:255
  163.6 6.6 %collective-permute-done.32.refs_1_ = bf16[64,2048]{1,0:T(8,128)(2,1)} collective-permute-done((bf16[64,2048]{1,0:T(8,128)(2,1)}, bf16[64,2048]{1,0:T(8,128)(2,1)}, u32[]{:S(2)}, u32[]{:S(2)}) %collective-permute-start.32) | collective-permute-done | bytes 262176 | tf_op jit(solution)/shard_map/ppermute | solution.py:255
  (147 shorter events, 49.7 us)
Async XLA Ops:
  7.5 29.0 %collective-permute-start.6 = (bf16[64,2176]{1,0:T(8,128)(2,1)}, bf16[64,2176]{1,0:T(8,128)(2,1)}, u32[]{:S(2)}, u32[]{:S(2)}) collective-permute-start(bf16[64,2176]{1,0:T(8,128)(2,1)} %get-tuple-element.101.refs_4_.refs_1_.refs_0_), channel_id=1, source_target_pairs={{0,8},{1,9},{2,10},{3,11},{4,12},{5,13},{6,14},{7,15},{8,0},{9,1},... | collective-permute-start | bytes 835592 | tf_op jit(solution)/shard_map/ppermute | solution.py:255
  11.6 6.1 %collective-permute-start.2 = (bf16[64,2176]{1,0:T(8,128)(2,1)}, bf16[64,2176]{1,0:T(8,128)(2,1)S(1)}, u32[]{:S(2)}, u32[]{:S(2)}) collective-permute-start(bf16[64,2176]{1,0:T(8,128)(2,1)} %get-tuple-element.101.refs_4_.refs_1_.refs_0_), channel_id=1, source_target_pairs={{0,1},{1,0},{2,3},{3,2},{4,5},{5,4},{6,7},{7,6},{8,9},{9,8},{10,11... | collective-permute-start | bytes 835592 | tf_op jit(solution)/shard_map/ppermute | solution.py:255
  11.6 14.2 %collective-permute-start.1 = (bf16[64,2176]{1,0:T(8,128)(2,1)}, bf16[64,2176]{1,0:T(8,128)(2,1)}, u32[]{:S(2)}, u32[]{:S(2)}) collective-permute-start(bf16[64,2176]{1,0:T(8,128)(2,1)} %get-tuple-element.101.refs_4_.refs_1_.refs_0_), channel_id=1, source_target_pairs={{0,4},{1,5},{2,6},{3,7},{4,0},{5,1},{6,2},{7,3},{8,12},{9,13},{10,... | collective-permute-start | bytes 835592 | tf_op jit(solution)/shard_map/ppermute | solution.py:255
  13.1 17.4 %collective-permute-start = (bf16[128,768]{1,0:T(8,128)(2,1)}, bf16[128,768]{1,0:T(8,128)(2,1)}, u32[]{:S(2)}, u32[]{:S(2)}) collective-permute-start(bf16[128,768]{1,0:T(8,128)(2,1)} %get-tuple-element.104), channel_id=1, source_target_pairs={{0,16},{16,0},{1,17},{17,1},{2,18},{18,2},{3,19},{19,3},{4,20},{20... | collective-permute-start | bytes 589832 | tf_op jit(solution)/shard_map/ppermute | solution.py:258
  27.5 19.0 %collective-permute-start.10 = (bf16[64,2176]{1,0:T(8,128)(2,1)}, bf16[64,2176]{1,0:T(8,128)(2,1)}, u32[]{:S(2)}, u32[]{:S(2)}) collective-permute-start(bf16[64,2176]{1,0:T(8,128)(2,1)} %get-tuple-element.110.refs_0_), channel_id=1, source_target_pairs={{0,2},{1,3},{2,0},{3,1},{4,6},{5,7},{6,4},{7,5},{8,10},{9,11},{10,... | collective-permute-start | bytes 835592 | tf_op jit(solution)/shard_map/ppermute | solution.py:255
  29.0 4.0 %collective-permute-start.3 = (bf16[64,2176]{1,0:T(8,128)(2,1)}, bf16[64,2176]{1,0:T(8,128)(2,1)S(1)}, u32[]{:S(2)}, u32[]{:S(2)}) collective-permute-start(bf16[64,2176]{1,0:T(8,128)(2,1)} %get-tuple-element.110.refs_0_), channel_id=1, source_target_pairs={{0,1},{1,0},{2,3},{3,2},{4,5},{5,4},{6,7},{7,6},{8,9},{9,8},{10,11... | collective-permute-start | bytes 835592 | tf_op jit(solution)/shard_map/ppermute | solution.py:255
  29.1 12.0 %collective-permute-start.8 = (bf16[128,768]{1,0:T(8,128)(2,1)}, bf16[128,768]{1,0:T(8,128)(2,1)}, u32[]{:S(2)}, u32[]{:S(2)}) collective-permute-start(bf16[128,768]{1,0:T(8,128)(2,1)} %get-tuple-element.116), channel_id=1, source_target_pairs={{0,16},{16,0},{1,17},{17,1},{2,18},{18,2},{3,19},{19,3},{4,20},{20... | collective-permute-start | bytes 589832 | tf_op jit(solution)/shard_map/ppermute | solution.py:258
  37.5 8.9 %collective-permute-start.7 = (bf16[64,2176]{1,0:T(8,128)(2,1)S(1)}, bf16[64,2176]{1,0:T(8,128)(2,1)S(1)}, u32[]{:S(2)}, u32[]{:S(2)}) collective-permute-start(bf16[64,2176]{1,0:T(8,128)(2,1)S(1)} %get-tuple-element.115.refs_0_), channel_id=1, source_target_pairs={{0,2},{1,3},{2,0},{3,1},{4,6},{5,7},{6,4},{7,5},{8,10},{9,11},{10,... | collective-permute-start | bytes 835592 | tf_op jit(solution)/shard_map/ppermute | solution.py:255
  38.1 13.9 %collective-permute-start.5 = (bf16[64,2176]{1,0:T(8,128)(2,1)}, bf16[64,2176]{1,0:T(8,128)(2,1)}, u32[]{:S(2)}, u32[]{:S(2)}) collective-permute-start(bf16[64,2176]{1,0:T(8,128)(2,1)} %get-tuple-element.113), channel_id=1, source_target_pairs={{0,12},{1,13},{2,14},{3,15},{4,8},{5,9},{6,10},{7,11},{8,4},{9,5},... | collective-permute-start | bytes 835592 | tf_op jit(solution)/shard_map/ppermute | solution.py:255
  40.5 13.5 %collective-permute-start.4 = (bf16[320,768]{1,0:T(8,128)(2,1)}, bf16[320,768]{1,0:T(8,128)(2,1)}, u32[]{:S(2)}, u32[]{:S(2)}) collective-permute-start(bf16[320,768]{1,0:T(8,128)(2,1)} %get-tuple-element.112), channel_id=1, source_target_pairs={{0,16},{16,0},{1,17},{17,1},{2,18},{18,2},{3,19},{19,3},{4,20},{20... | collective-permute-start | bytes 1474568 | tf_op jit(solution)/shard_map/ppermute | solution.py:258
  48.4 31.6 %collective-permute-start.13 = (bf16[64,2176]{1,0:T(8,128)(2,1)}, bf16[64,2176]{1,0:T(8,128)(2,1)}, u32[]{:S(2)}, u32[]{:S(2)}) collective-permute-start(bf16[64,2176]{1,0:T(8,128)(2,1)} %get-tuple-element.131.refs_0_), channel_id=1, source_target_pairs={{0,1},{1,0},{2,3},{3,2},{4,5},{5,4},{6,7},{7,6},{8,9},{9,8},{10,11... | collective-permute-start | bytes 835592 | tf_op jit(solution)/shard_map/ppermute | solution.py:255
  53.0 8.8 %collective-permute-start.11 = (bf16[64,2176]{1,0:T(8,128)(2,1)S(1)}, bf16[64,2176]{1,0:T(8,128)(2,1)S(1)}, u32[]{:S(2)}, u32[]{:S(2)}) collective-permute-start(bf16[64,2176]{1,0:T(8,128)(2,1)S(1)} %get-tuple-element.124.refs_0_), channel_id=1, source_target_pairs={{0,2},{1,3},{2,0},{3,1},{4,6},{5,7},{6,4},{7,5},{8,10},{9,11},{10,... | collective-permute-start | bytes 835592 | tf_op jit(solution)/shard_map/ppermute | solution.py:255
  53.6 22.8 %collective-permute-start.12 = (bf16[576,768]{1,0:T(8,128)(2,1)}, bf16[576,768]{1,0:T(8,128)(2,1)}, u32[]{:S(2)}, u32[]{:S(2)}) collective-permute-start(bf16[576,768]{1,0:T(8,128)(2,1)} %get-tuple-element.130), channel_id=1, source_target_pairs={{0,16},{16,0},{1,17},{17,1},{2,18},{18,2},{3,19},{19,3},{4,20},{20... | collective-permute-start | bytes 2654216 | tf_op jit(solution)/shard_map/ppermute | solution.py:258
  61.8 5.7 %collective-permute-start.14 = (bf16[128,2176]{1,0:T(8,128)(2,1)S(1)}, bf16[128,2176]{1,0:T(8,128)(2,1)S(1)}, u32[]{:S(2)}, u32[]{:S(2)}) collective-permute-start(bf16[128,2176]{1,0:T(8,128)(2,1)S(1)} %get-tuple-element.132.refs_0_), channel_id=1, source_target_pairs={{0,1},{1,0},{2,3},{3,2},{4,5},{5,4},{6,7},{7,6},{8,9},{9,8},{10,11... | collective-permute-start | bytes 1671176 | tf_op jit(solution)/shard_map/ppermute | solution.py:255
  70.8 16.2 %collective-permute-start.16 = (bf16[64,2176]{1,0:T(8,128)(2,1)}, bf16[64,2176]{1,0:T(8,128)(2,1)}, u32[]{:S(2)}, u32[]{:S(2)}) collective-permute-start(bf16[64,2176]{1,0:T(8,128)(2,1)} %get-tuple-element.141), channel_id=1, source_target_pairs={{0,2},{1,3},{2,0},{3,1},{4,6},{5,7},{6,4},{7,5},{8,10},{9,11},{10,... | collective-permute-start | bytes 835592 | tf_op jit(solution)/shard_map/ppermute | solution.py:255
  71.4 26.1 %collective-permute-start.17 = (bf16[640,768]{1,0:T(8,128)(2,1)}, bf16[640,768]{1,0:T(8,128)(2,1)}, u32[]{:S(2)}, u32[]{:S(2)}) collective-permute-start(bf16[640,768]{1,0:T(8,128)(2,1)} %get-tuple-element.145), channel_id=1, source_target_pairs={{0,16},{16,0},{1,17},{17,1},{2,18},{18,2},{3,19},{19,3},{4,20},{20... | collective-permute-start | bytes 2949128 | tf_op jit(solution)/shard_map/ppermute | solution.py:258
  86.5 27.9 %collective-permute-start.21 = (bf16[512,768]{1,0:T(8,128)(2,1)}, bf16[512,768]{1,0:T(8,128)(2,1)}, u32[]{:S(2)}, u32[]{:S(2)}) collective-permute-start(bf16[512,768]{1,0:T(8,128)(2,1)} %get-tuple-element.154), channel_id=1, source_target_pairs={{0,16},{16,0},{1,17},{17,1},{2,18},{18,2},{3,19},{19,3},{4,20},{20... | collective-permute-start | bytes 2359304 | tf_op jit(solution)/shard_map/ppermute | solution.py:258
  88.7 16.4 %collective-permute-start.19 = (bf16[64,2176]{1,0:T(8,128)(2,1)}, bf16[64,2176]{1,0:T(8,128)(2,1)}, u32[]{:S(2)}, u32[]{:S(2)}) collective-permute-start(bf16[64,2176]{1,0:T(8,128)(2,1)} %get-tuple-element.150.refs_0_), channel_id=1, source_target_pairs={{0,1},{1,0},{2,3},{3,2},{4,5},{5,4},{6,7},{7,6},{8,9},{9,8},{10,11... | collective-permute-start | bytes 835592 | tf_op jit(solution)/shard_map/ppermute | solution.py:255
  105.0 5.3 %collective-permute-start.18 = (bf16[64,2048]{1,0:T(8,128)(2,1)S(1)}, bf16[64,2048]{1,0:T(8,128)(2,1)S(1)}, u32[]{:S(2)}, u32[]{:S(2)}) collective-permute-start(bf16[64,2048]{1,0:T(8,128)(2,1)S(1)} %get-tuple-element.149), channel_id=1, source_target_pairs={{0,1},{1,0},{2,3},{3,2},{4,5},{5,4},{6,7},{7,6},{8,9},{9,8},{10,11... | collective-permute-start | bytes 786440 | tf_op jit(solution)/shard_map/ppermute | solution.py:255
  108.3 28.6 %collective-permute-start.26 = (bf16[256,768]{1,0:T(8,128)(2,1)}, bf16[256,768]{1,0:T(8,128)(2,1)}, u32[]{:S(2)}, u32[]{:S(2)}) collective-permute-start(bf16[256,768]{1,0:T(8,128)(2,1)} %get-tuple-element.168), channel_id=1, source_target_pairs={{0,16},{16,0},{1,17},{17,1},{2,18},{18,2},{3,19},{19,3},{4,20},{20... | collective-permute-start | bytes 1179656 | tf_op jit(solution)/shard_map/ppermute | solution.py:258
  108.7 22.5 %collective-permute-start.24 = (bf16[256,768]{1,0:T(8,128)(2,1)}, bf16[256,768]{1,0:T(8,128)(2,1)}, u32[]{:S(2)}, u32[]{:S(2)}) collective-permute-start(bf16[256,768]{1,0:T(8,128)(2,1)} %get-tuple-element.164.refs_2_), channel_id=1, source_target_pairs={{0,16},{16,0},{1,17},{17,1},{2,18},{18,2},{3,19},{19,3},{4,20},{20... | collective-permute-start | bytes 1179656 | tf_op jit(solution)/shard_map/ppermute | solution.py:258
  118.0 24.9 %collective-permute-start.29 = (bf16[128,768]{1,0:T(8,128)(2,1)}, bf16[128,768]{1,0:T(8,128)(2,1)}, u32[]{:S(2)}, u32[]{:S(2)}) collective-permute-start(bf16[128,768]{1,0:T(8,128)(2,1)} %get-tuple-element.174.refs_2_), channel_id=1, source_target_pairs={{0,16},{16,0},{1,17},{17,1},{2,18},{18,2},{3,19},{19,3},{4,20},{20... | collective-permute-start | bytes 589832 | tf_op jit(solution)/shard_map/ppermute | solution.py:258
  118.4 6.4 %collective-permute-start.20 = (bf16[64,2048]{1,0:T(8,128)(2,1)S(1)}, bf16[64,2048]{1,0:T(8,128)(2,1)S(1)}, u32[]{:S(2)}, u32[]{:S(2)}) collective-permute-start(bf16[64,2048]{1,0:T(8,128)(2,1)S(1)} %get-tuple-element.153), channel_id=1, source_target_pairs={{0,4},{1,5},{2,6},{3,7},{4,0},{5,1},{6,2},{7,3},{8,12},{9,13},{10,... | collective-permute-start | bytes 786440 | tf_op jit(solution)/shard_map/ppermute | solution.py:255
  125.0 9.9 %collective-permute-start.23 = (bf16[64,2048]{1,0:T(8,128)(2,1)S(1)}, bf16[64,2048]{1,0:T(8,128)(2,1)S(1)}, u32[]{:S(2)}, u32[]{:S(2)}) collective-permute-start(bf16[64,2048]{1,0:T(8,128)(2,1)S(1)} %get-tuple-element.163), channel_id=1, source_target_pairs={{0,2},{1,3},{2,0},{3,1},{4,6},{5,7},{6,4},{7,5},{8,10},{9,11},{10,... | collective-permute-start | bytes 786440 | tf_op jit(solution)/shard_map/ppermute | solution.py:255
  135.6 22.0 %collective-permute-start.25 = (bf16[64,2048]{1,0:T(8,128)(2,1)}, bf16[64,2048]{1,0:T(8,128)(2,1)}, u32[]{:S(2)}, u32[]{:S(2)}) collective-permute-start(bf16[64,2048]{1,0:T(8,128)(2,1)} %get-tuple-element.167), channel_id=1, source_target_pairs={{0,8},{1,9},{2,10},{3,11},{4,12},{5,13},{6,14},{7,15},{8,0},{9,1},... | collective-permute-start | bytes 786440 | tf_op jit(solution)/shard_map/ppermute | solution.py:255
  140.2 10.1 %collective-permute-start.28 = (bf16[128,768]{1,0:T(8,128)(2,1)}, bf16[128,768]{1,0:T(8,128)(2,1)}, u32[]{:S(2)}, u32[]{:S(2)}) collective-permute-start(bf16[128,768]{1,0:T(8,128)(2,1)} %get-tuple-element.173.refs_2_), channel_id=1, source_target_pairs={{0,16},{16,0},{1,17},{17,1},{2,18},{18,2},{3,19},{19,3},{4,20},{20... | collective-permute-start | bytes 589832 | tf_op jit(solution)/shard_map/ppermute | solution.py:258
  141.4 7.4 %collective-permute-start.31 = (bf16[64,2048]{1,0:T(8,128)(2,1)S(1)}, bf16[64,2048]{1,0:T(8,128)(2,1)S(1)}, u32[]{:S(2)}, u32[]{:S(2)}) collective-permute-start(bf16[64,2048]{1,0:T(8,128)(2,1)S(1)} %get-tuple-element.179), channel_id=1, source_target_pairs={{0,2},{1,3},{2,0},{3,1},{4,6},{5,7},{6,4},{7,5},{8,10},{9,11},{10,... | collective-permute-start | bytes 786440 | tf_op jit(solution)/shard_map/ppermute | solution.py:255
  145.8 3.8 %collective-permute-start.30 = (bf16[64,2048]{1,0:T(8,128)(2,1)S(1)}, bf16[64,2048]{1,0:T(8,128)(2,1)S(1)}, u32[]{:S(2)}, u32[]{:S(2)}) collective-permute-start(bf16[64,2048]{1,0:T(8,128)(2,1)S(1)} %get-tuple-element.177), channel_id=1, source_target_pairs={{0,1},{1,0},{2,3},{3,2},{4,5},{5,4},{6,7},{7,6},{8,9},{9,8},{10,11... | collective-permute-start | bytes 786440 | tf_op jit(solution)/shard_map/ppermute | solution.py:255
  153.1 5.5 %collective-permute-start.34 = (bf16[64,2048]{1,0:T(8,128)(2,1)S(1)}, bf16[64,2048]{1,0:T(8,128)(2,1)S(1)}, u32[]{:S(2)}, u32[]{:S(2)}) collective-permute-start(bf16[64,2048]{1,0:T(8,128)(2,1)S(1)} %get-tuple-element.188), channel_id=1, source_target_pairs={{0,1},{1,0},{2,3},{3,2},{4,5},{5,4},{6,7},{7,6},{8,9},{9,8},{10,11... | collective-permute-start | bytes 786440 | tf_op jit(solution)/shard_map/ppermute | solution.py:255
  153.2 10.3 %collective-permute-start.33 = (bf16[64,2048]{1,0:T(8,128)(2,1)}, bf16[64,2048]{1,0:T(8,128)(2,1)}, u32[]{:S(2)}, u32[]{:S(2)}) collective-permute-start(bf16[64,2048]{1,0:T(8,128)(2,1)} %get-tuple-element.186), channel_id=1, source_target_pairs={{0,6},{1,7},{2,4},{3,5},{4,2},{5,3},{6,0},{7,1},{8,14},{9,15},{10,... | collective-permute-start | bytes 786440 | tf_op jit(solution)/shard_map/ppermute | solution.py:255
  156.2 14.0 %collective-permute-start.32 = (bf16[64,2048]{1,0:T(8,128)(2,1)}, bf16[64,2048]{1,0:T(8,128)(2,1)}, u32[]{:S(2)}, u32[]{:S(2)}) collective-permute-start(bf16[64,2048]{1,0:T(8,128)(2,1)} %get-tuple-element.185), channel_id=1, source_target_pairs={{0,12},{1,13},{2,14},{3,15},{4,8},{5,9},{6,10},{7,11},{8,4},{9,5},... | collective-permute-start | bytes 786440 | tf_op jit(solution)/shard_map/ppermute | solution.py:255
  158.7 12.6 %collective-permute-start.35 = (bf16[64,2048]{1,0:T(8,128)(2,1)S(1)}, bf16[64,2048]{1,0:T(8,128)(2,1)S(1)}, u32[]{:S(2)}, u32[]{:S(2)}) collective-permute-start(bf16[64,2048]{1,0:T(8,128)(2,1)S(1)} %get-tuple-element.192), channel_id=1, source_target_pairs={{0,2},{1,3},{2,0},{3,1},{4,6},{5,7},{6,4},{7,5},{8,10},{9,11},{10,... | collective-permute-start | bytes 786440 | tf_op jit(solution)/shard_map/ppermute | solution.py:255
  (36 other events, 167.1 us)

commit v3 on v2

--- a/solution.py
+++ b/solution.py
@@ -66,14 +66,14 @@
 
 
 LANES = 128
-MIB = 1024 * 1024
-VMEM_LIMIT = 16 * MIB
+VMEM_LIMIT = 10 * 1024 * 1024
+COST = 8_000_000_000
+COSTS = {}
 TOKEN = jax.ShapeDtypeStruct((8, LANES), jnp.float32)
 HERE = pl.BlockSpec(memory_space=pltpu.VMEM)
-FAR = pl.BlockSpec(memory_space=pltpu.HBM)
-
-
-def call(kernel, inputs, outputs, after, scratch=(), relays=(), room=VMEM_LIMIT):
+
+
+def call(kernel, inputs, outputs, after, scratch=(), relays=(), cost=0):
     inputs = [v if isinstance(v, tuple) else (v, HERE) for v in inputs]
     flat = [value for group in relays for value in group]
     joined = [
@@ -105,8 +105,8 @@
         out_specs=[HERE] * (len(outputs) + len(joined) + 1),
         out_shape=list(outputs) + joined + [TOKEN],
         scratch_shapes=list(scratch),
-        compiler_params=pltpu.CompilerParams(vmem_limit_bytes=room),
-        cost_estimate=pl.CostEstimate(flops=100_000_000_000, bytes_accessed=1, transcendentals=0),
+        compiler_params=pltpu.CompilerParams(vmem_limit_bytes=VMEM_LIMIT),
+        cost_estimate=pl.CostEstimate(flops=cost, bytes_accessed=1, transcendentals=0),
     )(*[value for value, _ in inputs], *flat, after)
     return results[:-1], results[-1]
 
@@ -126,43 +126,6 @@
     out_ref[:, width:] = jnp.transpose(picked).astype(jnp.bfloat16)
 
 
-def load_kernel(mine, depth, gate_ref, up_ref, *refs):
-    *chunk, held_ref, total_ref, sems = refs
-    half = held_ref.shape[2]
-    owner = lax.axis_index("dp")
-    column = pl.multiple_of((owner if mine else 1 - owner) * half, LANES)
-    steps = held_ref.shape[1] // depth
-    copies = []
-    for n in range(steps):
-        for i, ref in enumerate((gate_ref, up_ref)):
-            copies.append(
-                pltpu.make_async_copy(
-                    ref.at[0, pl.ds(n * depth, depth), pl.ds(column, half)],
-                    held_ref.at[i, pl.ds(n * depth, depth), :],
-                    sems.at[n, i],
-                )
-            )
-            copies[-1].start()
-    for n in range(steps):
-        for i in range(2):
-            copies[2 * n + i].wait()
-            if not chunk:
-                continue
-            tokens_ref, out_ref = chunk
-            rows = tokens_ref.shape[0]
-            part = jnp.dot(
-                tokens_ref[:, n * depth : (n + 1) * depth],
-                held_ref[i, n * depth : (n + 1) * depth, :],
-                preferred_element_type=jnp.float32,
-            )
-            if n > 0:
-                part += total_ref[i]
-            if n < steps - 1:
-                total_ref[i] = part
-            else:
-                out_ref[i * rows : (i + 1) * rows, :] = part.astype(jnp.bfloat16)
-
-
 def collect(piece_refs, width, chunk_ref):
     start = 0
     for piece in piece_refs:
@@ -171,36 +134,42 @@
 
 
 def partial_kernel(pieces, riders, tile, *refs):
-    held_ref, *rider_refs, out_ref, chunk_ref = refs[pieces:]
+    gate_ref, up_ref, *rider_refs, out_ref, chunk_ref = refs[pieces:]
     rows, width = chunk_ref.shape
+    half = out_ref.shape[1]
+    column = (1 - lax.axis_index("dp")) * half
     collect(refs[:pieces], width, chunk_ref)
     start = 2 * rows
     for ref in rider_refs:
         out_ref[start : start + ref.shape[0], :] = ref[...]
         start += ref.shape[0]
 
-    @pl.loop(0, held_ref.shape[2] // tile)
+    @pl.loop(0, half // tile)
     def _(n):
-        here = pl.ds(pl.multiple_of(n * tile, LANES), tile)
-        for i in range(2):
-            part = jnp.dot(chunk_ref[...], held_ref[i, :, here], preferred_element_type=jnp.float32)
-            out_ref[i * rows : (i + 1) * rows, here] = part.astype(jnp.bfloat16)
+        here = pl.ds(pl.multiple_of(column + n * tile, LANES), tile)
+        there = pl.ds(pl.multiple_of(n * tile, LANES), tile)
+        for i, ref in enumerate((gate_ref, up_ref)):
+            part = jnp.dot(chunk_ref[...], ref[0, :, here], preferred_element_type=jnp.float32)
+            out_ref[i * rows : (i + 1) * rows, there] = part.astype(jnp.bfloat16)
 
 
 def hidden_kernel(pieces, tile, *refs):
-    held_ref, arrived_ref, out_ref, chunk_ref = refs[pieces:]
+    gate_ref, up_ref, arrived_ref, out_ref, chunk_ref = refs[pieces:]
     rows, width = chunk_ref.shape
+    half = out_ref.shape[1]
+    column = lax.axis_index("dp") * half
     collect(refs[:pieces], width, chunk_ref)
 
-    @pl.loop(0, held_ref.shape[2] // tile)
+    @pl.loop(0, half // tile)
     def _(n):
-        here = pl.ds(pl.multiple_of(n * tile, LANES), tile)
+        here = pl.ds(pl.multiple_of(column + n * tile, LANES), tile)
+        there = pl.ds(pl.multiple_of(n * tile, LANES), tile)
         gate_sum, up_sum = (
-            jnp.dot(chunk_ref[...], held_ref[i, :, here], preferred_element_type=jnp.float32)
-            + arrived_ref[i * rows : (i + 1) * rows, here].astype(jnp.float32)
-            for i in range(2)
-        )
-        out_ref[:, here] = (gate_sum / (1.0 + jnp.exp(-gate_sum)) * up_sum).astype(jnp.bfloat16)
+            jnp.dot(chunk_ref[...], ref[0, :, here], preferred_element_type=jnp.float32)
+            + arrived_ref[i * rows : (i + 1) * rows, there].astype(jnp.float32)
+            for i, ref in enumerate((gate_ref, up_ref))
+        )
+        out_ref[:, there] = (gate_sum / (1.0 + jnp.exp(-gate_sum)) * up_sum).astype(jnp.bfloat16)
 
 
 def output_kernel(pieces, sources, tile, behind, *refs):
@@ -249,7 +218,6 @@
     half = gate_proj.shape[2] // 2
     tile = 256 if half % 256 == 0 else half
     out_tile = 512 if width % 512 == 0 else width
-    depth = 512 if width % 512 == 0 else width
 
     def swap(value, r):
         return lax.ppermute(value, "expert", [(i, i ^ r) for i in range(sources)])
@@ -260,42 +228,34 @@
     def array(shape, dtype=jnp.bfloat16):
         return jax.ShapeDtypeStruct(shape, dtype)
 
-    tail = [jnp.zeros(TOKEN.shape, TOKEN.dtype)]
-
-    def step(kernel, inputs, outputs, scratch=(), relays=(), room=VMEM_LIMIT):
-        results, tail[0] = call(kernel, inputs, outputs, tail[0], scratch, relays, room)
+    tail, number = [jnp.zeros(TOKEN.shape, TOKEN.dtype)], [0]
+
+    def step(kernel, inputs, outputs, scratch=(), relays=()):
+        results, tail[0] = call(
+            kernel, inputs, outputs, tail[0], scratch, relays, COSTS.get(number[0], COST)
+        )
+        number[0] += 1
         return results
 
     def count(pieces):
         return sum(p.shape[0] for p in pieces)
-
-    def load(mine, chunk, room):
-        made = [array((2 * rows, half))] if chunk else []
-        *sent, held = step(
-            functools.partial(load_kernel, mine, depth),
-            [(gate_proj, FAR), (up_proj, FAR), *chunk],
-            made + [array((2, width, half))],
-            [pltpu.VMEM((2, rows, half), jnp.float32), pltpu.SemaphoreType.DMA((width // depth, 2))],
-            room=room,
-        )
-        return held, *sent
 
     def partials(pieces, riders=(), relays=()):
         total = count(pieces)
         sent, *relayed = step(
             functools.partial(partial_kernel, len(pieces), len(riders), tile),
-            [*pieces, held_other, *riders],
+            [*pieces, gate_proj, up_proj, *riders],
             [array((2 * total + count(riders), half))],
             [pltpu.VMEM((total, width), jnp.bfloat16)],
             relays,
         )
-        return cross(sent), *relayed
+        return sent, *relayed
 
     def hidden(pieces, arrived, relays=()):
         total = count(pieces)
         mine, *relayed = step(
             functools.partial(hidden_kernel, len(pieces), tile),
-            [*pieces, held_mine, arrived],
+            [*pieces, gate_proj, up_proj, arrived],
             [array((total, half))],
             [pltpu.VMEM((total, width), jnp.bfloat16)],
             relays,
@@ -331,79 +291,92 @@
     one, two, wide = array((rows, width)), array((2 * rows, width)), array((rows, width), jnp.float32)
     whole = [(0, 0), (1, 0)]
 
-    held_other, sent = load(False, [tokens], 52 * MIB)
-    y0 = cross(sent)
+    def gap():
+        step(None, [], [])
+
     (labelled,) = step(
         functools.partial(label_kernel, sources),
         [tokens, expert_ids.T, gate_weights.T],
         [array((rows, width + LANES))],
     )
-    b1 = swap(labelled, 1)
-    z4, z8 = swap(labelled, 4), swap(labelled, 8)
-    (held_mine,) = load(True, [], 46 * MIB)
-    (y1,) = partials([b1])
+    b1, z4 = swap(labelled, 1), swap(labelled, 4)
+    p0 = [labelled, b1]
+    (sent,) = partials(p0)
+    y0 = cross(sent)
+    (again,) = relay([labelled])
+    z8 = swap(again, 8)
     (b4,) = relay([z4])
     b5, x6 = swap(b4, 1), swap(b4, 2)
-    (h0,) = hidden([tokens], y0)
-    p2 = [b4, b5]
-    y2, again = partials(p2, [h0], relays=[[labelled]])
-    z12 = swap(again, 12)
-    (b8,) = relay([z8])
-    x10 = swap(b8, 2)
-    (h1,) = hidden([b1], y1)
+    gap()
+    p1 = [b4, b5]
+    (sent,) = partials(p1)
+    y1 = cross(sent)
+    (b6,) = relay([x6])
+    b7 = swap(b6, 1)
+    (h0,) = hidden(p0, y0)
+    p2 = [b6, b7]
+    (sent,) = partials(p2, [h0])
+    y2 = cross(sent)
+    b8, again = relay([z8], [again])
+    x10, z12 = swap(b8, 2), swap(again, 12)
+    (h1,) = hidden(p1, y1)
     (b8,) = relay([b8, x10])
     b9 = swap(b8, 1)
-    b6, again = relay([x6], [labelled])
-    b7 = swap(b6, 1)
+    gap()
     p3 = [b8, b9]
-    (y3,) = partials(p3, [h1])
+    (sent,) = partials(p3, [h1])
+    y3 = cross(sent)
+    (again,) = relay([again])
+    x2 = swap(again, 2)
+    (h2,) = hidden(p2, y2)
+    c0, c1 = outputs(p0, h0, y2, 4 * rows, rows)
     (b12,) = relay([z12])
     x14 = swap(b12, 2)
-    h2, again = hidden(p2, y2, relays=[[again]])
+    (total,) = add([c0, c1], (whole, wide))
     (b12,) = relay([b12, x14])
     b13 = swap(b12, 1)
-    c0, _ = outputs([labelled], h0, y2, 4 * rows, rows)
+    gap()
     p4 = [b12, b13]
-    y4, again = partials(p4, [h2], relays=[[again]])
-    x2 = swap(again, 2)
-    (h3,) = hidden(p3, y3)
-    p5 = [b6, b7]
-    (y5,) = partials(p5, [h3])
-    _, c1 = outputs([b1], h1, y3, 8 * rows, 0)
+    (sent,) = partials(p4, [h2])
+    y4 = cross(sent)
     (b2,) = relay([x2])
     b3 = swap(b2, 1)
-    (total,) = add([c0, c1], (whole, wide))
+    (h3,) = hidden(p3, y3)
+    t3 = cross(h3)
+    c4, c5 = outputs(p1, h1, y3, 8 * rows, rows)
+    gap()
+    (sent,) = add([c4, c5], (whole, one))
+    s4 = swap(sent, 4)
+    p5 = [b2, b3]
+    (later,) = partials(p5)
     (h4,) = hidden(p4, y4)
     t4 = cross(h4)
-    c4, c5 = outputs(p2, h2, y4, 8 * rows, rows)
-    p6 = [b2, b3]
-    (y6,) = partials(p6)
-    (sent,) = add([c4, c5], (whole, one))
-    s4 = swap(sent, 4)
+    total, sent = add([total, s4], (whole, wide), relays=[[later]])
+    y5 = cross(sent)
+    c6, c7 = outputs(p2, h2, y4, 8 * rows, rows)
+    gap()
+    (sent,) = add([c6, c7], (whole, one))
+    s6 = swap(sent, 6)
+    c8, c9 = outputs(p3, h3, t3, 0, 2 * rows)
+    gap()
+    kept8, sent = add([c8, c9], (whole, wide), ([(0, rows), (1, rows)], one))
+    x10 = swap(sent, 2)
+    c12, c13 = outputs(p4, h4, t4, 0, 2 * rows)
+    (total,) = add([total, s6], (whole, wide))
+    kept12, sent = add([c12, c13], (whole, wide), ([(0, rows), (1, rows)], one))
+    x14 = swap(sent, 2)
+    (sent,) = add([kept8, x10], (whole, one))
+    s8 = swap(sent, 8)
     (h5,) = hidden(p5, y5)
     t5 = cross(h5)
-    c8, c9 = outputs(p3, h3, y5, 4 * rows, 2 * rows)
-    (total,) = add([total, s4], (whole, wide))
-    kept, sent = add([c8, c9], (whole, wide), ([(0, rows), (1, rows)], one))
-    x10 = swap(sent, 2)
-    c12, c13 = outputs(p4, h4, t4, 0, 2 * rows)
-    (sent,) = add([kept, x10], (whole, one))
-    s8 = swap(sent, 8)
-    kept, sent = add([c12, c13], (whole, wide), ([(0, rows), (1, rows)], one))
-    x14 = swap(sent, 2)
-    (h6,) = hidden(p6, y6)
-    t6 = cross(h6)
-    c6, c7 = outputs(p5, h5, t5, 0, rows)
-    (sent,) = add([kept, x14], (whole, one))
+    (sent,) = add([kept12, x14], (whole, one))
     s12 = swap(sent, 12)
-    (sent,) = add([c6, c7], (whole, one))
-    s6 = swap(sent, 6)
-    c2, c3 = outputs(p6, h6, t6, 0, rows)
-    (total,) = add([total, s8], (whole, wide))
+    c2, c3 = outputs(p5, h5, t5, 0, rows)
+    gap()
     (sent,) = add([c2, c3], (whole, one))
     s2 = swap(sent, 2)
-    (total,) = add([total, s12, s6], (whole + [(2, 0)], wide))
-    (total,) = add([total, s2], (whole, one))
+    (total,) = add([total, s8], (whole, wide))
+    (total,) = add([total, s12, s2], (whole + [(2, 0)], one))
     return total
 
 

time: 173 us -> 145 us (0.84)
  the two profiles are of different devices: /device:TPU:0 before, /device:TPU:8 now
where the time goes in v3:
time: 145 us
  waiting for transfers between devices  75.8 us (52%)
  Pallas kernels  34.5 us (24%)
  starting transfers between devices  28.8 us (20%)
  local copies, waits for them, and re-layouts  5.28 us (4%)
    ppermute x26, waiting for transfers between devices, swap(): return lax.ppermute(value, 'expert', [(i, i ^ r) for i in range(sources)])  44.9 us
    pallas_call x47, Pallas kernels, call(): pl.pallas_call(run, in_specs=[spec for _, spec in inputs] + [HERE] * len(...  34.5 us
    ppermute x9, waiting for transfers between devices, cross(): return lax.ppermute(value, 'dp', [(0, 1), (1, 0)])  30.8 us
    ppermute x26, starting transfers between devices, swap(): return lax.ppermute(value, 'expert', [(i, i ^ r) for i in range(sources)])  16.6 us
    ppermute x9, starting transfers between devices, cross(): return lax.ppermute(value, 'dp', [(0, 1), (1, 0)])  12.2 us
    unnamed x14, local copies, waits for them, and re-layouts  5.28 us
  transfers between devices with their start and end apart: 35, of which 20 were waited for; matrix products, arithmetic and copies ran while one was open for 0% of the time, Pallas kernels for 23%

profile of v3, /device:TPU:8, one launch (start us, length us, event | category | flops | bytes accessed | tf_op | source)
XLA Modules:
  0.0 144.8 jit_solution(15257556347230117207)
XLA Ops:
  5.1 1.8 %copy-done.1 = bf16[1,2048,1536]{2,1,0:T(8,128)(2,1)S(1)} copy-done((bf16[1,2048,1536]{2,1,0:T(8,128)(2,1)S(1)}, bf16[1,2048,1536]{2,1,0:T(8,128)(2,1)}, u32[]{:S(2)}) %copy-start.1) | copy-done | bytes 6291480
  8.4 3.2 %collective-permute-done.2.refs_0_ = bf16[64,2176]{1,0:T(8,128)(2,1)S(1)} collective-permute-done((bf16[64,2176]{1,0:T(8,128)(2,1)S(1)}, bf16[64,2176]{1,0:T(8,128)(2,1)S(1)}, u32[]{:S(2)}, u32[]{:S(2)}) %collective-permute-start.2) | collective-permute-done | bytes 278560 | tf_op jit(solution)/shard_map/ppermute | solution.py:223
  14.7 2.6 %collective-permute-start.7 = (bf16[64,2176]{1,0:T(8,128)(2,1)S(1)}, bf16[64,2176]{1,0:T(8,128)(2,1)S(1)}, u32[]{:S(2)}, u32[]{:S(2)}) collective-permute-start(bf16[64,2176]{1,0:T(8,128)(2,1)S(1)} %get-tuple-element.107.refs_1_), channel_id=1, source_target_pairs={{0,8},{1,9},{2,10},{3,11},{4,12},{5,13},{6,14},{7,15},{8,0},{9,1},... | collective-permute-start | bytes 835592 | tf_op jit(solution)/shard_map/ppermute | solution.py:223
  21.6 3.5 %collective-permute-done.1.refs_4_ = bf16[256,768]{1,0:T(8,128)(2,1)S(1)} collective-permute-done((bf16[256,768]{1,0:T(8,128)(2,1)S(1)}, bf16[256,768]{1,0:T(8,128)(2,1)S(1)}, u32[]{:S(2)}, u32[]{:S(2)}) %collective-permute-start.1) | collective-permute-done | bytes 393248 | tf_op jit(solution)/shard_map/ppermute | solution.py:226
  31.9 1.7 %collective-permute-done.9.refs_4_ = bf16[256,768]{1,0:T(8,128)(2,1)S(1)} collective-permute-done((bf16[256,768]{1,0:T(8,128)(2,1)S(1)}, bf16[256,768]{1,0:T(8,128)(2,1)S(1)}, u32[]{:S(2)}, u32[]{:S(2)}) %collective-permute-start.9) | collective-permute-done | bytes 393248 | tf_op jit(solution)/shard_map/ppermute | solution.py:226
  35.0 3.1 %collective-permute-done.8.refs_1_ = bf16[64,2176]{1,0:T(8,128)(2,1)S(1)} collective-permute-done((bf16[64,2176]{1,0:T(8,128)(2,1)S(1)}, bf16[64,2176]{1,0:T(8,128)(2,1)S(1)}, u32[]{:S(2)}, u32[]{:S(2)}) %collective-permute-start.8) | collective-permute-done | bytes 278560 | tf_op jit(solution)/shard_map/ppermute | solution.py:223
  38.3 1.9 %collective-permute-done.10.refs_1_ = bf16[128,2176]{1,0:T(8,128)(2,1)S(1)} collective-permute-done((bf16[128,2176]{1,0:T(8,128)(2,1)S(1)}, bf16[128,2176]{1,0:T(8,128)(2,1)S(1)}, u32[]{:S(2)}, u32[]{:S(2)}) %collective-permute-start.10) | collective-permute-done | bytes 557088 | tf_op jit(solution)/shard_map/ppermute | solution.py:223
  40.2 2.2 %shard_map.77 = (bf16[640,768]{1,0:T(8,128)(2,1)S(1)}, f32[8,128]{1,0:T(8,128)S(1)}) custom-call(bf16[128,2176]{1,0:T(8,128)(2,1)S(1)} %get-tuple-element.114.refs_0_, bf16[128,2176]{1,0:T(8,128)(2,1)S(1)} %collective-permute-done.10.refs_1_, bf16[1,2048,1536]{2,1,0:T(8,128)(2,1)S(1)} %copy-done, bf16[1,2048,1536]{2,1,0:T(8,128)(2,1)S(1)} %copy-done.1, ...), custom_call_target="tpu_custom_call" | custom-call | flops 8000000000 | bytes 1 | tf_op jit(solution)/shard_map/pallas_call | solution.py:102
  42.5 3.2 %collective-permute-done.6.refs_4_.refs_3_ = bf16[384,768]{1,0:T(8,128)(2,1)S(1)} collective-permute-done((bf16[384,768]{1,0:T(8,128)(2,1)S(1)}, bf16[384,768]{1,0:T(8,128)(2,1)S(1)}, u32[]{:S(2)}, u32[]{:S(2)}) %collective-permute-start.6) | collective-permute-done | bytes 589856 | tf_op jit(solution)/shard_map/ppermute | solution.py:226
  47.4 1.7 %shard_map.80 = (f32[64,2048]{1,0:T(8,128)S(1)}, bf16[64,2048]{1,0:T(8,128)(2,1)S(1)}, f32[8,128]{1,0:T(8,128)S(1)}) custom-call(bf16[64,2176]{1,0:T(8,128)(2,1)S(1)} %get-tuple-element.94.refs_0_, bf16[64,2176]{1,0:T(8,128)(2,1)S(1)} %collective-permute-done.refs_1_, bf16[128,768]{1,0:T(8,128)(2,1)S(1)} %get-tuple-element.103.refs_4_.refs_2_, ...), custom_call_target="tpu_custom_call" | custom-call | flops 8000000000 | bytes 1 | tf_op jit(solution)/shard_map/pallas_call | solution.py:102
  52.9 12.5 %collective-permute-done.15.refs_1_ = bf16[64,2176]{1,0:T(8,128)(2,1)S(1)} collective-permute-done((bf16[64,2176]{1,0:T(8,128)(2,1)S(1)}, bf16[64,2176]{1,0:T(8,128)(2,1)S(1)}, u32[]{:S(2)}, u32[]{:S(2)}) %collective-permute-start.15) | collective-permute-done | bytes 278560 | tf_op jit(solution)/shard_map/ppermute | solution.py:223
  65.6 1.9 %collective-permute-done.16.refs_1_ = bf16[128,2176]{1,0:T(8,128)(2,1)S(1)} collective-permute-done((bf16[128,2176]{1,0:T(8,128)(2,1)S(1)}, bf16[128,2176]{1,0:T(8,128)(2,1)S(1)}, u32[]{:S(2)}, u32[]{:S(2)}) %collective-permute-start.16) | collective-permute-done | bytes 557088 | tf_op jit(solution)/shard_map/ppermute | solution.py:223
  67.5 2.2 %shard_map.85 = (bf16[640,768]{1,0:T(8,128)(2,1)S(1)}, f32[8,128]{1,0:T(8,128)S(1)}) custom-call(bf16[128,2176]{1,0:T(8,128)(2,1)S(1)} %get-tuple-element.129.refs_0_, bf16[128,2176]{1,0:T(8,128)(2,1)S(1)} %collective-permute-done.16.refs_1_, bf16[1,2048,1536]{2,1,0:T(8,128)(2,1)S(1)} %copy-done, bf16[1,2048,1536]{2,1,0:T(8,128)(2,1)S(1)} %copy-done.1, ...), custom_call_target="tpu_custom_call" | custom-call | flops 8000000000 | bytes 1 | tf_op jit(solution)/shard_map/pallas_call | solution.py:102
  70.5 3.1 %collective-permute-done.13.refs_4_.refs_3_ = bf16[640,768]{1,0:T(8,128)(2,1)S(1)} collective-permute-done((bf16[640,768]{1,0:T(8,128)(2,1)S(1)}, bf16[640,768]{1,0:T(8,128)(2,1)S(1)}, u32[]{:S(2)}, u32[]{:S(2)}) %collective-permute-start.13) | collective-permute-done | bytes 983072 | tf_op jit(solution)/shard_map/ppermute | solution.py:226
  73.6 2.3 %shard_map.87 = (bf16[256,768]{1,0:T(8,128)(2,1)S(1)}, f32[8,128]{1,0:T(8,128)S(1)}) custom-call(bf16[128,2176]{1,0:T(8,128)(2,1)S(1)} %get-tuple-element.114.refs_0_, bf16[128,2176]{1,0:T(8,128)(2,1)S(1)} %collective-permute-done.10.refs_1_, bf16[1,2048,1536]{2,1,0:T(8,128)(2,1)S(1)} %copy-done, bf16[1,2048,1536]{2,1,0:T(8,128)(2,1)S(1)} %copy-done.1, ...), custom_call_target="tpu_custom_call" | custom-call | flops 8000000000 | bytes 1 | tf_op jit(solution)/shard_map/pallas_call | solution.py:102
  75.9 1.7 %shard_map.88 = (f32[64,2048]{1,0:T(8,128)S(1)}, bf16[64,2048]{1,0:T(8,128)(2,1)S(1)}, f32[8,128]{1,0:T(8,128)S(1)}) custom-call(bf16[64,2176]{1,0:T(8,128)(2,1)S(1)} %get-tuple-element.99.refs_0_, bf16[64,2176]{1,0:T(8,128)(2,1)S(1)} %collective-permute-done.4.refs_1_, bf16[128,768]{1,0:T(8,128)(2,1)S(1)} %get-tuple-element.115.refs_4_.refs_2_, ...), custom_call_target="tpu_custom_call" | custom-call | flops 8000000000 | bytes 1 | tf_op jit(solution)/shard_map/pallas_call | solution.py:102
  77.7 1.8 %collective-permute-start.24 = (bf16[256,768]{1,0:T(8,128)(2,1)S(1)}, bf16[256,768]{1,0:T(8,128)(2,1)S(1)}, u32[]{:S(2)}, u32[]{:S(2)}) collective-permute-start(bf16[256,768]{1,0:T(8,128)(2,1)S(1)} %get-tuple-element.152.refs_2_), channel_id=1, source_target_pairs={{0,16},{16,0},{1,17},{17,1},{2,18},{18,2},{3,19},{19,3},{4,20},{20... | collective-permute-start | bytes 1179656 | tf_op jit(solution)/shard_map/ppermute | solution.py:226
  81.5 13.1 %collective-permute-done.20.refs_4_.refs_3_ = bf16[640,768]{1,0:T(8,128)(2,1)S(1)} collective-permute-done((bf16[640,768]{1,0:T(8,128)(2,1)S(1)}, bf16[640,768]{1,0:T(8,128)(2,1)S(1)}, u32[]{:S(2)}, u32[]{:S(2)}) %collective-permute-start.20) | collective-permute-done | bytes 983072 | tf_op jit(solution)/shard_map/ppermute | solution.py:226
  94.7 2.3 %shard_map.92 = (bf16[256,768]{1,0:T(8,128)(2,1)S(1)}, f32[8,128]{1,0:T(8,128)S(1)}) custom-call(bf16[128,2176]{1,0:T(8,128)(2,1)S(1)} %get-tuple-element.129.refs_0_, bf16[128,2176]{1,0:T(8,128)(2,1)S(1)} %collective-permute-done.16.refs_1_, bf16[1,2048,1536]{2,1,0:T(8,128)(2,1)S(1)} %copy-done, bf16[1,2048,1536]{2,1,0:T(8,128)(2,1)S(1)} %copy-done.1, ...), custom_call_target="tpu_custom_call" | custom-call | flops 8000000000 | bytes 1 | tf_op jit(solution)/shard_map/pallas_call | solution.py:102
  97.1 1.7 %shard_map.94 = (f32[64,2048]{1,0:T(8,128)S(1)}, bf16[64,2048]{1,0:T(8,128)(2,1)S(1)}, f32[8,128]{1,0:T(8,128)S(1)}) custom-call(bf16[64,2176]{1,0:T(8,128)(2,1)S(1)} %get-tuple-element.104.refs_0_, bf16[64,2176]{1,0:T(8,128)(2,1)S(1)} %collective-permute-done.5.refs_1_, bf16[128,768]{1,0:T(8,128)(2,1)S(1)} %get-tuple-element.130.refs_4_.refs_2_, ...), custom_call_target="tpu_custom_call" | custom-call | flops 8000000000 | bytes 1 | tf_op jit(solution)/shard_map/pallas_call | solution.py:102
  98.9 1.8 %collective-permute-start.23 = (bf16[256,768]{1,0:T(8,128)(2,1)S(1)}, bf16[256,768]{1,0:T(8,128)(2,1)S(1)}, u32[]{:S(2)}, u32[]{:S(2)}) collective-permute-start(bf16[256,768]{1,0:T(8,128)(2,1)S(1)} %get-tuple-element.151.refs_2_), channel_id=1, source_target_pairs={{0,16},{16,0},{1,17},{17,1},{2,18},{18,2},{3,19},{19,3},{4,20},{20... | collective-permute-start | bytes 1179656 | tf_op jit(solution)/shard_map/ppermute | solution.py:226
  101.5 1.6 %collective-permute-done.24.refs_3_ = bf16[256,768]{1,0:T(8,128)(2,1)S(1)} collective-permute-done((bf16[256,768]{1,0:T(8,128)(2,1)S(1)}, bf16[256,768]{1,0:T(8,128)(2,1)S(1)}, u32[]{:S(2)}, u32[]{:S(2)}) %collective-permute-start.24) | collective-permute-done | bytes 393248 | tf_op jit(solution)/shard_map/ppermute | solution.py:226
  103.1 2.5 %shard_map.97 = (f32[128,2048]{1,0:T(8,128)S(1)}, bf16[128,2048]{1,0:T(8,128)(2,1)S(1)}, f32[8,128]{1,0:T(8,128)S(1)}) custom-call(bf16[128,2176]{1,0:T(8,128)(2,1)S(1)} %get-tuple-element.114.refs_0_, bf16[128,2176]{1,0:T(8,128)(2,1)S(1)} %collective-permute-done.10.refs_1_, bf16[256,768]{1,0:T(8,128)(2,1)S(1)} %get-tuple-element.152.refs_2_, ...), custom_call_target="tpu_custom_call" | custom-call | flops 8000000000 | bytes 1 | tf_op jit(solution)/shard_map/pallas_call | solution.py:102
  105.6 1.9 %collective-permute-done.25.refs_1_ = bf16[128,2048]{1,0:T(8,128)(2,1)S(1)} collective-permute-done((bf16[128,2048]{1,0:T(8,128)(2,1)S(1)}, bf16[128,2048]{1,0:T(8,128)(2,1)S(1)}, u32[]{:S(2)}, u32[]{:S(2)}) %collective-permute-start.25) | collective-permute-done | bytes 524320 | tf_op jit(solution)/shard_map/ppermute | solution.py:223
  108.2 3.3 %collective-permute-done.23.refs_3_ = bf16[256,768]{1,0:T(8,128)(2,1)S(1)} collective-permute-done((bf16[256,768]{1,0:T(8,128)(2,1)S(1)}, bf16[256,768]{1,0:T(8,128)(2,1)S(1)}, u32[]{:S(2)}, u32[]{:S(2)}) %collective-permute-start.23) | collective-permute-done | bytes 393248 | tf_op jit(solution)/shard_map/ppermute | solution.py:226
  111.5 2.4 %shard_map.100 = (f32[128,2048]{1,0:T(8,128)S(1)}, bf16[128,2048]{1,0:T(8,128)(2,1)S(1)}, f32[8,128]{1,0:T(8,128)S(1)}) custom-call(bf16[128,2176]{1,0:T(8,128)(2,1)S(1)} %get-tuple-element.129.refs_0_, bf16[128,2176]{1,0:T(8,128)(2,1)S(1)} %collective-permute-done.16.refs_1_, bf16[256,768]{1,0:T(8,128)(2,1)S(1)} %get-tuple-element.151.refs_2_, ...), custom_call_target="tpu_custom_call" | custom-call | flops 8000000000 | bytes 1 | tf_op jit(solution)/shard_map/pallas_call | solution.py:102
  114.1 1.8 %collective-permute-done.27.refs_1_ = bf16[128,2048]{1,0:T(8,128)(2,1)S(1)} collective-permute-done((bf16[128,2048]{1,0:T(8,128)(2,1)S(1)}, bf16[128,2048]{1,0:T(8,128)(2,1)S(1)}, u32[]{:S(2)}, u32[]{:S(2)}) %collective-permute-start.27) | collective-permute-done | bytes 524320 | tf_op jit(solution)/shard_map/ppermute | solution.py:223
  116.1 2.7 %collective-permute-start.28 = (bf16[64,2048]{1,0:T(8,128)(2,1)S(1)}, bf16[64,2048]{1,0:T(8,128)(2,1)S(1)}, u32[]{:S(2)}, u32[]{:S(2)}) collective-permute-start(bf16[64,2048]{1,0:T(8,128)(2,1)S(1)} %get-tuple-element.166), channel_id=1, source_target_pairs={{0,8},{1,9},{2,10},{3,11},{4,12},{5,13},{6,14},{7,15},{8,0},{9,1},... | collective-permute-start | bytes 786440 | tf_op jit(solution)/shard_map/ppermute | solution.py:223
  122.8 4.1 %collective-permute-done.31.refs_1_ = bf16[64,2048]{1,0:T(8,128)(2,1)S(1)} collective-permute-done((bf16[64,2048]{1,0:T(8,128)(2,1)S(1)}, bf16[64,2048]{1,0:T(8,128)(2,1)S(1)}, u32[]{:S(2)}, u32[]{:S(2)}) %collective-permute-start.31) | collective-permute-done | bytes 262176 | tf_op jit(solution)/shard_map/ppermute | solution.py:223
  127.9 1.7 %shard_map.106 = (f32[64,2048]{1,0:T(8,128)S(1)}, bf16[64,2048]{1,0:T(8,128)(2,1)S(1)}, f32[8,128]{1,0:T(8,128)S(1)}) custom-call(bf16[64,2176]{1,0:T(8,128)(2,1)S(1)} %get-tuple-element.139.refs_0_, bf16[64,2176]{1,0:T(8,128)(2,1)S(1)} %collective-permute-done.19.refs_1_, bf16[128,768]{1,0:T(8,128)(2,1)S(1)} %get-tuple-element.169.refs_2_, ...), custom_call_target="tpu_custom_call" | custom-call | flops 8000000000 | bytes 1 | tf_op jit(solution)/shard_map/pallas_call | solution.py:102
  129.7 1.6 %collective-permute-start.33 = (bf16[64,2048]{1,0:T(8,128)(2,1)S(1)}, bf16[64,2048]{1,0:T(8,128)(2,1)S(1)}, u32[]{:S(2)}, u32[]{:S(2)}) collective-permute-start(bf16[64,2048]{1,0:T(8,128)(2,1)S(1)} %get-tuple-element.179), channel_id=1, source_target_pairs={{0,12},{1,13},{2,14},{3,15},{4,8},{5,9},{6,10},{7,11},{8,4},{9,5},... | collective-permute-start | bytes 786440 | tf_op jit(solution)/shard_map/ppermute | solution.py:223
  132.2 11.8 %collective-permute-done.33.refs_1_ = bf16[64,2048]{1,0:T(8,128)(2,1)S(1)} collective-permute-done((bf16[64,2048]{1,0:T(8,128)(2,1)S(1)}, bf16[64,2048]{1,0:T(8,128)(2,1)S(1)}, u32[]{:S(2)}, u32[]{:S(2)}) %collective-permute-start.33) | collective-permute-done | bytes 262176 | tf_op jit(solution)/shard_map/ppermute | solution.py:223
  (101 shorter events, 39.5 us)
Async XLA Ops:
  2.5 9.1 %collective-permute-start.2 = (bf16[64,2176]{1,0:T(8,128)(2,1)S(1)}, bf16[64,2176]{1,0:T(8,128)(2,1)S(1)}, u32[]{:S(2)}, u32[]{:S(2)}) collective-permute-start(bf16[64,2176]{1,0:T(8,128)(2,1)S(1)} %get-tuple-element.94.refs_0_), channel_id=1, source_target_pairs={{0,4},{1,5},{2,6},{3,7},{4,0},{5,1},{6,2},{7,3},{8,12},{9,13},{10,... | collective-permute-start | bytes 835592 | tf_op jit(solution)/shard_map/ppermute | solution.py:223
  11.6 8.3 %collective-permute-start.3 = (bf16[64,2176]{1,0:T(8,128)(2,1)S(1)}, bf16[64,2176]{1,0:T(8,128)(2,1)S(1)}, u32[]{:S(2)}, u32[]{:S(2)}) collective-permute-start(bf16[64,2176]{1,0:T(8,128)(2,1)S(1)} %get-tuple-element.99.refs_0_), channel_id=1, source_target_pairs={{0,2},{1,3},{2,0},{3,1},{4,6},{5,7},{6,4},{7,5},{8,10},{9,11},{10,... | collective-permute-start | bytes 835592 | tf_op jit(solution)/shard_map/ppermute | solution.py:223
  13.2 4.1 %collective-permute-start.4 = (bf16[64,2176]{1,0:T(8,128)(2,1)S(1)}, bf16[64,2176]{1,0:T(8,128)(2,1)S(1)}, u32[]{:S(2)}, u32[]{:S(2)}) collective-permute-start(bf16[64,2176]{1,0:T(8,128)(2,1)S(1)} %get-tuple-element.99.refs_0_), channel_id=1, source_target_pairs={{0,1},{1,0},{2,3},{3,2},{4,5},{5,4},{6,7},{7,6},{8,9},{9,8},{10,11... | collective-permute-start | bytes 835592 | tf_op jit(solution)/shard_map/ppermute | solution.py:223
  13.2 11.9 %collective-permute-start.1 = (bf16[256,768]{1,0:T(8,128)(2,1)S(1)}, bf16[256,768]{1,0:T(8,128)(2,1)S(1)}, u32[]{:S(2)}, u32[]{:S(2)}) collective-permute-start(bf16[256,768]{1,0:T(8,128)(2,1)S(1)} %get-tuple-element.96), channel_id=1, source_target_pairs={{0,16},{16,0},{1,17},{17,1},{2,18},{18,2},{3,19},{19,3},{4,20},{20... | collective-permute-start | bytes 1179656 | tf_op jit(solution)/shard_map/ppermute | solution.py:226
  14.7 14.9 %collective-permute-start.7 = (bf16[64,2176]{1,0:T(8,128)(2,1)S(1)}, bf16[64,2176]{1,0:T(8,128)(2,1)S(1)}, u32[]{:S(2)}, u32[]{:S(2)}) collective-permute-start(bf16[64,2176]{1,0:T(8,128)(2,1)S(1)} %get-tuple-element.107.refs_1_), channel_id=1, source_target_pairs={{0,8},{1,9},{2,10},{3,11},{4,12},{5,13},{6,14},{7,15},{8,0},{9,1},... | collective-permute-start | bytes 835592 | tf_op jit(solution)/shard_map/ppermute | solution.py:223
  19.9 6.7 %collective-permute-start.5 = (bf16[64,2176]{1,0:T(8,128)(2,1)S(1)}, bf16[64,2176]{1,0:T(8,128)(2,1)S(1)}, u32[]{:S(2)}, u32[]{:S(2)}) collective-permute-start(bf16[64,2176]{1,0:T(8,128)(2,1)S(1)} %get-tuple-element.104.refs_0_), channel_id=1, source_target_pairs={{0,1},{1,0},{2,3},{3,2},{4,5},{5,4},{6,7},{7,6},{8,9},{9,8},{10,11... | collective-permute-start | bytes 835592 | tf_op jit(solution)/shard_map/ppermute | solution.py:223
  20.0 13.5 %collective-permute-start.9 = (bf16[256,768]{1,0:T(8,128)(2,1)S(1)}, bf16[256,768]{1,0:T(8,128)(2,1)S(1)}, u32[]{:S(2)}, u32[]{:S(2)}) collective-permute-start(bf16[256,768]{1,0:T(8,128)(2,1)S(1)} %get-tuple-element.111), channel_id=1, source_target_pairs={{0,16},{16,0},{1,17},{17,1},{2,18},{18,2},{3,19},{19,3},{4,20},{20... | collective-permute-start | bytes 1179656 | tf_op jit(solution)/shard_map/ppermute | solution.py:226
  28.1 17.7 %collective-permute-start.6 = (bf16[384,768]{1,0:T(8,128)(2,1)S(1)}, bf16[384,768]{1,0:T(8,128)(2,1)S(1)}, u32[]{:S(2)}, u32[]{:S(2)}) collective-permute-start(bf16[384,768]{1,0:T(8,128)(2,1)S(1)} %get-tuple-element.106), channel_id=1, source_target_pairs={{0,16},{16,0},{1,17},{17,1},{2,18},{18,2},{3,19},{19,3},{4,20},{20... | collective-permute-start | bytes 1769480 | tf_op jit(solution)/shard_map/ppermute | solution.py:226
  29.7 8.5 %collective-permute-start.8 = (bf16[64,2176]{1,0:T(8,128)(2,1)S(1)}, bf16[64,2176]{1,0:T(8,128)(2,1)S(1)}, u32[]{:S(2)}, u32[]{:S(2)}) collective-permute-start(bf16[64,2176]{1,0:T(8,128)(2,1)S(1)} %get-tuple-element.110.refs_0_), channel_id=1, source_target_pairs={{0,2},{1,3},{2,0},{3,1},{4,6},{5,7},{6,4},{7,5},{8,10},{9,11},{10,... | collective-permute-start | bytes 835592 | tf_op jit(solution)/shard_map/ppermute | solution.py:223
  30.3 21.0 %collective-permute-start.12 = (bf16[64,2176]{1,0:T(8,128)(2,1)S(1)}, bf16[64,2176]{1,0:T(8,128)(2,1)S(1)}, u32[]{:S(2)}, u32[]{:S(2)}) collective-permute-start(bf16[64,2176]{1,0:T(8,128)(2,1)S(1)} %get-tuple-element.109.refs_0_), channel_id=1, source_target_pairs={{0,12},{1,13},{2,14},{3,15},{4,8},{5,9},{6,10},{7,11},{8,4},{9,5},... | collective-permute-start | bytes 835592 | tf_op jit(solution)/shard_map/ppermute | solution.py:223
  38.2 2.0 %collective-permute-start.10 = (bf16[128,2176]{1,0:T(8,128)(2,1)S(1)}, bf16[128,2176]{1,0:T(8,128)(2,1)S(1)}, u32[]{:S(2)}, u32[]{:S(2)}) collective-permute-start(bf16[128,2176]{1,0:T(8,128)(2,1)S(1)} %get-tuple-element.114.refs_0_), channel_id=1, source_target_pairs={{0,1},{1,0},{2,3},{3,2},{4,5},{5,4},{6,7},{7,6},{8,9},{9,8},{10,11... | collective-permute-start | bytes 1671176 | tf_op jit(solution)/shard_map/ppermute | solution.py:223
  49.1 3.8 %collective-permute-start.11 = (bf16[64,2048]{1,0:T(8,128)(2,1)S(1)}, bf16[64,2048]{1,0:T(8,128)(2,1)S(1)}, u32[]{:S(2)}, u32[]{:S(2)}) collective-permute-start(bf16[64,2048]{1,0:T(8,128)(2,1)S(1)} %get-tuple-element.121), channel_id=1, source_target_pairs={{0,1},{1,0},{2,3},{3,2},{4,5},{5,4},{6,7},{7,6},{8,9},{9,8},{10,11... | collective-permute-start | bytes 786440 | tf_op jit(solution)/shard_map/ppermute | solution.py:223
  49.1 24.5 %collective-permute-start.13 = (bf16[640,768]{1,0:T(8,128)(2,1)S(1)}, bf16[640,768]{1,0:T(8,128)(2,1)S(1)}, u32[]{:S(2)}, u32[]{:S(2)}) collective-permute-start(bf16[640,768]{1,0:T(8,128)(2,1)S(1)} %get-tuple-element.125), channel_id=1, source_target_pairs={{0,16},{16,0},{1,17},{17,1},{2,18},{18,2},{3,19},{19,3},{4,20},{20... | collective-permute-start | bytes 2949128 | tf_op jit(solution)/shard_map/ppermute | solution.py:226
  50.7 19.0 %collective-permute-start.14 = (bf16[64,2176]{1,0:T(8,128)(2,1)S(1)}, bf16[64,2176]{1,0:T(8,128)(2,1)S(1)}, u32[]{:S(2)}, u32[]{:S(2)}) collective-permute-start(bf16[64,2176]{1,0:T(8,128)(2,1)S(1)} %get-tuple-element.126), channel_id=1, source_target_pairs={{0,2},{1,3},{2,0},{3,1},{4,6},{5,7},{6,4},{7,5},{8,10},{9,11},{10,... | collective-permute-start | bytes 835592 | tf_op jit(solution)/shard_map/ppermute | solution.py:223
  51.3 14.1 %collective-permute-start.15 = (bf16[64,2176]{1,0:T(8,128)(2,1)S(1)}, bf16[64,2176]{1,0:T(8,128)(2,1)S(1)}, u32[]{:S(2)}, u32[]{:S(2)}) collective-permute-start(bf16[64,2176]{1,0:T(8,128)(2,1)S(1)} %get-tuple-element.127.refs_0_), channel_id=1, source_target_pairs={{0,2},{1,3},{2,0},{3,1},{4,6},{5,7},{6,4},{7,5},{8,10},{9,11},{10,... | collective-permute-start | bytes 835592 | tf_op jit(solution)/shard_map/ppermute | solution.py:223
  65.5 2.0 %collective-permute-start.16 = (bf16[128,2176]{1,0:T(8,128)(2,1)S(1)}, bf16[128,2176]{1,0:T(8,128)(2,1)S(1)}, u32[]{:S(2)}, u32[]{:S(2)}) collective-permute-start(bf16[128,2176]{1,0:T(8,128)(2,1)S(1)} %get-tuple-element.129.refs_0_), channel_id=1, source_target_pairs={{0,1},{1,0},{2,3},{3,2},{4,5},{5,4},{6,7},{7,6},{8,9},{9,8},{10,11... | collective-permute-start | bytes 1671176 | tf_op jit(solution)/shard_map/ppermute | solution.py:223
  69.8 10.3 %collective-permute-start.19 = (bf16[64,2176]{1,0:T(8,128)(2,1)S(1)}, bf16[64,2176]{1,0:T(8,128)(2,1)S(1)}, u32[]{:S(2)}, u32[]{:S(2)}) collective-permute-start(bf16[64,2176]{1,0:T(8,128)(2,1)S(1)} %get-tuple-element.139.refs_0_), channel_id=1, source_target_pairs={{0,1},{1,0},{2,3},{3,2},{4,5},{5,4},{6,7},{7,6},{8,9},{9,8},{10,11... | collective-permute-start | bytes 835592 | tf_op jit(solution)/shard_map/ppermute | solution.py:223
  70.0 24.7 %collective-permute-start.20 = (bf16[640,768]{1,0:T(8,128)(2,1)S(1)}, bf16[640,768]{1,0:T(8,128)(2,1)S(1)}, u32[]{:S(2)}, u32[]{:S(2)}) collective-permute-start(bf16[640,768]{1,0:T(8,128)(2,1)S(1)} %get-tuple-element.142), channel_id=1, source_target_pairs={{0,16},{16,0},{1,17},{17,1},{2,18},{18,2},{3,19},{19,3},{4,20},{20... | collective-permute-start | bytes 2949128 | tf_op jit(solution)/shard_map/ppermute | solution.py:226
  77.7 25.4 %collective-permute-start.24 = (bf16[256,768]{1,0:T(8,128)(2,1)S(1)}, bf16[256,768]{1,0:T(8,128)(2,1)S(1)}, u32[]{:S(2)}, u32[]{:S(2)}) collective-permute-start(bf16[256,768]{1,0:T(8,128)(2,1)S(1)} %get-tuple-element.152.refs_2_), channel_id=1, source_target_pairs={{0,16},{16,0},{1,17},{17,1},{2,18},{18,2},{3,19},{19,3},{4,20},{20... | collective-permute-start | bytes 1179656 | tf_op jit(solution)/shard_map/ppermute | solution.py:226
  79.6 17.4 %collective-permute-start.18 = (bf16[64,2048]{1,0:T(8,128)(2,1)S(1)}, bf16[64,2048]{1,0:T(8,128)(2,1)S(1)}, u32[]{:S(2)}, u32[]{:S(2)}) collective-permute-start(bf16[64,2048]{1,0:T(8,128)(2,1)S(1)} %get-tuple-element.138), channel_id=1, source_target_pairs={{0,4},{1,5},{2,6},{3,7},{4,0},{5,1},{6,2},{7,3},{8,12},{9,13},{10,... | collective-permute-start | bytes 786440 | tf_op jit(solution)/shard_map/ppermute | solution.py:223
  98.8 2.2 %collective-permute-start.21 = (bf16[64,2048]{1,0:T(8,128)(2,1)S(1)}, bf16[64,2048]{1,0:T(8,128)(2,1)S(1)}, u32[]{:S(2)}, u32[]{:S(2)}) collective-permute-start(bf16[64,2048]{1,0:T(8,128)(2,1)S(1)} %get-tuple-element.148), channel_id=1, source_target_pairs={{0,1},{1,0},{2,3},{3,2},{4,5},{5,4},{6,7},{7,6},{8,9},{9,8},{10,11... | collective-permute-start | bytes 786440 | tf_op jit(solution)/shard_map/ppermute | solution.py:223
  98.9 12.6 %collective-permute-start.23 = (bf16[256,768]{1,0:T(8,128)(2,1)S(1)}, bf16[256,768]{1,0:T(8,128)(2,1)S(1)}, u32[]{:S(2)}, u32[]{:S(2)}) collective-permute-start(bf16[256,768]{1,0:T(8,128)(2,1)S(1)} %get-tuple-element.151.refs_2_), channel_id=1, source_target_pairs={{0,16},{16,0},{1,17},{17,1},{2,18},{18,2},{3,19},{19,3},{4,20},{20... | collective-permute-start | bytes 1179656 | tf_op jit(solution)/shard_map/ppermute | solution.py:226
  100.7 19.0 %collective-permute-start.29 = (bf16[256,768]{1,0:T(8,128)(2,1)S(1)}, bf16[256,768]{1,0:T(8,128)(2,1)S(1)}, u32[]{:S(2)}, u32[]{:S(2)}) collective-permute-start(bf16[256,768]{1,0:T(8,128)(2,1)S(1)} %get-tuple-element.167), channel_id=1, source_target_pairs={{0,16},{16,0},{1,17},{17,1},{2,18},{18,2},{3,19},{19,3},{4,20},{20... | collective-permute-start | bytes 1179656 | tf_op jit(solution)/shard_map/ppermute | solution.py:226
  101.1 13.0 %collective-permute-start.22 = (bf16[64,2048]{1,0:T(8,128)(2,1)S(1)}, bf16[64,2048]{1,0:T(8,128)(2,1)S(1)}, u32[]{:S(2)}, u32[]{:S(2)}) collective-permute-start(bf16[64,2048]{1,0:T(8,128)(2,1)S(1)} %get-tuple-element.150), channel_id=1, source_target_pairs={{0,6},{1,7},{2,4},{3,5},{4,2},{5,3},{6,0},{7,1},{8,14},{9,15},{10,... | collective-permute-start | bytes 786440 | tf_op jit(solution)/shard_map/ppermute | solution.py:223
  105.5 2.0 %collective-permute-start.25 = (bf16[128,2048]{1,0:T(8,128)(2,1)S(1)}, bf16[128,2048]{1,0:T(8,128)(2,1)S(1)}, u32[]{:S(2)}, u32[]{:S(2)}) collective-permute-start(bf16[128,2048]{1,0:T(8,128)(2,1)S(1)} %get-tuple-element.155), channel_id=1, source_target_pairs={{0,1},{1,0},{2,3},{3,2},{4,5},{5,4},{6,7},{7,6},{8,9},{9,8},{10,11... | collective-permute-start | bytes 1572872 | tf_op jit(solution)/shard_map/ppermute | solution.py:223
  107.6 8.4 %collective-permute-start.26 = (bf16[64,2048]{1,0:T(8,128)(2,1)S(1)}, bf16[64,2048]{1,0:T(8,128)(2,1)S(1)}, u32[]{:S(2)}, u32[]{:S(2)}) collective-permute-start(bf16[64,2048]{1,0:T(8,128)(2,1)S(1)} %get-tuple-element.161), channel_id=1, source_target_pairs={{0,2},{1,3},{2,0},{3,1},{4,6},{5,7},{6,4},{7,5},{8,10},{9,11},{10,... | collective-permute-start | bytes 786440 | tf_op jit(solution)/shard_map/ppermute | solution.py:223
  114.0 2.0 %collective-permute-start.27 = (bf16[128,2048]{1,0:T(8,128)(2,1)S(1)}, bf16[128,2048]{1,0:T(8,128)(2,1)S(1)}, u32[]{:S(2)}, u32[]{:S(2)}) collective-permute-start(bf16[128,2048]{1,0:T(8,128)(2,1)S(1)} %get-tuple-element.163), channel_id=1, source_target_pairs={{0,1},{1,0},{2,3},{3,2},{4,5},{5,4},{6,7},{7,6},{8,9},{9,8},{10,11... | collective-permute-start | bytes 1572872 | tf_op jit(solution)/shard_map/ppermute | solution.py:223
  116.1 16.1 %collective-permute-start.28 = (bf16[64,2048]{1,0:T(8,128)(2,1)S(1)}, bf16[64,2048]{1,0:T(8,128)(2,1)S(1)}, u32[]{:S(2)}, u32[]{:S(2)}) collective-permute-start(bf16[64,2048]{1,0:T(8,128)(2,1)S(1)} %get-tuple-element.166), channel_id=1, source_target_pairs={{0,8},{1,9},{2,10},{3,11},{4,12},{5,13},{6,14},{7,15},{8,0},{9,1},... | collective-permute-start | bytes 786440 | tf_op jit(solution)/shard_map/ppermute | solution.py:223
  118.8 8.1 %collective-permute-start.31 = (bf16[64,2048]{1,0:T(8,128)(2,1)S(1)}, bf16[64,2048]{1,0:T(8,128)(2,1)S(1)}, u32[]{:S(2)}, u32[]{:S(2)}) collective-permute-start(bf16[64,2048]{1,0:T(8,128)(2,1)S(1)} %get-tuple-element.171), channel_id=1, source_target_pairs={{0,2},{1,3},{2,0},{3,1},{4,6},{5,7},{6,4},{7,5},{8,10},{9,11},{10,... | collective-permute-start | bytes 786440 | tf_op jit(solution)/shard_map/ppermute | solution.py:223
  121.2 6.7 %collective-permute-start.30 = (bf16[128,768]{1,0:T(8,128)(2,1)S(1)}, bf16[128,768]{1,0:T(8,128)(2,1)S(1)}, u32[]{:S(2)}, u32[]{:S(2)}) collective-permute-start(bf16[128,768]{1,0:T(8,128)(2,1)S(1)} %get-tuple-element.169.refs_2_), channel_id=1, source_target_pairs={{0,16},{16,0},{1,17},{17,1},{2,18},{18,2},{3,19},{19,3},{4,20},{20... | collective-permute-start | bytes 589832 | tf_op jit(solution)/shard_map/ppermute | solution.py:226
  129.7 14.3 %collective-permute-start.33 = (bf16[64,2048]{1,0:T(8,128)(2,1)S(1)}, bf16[64,2048]{1,0:T(8,128)(2,1)S(1)}, u32[]{:S(2)}, u32[]{:S(2)}) collective-permute-start(bf16[64,2048]{1,0:T(8,128)(2,1)S(1)} %get-tuple-element.179), channel_id=1, source_target_pairs={{0,12},{1,13},{2,14},{3,15},{4,8},{5,9},{6,10},{7,11},{8,4},{9,5},... | collective-permute-start | bytes 786440 | tf_op jit(solution)/shard_map/ppermute | solution.py:223
  131.3 12.7 %collective-permute-start.34 = (bf16[64,2048]{1,0:T(8,128)(2,1)S(1)}, bf16[64,2048]{1,0:T(8,128)(2,1)S(1)}, u32[]{:S(2)}, u32[]{:S(2)}) collective-permute-start(bf16[64,2048]{1,0:T(8,128)(2,1)S(1)} %get-tuple-element.180), channel_id=1, source_target_pairs={{0,2},{1,3},{2,0},{3,1},{4,6},{5,7},{6,4},{7,5},{8,10},{9,11},{10,... | collective-permute-start | bytes 786440 | tf_op jit(solution)/shard_map/ppermute | solution.py:223
  (10 other events, 21.3 us)

commit v4 on v3

--- a/solution.py
+++ b/solution.py
@@ -85,7 +85,7 @@
         refs = list(refs)
         taken = [refs.pop(0) for _ in inputs]
         carried = [refs.pop(0) for _ in flat]
-        refs.pop(0)
+        del refs[: len(after)]
         made = [refs.pop(0) for _ in outputs]
         joined_refs = [refs.pop(0) for _ in joined]
         token_ref = refs.pop(0)
@@ -101,13 +101,13 @@
 
     results = pl.pallas_call(
         run,
-        in_specs=[spec for _, spec in inputs] + [HERE] * len(flat) + [pl.BlockSpec(memory_space=pl.ANY)],
+        in_specs=[spec for _, spec in inputs] + [HERE] * len(flat) + [pl.BlockSpec(memory_space=pl.ANY)] * len(after),
         out_specs=[HERE] * (len(outputs) + len(joined) + 1),
         out_shape=list(outputs) + joined + [TOKEN],
         scratch_shapes=list(scratch),
         compiler_params=pltpu.CompilerParams(vmem_limit_bytes=VMEM_LIMIT),
         cost_estimate=pl.CostEstimate(flops=cost, bytes_accessed=1, transcendentals=0),
-    )(*[value for value, _ in inputs], *flat, after)
+    )(*[value for value, _ in inputs], *flat, *after)
     return results[:-1], results[-1]
 
 
@@ -231,9 +231,10 @@
     tail, number = [jnp.zeros(TOKEN.shape, TOKEN.dtype)], [0]
 
     def step(kernel, inputs, outputs, scratch=(), relays=()):
-        results, tail[0] = call(
-            kernel, inputs, outputs, tail[0], scratch, relays, COSTS.get(number[0], COST)
-        )
+        results, token = call(
+            kernel, inputs, outputs, list(tail), scratch, relays, COSTS.get(number[0], COST)
+        )
+        tail[:] = [token]
         number[0] += 1
         return results
 
@@ -294,6 +295,9 @@
     def gap():
         step(None, [], [])
 
+    def meet():
+        tail.append(swap(tail[0], 1))
+
     (labelled,) = step(
         functools.partial(label_kernel, sources),
         [tokens, expert_ids.T, gate_weights.T],
@@ -305,6 +309,7 @@
     y0 = cross(sent)
     (again,) = relay([labelled])
     z8 = swap(again, 8)
+    meet()
     (b4,) = relay([z4])
     b5, x6 = swap(b4, 1), swap(b4, 2)
     gap()
@@ -328,6 +333,7 @@
     y3 = cross(sent)
     (again,) = relay([again])
     x2 = swap(again, 2)
+    meet()
     (h2,) = hidden(p2, y2)
     c0, c1 = outputs(p0, h0, y2, 4 * rows, rows)
     (b12,) = relay([z12])

time: 145 us -> 142 us (0.979)
  starting transfers between devices: 28.8 us -> 25.6 us
    ppermute x26 -> x28, waiting for transfers between devices: 44.9 us -> 41.9 us  [swap(): return lax.ppermute(value, 'expert', [(i, i ^ r) for i in range(sources)])]
    ppermute x9, waiting for transfers between devices: 30.8 us -> 33.8 us  [cross(): return lax.ppermute(value, 'dp', [(0, 1), (1, 0)])]
    ppermute x9, starting transfers between devices: 12.2 us -> 9.95 us  [cross(): return lax.ppermute(value, 'dp', [(0, 1), (1, 0)])]
    ppermute x26 -> x28, starting transfers between devices: 16.6 us -> 15.7 us  [swap(): return lax.ppermute(value, 'expert', [(i, i ^ r) for i in range(sources)])]
  transfers between devices with their start and end apart: 35 -> 37, of which waited for: 20 -> 20; matrix products, arithmetic and copies ran while one was open for 0% -> 0% of each run, Pallas kernels for 23% -> 24%
where the time goes in v4:
time: 142 us; the launch traced here: 141 us
  waiting for transfers between devices  75.7 us (53%)
  Pallas kernels  34.5 us (24%)
  starting transfers between devices  25.6 us (18%)
  local copies, waits for them, and re-layouts  5.2 us (4%)
    ppermute x28, waiting for transfers between devices, swap(): return lax.ppermute(value, 'expert', [(i, i ^ r) for i in range(sources)])  41.9 us
    pallas_call x47, Pallas kernels, call(): pl.pallas_call(run, in_specs=[spec for _, spec in inputs] + [HERE] * len(...  34.5 us
    ppermute x9, waiting for transfers between devices, cross(): return lax.ppermute(value, 'dp', [(0, 1), (1, 0)])  33.8 us
    ppermute x28, starting transfers between devices, swap(): return lax.ppermute(value, 'expert', [(i, i ^ r) for i in range(sources)])  15.7 us
    ppermute x9, starting transfers between devices, cross(): return lax.ppermute(value, 'dp', [(0, 1), (1, 0)])  9.95 us
    unnamed x14, local copies, waits for them, and re-layouts  5.2 us
  transfers between devices with their start and end apart: 37, of which 20 were waited for; matrix products, arithmetic and copies ran while one was open for 0% of the time, Pallas kernels for 24%

profile of v4, /device:TPU:8, one launch (start us, length us, event | category | flops | bytes accessed | tf_op | source)
XLA Modules:
  0.0 141.4 jit_solution(5876162895069680811)
XLA Ops:
  5.1 1.8 %copy-done.1 = bf16[1,2048,1536]{2,1,0:T(8,128)(2,1)S(1)} copy-done((bf16[1,2048,1536]{2,1,0:T(8,128)(2,1)S(1)}, bf16[1,2048,1536]{2,1,0:T(8,128)(2,1)}, u32[]{:S(2)}) %copy-start.1) | copy-done | bytes 6291480
  8.5 1.6 %collective-permute-start.1 = (bf16[256,768]{1,0:T(8,128)(2,1)S(1)}, bf16[256,768]{1,0:T(8,128)(2,1)S(1)}, u32[]{:S(2)}, u32[]{:S(2)}) collective-permute-start(bf16[256,768]{1,0:T(8,128)(2,1)S(1)} %get-tuple-element.96), channel_id=1, source_target_pairs={{0,16},{16,0},{1,17},{17,1},{2,18},{18,2},{3,19},{19,3},{4,20},{20... | collective-permute-start | bytes 1179656 | tf_op jit(solution)/shard_map/ppermute | solution.py:226
  10.0 2.6 %collective-permute-start.8 = (bf16[64,2176]{1,0:T(8,128)(2,1)S(1)}, bf16[64,2176]{1,0:T(8,128)(2,1)S(1)}, u32[]{:S(2)}, u32[]{:S(2)}) collective-permute-start(bf16[64,2176]{1,0:T(8,128)(2,1)S(1)} %get-tuple-element.107.refs_1_), channel_id=1, source_target_pairs={{0,8},{1,9},{2,10},{3,11},{4,12},{5,13},{6,14},{7,15},{8,0},{9,1},... | collective-permute-start | bytes 835592 | tf_op jit(solution)/shard_map/ppermute | solution.py:223
  17.2 3.9 %collective-permute-done.4.refs_0_ = bf16[64,2176]{1,0:T(8,128)(2,1)S(1)} collective-permute-done((bf16[64,2176]{1,0:T(8,128)(2,1)S(1)}, bf16[64,2176]{1,0:T(8,128)(2,1)S(1)}, u32[]{:S(2)}, u32[]{:S(2)}) %collective-permute-start.4) | collective-permute-done | bytes 278560 | tf_op jit(solution)/shard_map/ppermute | solution.py:223
  24.8 1.6 %collective-permute-start.7 = (bf16[384,768]{1,0:T(8,128)(2,1)S(1)}, bf16[384,768]{1,0:T(8,128)(2,1)S(1)}, u32[]{:S(2)}, u32[]{:S(2)}) collective-permute-start(bf16[384,768]{1,0:T(8,128)(2,1)S(1)} %get-tuple-element.106), channel_id=1, source_target_pairs={{0,16},{16,0},{1,17},{17,1},{2,18},{18,2},{3,19},{19,3},{4,20},{20... | collective-permute-start | bytes 1769480 | tf_op jit(solution)/shard_map/ppermute | solution.py:226
  28.0 5.3 %collective-permute-done.10.refs_4_ = bf16[256,768]{1,0:T(8,128)(2,1)S(1)} collective-permute-done((bf16[256,768]{1,0:T(8,128)(2,1)S(1)}, bf16[256,768]{1,0:T(8,128)(2,1)S(1)}, u32[]{:S(2)}, u32[]{:S(2)}) %collective-permute-start.10) | collective-permute-done | bytes 393248 | tf_op jit(solution)/shard_map/ppermute | solution.py:226
  35.1 1.9 %collective-permute-done.11.refs_1_ = bf16[128,2176]{1,0:T(8,128)(2,1)S(1)} collective-permute-done((bf16[128,2176]{1,0:T(8,128)(2,1)S(1)}, bf16[128,2176]{1,0:T(8,128)(2,1)S(1)}, u32[]{:S(2)}, u32[]{:S(2)}) %collective-permute-start.11) | collective-permute-done | bytes 557088 | tf_op jit(solution)/shard_map/ppermute | solution.py:223
  37.0 2.2 %shard_map.77 = (bf16[640,768]{1,0:T(8,128)(2,1)S(1)}, f32[8,128]{1,0:T(8,128)S(1)}) custom-call(bf16[128,2176]{1,0:T(8,128)(2,1)S(1)} %get-tuple-element.114.refs_0_, bf16[128,2176]{1,0:T(8,128)(2,1)S(1)} %collective-permute-done.11.refs_1_, bf16[1,2048,1536]{2,1,0:T(8,128)(2,1)S(1)} %copy-done, bf16[1,2048,1536]{2,1,0:T(8,128)(2,1)S(1)} %copy-done.1, ...), custom_call_target="tpu_custom_call" | custom-call | flops 8000000000 | bytes 1 | tf_op jit(solution)/shard_map/pallas_call | solution.py:102
  42.8 3.1 %collective-permute-done.7.refs_4_.refs_3_ = bf16[384,768]{1,0:T(8,128)(2,1)S(1)} collective-permute-done((bf16[384,768]{1,0:T(8,128)(2,1)S(1)}, bf16[384,768]{1,0:T(8,128)(2,1)S(1)}, u32[]{:S(2)}, u32[]{:S(2)}) %collective-permute-start.7) | collective-permute-done | bytes 589856 | tf_op jit(solution)/shard_map/ppermute | solution.py:226
  47.4 1.7 %shard_map.80 = (f32[64,2048]{1,0:T(8,128)S(1)}, bf16[64,2048]{1,0:T(8,128)(2,1)S(1)}, f32[8,128]{1,0:T(8,128)S(1)}) custom-call(bf16[64,2176]{1,0:T(8,128)(2,1)S(1)} %get-tuple-element.94.refs_0_, bf16[64,2176]{1,0:T(8,128)(2,1)S(1)} %collective-permute-done.refs_1_, bf16[128,768]{1,0:T(8,128)(2,1)S(1)} %get-tuple-element.103.refs_4_.refs_2_, ...), custom_call_target="tpu_custom_call" | custom-call | flops 8000000000 | bytes 1 | tf_op jit(solution)/shard_map/pallas_call | solution.py:102
  49.2 5.2 %collective-permute-done.14.refs_0_ = bf16[64,2176]{1,0:T(8,128)(2,1)S(1)} collective-permute-done((bf16[64,2176]{1,0:T(8,128)(2,1)S(1)}, bf16[64,2176]{1,0:T(8,128)(2,1)S(1)}, u32[]{:S(2)}, u32[]{:S(2)}) %collective-permute-start.14) | collective-permute-done | bytes 278560 | tf_op jit(solution)/shard_map/ppermute | solution.py:223
  54.4 1.6 %collective-permute-start.17 = (bf16[64,2176]{1,0:T(8,128)(2,1)S(1)}, bf16[64,2176]{1,0:T(8,128)(2,1)S(1)}, u32[]{:S(2)}, u32[]{:S(2)}) collective-permute-start(bf16[64,2176]{1,0:T(8,128)(2,1)S(1)} %get-tuple-element.127.refs_0_), channel_id=1, source_target_pairs={{0,2},{1,3},{2,0},{3,1},{4,6},{5,7},{6,4},{7,5},{8,10},{9,11},{10,... | collective-permute-start | bytes 835592 | tf_op jit(solution)/shard_map/ppermute | solution.py:223
  56.1 6.6 %collective-permute-done.17.refs_1_ = bf16[64,2176]{1,0:T(8,128)(2,1)S(1)} collective-permute-done((bf16[64,2176]{1,0:T(8,128)(2,1)S(1)}, bf16[64,2176]{1,0:T(8,128)(2,1)S(1)}, u32[]{:S(2)}, u32[]{:S(2)}) %collective-permute-start.17) | collective-permute-done | bytes 278560 | tf_op jit(solution)/shard_map/ppermute | solution.py:223
  62.8 1.9 %collective-permute-done.18.refs_1_ = bf16[128,2176]{1,0:T(8,128)(2,1)S(1)} collective-permute-done((bf16[128,2176]{1,0:T(8,128)(2,1)S(1)}, bf16[128,2176]{1,0:T(8,128)(2,1)S(1)}, u32[]{:S(2)}, u32[]{:S(2)}) %collective-permute-start.18) | collective-permute-done | bytes 557088 | tf_op jit(solution)/shard_map/ppermute | solution.py:223
  64.7 2.2 %shard_map.85 = (bf16[640,768]{1,0:T(8,128)(2,1)S(1)}, f32[8,128]{1,0:T(8,128)S(1)}) custom-call(bf16[128,2176]{1,0:T(8,128)(2,1)S(1)} %get-tuple-element.129.refs_0_, bf16[128,2176]{1,0:T(8,128)(2,1)S(1)} %collective-permute-done.18.refs_1_, bf16[1,2048,1536]{2,1,0:T(8,128)(2,1)S(1)} %copy-done, bf16[1,2048,1536]{2,1,0:T(8,128)(2,1)S(1)} %copy-done.1, ...), custom_call_target="tpu_custom_call" | custom-call | flops 8000000000 | bytes 1 | tf_op jit(solution)/shard_map/pallas_call | solution.py:102
  67.7 2.3 %shard_map.87 = (bf16[256,768]{1,0:T(8,128)(2,1)S(1)}, f32[8,128]{1,0:T(8,128)S(1)}) custom-call(bf16[128,2176]{1,0:T(8,128)(2,1)S(1)} %get-tuple-element.114.refs_0_, bf16[128,2176]{1,0:T(8,128)(2,1)S(1)} %collective-permute-done.11.refs_1_, bf16[1,2048,1536]{2,1,0:T(8,128)(2,1)S(1)} %copy-done, bf16[1,2048,1536]{2,1,0:T(8,128)(2,1)S(1)} %copy-done.1, ...), custom_call_target="tpu_custom_call" | custom-call | flops 8000000000 | bytes 1 | tf_op jit(solution)/shard_map/pallas_call | solution.py:102
  70.0 1.7 %shard_map.88 = (f32[64,2048]{1,0:T(8,128)S(1)}, bf16[64,2048]{1,0:T(8,128)(2,1)S(1)}, f32[8,128]{1,0:T(8,128)S(1)}) custom-call(bf16[64,2176]{1,0:T(8,128)(2,1)S(1)} %get-tuple-element.99.refs_0_, bf16[64,2176]{1,0:T(8,128)(2,1)S(1)} %collective-permute-done.5.refs_1_, bf16[128,768]{1,0:T(8,128)(2,1)S(1)} %get-tuple-element.115.refs_4_.refs_2_, ...), custom_call_target="tpu_custom_call" | custom-call | flops 8000000000 | bytes 1 | tf_op jit(solution)/shard_map/pallas_call | solution.py:102
  75.1 16.7 %collective-permute-done.22.refs_4_.refs_3_ = bf16[640,768]{1,0:T(8,128)(2,1)S(1)} collective-permute-done((bf16[640,768]{1,0:T(8,128)(2,1)S(1)}, bf16[640,768]{1,0:T(8,128)(2,1)S(1)}, u32[]{:S(2)}, u32[]{:S(2)}) %collective-permute-start.22) | collective-permute-done | bytes 983072 | tf_op jit(solution)/shard_map/ppermute | solution.py:226
  91.8 2.3 %shard_map.92 = (bf16[256,768]{1,0:T(8,128)(2,1)S(1)}, f32[8,128]{1,0:T(8,128)S(1)}) custom-call(bf16[128,2176]{1,0:T(8,128)(2,1)S(1)} %get-tuple-element.129.refs_0_, bf16[128,2176]{1,0:T(8,128)(2,1)S(1)} %collective-permute-done.18.refs_1_, bf16[1,2048,1536]{2,1,0:T(8,128)(2,1)S(1)} %copy-done, bf16[1,2048,1536]{2,1,0:T(8,128)(2,1)S(1)} %copy-done.1, ...), custom_call_target="tpu_custom_call" | custom-call | flops 8000000000 | bytes 1 | tf_op jit(solution)/shard_map/pallas_call | solution.py:102
  94.2 1.7 %shard_map.94 = (f32[64,2048]{1,0:T(8,128)S(1)}, bf16[64,2048]{1,0:T(8,128)(2,1)S(1)}, f32[8,128]{1,0:T(8,128)S(1)}) custom-call(bf16[64,2176]{1,0:T(8,128)(2,1)S(1)} %get-tuple-element.104.refs_0_, bf16[64,2176]{1,0:T(8,128)(2,1)S(1)} %collective-permute-done.6.refs_1_, bf16[128,768]{1,0:T(8,128)(2,1)S(1)} %get-tuple-element.130.refs_4_.refs_2_, ...), custom_call_target="tpu_custom_call" | custom-call | flops 8000000000 | bytes 1 | tf_op jit(solution)/shard_map/pallas_call | solution.py:102
  98.2 1.9 %collective-permute-done.26.refs_3_ = bf16[256,768]{1,0:T(8,128)(2,1)S(1)} collective-permute-done((bf16[256,768]{1,0:T(8,128)(2,1)S(1)}, bf16[256,768]{1,0:T(8,128)(2,1)S(1)}, u32[]{:S(2)}, u32[]{:S(2)}) %collective-permute-start.26) | collective-permute-done | bytes 393248 | tf_op jit(solution)/shard_map/ppermute | solution.py:226
  100.1 2.5 %shard_map.97 = (f32[128,2048]{1,0:T(8,128)S(1)}, bf16[128,2048]{1,0:T(8,128)(2,1)S(1)}, f32[8,128]{1,0:T(8,128)S(1)}) custom-call(bf16[128,2176]{1,0:T(8,128)(2,1)S(1)} %get-tuple-element.114.refs_0_, bf16[128,2176]{1,0:T(8,128)(2,1)S(1)} %collective-permute-done.11.refs_1_, bf16[256,768]{1,0:T(8,128)(2,1)S(1)} %get-tuple-element.152.refs_2_, ...), custom_call_target="tpu_custom_call" | custom-call | flops 8000000000 | bytes 1 | tf_op jit(solution)/shard_map/pallas_call | solution.py:102
  102.7 1.9 %collective-permute-done.27.refs_1_ = bf16[128,2048]{1,0:T(8,128)(2,1)S(1)} collective-permute-done((bf16[128,2048]{1,0:T(8,128)(2,1)S(1)}, bf16[128,2048]{1,0:T(8,128)(2,1)S(1)}, u32[]{:S(2)}, u32[]{:S(2)}) %collective-permute-start.27) | collective-permute-done | bytes 524320 | tf_op jit(solution)/shard_map/ppermute | solution.py:223
  104.6 1.6 %collective-permute-start.28 = (bf16[64,2048]{1,0:T(8,128)(2,1)S(1)}, bf16[64,2048]{1,0:T(8,128)(2,1)S(1)}, u32[]{:S(2)}, u32[]{:S(2)}) collective-permute-start(bf16[64,2048]{1,0:T(8,128)(2,1)S(1)} %get-tuple-element.161), channel_id=1, source_target_pairs={{0,2},{1,3},{2,0},{3,1},{4,6},{5,7},{6,4},{7,5},{8,10},{9,11},{10,... | collective-permute-start | bytes 786440 | tf_op jit(solution)/shard_map/ppermute | solution.py:223
  106.2 2.3 %collective-permute-done.25.refs_3_ = bf16[256,768]{1,0:T(8,128)(2,1)S(1)} collective-permute-done((bf16[256,768]{1,0:T(8,128)(2,1)S(1)}, bf16[256,768]{1,0:T(8,128)(2,1)S(1)}, u32[]{:S(2)}, u32[]{:S(2)}) %collective-permute-start.25) | collective-permute-done | bytes 393248 | tf_op jit(solution)/shard_map/ppermute | solution.py:226
  108.5 2.5 %shard_map.100 = (f32[128,2048]{1,0:T(8,128)S(1)}, bf16[128,2048]{1,0:T(8,128)(2,1)S(1)}, f32[8,128]{1,0:T(8,128)S(1)}) custom-call(bf16[128,2176]{1,0:T(8,128)(2,1)S(1)} %get-tuple-element.129.refs_0_, bf16[128,2176]{1,0:T(8,128)(2,1)S(1)} %collective-permute-done.18.refs_1_, bf16[256,768]{1,0:T(8,128)(2,1)S(1)} %get-tuple-element.151.refs_2_, ...), custom_call_target="tpu_custom_call" | custom-call | flops 8000000000 | bytes 1 | tf_op jit(solution)/shard_map/pallas_call | solution.py:102
  111.2 1.8 %collective-permute-done.29.refs_1_ = bf16[128,2048]{1,0:T(8,128)(2,1)S(1)} collective-permute-done((bf16[128,2048]{1,0:T(8,128)(2,1)S(1)}, bf16[128,2048]{1,0:T(8,128)(2,1)S(1)}, u32[]{:S(2)}, u32[]{:S(2)}) %collective-permute-start.29) | collective-permute-done | bytes 524320 | tf_op jit(solution)/shard_map/ppermute | solution.py:223
  114.8 1.7 %collective-permute-done.31.refs_4_ = bf16[256,768]{1,0:T(8,128)(2,1)S(1)} collective-permute-done((bf16[256,768]{1,0:T(8,128)(2,1)S(1)}, bf16[256,768]{1,0:T(8,128)(2,1)S(1)}, u32[]{:S(2)}, u32[]{:S(2)}) %collective-permute-start.31) | collective-permute-done | bytes 393248 | tf_op jit(solution)/shard_map/ppermute | solution.py:226
  118.6 3.0 %collective-permute-done.33.refs_1_ = bf16[64,2048]{1,0:T(8,128)(2,1)S(1)} collective-permute-done((bf16[64,2048]{1,0:T(8,128)(2,1)S(1)}, bf16[64,2048]{1,0:T(8,128)(2,1)S(1)}, u32[]{:S(2)}, u32[]{:S(2)}) %collective-permute-start.33) | collective-permute-done | bytes 262176 | tf_op jit(solution)/shard_map/ppermute | solution.py:223
  121.7 2.8 %collective-permute-done.32.refs_3_ = bf16[128,768]{1,0:T(8,128)(2,1)S(1)} collective-permute-done((bf16[128,768]{1,0:T(8,128)(2,1)S(1)}, bf16[128,768]{1,0:T(8,128)(2,1)S(1)}, u32[]{:S(2)}, u32[]{:S(2)}) %collective-permute-start.32) | collective-permute-done | bytes 196640 | tf_op jit(solution)/shard_map/ppermute | solution.py:226
  124.5 1.7 %shard_map.106 = (f32[64,2048]{1,0:T(8,128)S(1)}, bf16[64,2048]{1,0:T(8,128)(2,1)S(1)}, f32[8,128]{1,0:T(8,128)S(1)}) custom-call(bf16[64,2176]{1,0:T(8,128)(2,1)S(1)} %get-tuple-element.139.refs_0_, bf16[64,2176]{1,0:T(8,128)(2,1)S(1)} %collective-permute-done.21.refs_1_, bf16[128,768]{1,0:T(8,128)(2,1)S(1)} %get-tuple-element.169.refs_2_, ...), custom_call_target="tpu_custom_call" | custom-call | flops 8000000000 | bytes 1 | tf_op jit(solution)/shard_map/pallas_call | solution.py:102
  129.5 11.1 %collective-permute-done.35.refs_1_ = bf16[64,2048]{1,0:T(8,128)(2,1)S(1)} collective-permute-done((bf16[64,2048]{1,0:T(8,128)(2,1)S(1)}, bf16[64,2048]{1,0:T(8,128)(2,1)S(1)}, u32[]{:S(2)}, u32[]{:S(2)}) %collective-permute-start.35) | collective-permute-done | bytes 262176 | tf_op jit(solution)/shard_map/ppermute | solution.py:223
  (105 shorter events, 38.2 us)
Async XLA Ops:
  2.5 10.1 %collective-permute-start.2 = (bf16[64,2176]{1,0:T(8,128)(2,1)S(1)}, bf16[64,2176]{1,0:T(8,128)(2,1)S(1)}, u32[]{:S(2)}, u32[]{:S(2)}) collective-permute-start(bf16[64,2176]{1,0:T(8,128)(2,1)S(1)} %get-tuple-element.94.refs_0_), channel_id=1, source_target_pairs={{0,4},{1,5},{2,6},{3,7},{4,0},{5,1},{6,2},{7,3},{8,12},{9,13},{10,... | collective-permute-start | bytes 835592 | tf_op jit(solution)/shard_map/ppermute | solution.py:223
  8.4 4.2 %collective-permute-start.3 = (f32[8,128]{1,0:T(8,128)S(1)}, f32[8,128]{1,0:T(8,128)S(1)}, u32[]{:S(2)}, u32[]{:S(2)}) collective-permute-start(f32[8,128]{1,0:T(8,128)S(1)} %get-tuple-element.98.refs_1_), channel_id=1, source_target_pairs={{0,1},{1,0},{2,3},{3,2},{4,5},{5,4},{6,7},{7,6},{8,9},{9,8},{10,11... | collective-permute-start | bytes 12296 | tf_op jit(solution)/shard_map/ppermute | solution.py:223
  8.5 13.4 %collective-permute-start.1 = (bf16[256,768]{1,0:T(8,128)(2,1)S(1)}, bf16[256,768]{1,0:T(8,128)(2,1)S(1)}, u32[]{:S(2)}, u32[]{:S(2)}) collective-permute-start(bf16[256,768]{1,0:T(8,128)(2,1)S(1)} %get-tuple-element.96), channel_id=1, source_target_pairs={{0,16},{16,0},{1,17},{17,1},{2,18},{18,2},{3,19},{19,3},{4,20},{20... | collective-permute-start | bytes 1179656 | tf_op jit(solution)/shard_map/ppermute | solution.py:226
  10.0 16.4 %collective-permute-start.8 = (bf16[64,2176]{1,0:T(8,128)(2,1)S(1)}, bf16[64,2176]{1,0:T(8,128)(2,1)S(1)}, u32[]{:S(2)}, u32[]{:S(2)}) collective-permute-start(bf16[64,2176]{1,0:T(8,128)(2,1)S(1)} %get-tuple-element.107.refs_1_), channel_id=1, source_target_pairs={{0,8},{1,9},{2,10},{3,11},{4,12},{5,13},{6,14},{7,15},{8,0},{9,1},... | collective-permute-start | bytes 835592 | tf_op jit(solution)/shard_map/ppermute | solution.py:223
  12.7 8.5 %collective-permute-start.4 = (bf16[64,2176]{1,0:T(8,128)(2,1)S(1)}, bf16[64,2176]{1,0:T(8,128)(2,1)S(1)}, u32[]{:S(2)}, u32[]{:S(2)}) collective-permute-start(bf16[64,2176]{1,0:T(8,128)(2,1)S(1)} %get-tuple-element.99.refs_0_), channel_id=1, source_target_pairs={{0,2},{1,3},{2,0},{3,1},{4,6},{5,7},{6,4},{7,5},{8,10},{9,11},{10,... | collective-permute-start | bytes 835592 | tf_op jit(solution)/shard_map/ppermute | solution.py:223
  21.2 2.2 %collective-permute-start.6 = (bf16[64,2176]{1,0:T(8,128)(2,1)S(1)}, bf16[64,2176]{1,0:T(8,128)(2,1)S(1)}, u32[]{:S(2)}, u32[]{:S(2)}) collective-permute-start(bf16[64,2176]{1,0:T(8,128)(2,1)S(1)} %get-tuple-element.104.refs_0_), channel_id=1, source_target_pairs={{0,1},{1,0},{2,3},{3,2},{4,5},{5,4},{6,7},{7,6},{8,9},{9,8},{10,11... | collective-permute-start | bytes 835592 | tf_op jit(solution)/shard_map/ppermute | solution.py:223
  21.3 12.0 %collective-permute-start.10 = (bf16[256,768]{1,0:T(8,128)(2,1)S(1)}, bf16[256,768]{1,0:T(8,128)(2,1)S(1)}, u32[]{:S(2)}, u32[]{:S(2)}) collective-permute-start(bf16[256,768]{1,0:T(8,128)(2,1)S(1)} %get-tuple-element.111), channel_id=1, source_target_pairs={{0,16},{16,0},{1,17},{17,1},{2,18},{18,2},{3,19},{19,3},{4,20},{20... | collective-permute-start | bytes 1179656 | tf_op jit(solution)/shard_map/ppermute | solution.py:226
  24.8 21.1 %collective-permute-start.7 = (bf16[384,768]{1,0:T(8,128)(2,1)S(1)}, bf16[384,768]{1,0:T(8,128)(2,1)S(1)}, u32[]{:S(2)}, u32[]{:S(2)}) collective-permute-start(bf16[384,768]{1,0:T(8,128)(2,1)S(1)} %get-tuple-element.106), channel_id=1, source_target_pairs={{0,16},{16,0},{1,17},{17,1},{2,18},{18,2},{3,19},{19,3},{4,20},{20... | collective-permute-start | bytes 1769480 | tf_op jit(solution)/shard_map/ppermute | solution.py:226
  26.4 8.5 %collective-permute-start.9 = (bf16[64,2176]{1,0:T(8,128)(2,1)S(1)}, bf16[64,2176]{1,0:T(8,128)(2,1)S(1)}, u32[]{:S(2)}, u32[]{:S(2)}) collective-permute-start(bf16[64,2176]{1,0:T(8,128)(2,1)S(1)} %get-tuple-element.110.refs_0_), channel_id=1, source_target_pairs={{0,2},{1,3},{2,0},{3,1},{4,6},{5,7},{6,4},{7,5},{8,10},{9,11},{10,... | collective-permute-start | bytes 835592 | tf_op jit(solution)/shard_map/ppermute | solution.py:223
  35.0 2.0 %collective-permute-start.11 = (bf16[128,2176]{1,0:T(8,128)(2,1)S(1)}, bf16[128,2176]{1,0:T(8,128)(2,1)S(1)}, u32[]{:S(2)}, u32[]{:S(2)}) collective-permute-start(bf16[128,2176]{1,0:T(8,128)(2,1)S(1)} %get-tuple-element.114.refs_0_), channel_id=1, source_target_pairs={{0,1},{1,0},{2,3},{3,2},{4,5},{5,4},{6,7},{7,6},{8,9},{9,8},{10,11... | collective-permute-start | bytes 1671176 | tf_op jit(solution)/shard_map/ppermute | solution.py:223
  39.3 6.6 %collective-permute-start.12 = (f32[8,128]{1,0:T(8,128)S(1)}, f32[8,128]{1,0:T(8,128)S(1)}, u32[]{:S(2)}, u32[]{:S(2)}) collective-permute-start(f32[8,128]{1,0:T(8,128)S(1)} %get-tuple-element.118.refs_5_), channel_id=1, source_target_pairs={{0,1},{1,0},{2,3},{3,2},{4,5},{5,4},{6,7},{7,6},{8,9},{9,8},{10,11... | collective-permute-start | bytes 12296 | tf_op jit(solution)/shard_map/ppermute | solution.py:223
  39.5 14.9 %collective-permute-start.14 = (bf16[64,2176]{1,0:T(8,128)(2,1)S(1)}, bf16[64,2176]{1,0:T(8,128)(2,1)S(1)}, u32[]{:S(2)}, u32[]{:S(2)}) collective-permute-start(bf16[64,2176]{1,0:T(8,128)(2,1)S(1)} %get-tuple-element.109.refs_0_), channel_id=1, source_target_pairs={{0,12},{1,13},{2,14},{3,15},{4,8},{5,9},{6,10},{7,11},{8,4},{9,5},... | collective-permute-start | bytes 835592 | tf_op jit(solution)/shard_map/ppermute | solution.py:223
  39.8 27.9 %collective-permute-start.15 = (bf16[640,768]{1,0:T(8,128)(2,1)S(1)}, bf16[640,768]{1,0:T(8,128)(2,1)S(1)}, u32[]{:S(2)}, u32[]{:S(2)}) collective-permute-start(bf16[640,768]{1,0:T(8,128)(2,1)S(1)} %get-tuple-element.125), channel_id=1, source_target_pairs={{0,16},{16,0},{1,17},{17,1},{2,18},{18,2},{3,19},{19,3},{4,20},{20... | collective-permute-start | bytes 2949128 | tf_op jit(solution)/shard_map/ppermute | solution.py:226
  41.3 25.6 %collective-permute-start.16 = (bf16[64,2176]{1,0:T(8,128)(2,1)S(1)}, bf16[64,2176]{1,0:T(8,128)(2,1)S(1)}, u32[]{:S(2)}, u32[]{:S(2)}) collective-permute-start(bf16[64,2176]{1,0:T(8,128)(2,1)S(1)} %get-tuple-element.126), channel_id=1, source_target_pairs={{0,2},{1,3},{2,0},{3,1},{4,6},{5,7},{6,4},{7,5},{8,10},{9,11},{10,... | collective-permute-start | bytes 835592 | tf_op jit(solution)/shard_map/ppermute | solution.py:223
  49.1 6.9 %collective-permute-start.13 = (bf16[64,2048]{1,0:T(8,128)(2,1)S(1)}, bf16[64,2048]{1,0:T(8,128)(2,1)S(1)}, u32[]{:S(2)}, u32[]{:S(2)}) collective-permute-start(bf16[64,2048]{1,0:T(8,128)(2,1)S(1)} %get-tuple-element.121), channel_id=1, source_target_pairs={{0,1},{1,0},{2,3},{3,2},{4,5},{5,4},{6,7},{7,6},{8,9},{9,8},{10,11... | collective-permute-start | bytes 786440 | tf_op jit(solution)/shard_map/ppermute | solution.py:223
  54.4 8.2 %collective-permute-start.17 = (bf16[64,2176]{1,0:T(8,128)(2,1)S(1)}, bf16[64,2176]{1,0:T(8,128)(2,1)S(1)}, u32[]{:S(2)}, u32[]{:S(2)}) collective-permute-start(bf16[64,2176]{1,0:T(8,128)(2,1)S(1)} %get-tuple-element.127.refs_0_), channel_id=1, source_target_pairs={{0,2},{1,3},{2,0},{3,1},{4,6},{5,7},{6,4},{7,5},{8,10},{9,11},{10,... | collective-permute-start | bytes 835592 | tf_op jit(solution)/shard_map/ppermute | solution.py:223
  62.7 2.0 %collective-permute-start.18 = (bf16[128,2176]{1,0:T(8,128)(2,1)S(1)}, bf16[128,2176]{1,0:T(8,128)(2,1)S(1)}, u32[]{:S(2)}, u32[]{:S(2)}) collective-permute-start(bf16[128,2176]{1,0:T(8,128)(2,1)S(1)} %get-tuple-element.129.refs_0_), channel_id=1, source_target_pairs={{0,1},{1,0},{2,3},{3,2},{4,5},{5,4},{6,7},{7,6},{8,9},{9,8},{10,11... | collective-permute-start | bytes 1671176 | tf_op jit(solution)/shard_map/ppermute | solution.py:223
  67.0 6.6 %collective-permute-start.21 = (bf16[64,2176]{1,0:T(8,128)(2,1)S(1)}, bf16[64,2176]{1,0:T(8,128)(2,1)S(1)}, u32[]{:S(2)}, u32[]{:S(2)}) collective-permute-start(bf16[64,2176]{1,0:T(8,128)(2,1)S(1)} %get-tuple-element.139.refs_0_), channel_id=1, source_target_pairs={{0,1},{1,0},{2,3},{3,2},{4,5},{5,4},{6,7},{7,6},{8,9},{9,8},{10,11... | collective-permute-start | bytes 835592 | tf_op jit(solution)/shard_map/ppermute | solution.py:223
  67.2 24.6 %collective-permute-start.22 = (bf16[640,768]{1,0:T(8,128)(2,1)S(1)}, bf16[640,768]{1,0:T(8,128)(2,1)S(1)}, u32[]{:S(2)}, u32[]{:S(2)}) collective-permute-start(bf16[640,768]{1,0:T(8,128)(2,1)S(1)} %get-tuple-element.142), channel_id=1, source_target_pairs={{0,16},{16,0},{1,17},{17,1},{2,18},{18,2},{3,19},{19,3},{4,20},{20... | collective-permute-start | bytes 2949128 | tf_op jit(solution)/shard_map/ppermute | solution.py:226
  71.9 28.2 %collective-permute-start.26 = (bf16[256,768]{1,0:T(8,128)(2,1)S(1)}, bf16[256,768]{1,0:T(8,128)(2,1)S(1)}, u32[]{:S(2)}, u32[]{:S(2)}) collective-permute-start(bf16[256,768]{1,0:T(8,128)(2,1)S(1)} %get-tuple-element.152.refs_2_), channel_id=1, source_target_pairs={{0,16},{16,0},{1,17},{17,1},{2,18},{18,2},{3,19},{19,3},{4,20},{20... | collective-permute-start | bytes 1179656 | tf_op jit(solution)/shard_map/ppermute | solution.py:226
  73.5 20.6 %collective-permute-start.20 = (bf16[64,2048]{1,0:T(8,128)(2,1)S(1)}, bf16[64,2048]{1,0:T(8,128)(2,1)S(1)}, u32[]{:S(2)}, u32[]{:S(2)}) collective-permute-start(bf16[64,2048]{1,0:T(8,128)(2,1)S(1)} %get-tuple-element.138), channel_id=1, source_target_pairs={{0,4},{1,5},{2,6},{3,7},{4,0},{5,1},{6,2},{7,3},{8,12},{9,13},{10,... | collective-permute-start | bytes 786440 | tf_op jit(solution)/shard_map/ppermute | solution.py:223
  95.9 2.2 %collective-permute-start.23 = (bf16[64,2048]{1,0:T(8,128)(2,1)S(1)}, bf16[64,2048]{1,0:T(8,128)(2,1)S(1)}, u32[]{:S(2)}, u32[]{:S(2)}) collective-permute-start(bf16[64,2048]{1,0:T(8,128)(2,1)S(1)} %get-tuple-element.148), channel_id=1, source_target_pairs={{0,1},{1,0},{2,3},{3,2},{4,5},{5,4},{6,7},{7,6},{8,9},{9,8},{10,11... | collective-permute-start | bytes 786440 | tf_op jit(solution)/shard_map/ppermute | solution.py:223
  96.0 12.5 %collective-permute-start.25 = (bf16[256,768]{1,0:T(8,128)(2,1)S(1)}, bf16[256,768]{1,0:T(8,128)(2,1)S(1)}, u32[]{:S(2)}, u32[]{:S(2)}) collective-permute-start(bf16[256,768]{1,0:T(8,128)(2,1)S(1)} %get-tuple-element.151.refs_2_), channel_id=1, source_target_pairs={{0,16},{16,0},{1,17},{17,1},{2,18},{18,2},{3,19},{19,3},{4,20},{20... | collective-permute-start | bytes 1179656 | tf_op jit(solution)/shard_map/ppermute | solution.py:226
  96.6 19.9 %collective-permute-start.31 = (bf16[256,768]{1,0:T(8,128)(2,1)S(1)}, bf16[256,768]{1,0:T(8,128)(2,1)S(1)}, u32[]{:S(2)}, u32[]{:S(2)}) collective-permute-start(bf16[256,768]{1,0:T(8,128)(2,1)S(1)} %get-tuple-element.167), channel_id=1, source_target_pairs={{0,16},{16,0},{1,17},{17,1},{2,18},{18,2},{3,19},{19,3},{4,20},{20... | collective-permute-start | bytes 1179656 | tf_op jit(solution)/shard_map/ppermute | solution.py:226
  98.2 12.9 %collective-permute-start.24 = (bf16[64,2048]{1,0:T(8,128)(2,1)S(1)}, bf16[64,2048]{1,0:T(8,128)(2,1)S(1)}, u32[]{:S(2)}, u32[]{:S(2)}) collective-permute-start(bf16[64,2048]{1,0:T(8,128)(2,1)S(1)} %get-tuple-element.150), channel_id=1, source_target_pairs={{0,6},{1,7},{2,4},{3,5},{4,2},{5,3},{6,0},{7,1},{8,14},{9,15},{10,... | collective-permute-start | bytes 786440 | tf_op jit(solution)/shard_map/ppermute | solution.py:223
  102.6 2.0 %collective-permute-start.27 = (bf16[128,2048]{1,0:T(8,128)(2,1)S(1)}, bf16[128,2048]{1,0:T(8,128)(2,1)S(1)}, u32[]{:S(2)}, u32[]{:S(2)}) collective-permute-start(bf16[128,2048]{1,0:T(8,128)(2,1)S(1)} %get-tuple-element.155), channel_id=1, source_target_pairs={{0,1},{1,0},{2,3},{3,2},{4,5},{5,4},{6,7},{7,6},{8,9},{9,8},{10,11... | collective-permute-start | bytes 1572872 | tf_op jit(solution)/shard_map/ppermute | solution.py:223
  104.6 8.4 %collective-permute-start.28 = (bf16[64,2048]{1,0:T(8,128)(2,1)S(1)}, bf16[64,2048]{1,0:T(8,128)(2,1)S(1)}, u32[]{:S(2)}, u32[]{:S(2)}) collective-permute-start(bf16[64,2048]{1,0:T(8,128)(2,1)S(1)} %get-tuple-element.161), channel_id=1, source_target_pairs={{0,2},{1,3},{2,0},{3,1},{4,6},{5,7},{6,4},{7,5},{8,10},{9,11},{10,... | collective-permute-start | bytes 786440 | tf_op jit(solution)/shard_map/ppermute | solution.py:223
  113.1 16.3 %collective-permute-start.30 = (bf16[64,2048]{1,0:T(8,128)(2,1)S(1)}, bf16[64,2048]{1,0:T(8,128)(2,1)S(1)}, u32[]{:S(2)}, u32[]{:S(2)}) collective-permute-start(bf16[64,2048]{1,0:T(8,128)(2,1)S(1)} %get-tuple-element.166), channel_id=1, source_target_pairs={{0,8},{1,9},{2,10},{3,11},{4,12},{5,13},{6,14},{7,15},{8,0},{9,1},... | collective-permute-start | bytes 786440 | tf_op jit(solution)/shard_map/ppermute | solution.py:223
  114.0 7.6 %collective-permute-start.33 = (bf16[64,2048]{1,0:T(8,128)(2,1)S(1)}, bf16[64,2048]{1,0:T(8,128)(2,1)S(1)}, u32[]{:S(2)}, u32[]{:S(2)}) collective-permute-start(bf16[64,2048]{1,0:T(8,128)(2,1)S(1)} %get-tuple-element.171), channel_id=1, source_target_pairs={{0,2},{1,3},{2,0},{3,1},{4,6},{5,7},{6,4},{7,5},{8,10},{9,11},{10,... | collective-permute-start | bytes 786440 | tf_op jit(solution)/shard_map/ppermute | solution.py:223
  118.0 6.5 %collective-permute-start.32 = (bf16[128,768]{1,0:T(8,128)(2,1)S(1)}, bf16[128,768]{1,0:T(8,128)(2,1)S(1)}, u32[]{:S(2)}, u32[]{:S(2)}) collective-permute-start(bf16[128,768]{1,0:T(8,128)(2,1)S(1)} %get-tuple-element.169.refs_2_), channel_id=1, source_target_pairs={{0,16},{16,0},{1,17},{17,1},{2,18},{18,2},{3,19},{19,3},{4,20},{20... | collective-permute-start | bytes 589832 | tf_op jit(solution)/shard_map/ppermute | solution.py:226
  126.3 14.3 %collective-permute-start.35 = (bf16[64,2048]{1,0:T(8,128)(2,1)S(1)}, bf16[64,2048]{1,0:T(8,128)(2,1)S(1)}, u32[]{:S(2)}, u32[]{:S(2)}) collective-permute-start(bf16[64,2048]{1,0:T(8,128)(2,1)S(1)} %get-tuple-element.179), channel_id=1, source_target_pairs={{0,12},{1,13},{2,14},{3,15},{4,8},{5,9},{6,10},{7,11},{8,4},{9,5},... | collective-permute-start | bytes 786440 | tf_op jit(solution)/shard_map/ppermute | solution.py:223
  127.9 12.8 %collective-permute-start.36 = (bf16[64,2048]{1,0:T(8,128)(2,1)S(1)}, bf16[64,2048]{1,0:T(8,128)(2,1)S(1)}, u32[]{:S(2)}, u32[]{:S(2)}) collective-permute-start(bf16[64,2048]{1,0:T(8,128)(2,1)S(1)} %get-tuple-element.180), channel_id=1, source_target_pairs={{0,2},{1,3},{2,0},{3,1},{4,6},{5,7},{6,4},{7,5},{8,10},{9,11},{10,... | collective-permute-start | bytes 786440 | tf_op jit(solution)/shard_map/ppermute | solution.py:223
  (12 other events, 30.3 us)

commit v5 on v4

--- a/solution.py
+++ b/solution.py
@@ -67,13 +67,11 @@
 
 LANES = 128
 VMEM_LIMIT = 10 * 1024 * 1024
-COST = 8_000_000_000
-COSTS = {}
 TOKEN = jax.ShapeDtypeStruct((8, LANES), jnp.float32)
 HERE = pl.BlockSpec(memory_space=pltpu.VMEM)
 
 
-def call(kernel, inputs, outputs, after, scratch=(), relays=(), cost=0):
+def call(kernel, inputs, outputs, after, scratch=(), relays=()):
     inputs = [v if isinstance(v, tuple) else (v, HERE) for v in inputs]
     flat = [value for group in relays for value in group]
     joined = [
@@ -106,7 +104,7 @@
         out_shape=list(outputs) + joined + [TOKEN],
         scratch_shapes=list(scratch),
         compiler_params=pltpu.CompilerParams(vmem_limit_bytes=VMEM_LIMIT),
-        cost_estimate=pl.CostEstimate(flops=cost, bytes_accessed=1, transcendentals=0),
+        cost_estimate=pl.CostEstimate(flops=8_000_000_000, bytes_accessed=1, transcendentals=0),
     )(*[value for value, _ in inputs], *flat, *after)
     return results[:-1], results[-1]
 
@@ -228,14 +226,13 @@
     def array(shape, dtype=jnp.bfloat16):
         return jax.ShapeDtypeStruct(shape, dtype)
 
-    tail, number = [jnp.zeros(TOKEN.shape, TOKEN.dtype)], [0]
+    tail = [jnp.zeros(TOKEN.shape, TOKEN.dtype)]
 
     def step(kernel, inputs, outputs, scratch=(), relays=()):
         results, token = call(
-            kernel, inputs, outputs, list(tail), scratch, relays, COSTS.get(number[0], COST)
+            kernel, inputs, outputs, list(tail), scratch, relays
         )
         tail[:] = [token]
-        number[0] += 1
         return results
 
     def count(pieces):
@@ -305,13 +302,14 @@
     )
     b1, z4 = swap(labelled, 1), swap(labelled, 4)
     p0 = [labelled, b1]
+    (again,) = relay([labelled])
+    z8 = swap(again, 8)
     (sent,) = partials(p0)
     y0 = cross(sent)
-    (again,) = relay([labelled])
-    z8 = swap(again, 8)
     meet()
     (b4,) = relay([z4])
     b5, x6 = swap(b4, 1), swap(b4, 2)
+    gap()
     gap()
     p1 = [b4, b5]
     (sent,) = partials(p1)
@@ -319,20 +317,22 @@
     (b6,) = relay([x6])
     b7 = swap(b6, 1)
     (h0,) = hidden(p0, y0)
+    (b8,) = relay([z8])
+    x10 = swap(b8, 2)
     p2 = [b6, b7]
     (sent,) = partials(p2, [h0])
     y2 = cross(sent)
-    b8, again = relay([z8], [again])
-    x10, z12 = swap(b8, 2), swap(again, 12)
-    (h1,) = hidden(p1, y1)
+    (again,) = relay([labelled])
+    z12 = swap(again, 12)
+    (again,) = relay([labelled])
+    x2 = swap(again, 2)
     (b8,) = relay([b8, x10])
     b9 = swap(b8, 1)
+    (h1,) = hidden(p1, y1)
     gap()
     p3 = [b8, b9]
     (sent,) = partials(p3, [h1])
     y3 = cross(sent)
-    (again,) = relay([again])
-    x2 = swap(again, 2)
     meet()
     (h2,) = hidden(p2, y2)
     c0, c1 = outputs(p0, h0, y2, 4 * rows, rows)
@@ -357,9 +357,11 @@
     (later,) = partials(p5)
     (h4,) = hidden(p4, y4)
     t4 = cross(h4)
-    total, sent = add([total, s4], (whole, wide), relays=[[later]])
-    y5 = cross(sent)
+    (later,) = relay([later])
+    y5 = cross(later)
     c6, c7 = outputs(p2, h2, y4, 8 * rows, rows)
+    gap()
+    (total,) = add([total, s4], (whole, wide))
     gap()
     (sent,) = add([c6, c7], (whole, one))
     s6 = swap(sent, 6)
@@ -368,6 +370,7 @@
     kept8, sent = add([c8, c9], (whole, wide), ([(0, rows), (1, rows)], one))
     x10 = swap(sent, 2)
     c12, c13 = outputs(p4, h4, t4, 0, 2 * rows)
+    note = swap(tail[0], 1)
     (total,) = add([total, s6], (whole, wide))
     kept12, sent = add([c12, c13], (whole, wide), ([(0, rows), (1, rows)], one))
     x14 = swap(sent, 2)
@@ -377,6 +380,7 @@
     t5 = cross(h5)
     (sent,) = add([kept12, x14], (whole, one))
     s12 = swap(sent, 12)
+    tail.append(note)
     c2, c3 = outputs(p5, h5, t5, 0, rows)
     gap()
     (sent,) = add([c2, c3], (whole, one))

time: 142 us -> 139 us (0.979)
  waiting for transfers between devices: 75.7 us -> 70.9 us
  starting transfers between devices: 25.6 us -> 28 us
    ppermute x9, waiting for transfers between devices: 33.8 us -> 29.8 us  [cross(): return lax.ppermute(value, 'dp', [(0, 1), (1, 0)])]
    ppermute x28 -> x29, starting transfers between devices: 15.7 us -> 18.4 us  [swap(): return lax.ppermute(value, 'expert', [(i, i ^ r) for i in range(sources)])]
    ppermute x28 -> x29, waiting for transfers between devices: 41.9 us -> 41.2 us  [swap(): return lax.ppermute(value, 'expert', [(i, i ^ r) for i in range(sources)])]
    pallas_call x47 -> x51, Pallas kernels: 34.5 us -> 34.4 us  [call(): pl.pallas_call(run, in_specs=[spec for _, spec in inputs] + [HERE] * len(...]
    unnamed x14 -> x18, local copies, waits for them, and re-layouts: 5.2 us -> 5.27 us
  transfers between devices with their start and end apart: 37 -> 38, of which waited for: 20 -> 23; matrix products, arithmetic and copies ran while one was open for 0% -> 0% of each run, Pallas kernels for 24% -> 24%
where the time goes in v5:
time: 139 us
  waiting for transfers between devices  70.9 us (51%)
  Pallas kernels  34.4 us (25%)
  starting transfers between devices  28 us (20%)
  local copies, waits for them, and re-layouts  5.27 us (4%)
    ppermute x29, waiting for transfers between devices, swap(): return lax.ppermute(value, 'expert', [(i, i ^ r) for i in range(sources)])  41.2 us
    pallas_call x51, Pallas kernels, call(): pl.pallas_call(run, in_specs=[spec for _, spec in inputs] + [HERE] * len(...  34.4 us
    ppermute x9, waiting for transfers between devices, cross(): return lax.ppermute(value, 'dp', [(0, 1), (1, 0)])  29.8 us
    ppermute x29, starting transfers between devices, swap(): return lax.ppermute(value, 'expert', [(i, i ^ r) for i in range(sources)])  18.4 us
    ppermute x9, starting transfers between devices, cross(): return lax.ppermute(value, 'dp', [(0, 1), (1, 0)])  9.55 us
    unnamed x18, local copies, waits for them, and re-layouts  5.27 us
  transfers between devices with their start and end apart: 38, of which 23 were waited for; matrix products, arithmetic and copies ran while one was open for 0% of the time, Pallas kernels for 24%

profile of v5, /device:TPU:8, one launch (start us, length us, event | category | flops | bytes accessed | tf_op | source)
XLA Modules:
  0.0 139.1 jit_solution(11991313678312879314)
XLA Ops:
  8.5 2.6 %collective-permute-start.7 = (bf16[64,2176]{1,0:T(8,128)(2,1)S(1)}, bf16[64,2176]{1,0:T(8,128)(2,1)S(1)}, u32[]{:S(2)}, u32[]{:S(2)}) collective-permute-start(bf16[64,2176]{1,0:T(8,128)(2,1)S(1)} %get-tuple-element.107), channel_id=1, source_target_pairs={{0,8},{1,9},{2,10},{3,11},{4,12},{5,13},{6,14},{7,15},{8,0},{9,1},... | collective-permute-start | bytes 835592 | tf_op jit(solution)/shard_map/ppermute | solution.py:221
  11.2 1.5 %collective-permute-start.1 = (bf16[256,768]{1,0:T(8,128)(2,1)S(1)}, bf16[256,768]{1,0:T(8,128)(2,1)S(1)}, u32[]{:S(2)}, u32[]{:S(2)}) collective-permute-start(bf16[256,768]{1,0:T(8,128)(2,1)S(1)} %get-tuple-element.99), channel_id=1, source_target_pairs={{0,16},{16,0},{1,17},{17,1},{2,18},{18,2},{3,19},{19,3},{4,20},{20... | collective-permute-start | bytes 1179656 | tf_op jit(solution)/shard_map/ppermute | solution.py:224
  12.7 1.6 %collective-permute-start.4 = (bf16[64,2176]{1,0:T(8,128)(2,1)S(1)}, bf16[64,2176]{1,0:T(8,128)(2,1)S(1)}, u32[]{:S(2)}, u32[]{:S(2)}) collective-permute-start(bf16[64,2176]{1,0:T(8,128)(2,1)S(1)} %get-tuple-element.101.refs_0_), channel_id=1, source_target_pairs={{0,2},{1,3},{2,0},{3,1},{4,6},{5,7},{6,4},{7,5},{8,10},{9,11},{10,... | collective-permute-start | bytes 835592 | tf_op jit(solution)/shard_map/ppermute | solution.py:221
  14.3 1.6 %collective-permute-done.5.refs_1_ = bf16[64,2176]{1,0:T(8,128)(2,1)S(1)} collective-permute-done((bf16[64,2176]{1,0:T(8,128)(2,1)S(1)}, bf16[64,2176]{1,0:T(8,128)(2,1)S(1)}, u32[]{:S(2)}, u32[]{:S(2)}) %collective-permute-start.5) | collective-permute-done | bytes 278560 | tf_op jit(solution)/shard_map/ppermute | solution.py:221
  17.3 4.0 %collective-permute-done.4.refs_0_ = bf16[64,2176]{1,0:T(8,128)(2,1)S(1)} collective-permute-done((bf16[64,2176]{1,0:T(8,128)(2,1)S(1)}, bf16[64,2176]{1,0:T(8,128)(2,1)S(1)}, u32[]{:S(2)}, u32[]{:S(2)}) %collective-permute-start.4) | collective-permute-done | bytes 278560 | tf_op jit(solution)/shard_map/ppermute | solution.py:221
  23.9 1.6 %collective-permute-start.9 = (bf16[64,2176]{1,0:T(8,128)(2,1)S(1)}, bf16[64,2176]{1,0:T(8,128)(2,1)S(1)}, u32[]{:S(2)}, u32[]{:S(2)}) collective-permute-start(bf16[64,2176]{1,0:T(8,128)(2,1)S(1)} %get-tuple-element.111.refs_0_), channel_id=1, source_target_pairs={{0,2},{1,3},{2,0},{3,1},{4,6},{5,7},{6,4},{7,5},{8,10},{9,11},{10,... | collective-permute-start | bytes 835592 | tf_op jit(solution)/shard_map/ppermute | solution.py:221
  26.9 1.5 %collective-permute-start.8 = (bf16[384,768]{1,0:T(8,128)(2,1)S(1)}, bf16[384,768]{1,0:T(8,128)(2,1)S(1)}, u32[]{:S(2)}, u32[]{:S(2)}) collective-permute-start(bf16[384,768]{1,0:T(8,128)(2,1)S(1)} %get-tuple-element.110), channel_id=1, source_target_pairs={{0,16},{16,0},{1,17},{17,1},{2,18},{18,2},{3,19},{19,3},{4,20},{20... | collective-permute-start | bytes 1769480 | tf_op jit(solution)/shard_map/ppermute | solution.py:224
  28.5 3.7 %collective-permute-done.9.refs_1_ = bf16[64,2176]{1,0:T(8,128)(2,1)S(1)} collective-permute-done((bf16[64,2176]{1,0:T(8,128)(2,1)S(1)}, bf16[64,2176]{1,0:T(8,128)(2,1)S(1)}, u32[]{:S(2)}, u32[]{:S(2)}) %collective-permute-start.9) | collective-permute-done | bytes 278560 | tf_op jit(solution)/shard_map/ppermute | solution.py:221
  34.8 2.2 %shard_map.80 = (bf16[640,768]{1,0:T(8,128)(2,1)S(1)}, f32[8,128]{1,0:T(8,128)S(1)}) custom-call(bf16[128,2176]{1,0:T(8,128)(2,1)S(1)} %get-tuple-element.115.refs_0_, bf16[128,2176]{1,0:T(8,128)(2,1)S(1)} %collective-permute-done.10.refs_1_, bf16[1,2048,1536]{2,1,0:T(8,128)(2,1)S(1)} %bitcast.3, bf16[1,2048,1536]{2,1,0:T(8,128)(2,1)S(1)} %bitcast.5, ...), custom_call_target="tpu_custom_call" | custom-call | flops 8000000000 | bytes 1 | tf_op jit(solution)/shard_map/pallas_call | solution.py:100
  38.1 1.5 %collective-permute-start.16 = (bf16[64,2176]{1,0:T(8,128)(2,1)S(1)}, bf16[64,2176]{1,0:T(8,128)(2,1)S(1)}, u32[]{:S(2)}, u32[]{:S(2)}) collective-permute-start(bf16[64,2176]{1,0:T(8,128)(2,1)S(1)} %get-tuple-element.129), channel_id=1, source_target_pairs={{0,2},{1,3},{2,0},{3,1},{4,6},{5,7},{6,4},{7,5},{8,10},{9,11},{10,... | collective-permute-start | bytes 835592 | tf_op jit(solution)/shard_map/ppermute | solution.py:221
  40.5 5.4 %collective-permute-done.8.refs_4_.refs_3_ = bf16[384,768]{1,0:T(8,128)(2,1)S(1)} collective-permute-done((bf16[384,768]{1,0:T(8,128)(2,1)S(1)}, bf16[384,768]{1,0:T(8,128)(2,1)S(1)}, u32[]{:S(2)}, u32[]{:S(2)}) %collective-permute-start.8) | collective-permute-done | bytes 589856 | tf_op jit(solution)/shard_map/ppermute | solution.py:224
  47.5 1.7 %shard_map.82 = (f32[64,2048]{1,0:T(8,128)S(1)}, bf16[64,2048]{1,0:T(8,128)(2,1)S(1)}, f32[8,128]{1,0:T(8,128)S(1)}) custom-call(bf16[64,2176]{1,0:T(8,128)(2,1)S(1)} %get-tuple-element.96.refs_0_, bf16[64,2176]{1,0:T(8,128)(2,1)S(1)} %collective-permute-done.refs_1_, bf16[128,768]{1,0:T(8,128)(2,1)S(1)} %get-tuple-element.105.refs_4_.refs_2_, ...), custom_call_target="tpu_custom_call" | custom-call | flops 8000000000 | bytes 1 | tf_op jit(solution)/shard_map/pallas_call | solution.py:100
  49.3 2.9 %collective-permute-done.14.refs_0_ = bf16[64,2176]{1,0:T(8,128)(2,1)S(1)} collective-permute-done((bf16[64,2176]{1,0:T(8,128)(2,1)S(1)}, bf16[64,2176]{1,0:T(8,128)(2,1)S(1)}, u32[]{:S(2)}, u32[]{:S(2)}) %collective-permute-start.14) | collective-permute-done | bytes 278560 | tf_op jit(solution)/shard_map/ppermute | solution.py:221
  52.2 1.6 %collective-permute-start.17 = (bf16[64,2176]{1,0:T(8,128)(2,1)S(1)}, bf16[64,2176]{1,0:T(8,128)(2,1)S(1)}, u32[]{:S(2)}, u32[]{:S(2)}) collective-permute-start(bf16[64,2176]{1,0:T(8,128)(2,1)S(1)} %get-tuple-element.130.refs_0_), channel_id=1, source_target_pairs={{0,2},{1,3},{2,0},{3,1},{4,6},{5,7},{6,4},{7,5},{8,10},{9,11},{10,... | collective-permute-start | bytes 835592 | tf_op jit(solution)/shard_map/ppermute | solution.py:221
  53.9 6.7 %collective-permute-done.17.refs_1_ = bf16[64,2176]{1,0:T(8,128)(2,1)S(1)} collective-permute-done((bf16[64,2176]{1,0:T(8,128)(2,1)S(1)}, bf16[64,2176]{1,0:T(8,128)(2,1)S(1)}, u32[]{:S(2)}, u32[]{:S(2)}) %collective-permute-start.17) | collective-permute-done | bytes 278560 | tf_op jit(solution)/shard_map/ppermute | solution.py:221
  60.7 1.9 %collective-permute-done.18.refs_1_ = bf16[128,2176]{1,0:T(8,128)(2,1)S(1)} collective-permute-done((bf16[128,2176]{1,0:T(8,128)(2,1)S(1)}, bf16[128,2176]{1,0:T(8,128)(2,1)S(1)}, u32[]{:S(2)}, u32[]{:S(2)}) %collective-permute-start.18) | collective-permute-done | bytes 557088 | tf_op jit(solution)/shard_map/ppermute | solution.py:221
  62.6 2.2 %shard_map.87 = (bf16[640,768]{1,0:T(8,128)(2,1)S(1)}, f32[8,128]{1,0:T(8,128)S(1)}) custom-call(bf16[128,2176]{1,0:T(8,128)(2,1)S(1)} %get-tuple-element.132.refs_0_, bf16[128,2176]{1,0:T(8,128)(2,1)S(1)} %collective-permute-done.18.refs_1_, bf16[1,2048,1536]{2,1,0:T(8,128)(2,1)S(1)} %bitcast.3, bf16[1,2048,1536]{2,1,0:T(8,128)(2,1)S(1)} %bitcast.5, ...), custom_call_target="tpu_custom_call" | custom-call | flops 8000000000 | bytes 1 | tf_op jit(solution)/shard_map/pallas_call | solution.py:100
  66.6 2.3 %shard_map.89 = (bf16[256,768]{1,0:T(8,128)(2,1)S(1)}, f32[8,128]{1,0:T(8,128)S(1)}) custom-call(bf16[128,2176]{1,0:T(8,128)(2,1)S(1)} %get-tuple-element.115.refs_0_, bf16[128,2176]{1,0:T(8,128)(2,1)S(1)} %collective-permute-done.10.refs_1_, bf16[1,2048,1536]{2,1,0:T(8,128)(2,1)S(1)} %bitcast.3, bf16[1,2048,1536]{2,1,0:T(8,128)(2,1)S(1)} %bitcast.5, ...), custom_call_target="tpu_custom_call" | custom-call | flops 8000000000 | bytes 1 | tf_op jit(solution)/shard_map/pallas_call | solution.py:100
  68.9 1.7 %shard_map.90 = (f32[64,2048]{1,0:T(8,128)S(1)}, bf16[64,2048]{1,0:T(8,128)(2,1)S(1)}, f32[8,128]{1,0:T(8,128)S(1)}) custom-call(bf16[64,2176]{1,0:T(8,128)(2,1)S(1)} %get-tuple-element.101.refs_0_, bf16[64,2176]{1,0:T(8,128)(2,1)S(1)} %collective-permute-done.5.refs_1_, bf16[128,768]{1,0:T(8,128)(2,1)S(1)} %get-tuple-element.118.refs_4_.refs_2_, ...), custom_call_target="tpu_custom_call" | custom-call | flops 8000000000 | bytes 1 | tf_op jit(solution)/shard_map/pallas_call | solution.py:100
  75.1 14.4 %collective-permute-done.21.refs_4_.refs_3_ = bf16[640,768]{1,0:T(8,128)(2,1)S(1)} collective-permute-done((bf16[640,768]{1,0:T(8,128)(2,1)S(1)}, bf16[640,768]{1,0:T(8,128)(2,1)S(1)}, u32[]{:S(2)}, u32[]{:S(2)}) %collective-permute-start.21) | collective-permute-done | bytes 983072 | tf_op jit(solution)/shard_map/ppermute | solution.py:224
  89.5 2.3 %shard_map.94 = (bf16[256,768]{1,0:T(8,128)(2,1)S(1)}, f32[8,128]{1,0:T(8,128)S(1)}) custom-call(bf16[128,2176]{1,0:T(8,128)(2,1)S(1)} %get-tuple-element.132.refs_0_, bf16[128,2176]{1,0:T(8,128)(2,1)S(1)} %collective-permute-done.18.refs_1_, bf16[1,2048,1536]{2,1,0:T(8,128)(2,1)S(1)} %bitcast.3, bf16[1,2048,1536]{2,1,0:T(8,128)(2,1)S(1)} %bitcast.5, ...), custom_call_target="tpu_custom_call" | custom-call | flops 8000000000 | bytes 1 | tf_op jit(solution)/shard_map/pallas_call | solution.py:100
  91.9 1.7 %shard_map.96 = (f32[64,2048]{1,0:T(8,128)S(1)}, bf16[64,2048]{1,0:T(8,128)(2,1)S(1)}, f32[8,128]{1,0:T(8,128)S(1)}) custom-call(bf16[64,2176]{1,0:T(8,128)(2,1)S(1)} %get-tuple-element.106.refs_0_, bf16[64,2176]{1,0:T(8,128)(2,1)S(1)} %collective-permute-done.6.refs_1_, bf16[128,768]{1,0:T(8,128)(2,1)S(1)} %get-tuple-element.133.refs_4_.refs_2_, ...), custom_call_target="tpu_custom_call" | custom-call | flops 8000000000 | bytes 1 | tf_op jit(solution)/shard_map/pallas_call | solution.py:100
  97.3 2.4 %shard_map.101 = (f32[128,2048]{1,0:T(8,128)S(1)}, bf16[128,2048]{1,0:T(8,128)(2,1)S(1)}, f32[8,128]{1,0:T(8,128)S(1)}) custom-call(bf16[128,2176]{1,0:T(8,128)(2,1)S(1)} %get-tuple-element.115.refs_0_, bf16[128,2176]{1,0:T(8,128)(2,1)S(1)} %collective-permute-done.10.refs_1_, bf16[256,768]{1,0:T(8,128)(2,1)S(1)} %get-tuple-element.156.refs_2_, ...), custom_call_target="tpu_custom_call" | custom-call | flops 8000000000 | bytes 1 | tf_op jit(solution)/shard_map/pallas_call | solution.py:100
  99.8 1.9 %collective-permute-done.27.refs_1_ = bf16[128,2048]{1,0:T(8,128)(2,1)S(1)} collective-permute-done((bf16[128,2048]{1,0:T(8,128)(2,1)S(1)}, bf16[128,2048]{1,0:T(8,128)(2,1)S(1)}, u32[]{:S(2)}, u32[]{:S(2)}) %collective-permute-start.27) | collective-permute-done | bytes 524320 | tf_op jit(solution)/shard_map/ppermute | solution.py:221
  101.8 1.6 %collective-permute-start.28 = (bf16[64,2048]{1,0:T(8,128)(2,1)S(1)}, bf16[64,2048]{1,0:T(8,128)(2,1)S(1)}, u32[]{:S(2)}, u32[]{:S(2)}) collective-permute-start(bf16[64,2048]{1,0:T(8,128)(2,1)S(1)} %get-tuple-element.165), channel_id=1, source_target_pairs={{0,2},{1,3},{2,0},{3,1},{4,6},{5,7},{6,4},{7,5},{8,10},{9,11},{10,... | collective-permute-start | bytes 786440 | tf_op jit(solution)/shard_map/ppermute | solution.py:221
  103.4 2.5 %collective-permute-done.25.refs_3_ = bf16[256,768]{1,0:T(8,128)(2,1)S(1)} collective-permute-done((bf16[256,768]{1,0:T(8,128)(2,1)S(1)}, bf16[256,768]{1,0:T(8,128)(2,1)S(1)}, u32[]{:S(2)}, u32[]{:S(2)}) %collective-permute-start.25) | collective-permute-done | bytes 393248 | tf_op jit(solution)/shard_map/ppermute | solution.py:224
  105.8 2.5 %shard_map.104 = (f32[128,2048]{1,0:T(8,128)S(1)}, bf16[128,2048]{1,0:T(8,128)(2,1)S(1)}, f32[8,128]{1,0:T(8,128)S(1)}) custom-call(bf16[128,2176]{1,0:T(8,128)(2,1)S(1)} %get-tuple-element.132.refs_0_, bf16[128,2176]{1,0:T(8,128)(2,1)S(1)} %collective-permute-done.18.refs_1_, bf16[256,768]{1,0:T(8,128)(2,1)S(1)} %get-tuple-element.155.refs_2_, ...), custom_call_target="tpu_custom_call" | custom-call | flops 8000000000 | bytes 1 | tf_op jit(solution)/shard_map/pallas_call | solution.py:100
  116.4 2.9 %collective-permute-done.33.refs_1_ = bf16[64,2048]{1,0:T(8,128)(2,1)S(1)} collective-permute-done((bf16[64,2048]{1,0:T(8,128)(2,1)S(1)}, bf16[64,2048]{1,0:T(8,128)(2,1)S(1)}, u32[]{:S(2)}, u32[]{:S(2)}) %collective-permute-start.33) | collective-permute-done | bytes 262176 | tf_op jit(solution)/shard_map/ppermute | solution.py:221
  119.4 2.8 %collective-permute-done.32.refs_3_ = bf16[128,768]{1,0:T(8,128)(2,1)S(1)} collective-permute-done((bf16[128,768]{1,0:T(8,128)(2,1)S(1)}, bf16[128,768]{1,0:T(8,128)(2,1)S(1)}, u32[]{:S(2)}, u32[]{:S(2)}) %collective-permute-start.32) | collective-permute-done | bytes 196640 | tf_op jit(solution)/shard_map/ppermute | solution.py:224
  122.2 1.7 %shard_map.110 = (f32[64,2048]{1,0:T(8,128)S(1)}, bf16[64,2048]{1,0:T(8,128)(2,1)S(1)}, f32[8,128]{1,0:T(8,128)S(1)}) custom-call(bf16[64,2176]{1,0:T(8,128)(2,1)S(1)} %get-tuple-element.143.refs_0_, bf16[64,2176]{1,0:T(8,128)(2,1)S(1)} %collective-permute-done.22.refs_1_, bf16[128,768]{1,0:T(8,128)(2,1)S(1)} %get-tuple-element.173.refs_2_, ...), custom_call_target="tpu_custom_call" | custom-call | flops 8000000000 | bytes 1 | tf_op jit(solution)/shard_map/pallas_call | solution.py:100
  125.6 1.5 %collective-permute-start.37 = (bf16[64,2048]{1,0:T(8,128)(2,1)S(1)}, bf16[64,2048]{1,0:T(8,128)(2,1)S(1)}, u32[]{:S(2)}, u32[]{:S(2)}) collective-permute-start(bf16[64,2048]{1,0:T(8,128)(2,1)S(1)} %get-tuple-element.184), channel_id=1, source_target_pairs={{0,2},{1,3},{2,0},{3,1},{4,6},{5,7},{6,4},{7,5},{8,10},{9,11},{10,... | collective-permute-start | bytes 786440 | tf_op jit(solution)/shard_map/ppermute | solution.py:221
  127.2 11.2 %collective-permute-done.36.refs_1_ = bf16[64,2048]{1,0:T(8,128)(2,1)S(1)} collective-permute-done((bf16[64,2048]{1,0:T(8,128)(2,1)S(1)}, bf16[64,2048]{1,0:T(8,128)(2,1)S(1)}, u32[]{:S(2)}, u32[]{:S(2)}) %collective-permute-start.36) | collective-permute-done | bytes 262176 | tf_op jit(solution)/shard_map/ppermute | solution.py:221
  (117 shorter events, 40.9 us)
Async XLA Ops:
  2.5 10.1 %collective-permute-start.2 = (bf16[64,2176]{1,0:T(8,128)(2,1)S(1)}, bf16[64,2176]{1,0:T(8,128)(2,1)S(1)}, u32[]{:S(2)}, u32[]{:S(2)}) collective-permute-start(bf16[64,2176]{1,0:T(8,128)(2,1)S(1)} %get-tuple-element.96.refs_0_), channel_id=1, source_target_pairs={{0,4},{1,5},{2,6},{3,7},{4,0},{5,1},{6,2},{7,3},{8,12},{9,13},{10,... | collective-permute-start | bytes 835592 | tf_op jit(solution)/shard_map/ppermute | solution.py:221
  8.5 4.2 %collective-permute-start.3 = (f32[8,128]{1,0:T(8,128)S(1)}, f32[8,128]{1,0:T(8,128)S(1)}, u32[]{:S(2)}, u32[]{:S(2)}) collective-permute-start(f32[8,128]{1,0:T(8,128)S(1)} %get-tuple-element.100.refs_1_), channel_id=1, source_target_pairs={{0,1},{1,0},{2,3},{3,2},{4,5},{5,4},{6,7},{7,6},{8,9},{9,8},{10,11... | collective-permute-start | bytes 12296 | tf_op jit(solution)/shard_map/ppermute | solution.py:221
  8.5 15.3 %collective-permute-start.7 = (bf16[64,2176]{1,0:T(8,128)(2,1)S(1)}, bf16[64,2176]{1,0:T(8,128)(2,1)S(1)}, u32[]{:S(2)}, u32[]{:S(2)}) collective-permute-start(bf16[64,2176]{1,0:T(8,128)(2,1)S(1)} %get-tuple-element.107), channel_id=1, source_target_pairs={{0,8},{1,9},{2,10},{3,11},{4,12},{5,13},{6,14},{7,15},{8,0},{9,1},... | collective-permute-start | bytes 835592 | tf_op jit(solution)/shard_map/ppermute | solution.py:221
  11.2 11.2 %collective-permute-start.1 = (bf16[256,768]{1,0:T(8,128)(2,1)S(1)}, bf16[256,768]{1,0:T(8,128)(2,1)S(1)}, u32[]{:S(2)}, u32[]{:S(2)}) collective-permute-start(bf16[256,768]{1,0:T(8,128)(2,1)S(1)} %get-tuple-element.99), channel_id=1, source_target_pairs={{0,16},{16,0},{1,17},{17,1},{2,18},{18,2},{3,19},{19,3},{4,20},{20... | collective-permute-start | bytes 1179656 | tf_op jit(solution)/shard_map/ppermute | solution.py:224
  12.7 8.5 %collective-permute-start.4 = (bf16[64,2176]{1,0:T(8,128)(2,1)S(1)}, bf16[64,2176]{1,0:T(8,128)(2,1)S(1)}, u32[]{:S(2)}, u32[]{:S(2)}) collective-permute-start(bf16[64,2176]{1,0:T(8,128)(2,1)S(1)} %get-tuple-element.101.refs_0_), channel_id=1, source_target_pairs={{0,2},{1,3},{2,0},{3,1},{4,6},{5,7},{6,4},{7,5},{8,10},{9,11},{10,... | collective-permute-start | bytes 835592 | tf_op jit(solution)/shard_map/ppermute | solution.py:221
  21.3 4.2 %collective-permute-start.6 = (bf16[64,2176]{1,0:T(8,128)(2,1)S(1)}, bf16[64,2176]{1,0:T(8,128)(2,1)S(1)}, u32[]{:S(2)}, u32[]{:S(2)}) collective-permute-start(bf16[64,2176]{1,0:T(8,128)(2,1)S(1)} %get-tuple-element.106.refs_0_), channel_id=1, source_target_pairs={{0,1},{1,0},{2,3},{3,2},{4,5},{5,4},{6,7},{7,6},{8,9},{9,8},{10,11... | collective-permute-start | bytes 835592 | tf_op jit(solution)/shard_map/ppermute | solution.py:221
  21.3 12.0 %collective-permute-start.11 = (bf16[256,768]{1,0:T(8,128)(2,1)S(1)}, bf16[256,768]{1,0:T(8,128)(2,1)S(1)}, u32[]{:S(2)}, u32[]{:S(2)}) collective-permute-start(bf16[256,768]{1,0:T(8,128)(2,1)S(1)} %get-tuple-element.116), channel_id=1, source_target_pairs={{0,16},{16,0},{1,17},{17,1},{2,18},{18,2},{3,19},{19,3},{4,20},{20... | collective-permute-start | bytes 1179656 | tf_op jit(solution)/shard_map/ppermute | solution.py:224
  23.9 8.4 %collective-permute-start.9 = (bf16[64,2176]{1,0:T(8,128)(2,1)S(1)}, bf16[64,2176]{1,0:T(8,128)(2,1)S(1)}, u32[]{:S(2)}, u32[]{:S(2)}) collective-permute-start(bf16[64,2176]{1,0:T(8,128)(2,1)S(1)} %get-tuple-element.111.refs_0_), channel_id=1, source_target_pairs={{0,2},{1,3},{2,0},{3,1},{4,6},{5,7},{6,4},{7,5},{8,10},{9,11},{10,... | collective-permute-start | bytes 835592 | tf_op jit(solution)/shard_map/ppermute | solution.py:221
  26.9 19.0 %collective-permute-start.8 = (bf16[384,768]{1,0:T(8,128)(2,1)S(1)}, bf16[384,768]{1,0:T(8,128)(2,1)S(1)}, u32[]{:S(2)}, u32[]{:S(2)}) collective-permute-start(bf16[384,768]{1,0:T(8,128)(2,1)S(1)} %get-tuple-element.110), channel_id=1, source_target_pairs={{0,16},{16,0},{1,17},{17,1},{2,18},{18,2},{3,19},{19,3},{4,20},{20... | collective-permute-start | bytes 1769480 | tf_op jit(solution)/shard_map/ppermute | solution.py:224
  32.3 2.5 %collective-permute-start.10 = (bf16[128,2176]{1,0:T(8,128)(2,1)S(1)}, bf16[128,2176]{1,0:T(8,128)(2,1)S(1)}, u32[]{:S(2)}, u32[]{:S(2)}) collective-permute-start(bf16[128,2176]{1,0:T(8,128)(2,1)S(1)} %get-tuple-element.115.refs_0_), channel_id=1, source_target_pairs={{0,1},{1,0},{2,3},{3,2},{4,5},{5,4},{6,7},{7,6},{8,9},{9,8},{10,11... | collective-permute-start | bytes 1671176 | tf_op jit(solution)/shard_map/ppermute | solution.py:221
  37.1 8.9 %collective-permute-start.12 = (f32[8,128]{1,0:T(8,128)S(1)}, f32[8,128]{1,0:T(8,128)S(1)}, u32[]{:S(2)}, u32[]{:S(2)}) collective-permute-start(f32[8,128]{1,0:T(8,128)S(1)} %get-tuple-element.120.refs_5_), channel_id=1, source_target_pairs={{0,1},{1,0},{2,3},{3,2},{4,5},{5,4},{6,7},{7,6},{8,9},{9,8},{10,11... | collective-permute-start | bytes 12296 | tf_op jit(solution)/shard_map/ppermute | solution.py:221
  37.2 15.0 %collective-permute-start.14 = (bf16[64,2176]{1,0:T(8,128)(2,1)S(1)}, bf16[64,2176]{1,0:T(8,128)(2,1)S(1)}, u32[]{:S(2)}, u32[]{:S(2)}) collective-permute-start(bf16[64,2176]{1,0:T(8,128)(2,1)S(1)} %get-tuple-element.124), channel_id=1, source_target_pairs={{0,12},{1,13},{2,14},{3,15},{4,8},{5,9},{6,10},{7,11},{8,4},{9,5},... | collective-permute-start | bytes 835592 | tf_op jit(solution)/shard_map/ppermute | solution.py:221
  38.1 27.7 %collective-permute-start.16 = (bf16[64,2176]{1,0:T(8,128)(2,1)S(1)}, bf16[64,2176]{1,0:T(8,128)(2,1)S(1)}, u32[]{:S(2)}, u32[]{:S(2)}) collective-permute-start(bf16[64,2176]{1,0:T(8,128)(2,1)S(1)} %get-tuple-element.129), channel_id=1, source_target_pairs={{0,2},{1,3},{2,0},{3,1},{4,6},{5,7},{6,4},{7,5},{8,10},{9,11},{10,... | collective-permute-start | bytes 835592 | tf_op jit(solution)/shard_map/ppermute | solution.py:221
  39.6 27.0 %collective-permute-start.15 = (bf16[640,768]{1,0:T(8,128)(2,1)S(1)}, bf16[640,768]{1,0:T(8,128)(2,1)S(1)}, u32[]{:S(2)}, u32[]{:S(2)}) collective-permute-start(bf16[640,768]{1,0:T(8,128)(2,1)S(1)} %get-tuple-element.128), channel_id=1, source_target_pairs={{0,16},{16,0},{1,17},{17,1},{2,18},{18,2},{3,19},{19,3},{4,20},{20... | collective-permute-start | bytes 2949128 | tf_op jit(solution)/shard_map/ppermute | solution.py:224
  49.2 4.6 %collective-permute-start.13 = (bf16[64,2048]{1,0:T(8,128)(2,1)S(1)}, bf16[64,2048]{1,0:T(8,128)(2,1)S(1)}, u32[]{:S(2)}, u32[]{:S(2)}) collective-permute-start(bf16[64,2048]{1,0:T(8,128)(2,1)S(1)} %get-tuple-element.123), channel_id=1, source_target_pairs={{0,1},{1,0},{2,3},{3,2},{4,5},{5,4},{6,7},{7,6},{8,9},{9,8},{10,11... | collective-permute-start | bytes 786440 | tf_op jit(solution)/shard_map/ppermute | solution.py:221
  52.2 8.3 %collective-permute-start.17 = (bf16[64,2176]{1,0:T(8,128)(2,1)S(1)}, bf16[64,2176]{1,0:T(8,128)(2,1)S(1)}, u32[]{:S(2)}, u32[]{:S(2)}) collective-permute-start(bf16[64,2176]{1,0:T(8,128)(2,1)S(1)} %get-tuple-element.130.refs_0_), channel_id=1, source_target_pairs={{0,2},{1,3},{2,0},{3,1},{4,6},{5,7},{6,4},{7,5},{8,10},{9,11},{10,... | collective-permute-start | bytes 835592 | tf_op jit(solution)/shard_map/ppermute | solution.py:221
  60.6 2.0 %collective-permute-start.18 = (bf16[128,2176]{1,0:T(8,128)(2,1)S(1)}, bf16[128,2176]{1,0:T(8,128)(2,1)S(1)}, u32[]{:S(2)}, u32[]{:S(2)}) collective-permute-start(bf16[128,2176]{1,0:T(8,128)(2,1)S(1)} %get-tuple-element.132.refs_0_), channel_id=1, source_target_pairs={{0,1},{1,0},{2,3},{3,2},{4,5},{5,4},{6,7},{7,6},{8,9},{9,8},{10,11... | collective-permute-start | bytes 1671176 | tf_op jit(solution)/shard_map/ppermute | solution.py:221
  64.8 24.7 %collective-permute-start.21 = (bf16[640,768]{1,0:T(8,128)(2,1)S(1)}, bf16[640,768]{1,0:T(8,128)(2,1)S(1)}, u32[]{:S(2)}, u32[]{:S(2)}) collective-permute-start(bf16[640,768]{1,0:T(8,128)(2,1)S(1)} %get-tuple-element.142), channel_id=1, source_target_pairs={{0,16},{16,0},{1,17},{17,1},{2,18},{18,2},{3,19},{19,3},{4,20},{20... | collective-permute-start | bytes 2949128 | tf_op jit(solution)/shard_map/ppermute | solution.py:224
  65.8 7.8 %collective-permute-start.22 = (bf16[64,2176]{1,0:T(8,128)(2,1)S(1)}, bf16[64,2176]{1,0:T(8,128)(2,1)S(1)}, u32[]{:S(2)}, u32[]{:S(2)}) collective-permute-start(bf16[64,2176]{1,0:T(8,128)(2,1)S(1)} %get-tuple-element.143.refs_0_), channel_id=1, source_target_pairs={{0,1},{1,0},{2,3},{3,2},{4,5},{5,4},{6,7},{7,6},{8,9},{9,8},{10,11... | collective-permute-start | bytes 835592 | tf_op jit(solution)/shard_map/ppermute | solution.py:221
  70.7 26.6 %collective-permute-start.26 = (bf16[256,768]{1,0:T(8,128)(2,1)S(1)}, bf16[256,768]{1,0:T(8,128)(2,1)S(1)}, u32[]{:S(2)}, u32[]{:S(2)}) collective-permute-start(bf16[256,768]{1,0:T(8,128)(2,1)S(1)} %get-tuple-element.156.refs_2_), channel_id=1, source_target_pairs={{0,16},{16,0},{1,17},{17,1},{2,18},{18,2},{3,19},{19,3},{4,20},{20... | collective-permute-start | bytes 1179656 | tf_op jit(solution)/shard_map/ppermute | solution.py:224
  72.3 21.4 %collective-permute-start.20 = (bf16[64,2048]{1,0:T(8,128)(2,1)S(1)}, bf16[64,2048]{1,0:T(8,128)(2,1)S(1)}, u32[]{:S(2)}, u32[]{:S(2)}) collective-permute-start(bf16[64,2048]{1,0:T(8,128)(2,1)S(1)} %get-tuple-element.141), channel_id=1, source_target_pairs={{0,4},{1,5},{2,6},{3,7},{4,0},{5,1},{6,2},{7,3},{8,12},{9,13},{10,... | collective-permute-start | bytes 786440 | tf_op jit(solution)/shard_map/ppermute | solution.py:221
  93.6 2.2 %collective-permute-start.23 = (bf16[64,2048]{1,0:T(8,128)(2,1)S(1)}, bf16[64,2048]{1,0:T(8,128)(2,1)S(1)}, u32[]{:S(2)}, u32[]{:S(2)}) collective-permute-start(bf16[64,2048]{1,0:T(8,128)(2,1)S(1)} %get-tuple-element.152), channel_id=1, source_target_pairs={{0,1},{1,0},{2,3},{3,2},{4,5},{5,4},{6,7},{7,6},{8,9},{9,8},{10,11... | collective-permute-start | bytes 786440 | tf_op jit(solution)/shard_map/ppermute | solution.py:221
  93.8 12.1 %collective-permute-start.25 = (bf16[256,768]{1,0:T(8,128)(2,1)S(1)}, bf16[256,768]{1,0:T(8,128)(2,1)S(1)}, u32[]{:S(2)}, u32[]{:S(2)}) collective-permute-start(bf16[256,768]{1,0:T(8,128)(2,1)S(1)} %get-tuple-element.155.refs_2_), channel_id=1, source_target_pairs={{0,16},{16,0},{1,17},{17,1},{2,18},{18,2},{3,19},{19,3},{4,20},{20... | collective-permute-start | bytes 1179656 | tf_op jit(solution)/shard_map/ppermute | solution.py:224
  94.7 19.3 %collective-permute-start.31 = (bf16[256,768]{1,0:T(8,128)(2,1)S(1)}, bf16[256,768]{1,0:T(8,128)(2,1)S(1)}, u32[]{:S(2)}, u32[]{:S(2)}) collective-permute-start(bf16[256,768]{1,0:T(8,128)(2,1)S(1)} %get-tuple-element.171), channel_id=1, source_target_pairs={{0,16},{16,0},{1,17},{17,1},{2,18},{18,2},{3,19},{19,3},{4,20},{20... | collective-permute-start | bytes 1179656 | tf_op jit(solution)/shard_map/ppermute | solution.py:224
  95.9 12.9 %collective-permute-start.24 = (bf16[64,2048]{1,0:T(8,128)(2,1)S(1)}, bf16[64,2048]{1,0:T(8,128)(2,1)S(1)}, u32[]{:S(2)}, u32[]{:S(2)}) collective-permute-start(bf16[64,2048]{1,0:T(8,128)(2,1)S(1)} %get-tuple-element.154), channel_id=1, source_target_pairs={{0,6},{1,7},{2,4},{3,5},{4,2},{5,3},{6,0},{7,1},{8,14},{9,15},{10,... | collective-permute-start | bytes 786440 | tf_op jit(solution)/shard_map/ppermute | solution.py:221
  101.8 8.8 %collective-permute-start.28 = (bf16[64,2048]{1,0:T(8,128)(2,1)S(1)}, bf16[64,2048]{1,0:T(8,128)(2,1)S(1)}, u32[]{:S(2)}, u32[]{:S(2)}) collective-permute-start(bf16[64,2048]{1,0:T(8,128)(2,1)S(1)} %get-tuple-element.165), channel_id=1, source_target_pairs={{0,2},{1,3},{2,0},{3,1},{4,6},{5,7},{6,4},{7,5},{8,10},{9,11},{10,... | collective-permute-start | bytes 786440 | tf_op jit(solution)/shard_map/ppermute | solution.py:221
  108.4 11.1 %collective-permute-start.34 = (f32[8,128]{1,0:T(8,128)S(1)}, f32[8,128]{1,0:T(8,128)S(1)}, u32[]{:S(2)}, u32[]{:S(2)}) collective-permute-start(f32[8,128]{1,0:T(8,128)S(1)} %get-tuple-element.162.refs_2_), channel_id=1, source_target_pairs={{0,1},{1,0},{2,3},{3,2},{4,5},{5,4},{6,7},{7,6},{8,9},{9,8},{10,11... | collective-permute-start | bytes 12296 | tf_op jit(solution)/shard_map/ppermute | solution.py:221
  110.7 16.4 %collective-permute-start.30 = (bf16[64,2048]{1,0:T(8,128)(2,1)S(1)}, bf16[64,2048]{1,0:T(8,128)(2,1)S(1)}, u32[]{:S(2)}, u32[]{:S(2)}) collective-permute-start(bf16[64,2048]{1,0:T(8,128)(2,1)S(1)} %get-tuple-element.170), channel_id=1, source_target_pairs={{0,8},{1,9},{2,10},{3,11},{4,12},{5,13},{6,14},{7,15},{8,0},{9,1},... | collective-permute-start | bytes 786440 | tf_op jit(solution)/shard_map/ppermute | solution.py:221
  112.1 7.2 %collective-permute-start.33 = (bf16[64,2048]{1,0:T(8,128)(2,1)S(1)}, bf16[64,2048]{1,0:T(8,128)(2,1)S(1)}, u32[]{:S(2)}, u32[]{:S(2)}) collective-permute-start(bf16[64,2048]{1,0:T(8,128)(2,1)S(1)} %get-tuple-element.175), channel_id=1, source_target_pairs={{0,2},{1,3},{2,0},{3,1},{4,6},{5,7},{6,4},{7,5},{8,10},{9,11},{10,... | collective-permute-start | bytes 786440 | tf_op jit(solution)/shard_map/ppermute | solution.py:221
  115.5 6.7 %collective-permute-start.32 = (bf16[128,768]{1,0:T(8,128)(2,1)S(1)}, bf16[128,768]{1,0:T(8,128)(2,1)S(1)}, u32[]{:S(2)}, u32[]{:S(2)}) collective-permute-start(bf16[128,768]{1,0:T(8,128)(2,1)S(1)} %get-tuple-element.173.refs_2_), channel_id=1, source_target_pairs={{0,16},{16,0},{1,17},{17,1},{2,18},{18,2},{3,19},{19,3},{4,20},{20... | collective-permute-start | bytes 589832 | tf_op jit(solution)/shard_map/ppermute | solution.py:224
  124.0 14.3 %collective-permute-start.36 = (bf16[64,2048]{1,0:T(8,128)(2,1)S(1)}, bf16[64,2048]{1,0:T(8,128)(2,1)S(1)}, u32[]{:S(2)}, u32[]{:S(2)}) collective-permute-start(bf16[64,2048]{1,0:T(8,128)(2,1)S(1)} %get-tuple-element.183), channel_id=1, source_target_pairs={{0,12},{1,13},{2,14},{3,15},{4,8},{5,9},{6,10},{7,11},{8,4},{9,5},... | collective-permute-start | bytes 786440 | tf_op jit(solution)/shard_map/ppermute | solution.py:221
  125.6 12.8 %collective-permute-start.37 = (bf16[64,2048]{1,0:T(8,128)(2,1)S(1)}, bf16[64,2048]{1,0:T(8,128)(2,1)S(1)}, u32[]{:S(2)}, u32[]{:S(2)}) collective-permute-start(bf16[64,2048]{1,0:T(8,128)(2,1)S(1)} %get-tuple-element.184), channel_id=1, source_target_pairs={{0,2},{1,3},{2,0},{3,1},{4,6},{5,7},{6,4},{7,5},{8,10},{9,11},{10,... | collective-permute-start | bytes 786440 | tf_op jit(solution)/shard_map/ppermute | solution.py:221
  (15 other events, 42.6 us)

commit v6 on v5

--- a/solution.py
+++ b/solution.py
@@ -67,11 +67,12 @@
 
 LANES = 128
 VMEM_LIMIT = 10 * 1024 * 1024
+COST = 8_000_000_000
 TOKEN = jax.ShapeDtypeStruct((8, LANES), jnp.float32)
 HERE = pl.BlockSpec(memory_space=pltpu.VMEM)
 
 
-def call(kernel, inputs, outputs, after, scratch=(), relays=()):
+def call(kernel, inputs, outputs, after, scratch=(), relays=(), cost=0):
     inputs = [v if isinstance(v, tuple) else (v, HERE) for v in inputs]
     flat = [value for group in relays for value in group]
     joined = [
@@ -104,7 +105,7 @@
         out_shape=list(outputs) + joined + [TOKEN],
         scratch_shapes=list(scratch),
         compiler_params=pltpu.CompilerParams(vmem_limit_bytes=VMEM_LIMIT),
-        cost_estimate=pl.CostEstimate(flops=8_000_000_000, bytes_accessed=1, transcendentals=0),
+        cost_estimate=pl.CostEstimate(flops=cost, bytes_accessed=1, transcendentals=0),
     )(*[value for value, _ in inputs], *flat, *after)
     return results[:-1], results[-1]
 
@@ -226,11 +227,11 @@
     def array(shape, dtype=jnp.bfloat16):
         return jax.ShapeDtypeStruct(shape, dtype)
 
-    tail = [jnp.zeros(TOKEN.shape, TOKEN.dtype)]
+    tail, cost = [jnp.zeros(TOKEN.shape, TOKEN.dtype)], [COST]
 
     def step(kernel, inputs, outputs, scratch=(), relays=()):
         results, token = call(
-            kernel, inputs, outputs, list(tail), scratch, relays
+            kernel, inputs, outputs, list(tail), scratch, relays, cost[0]
         )
         tail[:] = [token]
         return results
@@ -306,7 +307,9 @@
     z8 = swap(again, 8)
     (sent,) = partials(p0)
     y0 = cross(sent)
+    cost[0] = 1
     meet()
+    cost[0] = COST
     (b4,) = relay([z4])
     b5, x6 = swap(b4, 1), swap(b4, 2)
     gap()
@@ -314,26 +317,27 @@
     p1 = [b4, b5]
     (sent,) = partials(p1)
     y1 = cross(sent)
+    note3 = swap(tail[0], 1)
+    (h0,) = hidden(p0, y0)
+    tail.append(note3)
     (b6,) = relay([x6])
     b7 = swap(b6, 1)
-    (h0,) = hidden(p0, y0)
     (b8,) = relay([z8])
     x10 = swap(b8, 2)
     p2 = [b6, b7]
     (sent,) = partials(p2, [h0])
     y2 = cross(sent)
+    (h1,) = hidden(p1, y1)
     (again,) = relay([labelled])
     z12 = swap(again, 12)
-    (again,) = relay([labelled])
-    x2 = swap(again, 2)
     (b8,) = relay([b8, x10])
     b9 = swap(b8, 1)
-    (h1,) = hidden(p1, y1)
     gap()
     p3 = [b8, b9]
     (sent,) = partials(p3, [h1])
     y3 = cross(sent)
-    meet()
+    (again,) = relay([labelled])
+    x2 = swap(again, 2)
     (h2,) = hidden(p2, y2)
     c0, c1 = outputs(p0, h0, y2, 4 * rows, rows)
     (b12,) = relay([z12])
@@ -353,14 +357,15 @@
     gap()
     (sent,) = add([c4, c5], (whole, one))
     s4 = swap(sent, 4)
-    p5 = [b2, b3]
-    (later,) = partials(p5)
+    (latera,) = partials([b3])
+    (later,) = partials([b2])
     (h4,) = hidden(p4, y4)
     t4 = cross(h4)
+    (latera,) = relay([latera])
+    y5a = cross(latera)
     (later,) = relay([later])
     y5 = cross(later)
     c6, c7 = outputs(p2, h2, y4, 8 * rows, rows)
-    gap()
     (total,) = add([total, s4], (whole, wide))
     gap()
     (sent,) = add([c6, c7], (whole, one))
@@ -370,18 +375,21 @@
     kept8, sent = add([c8, c9], (whole, wide), ([(0, rows), (1, rows)], one))
     x10 = swap(sent, 2)
     c12, c13 = outputs(p4, h4, t4, 0, 2 * rows)
-    note = swap(tail[0], 1)
+    note2 = swap(tail[0], 1)
     (total,) = add([total, s6], (whole, wide))
+    (h5a,) = hidden([b3], y5a)
+    t5a = cross(h5a)
     kept12, sent = add([c12, c13], (whole, wide), ([(0, rows), (1, rows)], one))
     x14 = swap(sent, 2)
     (sent,) = add([kept8, x10], (whole, one))
     s8 = swap(sent, 8)
-    (h5,) = hidden(p5, y5)
+    _, c3 = outputs([b3], h5a, t5a, 0, 0)
+    (h5,) = hidden([b2], y5)
     t5 = cross(h5)
     (sent,) = add([kept12, x14], (whole, one))
     s12 = swap(sent, 12)
-    tail.append(note)
-    c2, c3 = outputs(p5, h5, t5, 0, rows)
+    tail.append(note2)
+    c2, _ = outputs([b2], h5, t5, 0, rows)
     gap()
     (sent,) = add([c2, c3], (whole, one))
     s2 = swap(sent, 2)

time: 139 us -> 135 us (0.971)
  waiting for transfers between devices: 70.9 us -> 57.2 us
  starting transfers between devices: 28 us -> 33 us
  Pallas kernels: 34.4 us -> 39.2 us
    ppermute x29, waiting for transfers between devices: 41.2 us -> 27.6 us  [swap(): return lax.ppermute(value, 'expert', [(i, i ^ r) for i in range(sources)])]
    ppermute x9 -> x11, starting transfers between devices: 9.55 us -> 15.1 us  [cross(): return lax.ppermute(value, 'dp', [(0, 1), (1, 0)])]
    pallas_call x51 -> x54, Pallas kernels: 34.4 us -> 39.2 us  [call(): pl.pallas_call(run, in_specs=[spec for _, spec in inputs] + [HERE] * len(...]
    ppermute x9 -> x11, waiting for transfers between devices: 29.8 us -> 29.6 us  [cross(): return lax.ppermute(value, 'dp', [(0, 1), (1, 0)])]
  transfers between devices with their start and end apart: 38 -> 40, of which waited for: 23 -> 18; matrix products, arithmetic and copies ran while one was open for 0% -> 0% of each run, Pallas kernels for 24% -> 28%
where the time goes in v6:
time: 135 us
  waiting for transfers between devices  57.2 us (42%)
  Pallas kernels  39.2 us (29%)
  starting transfers between devices  33 us (24%)
  local copies, waits for them, and re-layouts  5.27 us (4%)
    pallas_call x54, Pallas kernels, call(): pl.pallas_call(run, in_specs=[spec for _, spec in inputs] + [HERE] * len(...  39.2 us
    ppermute x11, waiting for transfers between devices, cross(): return lax.ppermute(value, 'dp', [(0, 1), (1, 0)])  29.6 us
    ppermute x29, waiting for transfers between devices, swap(): return lax.ppermute(value, 'expert', [(i, i ^ r) for i in range(sources)])  27.6 us
    ppermute x29, starting transfers between devices, swap(): return lax.ppermute(value, 'expert', [(i, i ^ r) for i in range(sources)])  17.9 us
    ppermute x11, starting transfers between devices, cross(): return lax.ppermute(value, 'dp', [(0, 1), (1, 0)])  15.1 us
    unnamed x18, local copies, waits for them, and re-layouts  5.27 us
  transfers between devices with their start and end apart: 40, of which 18 were waited for; matrix products, arithmetic and copies ran while one was open for 0% of the time, Pallas kernels for 28%

profile of v6, /device:TPU:8, one launch (start us, length us, event | category | flops | bytes accessed | tf_op | source)
XLA Modules:
  0.0 135.3 jit_solution(7347254620062257292)
XLA Ops:
  8.5 2.7 %collective-permute-start.8 = (bf16[64,2176]{1,0:T(8,128)(2,1)S(1)}, bf16[64,2176]{1,0:T(8,128)(2,1)S(1)}, u32[]{:S(2)}, u32[]{:S(2)}) collective-permute-start(bf16[64,2176]{1,0:T(8,128)(2,1)S(1)} %get-tuple-element.114), channel_id=1, source_target_pairs={{0,8},{1,9},{2,10},{3,11},{4,12},{5,13},{6,14},{7,15},{8,0},{9,1},... | collective-permute-start | bytes 835592 | tf_op jit(solution)/shard_map/ppermute | solution.py:222
  12.8 1.6 %collective-permute-start.5 = (bf16[64,2176]{1,0:T(8,128)(2,1)S(1)}, bf16[64,2176]{1,0:T(8,128)(2,1)S(1)}, u32[]{:S(2)}, u32[]{:S(2)}) collective-permute-start(bf16[64,2176]{1,0:T(8,128)(2,1)S(1)} %get-tuple-element.108.refs_0_), channel_id=1, source_target_pairs={{0,2},{1,3},{2,0},{3,1},{4,6},{5,7},{6,4},{7,5},{8,10},{9,11},{10,... | collective-permute-start | bytes 835592 | tf_op jit(solution)/shard_map/ppermute | solution.py:222
  16.5 6.6 %collective-permute-done.1.refs_4_ = bf16[256,768]{1,0:T(8,128)(2,1)S(1)} collective-permute-done((bf16[256,768]{1,0:T(8,128)(2,1)S(1)}, bf16[256,768]{1,0:T(8,128)(2,1)S(1)}, u32[]{:S(2)}, u32[]{:S(2)}) %collective-permute-start.1) | collective-permute-done | bytes 393248 | tf_op jit(solution)/shard_map/ppermute | solution.py:225
  27.8 1.6 %collective-permute-start.9 = (bf16[384,768]{1,0:T(8,128)(2,1)S(1)}, bf16[384,768]{1,0:T(8,128)(2,1)S(1)}, u32[]{:S(2)}, u32[]{:S(2)}) collective-permute-start(bf16[384,768]{1,0:T(8,128)(2,1)S(1)} %get-tuple-element.117), channel_id=1, source_target_pairs={{0,16},{16,0},{1,17},{17,1},{2,18},{18,2},{3,19},{19,3},{4,20},{20... | collective-permute-start | bytes 1769480 | tf_op jit(solution)/shard_map/ppermute | solution.py:225
  34.1 1.9 %collective-permute-done.12.refs_1_ = bf16[128,2176]{1,0:T(8,128)(2,1)S(1)} collective-permute-done((bf16[128,2176]{1,0:T(8,128)(2,1)S(1)}, bf16[128,2176]{1,0:T(8,128)(2,1)S(1)}, u32[]{:S(2)}, u32[]{:S(2)}) %collective-permute-start.12) | collective-permute-done | bytes 557088 | tf_op jit(solution)/shard_map/ppermute | solution.py:222
  36.0 2.2 %shard_map.79 = (bf16[640,768]{1,0:T(8,128)(2,1)S(1)}, f32[8,128]{1,0:T(8,128)S(1)}) custom-call(bf16[128,2176]{1,0:T(8,128)(2,1)S(1)} %get-tuple-element.123.refs_0_, bf16[128,2176]{1,0:T(8,128)(2,1)S(1)} %collective-permute-done.12.refs_1_, bf16[1,2048,1536]{2,1,0:T(8,128)(2,1)S(1)} %bitcast.3, bf16[1,2048,1536]{2,1,0:T(8,128)(2,1)S(1)} %bitcast.5, ...), custom_call_target="tpu_custom_call" | custom-call | flops 8000000000 | bytes 1 | tf_op jit(solution)/shard_map/pallas_call | solution.py:101
  38.3 1.6 %collective-permute-start.15 = (bf16[640,768]{1,0:T(8,128)(2,1)S(1)}, bf16[640,768]{1,0:T(8,128)(2,1)S(1)}, u32[]{:S(2)}, u32[]{:S(2)}) collective-permute-start(bf16[640,768]{1,0:T(8,128)(2,1)S(1)} %get-tuple-element.135), channel_id=1, source_target_pairs={{0,16},{16,0},{1,17},{17,1},{2,18},{18,2},{3,19},{19,3},{4,20},{20... | collective-permute-start | bytes 2949128 | tf_op jit(solution)/shard_map/ppermute | solution.py:225
  41.4 2.7 %collective-permute-done.9.refs_4_.refs_3_ = bf16[384,768]{1,0:T(8,128)(2,1)S(1)} collective-permute-done((bf16[384,768]{1,0:T(8,128)(2,1)S(1)}, bf16[384,768]{1,0:T(8,128)(2,1)S(1)}, u32[]{:S(2)}, u32[]{:S(2)}) %collective-permute-start.9) | collective-permute-done | bytes 589856 | tf_op jit(solution)/shard_map/ppermute | solution.py:225
  45.6 1.7 %shard_map.82 = (f32[64,2048]{1,0:T(8,128)S(1)}, bf16[64,2048]{1,0:T(8,128)(2,1)S(1)}, f32[8,128]{1,0:T(8,128)S(1)}) custom-call(bf16[64,2176]{1,0:T(8,128)(2,1)S(1)} %get-tuple-element.103.refs_0_, bf16[64,2176]{1,0:T(8,128)(2,1)S(1)} %collective-permute-done.refs_1_, bf16[128,768]{1,0:T(8,128)(2,1)S(1)} %get-tuple-element.111.refs_4_.refs_2_, ...), custom_call_target="tpu_custom_call" | custom-call | flops 8000000000 | bytes 1 | tf_op jit(solution)/shard_map/pallas_call | solution.py:101
  47.4 1.7 %collective-permute-done.14.refs_0_ = bf16[64,2176]{1,0:T(8,128)(2,1)S(1)} collective-permute-done((bf16[64,2176]{1,0:T(8,128)(2,1)S(1)}, bf16[64,2176]{1,0:T(8,128)(2,1)S(1)}, u32[]{:S(2)}, u32[]{:S(2)}) %collective-permute-start.14) | collective-permute-done | bytes 278560 | tf_op jit(solution)/shard_map/ppermute | solution.py:222
  50.7 6.7 %collective-permute-done.17.refs_1_ = bf16[64,2176]{1,0:T(8,128)(2,1)S(1)} collective-permute-done((bf16[64,2176]{1,0:T(8,128)(2,1)S(1)}, bf16[64,2176]{1,0:T(8,128)(2,1)S(1)}, u32[]{:S(2)}, u32[]{:S(2)}) %collective-permute-start.17) | collective-permute-done | bytes 278560 | tf_op jit(solution)/shard_map/ppermute | solution.py:222
  57.5 1.9 %collective-permute-done.18.refs_1_ = bf16[128,2176]{1,0:T(8,128)(2,1)S(1)} collective-permute-done((bf16[128,2176]{1,0:T(8,128)(2,1)S(1)}, bf16[128,2176]{1,0:T(8,128)(2,1)S(1)}, u32[]{:S(2)}, u32[]{:S(2)}) %collective-permute-start.18) | collective-permute-done | bytes 557088 | tf_op jit(solution)/shard_map/ppermute | solution.py:222
  59.5 2.2 %shard_map.87 = (bf16[640,768]{1,0:T(8,128)(2,1)S(1)}, f32[8,128]{1,0:T(8,128)S(1)}) custom-call(bf16[128,2176]{1,0:T(8,128)(2,1)S(1)} %get-tuple-element.139.refs_0_, bf16[128,2176]{1,0:T(8,128)(2,1)S(1)} %collective-permute-done.18.refs_1_, bf16[1,2048,1536]{2,1,0:T(8,128)(2,1)S(1)} %bitcast.3, bf16[1,2048,1536]{2,1,0:T(8,128)(2,1)S(1)} %bitcast.5, ...), custom_call_target="tpu_custom_call" | custom-call | flops 8000000000 | bytes 1 | tf_op jit(solution)/shard_map/pallas_call | solution.py:101
  61.7 1.6 %collective-permute-start.21 = (bf16[640,768]{1,0:T(8,128)(2,1)S(1)}, bf16[640,768]{1,0:T(8,128)(2,1)S(1)}, u32[]{:S(2)}, u32[]{:S(2)}) collective-permute-start(bf16[640,768]{1,0:T(8,128)(2,1)S(1)} %get-tuple-element.149), channel_id=1, source_target_pairs={{0,16},{16,0},{1,17},{17,1},{2,18},{18,2},{3,19},{19,3},{4,20},{20... | collective-permute-start | bytes 2949128 | tf_op jit(solution)/shard_map/ppermute | solution.py:225
  64.5 2.3 %shard_map.89 = (bf16[256,768]{1,0:T(8,128)(2,1)S(1)}, f32[8,128]{1,0:T(8,128)S(1)}) custom-call(bf16[128,2176]{1,0:T(8,128)(2,1)S(1)} %get-tuple-element.123.refs_0_, bf16[128,2176]{1,0:T(8,128)(2,1)S(1)} %collective-permute-done.12.refs_1_, bf16[1,2048,1536]{2,1,0:T(8,128)(2,1)S(1)} %bitcast.3, bf16[1,2048,1536]{2,1,0:T(8,128)(2,1)S(1)} %bitcast.5, ...), custom_call_target="tpu_custom_call" | custom-call | flops 8000000000 | bytes 1 | tf_op jit(solution)/shard_map/pallas_call | solution.py:101
  66.9 1.7 %shard_map.90 = (f32[64,2048]{1,0:T(8,128)S(1)}, bf16[64,2048]{1,0:T(8,128)(2,1)S(1)}, f32[8,128]{1,0:T(8,128)S(1)}) custom-call(bf16[64,2176]{1,0:T(8,128)(2,1)S(1)} %get-tuple-element.108.refs_0_, bf16[64,2176]{1,0:T(8,128)(2,1)S(1)} %collective-permute-done.4.refs_1_, bf16[128,768]{1,0:T(8,128)(2,1)S(1)} %get-tuple-element.124.refs_4_.refs_2_, ...), custom_call_target="tpu_custom_call" | custom-call | flops 8000000000 | bytes 1 | tf_op jit(solution)/shard_map/pallas_call | solution.py:101
  68.6 1.6 %collective-permute-start.26 = (bf16[256,768]{1,0:T(8,128)(2,1)S(1)}, bf16[256,768]{1,0:T(8,128)(2,1)S(1)}, u32[]{:S(2)}, u32[]{:S(2)}) collective-permute-start(bf16[256,768]{1,0:T(8,128)(2,1)S(1)} %get-tuple-element.166.refs_2_), channel_id=1, source_target_pairs={{0,16},{16,0},{1,17},{17,1},{2,18},{18,2},{3,19},{19,3},{4,20},{20... | collective-permute-start | bytes 1179656 | tf_op jit(solution)/shard_map/ppermute | solution.py:225
  74.4 12.0 %collective-permute-done.21.refs_4_.refs_3_ = bf16[640,768]{1,0:T(8,128)(2,1)S(1)} collective-permute-done((bf16[640,768]{1,0:T(8,128)(2,1)S(1)}, bf16[640,768]{1,0:T(8,128)(2,1)S(1)}, u32[]{:S(2)}, u32[]{:S(2)}) %collective-permute-start.21) | collective-permute-done | bytes 983072 | tf_op jit(solution)/shard_map/ppermute | solution.py:225
  86.4 2.3 %shard_map.95 = (bf16[256,768]{1,0:T(8,128)(2,1)S(1)}, f32[8,128]{1,0:T(8,128)S(1)}) custom-call(bf16[128,2176]{1,0:T(8,128)(2,1)S(1)} %get-tuple-element.139.refs_0_, bf16[128,2176]{1,0:T(8,128)(2,1)S(1)} %collective-permute-done.18.refs_1_, bf16[1,2048,1536]{2,1,0:T(8,128)(2,1)S(1)} %bitcast.3, bf16[1,2048,1536]{2,1,0:T(8,128)(2,1)S(1)} %bitcast.5, ...), custom_call_target="tpu_custom_call" | custom-call | flops 8000000000 | bytes 1 | tf_op jit(solution)/shard_map/pallas_call | solution.py:101
  88.8 1.7 %shard_map.98 = (f32[64,2048]{1,0:T(8,128)S(1)}, bf16[64,2048]{1,0:T(8,128)(2,1)S(1)}, f32[8,128]{1,0:T(8,128)S(1)}) custom-call(bf16[64,2176]{1,0:T(8,128)(2,1)S(1)} %get-tuple-element.113.refs_0_, bf16[64,2176]{1,0:T(8,128)(2,1)S(1)} %collective-permute-done.7.refs_1_, bf16[128,768]{1,0:T(8,128)(2,1)S(1)} %get-tuple-element.140.refs_4_.refs_2_, ...), custom_call_target="tpu_custom_call" | custom-call | flops 8000000000 | bytes 1 | tf_op jit(solution)/shard_map/pallas_call | solution.py:101
  90.7 1.6 %collective-permute-start.25 = (bf16[256,768]{1,0:T(8,128)(2,1)S(1)}, bf16[256,768]{1,0:T(8,128)(2,1)S(1)}, u32[]{:S(2)}, u32[]{:S(2)}) collective-permute-start(bf16[256,768]{1,0:T(8,128)(2,1)S(1)} %get-tuple-element.165.refs_2_), channel_id=1, source_target_pairs={{0,16},{16,0},{1,17},{17,1},{2,18},{18,2},{3,19},{19,3},{4,20},{20... | collective-permute-start | bytes 1179656 | tf_op jit(solution)/shard_map/ppermute | solution.py:225
  95.5 2.4 %shard_map.102 = (f32[128,2048]{1,0:T(8,128)S(1)}, bf16[128,2048]{1,0:T(8,128)(2,1)S(1)}, f32[8,128]{1,0:T(8,128)S(1)}) custom-call(bf16[128,2176]{1,0:T(8,128)(2,1)S(1)} %get-tuple-element.123.refs_0_, bf16[128,2176]{1,0:T(8,128)(2,1)S(1)} %collective-permute-done.12.refs_1_, bf16[256,768]{1,0:T(8,128)(2,1)S(1)} %get-tuple-element.166.refs_2_, ...), custom_call_target="tpu_custom_call" | custom-call | flops 8000000000 | bytes 1 | tf_op jit(solution)/shard_map/pallas_call | solution.py:101
  98.1 1.9 %collective-permute-done.27.refs_1_ = bf16[128,2048]{1,0:T(8,128)(2,1)S(1)} collective-permute-done((bf16[128,2048]{1,0:T(8,128)(2,1)S(1)}, bf16[128,2048]{1,0:T(8,128)(2,1)S(1)}, u32[]{:S(2)}, u32[]{:S(2)}) %collective-permute-start.27) | collective-permute-done | bytes 524320 | tf_op jit(solution)/shard_map/ppermute | solution.py:222
  100.7 2.0 %collective-permute-done.25.refs_3_ = bf16[256,768]{1,0:T(8,128)(2,1)S(1)} collective-permute-done((bf16[256,768]{1,0:T(8,128)(2,1)S(1)}, bf16[256,768]{1,0:T(8,128)(2,1)S(1)}, u32[]{:S(2)}, u32[]{:S(2)}) %collective-permute-start.25) | collective-permute-done | bytes 393248 | tf_op jit(solution)/shard_map/ppermute | solution.py:225
  102.7 2.5 %shard_map.105 = (f32[128,2048]{1,0:T(8,128)S(1)}, bf16[128,2048]{1,0:T(8,128)(2,1)S(1)}, f32[8,128]{1,0:T(8,128)S(1)}) custom-call(bf16[128,2176]{1,0:T(8,128)(2,1)S(1)} %get-tuple-element.139.refs_0_, bf16[128,2176]{1,0:T(8,128)(2,1)S(1)} %collective-permute-done.18.refs_1_, bf16[256,768]{1,0:T(8,128)(2,1)S(1)} %get-tuple-element.165.refs_2_, ...), custom_call_target="tpu_custom_call" | custom-call | flops 8000000000 | bytes 1 | tf_op jit(solution)/shard_map/pallas_call | solution.py:101
  108.5 1.6 %collective-permute-start.33 = (bf16[64,768]{1,0:T(8,128)(2,1)S(1)}, bf16[64,768]{1,0:T(8,128)(2,1)S(1)}, u32[]{:S(2)}, u32[]{:S(2)}) collective-permute-start(bf16[64,768]{1,0:T(8,128)(2,1)S(1)} %get-tuple-element.184.refs_1_), channel_id=1, source_target_pairs={{0,16},{16,0},{1,17},{17,1},{2,18},{18,2},{3,19},{19,3},{4,20},{20... | collective-permute-start | bytes 294920 | tf_op jit(solution)/shard_map/ppermute | solution.py:225
  110.2 1.8 %collective-permute-start.31 = (bf16[64,2048]{1,0:T(8,128)(2,1)S(1)}, bf16[64,2048]{1,0:T(8,128)(2,1)S(1)}, u32[]{:S(2)}, u32[]{:S(2)}) collective-permute-start(bf16[64,2048]{1,0:T(8,128)(2,1)S(1)} %get-tuple-element.182), channel_id=1, source_target_pairs={{0,8},{1,9},{2,10},{3,11},{4,12},{5,13},{6,14},{7,15},{8,0},{9,1},... | collective-permute-start | bytes 786440 | tf_op jit(solution)/shard_map/ppermute | solution.py:222
  113.2 1.7 %shard_map.110 = (bf16[64,2048]{1,0:T(8,128)(2,1)S(1)}, f32[8,128]{1,0:T(8,128)S(1)}) custom-call(bf16[64,2176]{1,0:T(8,128)(2,1)S(1)} %collective-permute-done.22.refs_0_, bf16[64,768]{1,0:T(8,128)(2,1)S(1)} %get-tuple-element.184.refs_1_, bf16[64,768]{1,0:T(8,128)(2,1)S(1)} %collective-permute-done.33.refs_2_, bf16[1,1536,2048]{2,1,0:T(8,128)(2,1)S(1)} %bitcast.7, ...), custom_call_target="tpu_custom_call" | custom-call | flops 8000000000 | bytes 1 | tf_op jit(solution)/shard_map/pallas_call | solution.py:101
  116.4 1.6 %collective-permute-start.34 = (bf16[64,768]{1,0:T(8,128)(2,1)S(1)}, bf16[64,768]{1,0:T(8,128)(2,1)S(1)}, u32[]{:S(2)}, u32[]{:S(2)}) collective-permute-start(bf16[64,768]{1,0:T(8,128)(2,1)S(1)} %get-tuple-element.187.refs_1_), channel_id=1, source_target_pairs={{0,16},{16,0},{1,17},{17,1},{2,18},{18,2},{3,19},{19,3},{4,20},{20... | collective-permute-start | bytes 294920 | tf_op jit(solution)/shard_map/ppermute | solution.py:225
  119.0 2.0 %collective-permute-done.34.refs_2_ = bf16[64,768]{1,0:T(8,128)(2,1)S(1)} collective-permute-done((bf16[64,768]{1,0:T(8,128)(2,1)S(1)}, bf16[64,768]{1,0:T(8,128)(2,1)S(1)}, u32[]{:S(2)}, u32[]{:S(2)}) %collective-permute-start.34) | collective-permute-done | bytes 98336 | tf_op jit(solution)/shard_map/ppermute | solution.py:225
  121.0 1.7 %shard_map.113 = (f32[64,2048]{1,0:T(8,128)S(1)}, f32[8,128]{1,0:T(8,128)S(1)}) custom-call(bf16[64,2176]{1,0:T(8,128)(2,1)S(1)} %get-tuple-element.150.refs_0_, bf16[64,768]{1,0:T(8,128)(2,1)S(1)} %get-tuple-element.187.refs_1_, bf16[64,768]{1,0:T(8,128)(2,1)S(1)} %collective-permute-done.34.refs_2_, bf16[1,1536,2048]{2,1,0:T(8,128)(2,1)S(1)} %bitcast.7, ...), custom_call_target="tpu_custom_call" | custom-call | flops 8000000000 | bytes 1 | tf_op jit(solution)/shard_map/pallas_call | solution.py:101
  124.9 9.5 %collective-permute-done.38.refs_1_ = bf16[64,2048]{1,0:T(8,128)(2,1)S(1)} collective-permute-done((bf16[64,2048]{1,0:T(8,128)(2,1)S(1)}, bf16[64,2048]{1,0:T(8,128)(2,1)S(1)}, u32[]{:S(2)}, u32[]{:S(2)}) %collective-permute-start.38) | collective-permute-done | bytes 262176 | tf_op jit(solution)/shard_map/ppermute | solution.py:222
  (124 shorter events, 46.3 us)
Async XLA Ops:
  2.5 10.1 %collective-permute-start.2 = (bf16[64,2176]{1,0:T(8,128)(2,1)S(1)}, bf16[64,2176]{1,0:T(8,128)(2,1)S(1)}, u32[]{:S(2)}, u32[]{:S(2)}) collective-permute-start(bf16[64,2176]{1,0:T(8,128)(2,1)S(1)} %get-tuple-element.103.refs_0_), channel_id=1, source_target_pairs={{0,4},{1,5},{2,6},{3,7},{4,0},{5,1},{6,2},{7,3},{8,12},{9,13},{10,... | collective-permute-start | bytes 835592 | tf_op jit(solution)/shard_map/ppermute | solution.py:222
  8.5 4.2 %collective-permute-start.3 = (f32[8,128]{1,0:T(8,128)S(1)}, f32[8,128]{1,0:T(8,128)S(1)}, u32[]{:S(2)}, u32[]{:S(2)}) collective-permute-start(f32[8,128]{1,0:T(8,128)S(1)} %get-tuple-element.107.refs_1_), channel_id=1, source_target_pairs={{0,1},{1,0},{2,3},{3,2},{4,5},{5,4},{6,7},{7,6},{8,9},{9,8},{10,11... | collective-permute-start | bytes 12296 | tf_op jit(solution)/shard_map/ppermute | solution.py:222
  8.5 16.2 %collective-permute-start.8 = (bf16[64,2176]{1,0:T(8,128)(2,1)S(1)}, bf16[64,2176]{1,0:T(8,128)(2,1)S(1)}, u32[]{:S(2)}, u32[]{:S(2)}) collective-permute-start(bf16[64,2176]{1,0:T(8,128)(2,1)S(1)} %get-tuple-element.114), channel_id=1, source_target_pairs={{0,8},{1,9},{2,10},{3,11},{4,12},{5,13},{6,14},{7,15},{8,0},{9,1},... | collective-permute-start | bytes 835592 | tf_op jit(solution)/shard_map/ppermute | solution.py:222
  11.2 12.0 %collective-permute-start.1 = (bf16[256,768]{1,0:T(8,128)(2,1)S(1)}, bf16[256,768]{1,0:T(8,128)(2,1)S(1)}, u32[]{:S(2)}, u32[]{:S(2)}) collective-permute-start(bf16[256,768]{1,0:T(8,128)(2,1)S(1)} %get-tuple-element.106), channel_id=1, source_target_pairs={{0,16},{16,0},{1,17},{17,1},{2,18},{18,2},{3,19},{19,3},{4,20},{20... | collective-permute-start | bytes 1179656 | tf_op jit(solution)/shard_map/ppermute | solution.py:225
  12.8 11.9 %collective-permute-start.5 = (bf16[64,2176]{1,0:T(8,128)(2,1)S(1)}, bf16[64,2176]{1,0:T(8,128)(2,1)S(1)}, u32[]{:S(2)}, u32[]{:S(2)}) collective-permute-start(bf16[64,2176]{1,0:T(8,128)(2,1)S(1)} %get-tuple-element.108.refs_0_), channel_id=1, source_target_pairs={{0,2},{1,3},{2,0},{3,1},{4,6},{5,7},{6,4},{7,5},{8,10},{9,11},{10,... | collective-permute-start | bytes 835592 | tf_op jit(solution)/shard_map/ppermute | solution.py:222
  15.8 8.9 %collective-permute-start.6 = (f32[8,128]{1,0:T(8,128)S(1)}, f32[8,128]{1,0:T(8,128)S(1)}, u32[]{:S(2)}, u32[]{:S(2)}) collective-permute-start(f32[8,128]{1,0:T(8,128)S(1)} %get-tuple-element.110.refs_5_), channel_id=1, source_target_pairs={{0,1},{1,0},{2,3},{3,2},{4,5},{5,4},{6,7},{7,6},{8,9},{9,8},{10,11... | collective-permute-start | bytes 12296 | tf_op jit(solution)/shard_map/ppermute | solution.py:222
  16.0 14.8 %collective-permute-start.11 = (bf16[256,768]{1,0:T(8,128)(2,1)S(1)}, bf16[256,768]{1,0:T(8,128)(2,1)S(1)}, u32[]{:S(2)}, u32[]{:S(2)}) collective-permute-start(bf16[256,768]{1,0:T(8,128)(2,1)S(1)} %get-tuple-element.119), channel_id=1, source_target_pairs={{0,16},{16,0},{1,17},{17,1},{2,18},{18,2},{3,19},{19,3},{4,20},{20... | collective-permute-start | bytes 1179656 | tf_op jit(solution)/shard_map/ppermute | solution.py:225
  24.8 9.1 %collective-permute-start.10 = (bf16[64,2176]{1,0:T(8,128)(2,1)S(1)}, bf16[64,2176]{1,0:T(8,128)(2,1)S(1)}, u32[]{:S(2)}, u32[]{:S(2)}) collective-permute-start(bf16[64,2176]{1,0:T(8,128)(2,1)S(1)} %get-tuple-element.118.refs_0_), channel_id=1, source_target_pairs={{0,2},{1,3},{2,0},{3,1},{4,6},{5,7},{6,4},{7,5},{8,10},{9,11},{10,... | collective-permute-start | bytes 835592 | tf_op jit(solution)/shard_map/ppermute | solution.py:222
  27.8 16.2 %collective-permute-start.9 = (bf16[384,768]{1,0:T(8,128)(2,1)S(1)}, bf16[384,768]{1,0:T(8,128)(2,1)S(1)}, u32[]{:S(2)}, u32[]{:S(2)}) collective-permute-start(bf16[384,768]{1,0:T(8,128)(2,1)S(1)} %get-tuple-element.117), channel_id=1, source_target_pairs={{0,16},{16,0},{1,17},{17,1},{2,18},{18,2},{3,19},{19,3},{4,20},{20... | collective-permute-start | bytes 1769480 | tf_op jit(solution)/shard_map/ppermute | solution.py:225
  34.0 15.0 %collective-permute-start.14 = (bf16[64,2176]{1,0:T(8,128)(2,1)S(1)}, bf16[64,2176]{1,0:T(8,128)(2,1)S(1)}, u32[]{:S(2)}, u32[]{:S(2)}) collective-permute-start(bf16[64,2176]{1,0:T(8,128)(2,1)S(1)} %get-tuple-element.131), channel_id=1, source_target_pairs={{0,12},{1,13},{2,14},{3,15},{4,8},{5,9},{6,10},{7,11},{8,4},{9,5},... | collective-permute-start | bytes 835592 | tf_op jit(solution)/shard_map/ppermute | solution.py:222
  38.3 26.3 %collective-permute-start.15 = (bf16[640,768]{1,0:T(8,128)(2,1)S(1)}, bf16[640,768]{1,0:T(8,128)(2,1)S(1)}, u32[]{:S(2)}, u32[]{:S(2)}) collective-permute-start(bf16[640,768]{1,0:T(8,128)(2,1)S(1)} %get-tuple-element.135), channel_id=1, source_target_pairs={{0,16},{16,0},{1,17},{17,1},{2,18},{18,2},{3,19},{19,3},{4,20},{20... | collective-permute-start | bytes 2949128 | tf_op jit(solution)/shard_map/ppermute | solution.py:225
  39.9 23.4 %collective-permute-start.16 = (bf16[64,2176]{1,0:T(8,128)(2,1)S(1)}, bf16[64,2176]{1,0:T(8,128)(2,1)S(1)}, u32[]{:S(2)}, u32[]{:S(2)}) collective-permute-start(bf16[64,2176]{1,0:T(8,128)(2,1)S(1)} %get-tuple-element.136), channel_id=1, source_target_pairs={{0,2},{1,3},{2,0},{3,1},{4,6},{5,7},{6,4},{7,5},{8,10},{9,11},{10,... | collective-permute-start | bytes 835592 | tf_op jit(solution)/shard_map/ppermute | solution.py:222
  49.1 8.3 %collective-permute-start.17 = (bf16[64,2176]{1,0:T(8,128)(2,1)S(1)}, bf16[64,2176]{1,0:T(8,128)(2,1)S(1)}, u32[]{:S(2)}, u32[]{:S(2)}) collective-permute-start(bf16[64,2176]{1,0:T(8,128)(2,1)S(1)} %get-tuple-element.137.refs_0_), channel_id=1, source_target_pairs={{0,2},{1,3},{2,0},{3,1},{4,6},{5,7},{6,4},{7,5},{8,10},{9,11},{10,... | collective-permute-start | bytes 835592 | tf_op jit(solution)/shard_map/ppermute | solution.py:222
  61.7 24.7 %collective-permute-start.21 = (bf16[640,768]{1,0:T(8,128)(2,1)S(1)}, bf16[640,768]{1,0:T(8,128)(2,1)S(1)}, u32[]{:S(2)}, u32[]{:S(2)}) collective-permute-start(bf16[640,768]{1,0:T(8,128)(2,1)S(1)} %get-tuple-element.149), channel_id=1, source_target_pairs={{0,16},{16,0},{1,17},{17,1},{2,18},{18,2},{3,19},{19,3},{4,20},{20... | collective-permute-start | bytes 2949128 | tf_op jit(solution)/shard_map/ppermute | solution.py:225
  63.3 8.1 %collective-permute-start.22 = (bf16[64,2176]{1,0:T(8,128)(2,1)S(1)}, bf16[64,2176]{1,0:T(8,128)(2,1)S(1)}, u32[]{:S(2)}, u32[]{:S(2)}) collective-permute-start(bf16[64,2176]{1,0:T(8,128)(2,1)S(1)} %get-tuple-element.150.refs_0_), channel_id=1, source_target_pairs={{0,1},{1,0},{2,3},{3,2},{4,5},{5,4},{6,7},{7,6},{8,9},{9,8},{10,11... | collective-permute-start | bytes 835592 | tf_op jit(solution)/shard_map/ppermute | solution.py:222
  68.6 26.9 %collective-permute-start.26 = (bf16[256,768]{1,0:T(8,128)(2,1)S(1)}, bf16[256,768]{1,0:T(8,128)(2,1)S(1)}, u32[]{:S(2)}, u32[]{:S(2)}) collective-permute-start(bf16[256,768]{1,0:T(8,128)(2,1)S(1)} %get-tuple-element.166.refs_2_), channel_id=1, source_target_pairs={{0,16},{16,0},{1,17},{17,1},{2,18},{18,2},{3,19},{19,3},{4,20},{20... | collective-permute-start | bytes 1179656 | tf_op jit(solution)/shard_map/ppermute | solution.py:225
  70.3 20.3 %collective-permute-start.20 = (bf16[64,2048]{1,0:T(8,128)(2,1)S(1)}, bf16[64,2048]{1,0:T(8,128)(2,1)S(1)}, u32[]{:S(2)}, u32[]{:S(2)}) collective-permute-start(bf16[64,2048]{1,0:T(8,128)(2,1)S(1)} %get-tuple-element.148), channel_id=1, source_target_pairs={{0,4},{1,5},{2,6},{3,7},{4,0},{5,1},{6,2},{7,3},{8,12},{9,13},{10,... | collective-permute-start | bytes 786440 | tf_op jit(solution)/shard_map/ppermute | solution.py:222
  90.5 3.8 %collective-permute-start.23 = (bf16[64,2048]{1,0:T(8,128)(2,1)S(1)}, bf16[64,2048]{1,0:T(8,128)(2,1)S(1)}, u32[]{:S(2)}, u32[]{:S(2)}) collective-permute-start(bf16[64,2048]{1,0:T(8,128)(2,1)S(1)} %get-tuple-element.162), channel_id=1, source_target_pairs={{0,1},{1,0},{2,3},{3,2},{4,5},{5,4},{6,7},{7,6},{8,9},{9,8},{10,11... | collective-permute-start | bytes 786440 | tf_op jit(solution)/shard_map/ppermute | solution.py:222
  90.7 12.1 %collective-permute-start.25 = (bf16[256,768]{1,0:T(8,128)(2,1)S(1)}, bf16[256,768]{1,0:T(8,128)(2,1)S(1)}, u32[]{:S(2)}, u32[]{:S(2)}) collective-permute-start(bf16[256,768]{1,0:T(8,128)(2,1)S(1)} %get-tuple-element.165.refs_2_), channel_id=1, source_target_pairs={{0,16},{16,0},{1,17},{17,1},{2,18},{18,2},{3,19},{19,3},{4,20},{20... | collective-permute-start | bytes 1179656 | tf_op jit(solution)/shard_map/ppermute | solution.py:225
  92.2 14.7 %collective-permute-start.30 = (bf16[128,768]{1,0:T(8,128)(2,1)S(1)}, bf16[128,768]{1,0:T(8,128)(2,1)S(1)}, u32[]{:S(2)}, u32[]{:S(2)}) collective-permute-start(bf16[128,768]{1,0:T(8,128)(2,1)S(1)} %get-tuple-element.178), channel_id=1, source_target_pairs={{0,16},{16,0},{1,17},{17,1},{2,18},{18,2},{3,19},{19,3},{4,20},{20... | collective-permute-start | bytes 589832 | tf_op jit(solution)/shard_map/ppermute | solution.py:225
  92.8 22.1 %collective-permute-start.32 = (bf16[128,768]{1,0:T(8,128)(2,1)S(1)}, bf16[128,768]{1,0:T(8,128)(2,1)S(1)}, u32[]{:S(2)}, u32[]{:S(2)}) collective-permute-start(bf16[128,768]{1,0:T(8,128)(2,1)S(1)} %get-tuple-element.183), channel_id=1, source_target_pairs={{0,16},{16,0},{1,17},{17,1},{2,18},{18,2},{3,19},{19,3},{4,20},{20... | collective-permute-start | bytes 589832 | tf_op jit(solution)/shard_map/ppermute | solution.py:225
  94.3 10.9 %collective-permute-start.24 = (bf16[64,2048]{1,0:T(8,128)(2,1)S(1)}, bf16[64,2048]{1,0:T(8,128)(2,1)S(1)}, u32[]{:S(2)}, u32[]{:S(2)}) collective-permute-start(bf16[64,2048]{1,0:T(8,128)(2,1)S(1)} %get-tuple-element.164), channel_id=1, source_target_pairs={{0,6},{1,7},{2,4},{3,5},{4,2},{5,3},{6,0},{7,1},{8,14},{9,15},{10,... | collective-permute-start | bytes 786440 | tf_op jit(solution)/shard_map/ppermute | solution.py:222
  100.1 10.1 %collective-permute-start.28 = (bf16[64,2048]{1,0:T(8,128)(2,1)S(1)}, bf16[64,2048]{1,0:T(8,128)(2,1)S(1)}, u32[]{:S(2)}, u32[]{:S(2)}) collective-permute-start(bf16[64,2048]{1,0:T(8,128)(2,1)S(1)} %get-tuple-element.175), channel_id=1, source_target_pairs={{0,2},{1,3},{2,0},{3,1},{4,6},{5,7},{6,4},{7,5},{8,10},{9,11},{10,... | collective-permute-start | bytes 786440 | tf_op jit(solution)/shard_map/ppermute | solution.py:222
  105.2 4.9 %collective-permute-start.29 = (bf16[128,2048]{1,0:T(8,128)(2,1)S(1)}, bf16[128,2048]{1,0:T(8,128)(2,1)S(1)}, u32[]{:S(2)}, u32[]{:S(2)}) collective-permute-start(bf16[128,2048]{1,0:T(8,128)(2,1)S(1)} %get-tuple-element.177), channel_id=1, source_target_pairs={{0,1},{1,0},{2,3},{3,2},{4,5},{5,4},{6,7},{7,6},{8,9},{9,8},{10,11... | collective-permute-start | bytes 1572872 | tf_op jit(solution)/shard_map/ppermute | solution.py:222
  105.3 13.8 %collective-permute-start.36 = (f32[8,128]{1,0:T(8,128)S(1)}, f32[8,128]{1,0:T(8,128)S(1)}, u32[]{:S(2)}, u32[]{:S(2)}) collective-permute-start(f32[8,128]{1,0:T(8,128)S(1)} %get-tuple-element.172.refs_2_), channel_id=1, source_target_pairs={{0,1},{1,0},{2,3},{3,2},{4,5},{5,4},{6,7},{7,6},{8,9},{9,8},{10,11... | collective-permute-start | bytes 12296 | tf_op jit(solution)/shard_map/ppermute | solution.py:222
  108.5 4.7 %collective-permute-start.33 = (bf16[64,768]{1,0:T(8,128)(2,1)S(1)}, bf16[64,768]{1,0:T(8,128)(2,1)S(1)}, u32[]{:S(2)}, u32[]{:S(2)}) collective-permute-start(bf16[64,768]{1,0:T(8,128)(2,1)S(1)} %get-tuple-element.184.refs_1_), channel_id=1, source_target_pairs={{0,16},{16,0},{1,17},{17,1},{2,18},{18,2},{3,19},{19,3},{4,20},{20... | collective-permute-start | bytes 294920 | tf_op jit(solution)/shard_map/ppermute | solution.py:225
  110.2 14.6 %collective-permute-start.31 = (bf16[64,2048]{1,0:T(8,128)(2,1)S(1)}, bf16[64,2048]{1,0:T(8,128)(2,1)S(1)}, u32[]{:S(2)}, u32[]{:S(2)}) collective-permute-start(bf16[64,2048]{1,0:T(8,128)(2,1)S(1)} %get-tuple-element.182), channel_id=1, source_target_pairs={{0,8},{1,9},{2,10},{3,11},{4,12},{5,13},{6,14},{7,15},{8,0},{9,1},... | collective-permute-start | bytes 786440 | tf_op jit(solution)/shard_map/ppermute | solution.py:222
  112.0 7.0 %collective-permute-start.35 = (bf16[64,2048]{1,0:T(8,128)(2,1)S(1)}, bf16[64,2048]{1,0:T(8,128)(2,1)S(1)}, u32[]{:S(2)}, u32[]{:S(2)}) collective-permute-start(bf16[64,2048]{1,0:T(8,128)(2,1)S(1)} %get-tuple-element.189), channel_id=1, source_target_pairs={{0,2},{1,3},{2,0},{3,1},{4,6},{5,7},{6,4},{7,5},{8,10},{9,11},{10,... | collective-permute-start | bytes 786440 | tf_op jit(solution)/shard_map/ppermute | solution.py:222
  116.4 4.7 %collective-permute-start.34 = (bf16[64,768]{1,0:T(8,128)(2,1)S(1)}, bf16[64,768]{1,0:T(8,128)(2,1)S(1)}, u32[]{:S(2)}, u32[]{:S(2)}) collective-permute-start(bf16[64,768]{1,0:T(8,128)(2,1)S(1)} %get-tuple-element.187.refs_1_), channel_id=1, source_target_pairs={{0,16},{16,0},{1,17},{17,1},{2,18},{18,2},{3,19},{19,3},{4,20},{20... | collective-permute-start | bytes 294920 | tf_op jit(solution)/shard_map/ppermute | solution.py:225
  118.0 5.4 %collective-permute-start.37 = (bf16[64,2048]{1,0:T(8,128)(2,1)S(1)}, bf16[64,2048]{1,0:T(8,128)(2,1)S(1)}, u32[]{:S(2)}, u32[]{:S(2)}) collective-permute-start(bf16[64,2048]{1,0:T(8,128)(2,1)S(1)} %get-tuple-element.193), channel_id=1, source_target_pairs={{0,1},{1,0},{2,3},{3,2},{4,5},{5,4},{6,7},{7,6},{8,9},{9,8},{10,11... | collective-permute-start | bytes 786440 | tf_op jit(solution)/shard_map/ppermute | solution.py:222
  122.7 11.7 %collective-permute-start.38 = (bf16[64,2048]{1,0:T(8,128)(2,1)S(1)}, bf16[64,2048]{1,0:T(8,128)(2,1)S(1)}, u32[]{:S(2)}, u32[]{:S(2)}) collective-permute-start(bf16[64,2048]{1,0:T(8,128)(2,1)S(1)} %get-tuple-element.197), channel_id=1, source_target_pairs={{0,12},{1,13},{2,14},{3,15},{4,8},{5,9},{6,10},{7,11},{8,4},{9,5},... | collective-permute-start | bytes 786440 | tf_op jit(solution)/shard_map/ppermute | solution.py:222
  123.5 11.0 %collective-permute-start.39 = (bf16[64,2048]{1,0:T(8,128)(2,1)S(1)}, bf16[64,2048]{1,0:T(8,128)(2,1)S(1)}, u32[]{:S(2)}, u32[]{:S(2)}) collective-permute-start(bf16[64,2048]{1,0:T(8,128)(2,1)S(1)} %get-tuple-element.198), channel_id=1, source_target_pairs={{0,2},{1,3},{2,0},{3,1},{4,6},{5,7},{6,4},{7,5},{8,10},{9,11},{10,... | collective-permute-start | bytes 786440 | tf_op jit(solution)/shard_map/ppermute | solution.py:222
  (17 other events, 44.0 us)

commit v7 on v6

--- a/solution.py
+++ b/solution.py
@@ -67,12 +67,11 @@
 
 LANES = 128
 VMEM_LIMIT = 10 * 1024 * 1024
-COST = 8_000_000_000
 TOKEN = jax.ShapeDtypeStruct((8, LANES), jnp.float32)
 HERE = pl.BlockSpec(memory_space=pltpu.VMEM)
 
 
-def call(kernel, inputs, outputs, after, scratch=(), relays=(), cost=0):
+def call(kernel, inputs, outputs, after, scratch=(), relays=()):
     inputs = [v if isinstance(v, tuple) else (v, HERE) for v in inputs]
     flat = [value for group in relays for value in group]
     joined = [
@@ -105,7 +104,7 @@
         out_shape=list(outputs) + joined + [TOKEN],
         scratch_shapes=list(scratch),
         compiler_params=pltpu.CompilerParams(vmem_limit_bytes=VMEM_LIMIT),
-        cost_estimate=pl.CostEstimate(flops=cost, bytes_accessed=1, transcendentals=0),
+        cost_estimate=pl.CostEstimate(flops=8_000_000_000, bytes_accessed=1, transcendentals=0),
     )(*[value for value, _ in inputs], *flat, *after)
     return results[:-1], results[-1]
 
@@ -227,12 +226,10 @@
     def array(shape, dtype=jnp.bfloat16):
         return jax.ShapeDtypeStruct(shape, dtype)
 
-    tail, cost = [jnp.zeros(TOKEN.shape, TOKEN.dtype)], [COST]
+    tail = [jnp.zeros(TOKEN.shape, TOKEN.dtype)]
 
     def step(kernel, inputs, outputs, scratch=(), relays=()):
-        results, token = call(
-            kernel, inputs, outputs, list(tail), scratch, relays, cost[0]
-        )
+        results, token = call(kernel, inputs, outputs, list(tail), scratch, relays)
         tail[:] = [token]
         return results
 
@@ -301,15 +298,11 @@
         [tokens, expert_ids.T, gate_weights.T],
         [array((rows, width + LANES))],
     )
-    b1, z4 = swap(labelled, 1), swap(labelled, 4)
+    b1, z4, z8 = swap(labelled, 1), swap(labelled, 4), swap(labelled, 8)
     p0 = [labelled, b1]
-    (again,) = relay([labelled])
-    z8 = swap(again, 8)
     (sent,) = partials(p0)
     y0 = cross(sent)
-    cost[0] = 1
     meet()
-    cost[0] = COST
     (b4,) = relay([z4])
     b5, x6 = swap(b4, 1), swap(b4, 2)
     gap()
@@ -317,9 +310,9 @@
     p1 = [b4, b5]
     (sent,) = partials(p1)
     y1 = cross(sent)
-    note3 = swap(tail[0], 1)
+    note = swap(tail[0], 1)
     (h0,) = hidden(p0, y0)
-    tail.append(note3)
+    tail.append(note)
     (b6,) = relay([x6])
     b7 = swap(b6, 1)
     (b8,) = relay([z8])
@@ -375,7 +368,6 @@
     kept8, sent = add([c8, c9], (whole, wide), ([(0, rows), (1, rows)], one))
     x10 = swap(sent, 2)
     c12, c13 = outputs(p4, h4, t4, 0, 2 * rows)
-    note2 = swap(tail[0], 1)
     (total,) = add([total, s6], (whole, wide))
     (h5a,) = hidden([b3], y5a)
     t5a = cross(h5a)
@@ -388,7 +380,6 @@
     t5 = cross(h5)
     (sent,) = add([kept12, x14], (whole, one))
     s12 = swap(sent, 12)
-    tail.append(note2)
     c2, _ = outputs([b2], h5, t5, 0, rows)
     gap()
     (sent,) = add([c2, c3], (whole, one))

time: 135 us -> 135 us (level)
    ppermute x29 -> x28, starting transfers between devices: 17.9 us -> 17.4 us  [swap(): return lax.ppermute(value, 'expert', [(i, i ^ r) for i in range(sources)])]
    unnamed x18 -> x14, local copies, waits for them, and re-layouts: 5.27 us -> 5.2 us
    pallas_call x54 -> x53, Pallas kernels: 39.2 us -> 39.1 us  [call(): pl.pallas_call(run, in_specs=[spec for _, spec in inputs] + [HERE] * len(...]
    ppermute x29 -> x28, waiting for transfers between devices: 27.6 us -> 27.7 us  [swap(): return lax.ppermute(value, 'expert', [(i, i ^ r) for i in range(sources)])]
  transfers between devices with their start and end apart: 40 -> 39, of which waited for: 18 -> 18; matrix products, arithmetic and copies ran while one was open for 0% -> 0% of each run, Pallas kernels for 28% -> 28%
where the time goes in v7:
time: 135 us
  waiting for transfers between devices  57.9 us (43%)
  Pallas kernels  39.1 us (29%)
  starting transfers between devices  32.4 us (24%)
  local copies, waits for them, and re-layouts  5.2 us (4%)
    pallas_call x53, Pallas kernels, call(): pl.pallas_call(run, in_specs=[spec for _, spec in inputs] + [HERE] * len(...  39.1 us
    ppermute x11, waiting for transfers between devices, cross(): return lax.ppermute(value, 'dp', [(0, 1), (1, 0)])  30.2 us
    ppermute x28, waiting for transfers between devices, swap(): return lax.ppermute(value, 'expert', [(i, i ^ r) for i in range(sources)])  27.7 us
    ppermute x28, starting transfers between devices, swap(): return lax.ppermute(value, 'expert', [(i, i ^ r) for i in range(sources)])  17.4 us
    ppermute x11, starting transfers between devices, cross(): return lax.ppermute(value, 'dp', [(0, 1), (1, 0)])  15 us
    unnamed x14, local copies, waits for them, and re-layouts  5.2 us
  transfers between devices with their start and end apart: 39, of which 18 were waited for; matrix products, arithmetic and copies ran while one was open for 0% of the time, Pallas kernels for 28%

profile of v7, /device:TPU:8, one launch (start us, length us, event | category | flops | bytes accessed | tf_op | source)
XLA Modules:
  0.0 135.2 jit_solution(12439467861972068206)
XLA Ops:
  5.1 1.8 %copy-done.1 = bf16[1,2048,1536]{2,1,0:T(8,128)(2,1)S(1)} copy-done((bf16[1,2048,1536]{2,1,0:T(8,128)(2,1)S(1)}, bf16[1,2048,1536]{2,1,0:T(8,128)(2,1)}, u32[]{:S(2)}) %copy-start.1) | copy-done | bytes 6291480
  8.4 2.7 %collective-permute-start.8 = (bf16[64,2176]{1,0:T(8,128)(2,1)S(1)}, bf16[64,2176]{1,0:T(8,128)(2,1)S(1)}, u32[]{:S(2)}, u32[]{:S(2)}) collective-permute-start(bf16[64,2176]{1,0:T(8,128)(2,1)S(1)} %get-tuple-element.101.refs_0_), channel_id=1, source_target_pairs={{0,8},{1,9},{2,10},{3,11},{4,12},{5,13},{6,14},{7,15},{8,0},{9,1},... | collective-permute-start | bytes 835592 | tf_op jit(solution)/shard_map/ppermute | solution.py:221
  16.4 6.6 %collective-permute-done.1.refs_4_ = bf16[256,768]{1,0:T(8,128)(2,1)S(1)} collective-permute-done((bf16[256,768]{1,0:T(8,128)(2,1)S(1)}, bf16[256,768]{1,0:T(8,128)(2,1)S(1)}, u32[]{:S(2)}, u32[]{:S(2)}) %collective-permute-start.1) | collective-permute-done | bytes 393248 | tf_op jit(solution)/shard_map/ppermute | solution.py:224
  27.7 1.6 %collective-permute-start.9 = (bf16[384,768]{1,0:T(8,128)(2,1)S(1)}, bf16[384,768]{1,0:T(8,128)(2,1)S(1)}, u32[]{:S(2)}, u32[]{:S(2)}) collective-permute-start(bf16[384,768]{1,0:T(8,128)(2,1)S(1)} %get-tuple-element.113), channel_id=1, source_target_pairs={{0,16},{16,0},{1,17},{17,1},{2,18},{18,2},{3,19},{19,3},{4,20},{20... | collective-permute-start | bytes 1769480 | tf_op jit(solution)/shard_map/ppermute | solution.py:224
  34.1 1.9 %collective-permute-done.12.refs_1_ = bf16[128,2176]{1,0:T(8,128)(2,1)S(1)} collective-permute-done((bf16[128,2176]{1,0:T(8,128)(2,1)S(1)}, bf16[128,2176]{1,0:T(8,128)(2,1)S(1)}, u32[]{:S(2)}, u32[]{:S(2)}) %collective-permute-start.12) | collective-permute-done | bytes 557088 | tf_op jit(solution)/shard_map/ppermute | solution.py:221
  35.9 2.2 %shard_map.78 = (bf16[640,768]{1,0:T(8,128)(2,1)S(1)}, f32[8,128]{1,0:T(8,128)S(1)}) custom-call(bf16[128,2176]{1,0:T(8,128)(2,1)S(1)} %get-tuple-element.119.refs_0_, bf16[128,2176]{1,0:T(8,128)(2,1)S(1)} %collective-permute-done.12.refs_1_, bf16[1,2048,1536]{2,1,0:T(8,128)(2,1)S(1)} %copy-done, bf16[1,2048,1536]{2,1,0:T(8,128)(2,1)S(1)} %copy-done.1, ...), custom_call_target="tpu_custom_call" | custom-call | flops 8000000000 | bytes 1 | tf_op jit(solution)/shard_map/pallas_call | solution.py:100
  39.8 1.6 %collective-permute-start.16 = (bf16[64,2176]{1,0:T(8,128)(2,1)S(1)}, bf16[64,2176]{1,0:T(8,128)(2,1)S(1)}, u32[]{:S(2)}, u32[]{:S(2)}) collective-permute-start(bf16[64,2176]{1,0:T(8,128)(2,1)S(1)} %get-tuple-element.132), channel_id=1, source_target_pairs={{0,2},{1,3},{2,0},{3,1},{4,6},{5,7},{6,4},{7,5},{8,10},{9,11},{10,... | collective-permute-start | bytes 835592 | tf_op jit(solution)/shard_map/ppermute | solution.py:221
  41.3 2.6 %collective-permute-done.9.refs_4_.refs_3_ = bf16[384,768]{1,0:T(8,128)(2,1)S(1)} collective-permute-done((bf16[384,768]{1,0:T(8,128)(2,1)S(1)}, bf16[384,768]{1,0:T(8,128)(2,1)S(1)}, u32[]{:S(2)}, u32[]{:S(2)}) %collective-permute-start.9) | collective-permute-done | bytes 589856 | tf_op jit(solution)/shard_map/ppermute | solution.py:224
  45.5 1.7 %shard_map.81 = (f32[64,2048]{1,0:T(8,128)S(1)}, bf16[64,2048]{1,0:T(8,128)(2,1)S(1)}, f32[8,128]{1,0:T(8,128)S(1)}) custom-call(bf16[64,2176]{1,0:T(8,128)(2,1)S(1)} %get-tuple-element.101.refs_0_, bf16[64,2176]{1,0:T(8,128)(2,1)S(1)} %collective-permute-done.refs_1_, bf16[128,768]{1,0:T(8,128)(2,1)S(1)} %get-tuple-element.108.refs_4_.refs_2_, ...), custom_call_target="tpu_custom_call" | custom-call | flops 8000000000 | bytes 1 | tf_op jit(solution)/shard_map/pallas_call | solution.py:100
  47.3 1.7 %collective-permute-done.14.refs_0_ = bf16[64,2176]{1,0:T(8,128)(2,1)S(1)} collective-permute-done((bf16[64,2176]{1,0:T(8,128)(2,1)S(1)}, bf16[64,2176]{1,0:T(8,128)(2,1)S(1)}, u32[]{:S(2)}, u32[]{:S(2)}) %collective-permute-start.14) | collective-permute-done | bytes 278560 | tf_op jit(solution)/shard_map/ppermute | solution.py:221
  50.6 6.7 %collective-permute-done.17.refs_1_ = bf16[64,2176]{1,0:T(8,128)(2,1)S(1)} collective-permute-done((bf16[64,2176]{1,0:T(8,128)(2,1)S(1)}, bf16[64,2176]{1,0:T(8,128)(2,1)S(1)}, u32[]{:S(2)}, u32[]{:S(2)}) %collective-permute-start.17) | collective-permute-done | bytes 278560 | tf_op jit(solution)/shard_map/ppermute | solution.py:221
  57.5 1.9 %collective-permute-done.18.refs_1_ = bf16[128,2176]{1,0:T(8,128)(2,1)S(1)} collective-permute-done((bf16[128,2176]{1,0:T(8,128)(2,1)S(1)}, bf16[128,2176]{1,0:T(8,128)(2,1)S(1)}, u32[]{:S(2)}, u32[]{:S(2)}) %collective-permute-start.18) | collective-permute-done | bytes 557088 | tf_op jit(solution)/shard_map/ppermute | solution.py:221
  59.4 2.2 %shard_map.86 = (bf16[640,768]{1,0:T(8,128)(2,1)S(1)}, f32[8,128]{1,0:T(8,128)S(1)}) custom-call(bf16[128,2176]{1,0:T(8,128)(2,1)S(1)} %get-tuple-element.135.refs_0_, bf16[128,2176]{1,0:T(8,128)(2,1)S(1)} %collective-permute-done.18.refs_1_, bf16[1,2048,1536]{2,1,0:T(8,128)(2,1)S(1)} %copy-done, bf16[1,2048,1536]{2,1,0:T(8,128)(2,1)S(1)} %copy-done.1, ...), custom_call_target="tpu_custom_call" | custom-call | flops 8000000000 | bytes 1 | tf_op jit(solution)/shard_map/pallas_call | solution.py:100
  64.4 2.3 %shard_map.88 = (bf16[256,768]{1,0:T(8,128)(2,1)S(1)}, f32[8,128]{1,0:T(8,128)S(1)}) custom-call(bf16[128,2176]{1,0:T(8,128)(2,1)S(1)} %get-tuple-element.119.refs_0_, bf16[128,2176]{1,0:T(8,128)(2,1)S(1)} %collective-permute-done.12.refs_1_, bf16[1,2048,1536]{2,1,0:T(8,128)(2,1)S(1)} %copy-done, bf16[1,2048,1536]{2,1,0:T(8,128)(2,1)S(1)} %copy-done.1, ...), custom_call_target="tpu_custom_call" | custom-call | flops 8000000000 | bytes 1 | tf_op jit(solution)/shard_map/pallas_call | solution.py:100
  66.8 1.7 %shard_map.89 = (f32[64,2048]{1,0:T(8,128)S(1)}, bf16[64,2048]{1,0:T(8,128)(2,1)S(1)}, f32[8,128]{1,0:T(8,128)S(1)}) custom-call(bf16[64,2176]{1,0:T(8,128)(2,1)S(1)} %get-tuple-element.105.refs_0_, bf16[64,2176]{1,0:T(8,128)(2,1)S(1)} %collective-permute-done.4.refs_1_, bf16[128,768]{1,0:T(8,128)(2,1)S(1)} %get-tuple-element.120.refs_4_.refs_2_, ...), custom_call_target="tpu_custom_call" | custom-call | flops 8000000000 | bytes 1 | tf_op jit(solution)/shard_map/pallas_call | solution.py:100
  68.6 1.6 %collective-permute-start.26 = (bf16[256,768]{1,0:T(8,128)(2,1)S(1)}, bf16[256,768]{1,0:T(8,128)(2,1)S(1)}, u32[]{:S(2)}, u32[]{:S(2)}) collective-permute-start(bf16[256,768]{1,0:T(8,128)(2,1)S(1)} %get-tuple-element.162.refs_2_), channel_id=1, source_target_pairs={{0,16},{16,0},{1,17},{17,1},{2,18},{18,2},{3,19},{19,3},{4,20},{20... | collective-permute-start | bytes 1179656 | tf_op jit(solution)/shard_map/ppermute | solution.py:224
  74.3 12.0 %collective-permute-done.21.refs_4_.refs_3_ = bf16[640,768]{1,0:T(8,128)(2,1)S(1)} collective-permute-done((bf16[640,768]{1,0:T(8,128)(2,1)S(1)}, bf16[640,768]{1,0:T(8,128)(2,1)S(1)}, u32[]{:S(2)}, u32[]{:S(2)}) %collective-permute-start.21) | collective-permute-done | bytes 983072 | tf_op jit(solution)/shard_map/ppermute | solution.py:224
  86.3 2.3 %shard_map.94 = (bf16[256,768]{1,0:T(8,128)(2,1)S(1)}, f32[8,128]{1,0:T(8,128)S(1)}) custom-call(bf16[128,2176]{1,0:T(8,128)(2,1)S(1)} %get-tuple-element.135.refs_0_, bf16[128,2176]{1,0:T(8,128)(2,1)S(1)} %collective-permute-done.18.refs_1_, bf16[1,2048,1536]{2,1,0:T(8,128)(2,1)S(1)} %copy-done, bf16[1,2048,1536]{2,1,0:T(8,128)(2,1)S(1)} %copy-done.1, ...), custom_call_target="tpu_custom_call" | custom-call | flops 8000000000 | bytes 1 | tf_op jit(solution)/shard_map/pallas_call | solution.py:100
  88.7 1.7 %shard_map.97 = (f32[64,2048]{1,0:T(8,128)S(1)}, bf16[64,2048]{1,0:T(8,128)(2,1)S(1)}, f32[8,128]{1,0:T(8,128)S(1)}) custom-call(bf16[64,2176]{1,0:T(8,128)(2,1)S(1)} %get-tuple-element.110.refs_0_, bf16[64,2176]{1,0:T(8,128)(2,1)S(1)} %collective-permute-done.7.refs_1_, bf16[128,768]{1,0:T(8,128)(2,1)S(1)} %get-tuple-element.136.refs_4_.refs_2_, ...), custom_call_target="tpu_custom_call" | custom-call | flops 8000000000 | bytes 1 | tf_op jit(solution)/shard_map/pallas_call | solution.py:100
  90.6 1.6 %collective-permute-start.25 = (bf16[256,768]{1,0:T(8,128)(2,1)S(1)}, bf16[256,768]{1,0:T(8,128)(2,1)S(1)}, u32[]{:S(2)}, u32[]{:S(2)}) collective-permute-start(bf16[256,768]{1,0:T(8,128)(2,1)S(1)} %get-tuple-element.161.refs_2_), channel_id=1, source_target_pairs={{0,16},{16,0},{1,17},{17,1},{2,18},{18,2},{3,19},{19,3},{4,20},{20... | collective-permute-start | bytes 1179656 | tf_op jit(solution)/shard_map/ppermute | solution.py:224
  95.4 2.4 %shard_map.101 = (f32[128,2048]{1,0:T(8,128)S(1)}, bf16[128,2048]{1,0:T(8,128)(2,1)S(1)}, f32[8,128]{1,0:T(8,128)S(1)}) custom-call(bf16[128,2176]{1,0:T(8,128)(2,1)S(1)} %get-tuple-element.119.refs_0_, bf16[128,2176]{1,0:T(8,128)(2,1)S(1)} %collective-permute-done.12.refs_1_, bf16[256,768]{1,0:T(8,128)(2,1)S(1)} %get-tuple-element.162.refs_2_, ...), custom_call_target="tpu_custom_call" | custom-call | flops 8000000000 | bytes 1 | tf_op jit(solution)/shard_map/pallas_call | solution.py:100
  98.0 1.9 %collective-permute-done.27.refs_1_ = bf16[128,2048]{1,0:T(8,128)(2,1)S(1)} collective-permute-done((bf16[128,2048]{1,0:T(8,128)(2,1)S(1)}, bf16[128,2048]{1,0:T(8,128)(2,1)S(1)}, u32[]{:S(2)}, u32[]{:S(2)}) %collective-permute-start.27) | collective-permute-done | bytes 524320 | tf_op jit(solution)/shard_map/ppermute | solution.py:221
  100.6 2.0 %collective-permute-done.25.refs_3_ = bf16[256,768]{1,0:T(8,128)(2,1)S(1)} collective-permute-done((bf16[256,768]{1,0:T(8,128)(2,1)S(1)}, bf16[256,768]{1,0:T(8,128)(2,1)S(1)}, u32[]{:S(2)}, u32[]{:S(2)}) %collective-permute-start.25) | collective-permute-done | bytes 393248 | tf_op jit(solution)/shard_map/ppermute | solution.py:224
  102.6 2.5 %shard_map.104 = (f32[128,2048]{1,0:T(8,128)S(1)}, bf16[128,2048]{1,0:T(8,128)(2,1)S(1)}, f32[8,128]{1,0:T(8,128)S(1)}) custom-call(bf16[128,2176]{1,0:T(8,128)(2,1)S(1)} %get-tuple-element.135.refs_0_, bf16[128,2176]{1,0:T(8,128)(2,1)S(1)} %collective-permute-done.18.refs_1_, bf16[256,768]{1,0:T(8,128)(2,1)S(1)} %get-tuple-element.161.refs_2_, ...), custom_call_target="tpu_custom_call" | custom-call | flops 8000000000 | bytes 1 | tf_op jit(solution)/shard_map/pallas_call | solution.py:100
  105.2 1.6 %collective-permute-done.30.refs_3_ = bf16[128,768]{1,0:T(8,128)(2,1)S(1)} collective-permute-done((bf16[128,768]{1,0:T(8,128)(2,1)S(1)}, bf16[128,768]{1,0:T(8,128)(2,1)S(1)}, u32[]{:S(2)}, u32[]{:S(2)}) %collective-permute-start.30) | collective-permute-done | bytes 196640 | tf_op jit(solution)/shard_map/ppermute | solution.py:224
  108.4 1.6 %collective-permute-start.33 = (bf16[64,768]{1,0:T(8,128)(2,1)S(1)}, bf16[64,768]{1,0:T(8,128)(2,1)S(1)}, u32[]{:S(2)}, u32[]{:S(2)}) collective-permute-start(bf16[64,768]{1,0:T(8,128)(2,1)S(1)} %get-tuple-element.180.refs_1_), channel_id=1, source_target_pairs={{0,16},{16,0},{1,17},{17,1},{2,18},{18,2},{3,19},{19,3},{4,20},{20... | collective-permute-start | bytes 294920 | tf_op jit(solution)/shard_map/ppermute | solution.py:224
  110.1 1.8 %collective-permute-start.31 = (bf16[64,2048]{1,0:T(8,128)(2,1)S(1)}, bf16[64,2048]{1,0:T(8,128)(2,1)S(1)}, u32[]{:S(2)}, u32[]{:S(2)}) collective-permute-start(bf16[64,2048]{1,0:T(8,128)(2,1)S(1)} %get-tuple-element.178), channel_id=1, source_target_pairs={{0,8},{1,9},{2,10},{3,11},{4,12},{5,13},{6,14},{7,15},{8,0},{9,1},... | collective-permute-start | bytes 786440 | tf_op jit(solution)/shard_map/ppermute | solution.py:221
  113.1 1.7 %shard_map.109 = (bf16[64,2048]{1,0:T(8,128)(2,1)S(1)}, f32[8,128]{1,0:T(8,128)S(1)}) custom-call(bf16[64,2176]{1,0:T(8,128)(2,1)S(1)} %collective-permute-done.22.refs_0_, bf16[64,768]{1,0:T(8,128)(2,1)S(1)} %get-tuple-element.180.refs_1_, bf16[64,768]{1,0:T(8,128)(2,1)S(1)} %collective-permute-done.33.refs_2_, bf16[1,1536,2048]{2,1,0:T(8,128)(2,1)S(1)} %bitcast.3, ...), custom_call_target="tpu_custom_call" | custom-call | flops 8000000000 | bytes 1 | tf_op jit(solution)/shard_map/pallas_call | solution.py:100
  116.3 1.6 %collective-permute-start.34 = (bf16[64,768]{1,0:T(8,128)(2,1)S(1)}, bf16[64,768]{1,0:T(8,128)(2,1)S(1)}, u32[]{:S(2)}, u32[]{:S(2)}) collective-permute-start(bf16[64,768]{1,0:T(8,128)(2,1)S(1)} %get-tuple-element.183.refs_1_), channel_id=1, source_target_pairs={{0,16},{16,0},{1,17},{17,1},{2,18},{18,2},{3,19},{19,3},{4,20},{20... | collective-permute-start | bytes 294920 | tf_op jit(solution)/shard_map/ppermute | solution.py:224
  118.9 2.0 %collective-permute-done.34.refs_2_ = bf16[64,768]{1,0:T(8,128)(2,1)S(1)} collective-permute-done((bf16[64,768]{1,0:T(8,128)(2,1)S(1)}, bf16[64,768]{1,0:T(8,128)(2,1)S(1)}, u32[]{:S(2)}, u32[]{:S(2)}) %collective-permute-start.34) | collective-permute-done | bytes 98336 | tf_op jit(solution)/shard_map/ppermute | solution.py:224
  121.0 1.7 %shard_map.112 = (f32[64,2048]{1,0:T(8,128)S(1)}, f32[8,128]{1,0:T(8,128)S(1)}) custom-call(bf16[64,2176]{1,0:T(8,128)(2,1)S(1)} %get-tuple-element.146.refs_0_, bf16[64,768]{1,0:T(8,128)(2,1)S(1)} %get-tuple-element.183.refs_1_, bf16[64,768]{1,0:T(8,128)(2,1)S(1)} %collective-permute-done.34.refs_2_, bf16[1,1536,2048]{2,1,0:T(8,128)(2,1)S(1)} %bitcast.3, ...), custom_call_target="tpu_custom_call" | custom-call | flops 8000000000 | bytes 1 | tf_op jit(solution)/shard_map/pallas_call | solution.py:100
  124.8 9.6 %collective-permute-done.37.refs_1_ = bf16[64,2048]{1,0:T(8,128)(2,1)S(1)} collective-permute-done((bf16[64,2048]{1,0:T(8,128)(2,1)S(1)}, bf16[64,2048]{1,0:T(8,128)(2,1)S(1)}, u32[]{:S(2)}, u32[]{:S(2)}) %collective-permute-start.37) | collective-permute-done | bytes 262176 | tf_op jit(solution)/shard_map/ppermute | solution.py:221
  (115 shorter events, 45.8 us)
Async XLA Ops:
  2.5 10.1 %collective-permute-start.2 = (bf16[64,2176]{1,0:T(8,128)(2,1)S(1)}, bf16[64,2176]{1,0:T(8,128)(2,1)S(1)}, u32[]{:S(2)}, u32[]{:S(2)}) collective-permute-start(bf16[64,2176]{1,0:T(8,128)(2,1)S(1)} %get-tuple-element.101.refs_0_), channel_id=1, source_target_pairs={{0,4},{1,5},{2,6},{3,7},{4,0},{5,1},{6,2},{7,3},{8,12},{9,13},{10,... | collective-permute-start | bytes 835592 | tf_op jit(solution)/shard_map/ppermute | solution.py:221
  8.4 4.2 %collective-permute-start.3 = (f32[8,128]{1,0:T(8,128)S(1)}, f32[8,128]{1,0:T(8,128)S(1)}, u32[]{:S(2)}, u32[]{:S(2)}) collective-permute-start(f32[8,128]{1,0:T(8,128)S(1)} %get-tuple-element.104.refs_1_), channel_id=1, source_target_pairs={{0,1},{1,0},{2,3},{3,2},{4,5},{5,4},{6,7},{7,6},{8,9},{9,8},{10,11... | collective-permute-start | bytes 12296 | tf_op jit(solution)/shard_map/ppermute | solution.py:221
  8.4 16.3 %collective-permute-start.8 = (bf16[64,2176]{1,0:T(8,128)(2,1)S(1)}, bf16[64,2176]{1,0:T(8,128)(2,1)S(1)}, u32[]{:S(2)}, u32[]{:S(2)}) collective-permute-start(bf16[64,2176]{1,0:T(8,128)(2,1)S(1)} %get-tuple-element.101.refs_0_), channel_id=1, source_target_pairs={{0,8},{1,9},{2,10},{3,11},{4,12},{5,13},{6,14},{7,15},{8,0},{9,1},... | collective-permute-start | bytes 835592 | tf_op jit(solution)/shard_map/ppermute | solution.py:221
  11.1 12.0 %collective-permute-start.1 = (bf16[256,768]{1,0:T(8,128)(2,1)S(1)}, bf16[256,768]{1,0:T(8,128)(2,1)S(1)}, u32[]{:S(2)}, u32[]{:S(2)}) collective-permute-start(bf16[256,768]{1,0:T(8,128)(2,1)S(1)} %get-tuple-element.103), channel_id=1, source_target_pairs={{0,16},{16,0},{1,17},{17,1},{2,18},{18,2},{3,19},{19,3},{4,20},{20... | collective-permute-start | bytes 1179656 | tf_op jit(solution)/shard_map/ppermute | solution.py:224
  12.7 11.9 %collective-permute-start.5 = (bf16[64,2176]{1,0:T(8,128)(2,1)S(1)}, bf16[64,2176]{1,0:T(8,128)(2,1)S(1)}, u32[]{:S(2)}, u32[]{:S(2)}) collective-permute-start(bf16[64,2176]{1,0:T(8,128)(2,1)S(1)} %get-tuple-element.105.refs_0_), channel_id=1, source_target_pairs={{0,2},{1,3},{2,0},{3,1},{4,6},{5,7},{6,4},{7,5},{8,10},{9,11},{10,... | collective-permute-start | bytes 835592 | tf_op jit(solution)/shard_map/ppermute | solution.py:221
  15.7 8.9 %collective-permute-start.6 = (f32[8,128]{1,0:T(8,128)S(1)}, f32[8,128]{1,0:T(8,128)S(1)}, u32[]{:S(2)}, u32[]{:S(2)}) collective-permute-start(f32[8,128]{1,0:T(8,128)S(1)} %get-tuple-element.107.refs_5_), channel_id=1, source_target_pairs={{0,1},{1,0},{2,3},{3,2},{4,5},{5,4},{6,7},{7,6},{8,9},{9,8},{10,11... | collective-permute-start | bytes 12296 | tf_op jit(solution)/shard_map/ppermute | solution.py:221
  15.9 14.8 %collective-permute-start.11 = (bf16[256,768]{1,0:T(8,128)(2,1)S(1)}, bf16[256,768]{1,0:T(8,128)(2,1)S(1)}, u32[]{:S(2)}, u32[]{:S(2)}) collective-permute-start(bf16[256,768]{1,0:T(8,128)(2,1)S(1)} %get-tuple-element.115), channel_id=1, source_target_pairs={{0,16},{16,0},{1,17},{17,1},{2,18},{18,2},{3,19},{19,3},{4,20},{20... | collective-permute-start | bytes 1179656 | tf_op jit(solution)/shard_map/ppermute | solution.py:224
  24.7 9.1 %collective-permute-start.10 = (bf16[64,2176]{1,0:T(8,128)(2,1)S(1)}, bf16[64,2176]{1,0:T(8,128)(2,1)S(1)}, u32[]{:S(2)}, u32[]{:S(2)}) collective-permute-start(bf16[64,2176]{1,0:T(8,128)(2,1)S(1)} %get-tuple-element.114.refs_0_), channel_id=1, source_target_pairs={{0,2},{1,3},{2,0},{3,1},{4,6},{5,7},{6,4},{7,5},{8,10},{9,11},{10,... | collective-permute-start | bytes 835592 | tf_op jit(solution)/shard_map/ppermute | solution.py:221
  27.7 16.2 %collective-permute-start.9 = (bf16[384,768]{1,0:T(8,128)(2,1)S(1)}, bf16[384,768]{1,0:T(8,128)(2,1)S(1)}, u32[]{:S(2)}, u32[]{:S(2)}) collective-permute-start(bf16[384,768]{1,0:T(8,128)(2,1)S(1)} %get-tuple-element.113), channel_id=1, source_target_pairs={{0,16},{16,0},{1,17},{17,1},{2,18},{18,2},{3,19},{19,3},{4,20},{20... | collective-permute-start | bytes 1769480 | tf_op jit(solution)/shard_map/ppermute | solution.py:224
  34.0 15.0 %collective-permute-start.14 = (bf16[64,2176]{1,0:T(8,128)(2,1)S(1)}, bf16[64,2176]{1,0:T(8,128)(2,1)S(1)}, u32[]{:S(2)}, u32[]{:S(2)}) collective-permute-start(bf16[64,2176]{1,0:T(8,128)(2,1)S(1)} %get-tuple-element.127), channel_id=1, source_target_pairs={{0,12},{1,13},{2,14},{3,15},{4,8},{5,9},{6,10},{7,11},{8,4},{9,5},... | collective-permute-start | bytes 835592 | tf_op jit(solution)/shard_map/ppermute | solution.py:221
  38.2 26.3 %collective-permute-start.15 = (bf16[640,768]{1,0:T(8,128)(2,1)S(1)}, bf16[640,768]{1,0:T(8,128)(2,1)S(1)}, u32[]{:S(2)}, u32[]{:S(2)}) collective-permute-start(bf16[640,768]{1,0:T(8,128)(2,1)S(1)} %get-tuple-element.131), channel_id=1, source_target_pairs={{0,16},{16,0},{1,17},{17,1},{2,18},{18,2},{3,19},{19,3},{4,20},{20... | collective-permute-start | bytes 2949128 | tf_op jit(solution)/shard_map/ppermute | solution.py:224
  39.8 23.4 %collective-permute-start.16 = (bf16[64,2176]{1,0:T(8,128)(2,1)S(1)}, bf16[64,2176]{1,0:T(8,128)(2,1)S(1)}, u32[]{:S(2)}, u32[]{:S(2)}) collective-permute-start(bf16[64,2176]{1,0:T(8,128)(2,1)S(1)} %get-tuple-element.132), channel_id=1, source_target_pairs={{0,2},{1,3},{2,0},{3,1},{4,6},{5,7},{6,4},{7,5},{8,10},{9,11},{10,... | collective-permute-start | bytes 835592 | tf_op jit(solution)/shard_map/ppermute | solution.py:221
  47.2 3.4 %collective-permute-start.13 = (bf16[64,2048]{1,0:T(8,128)(2,1)S(1)}, bf16[64,2048]{1,0:T(8,128)(2,1)S(1)}, u32[]{:S(2)}, u32[]{:S(2)}) collective-permute-start(bf16[64,2048]{1,0:T(8,128)(2,1)S(1)} %get-tuple-element.126), channel_id=1, source_target_pairs={{0,1},{1,0},{2,3},{3,2},{4,5},{5,4},{6,7},{7,6},{8,9},{9,8},{10,11... | collective-permute-start | bytes 786440 | tf_op jit(solution)/shard_map/ppermute | solution.py:221
  49.0 8.3 %collective-permute-start.17 = (bf16[64,2176]{1,0:T(8,128)(2,1)S(1)}, bf16[64,2176]{1,0:T(8,128)(2,1)S(1)}, u32[]{:S(2)}, u32[]{:S(2)}) collective-permute-start(bf16[64,2176]{1,0:T(8,128)(2,1)S(1)} %get-tuple-element.133.refs_0_), channel_id=1, source_target_pairs={{0,2},{1,3},{2,0},{3,1},{4,6},{5,7},{6,4},{7,5},{8,10},{9,11},{10,... | collective-permute-start | bytes 835592 | tf_op jit(solution)/shard_map/ppermute | solution.py:221
  61.6 24.7 %collective-permute-start.21 = (bf16[640,768]{1,0:T(8,128)(2,1)S(1)}, bf16[640,768]{1,0:T(8,128)(2,1)S(1)}, u32[]{:S(2)}, u32[]{:S(2)}) collective-permute-start(bf16[640,768]{1,0:T(8,128)(2,1)S(1)} %get-tuple-element.145), channel_id=1, source_target_pairs={{0,16},{16,0},{1,17},{17,1},{2,18},{18,2},{3,19},{19,3},{4,20},{20... | collective-permute-start | bytes 2949128 | tf_op jit(solution)/shard_map/ppermute | solution.py:224
  63.2 8.1 %collective-permute-start.22 = (bf16[64,2176]{1,0:T(8,128)(2,1)S(1)}, bf16[64,2176]{1,0:T(8,128)(2,1)S(1)}, u32[]{:S(2)}, u32[]{:S(2)}) collective-permute-start(bf16[64,2176]{1,0:T(8,128)(2,1)S(1)} %get-tuple-element.146.refs_0_), channel_id=1, source_target_pairs={{0,1},{1,0},{2,3},{3,2},{4,5},{5,4},{6,7},{7,6},{8,9},{9,8},{10,11... | collective-permute-start | bytes 835592 | tf_op jit(solution)/shard_map/ppermute | solution.py:221
  68.6 26.9 %collective-permute-start.26 = (bf16[256,768]{1,0:T(8,128)(2,1)S(1)}, bf16[256,768]{1,0:T(8,128)(2,1)S(1)}, u32[]{:S(2)}, u32[]{:S(2)}) collective-permute-start(bf16[256,768]{1,0:T(8,128)(2,1)S(1)} %get-tuple-element.162.refs_2_), channel_id=1, source_target_pairs={{0,16},{16,0},{1,17},{17,1},{2,18},{18,2},{3,19},{19,3},{4,20},{20... | collective-permute-start | bytes 1179656 | tf_op jit(solution)/shard_map/ppermute | solution.py:224
  70.2 20.3 %collective-permute-start.20 = (bf16[64,2048]{1,0:T(8,128)(2,1)S(1)}, bf16[64,2048]{1,0:T(8,128)(2,1)S(1)}, u32[]{:S(2)}, u32[]{:S(2)}) collective-permute-start(bf16[64,2048]{1,0:T(8,128)(2,1)S(1)} %get-tuple-element.144), channel_id=1, source_target_pairs={{0,4},{1,5},{2,6},{3,7},{4,0},{5,1},{6,2},{7,3},{8,12},{9,13},{10,... | collective-permute-start | bytes 786440 | tf_op jit(solution)/shard_map/ppermute | solution.py:221
  90.4 3.8 %collective-permute-start.23 = (bf16[64,2048]{1,0:T(8,128)(2,1)S(1)}, bf16[64,2048]{1,0:T(8,128)(2,1)S(1)}, u32[]{:S(2)}, u32[]{:S(2)}) collective-permute-start(bf16[64,2048]{1,0:T(8,128)(2,1)S(1)} %get-tuple-element.158), channel_id=1, source_target_pairs={{0,1},{1,0},{2,3},{3,2},{4,5},{5,4},{6,7},{7,6},{8,9},{9,8},{10,11... | collective-permute-start | bytes 786440 | tf_op jit(solution)/shard_map/ppermute | solution.py:221
  90.6 12.1 %collective-permute-start.25 = (bf16[256,768]{1,0:T(8,128)(2,1)S(1)}, bf16[256,768]{1,0:T(8,128)(2,1)S(1)}, u32[]{:S(2)}, u32[]{:S(2)}) collective-permute-start(bf16[256,768]{1,0:T(8,128)(2,1)S(1)} %get-tuple-element.161.refs_2_), channel_id=1, source_target_pairs={{0,16},{16,0},{1,17},{17,1},{2,18},{18,2},{3,19},{19,3},{4,20},{20... | collective-permute-start | bytes 1179656 | tf_op jit(solution)/shard_map/ppermute | solution.py:224
  92.2 14.7 %collective-permute-start.30 = (bf16[128,768]{1,0:T(8,128)(2,1)S(1)}, bf16[128,768]{1,0:T(8,128)(2,1)S(1)}, u32[]{:S(2)}, u32[]{:S(2)}) collective-permute-start(bf16[128,768]{1,0:T(8,128)(2,1)S(1)} %get-tuple-element.174), channel_id=1, source_target_pairs={{0,16},{16,0},{1,17},{17,1},{2,18},{18,2},{3,19},{19,3},{4,20},{20... | collective-permute-start | bytes 589832 | tf_op jit(solution)/shard_map/ppermute | solution.py:224
  92.7 22.1 %collective-permute-start.32 = (bf16[128,768]{1,0:T(8,128)(2,1)S(1)}, bf16[128,768]{1,0:T(8,128)(2,1)S(1)}, u32[]{:S(2)}, u32[]{:S(2)}) collective-permute-start(bf16[128,768]{1,0:T(8,128)(2,1)S(1)} %get-tuple-element.179), channel_id=1, source_target_pairs={{0,16},{16,0},{1,17},{17,1},{2,18},{18,2},{3,19},{19,3},{4,20},{20... | collective-permute-start | bytes 589832 | tf_op jit(solution)/shard_map/ppermute | solution.py:224
  94.2 10.9 %collective-permute-start.24 = (bf16[64,2048]{1,0:T(8,128)(2,1)S(1)}, bf16[64,2048]{1,0:T(8,128)(2,1)S(1)}, u32[]{:S(2)}, u32[]{:S(2)}) collective-permute-start(bf16[64,2048]{1,0:T(8,128)(2,1)S(1)} %get-tuple-element.160), channel_id=1, source_target_pairs={{0,6},{1,7},{2,4},{3,5},{4,2},{5,3},{6,0},{7,1},{8,14},{9,15},{10,... | collective-permute-start | bytes 786440 | tf_op jit(solution)/shard_map/ppermute | solution.py:221
  99.9 10.1 %collective-permute-start.28 = (bf16[64,2048]{1,0:T(8,128)(2,1)S(1)}, bf16[64,2048]{1,0:T(8,128)(2,1)S(1)}, u32[]{:S(2)}, u32[]{:S(2)}) collective-permute-start(bf16[64,2048]{1,0:T(8,128)(2,1)S(1)} %get-tuple-element.171), channel_id=1, source_target_pairs={{0,2},{1,3},{2,0},{3,1},{4,6},{5,7},{6,4},{7,5},{8,10},{9,11},{10,... | collective-permute-start | bytes 786440 | tf_op jit(solution)/shard_map/ppermute | solution.py:221
  105.1 4.9 %collective-permute-start.29 = (bf16[128,2048]{1,0:T(8,128)(2,1)S(1)}, bf16[128,2048]{1,0:T(8,128)(2,1)S(1)}, u32[]{:S(2)}, u32[]{:S(2)}) collective-permute-start(bf16[128,2048]{1,0:T(8,128)(2,1)S(1)} %get-tuple-element.173), channel_id=1, source_target_pairs={{0,1},{1,0},{2,3},{3,2},{4,5},{5,4},{6,7},{7,6},{8,9},{9,8},{10,11... | collective-permute-start | bytes 1572872 | tf_op jit(solution)/shard_map/ppermute | solution.py:221
  108.4 4.7 %collective-permute-start.33 = (bf16[64,768]{1,0:T(8,128)(2,1)S(1)}, bf16[64,768]{1,0:T(8,128)(2,1)S(1)}, u32[]{:S(2)}, u32[]{:S(2)}) collective-permute-start(bf16[64,768]{1,0:T(8,128)(2,1)S(1)} %get-tuple-element.180.refs_1_), channel_id=1, source_target_pairs={{0,16},{16,0},{1,17},{17,1},{2,18},{18,2},{3,19},{19,3},{4,20},{20... | collective-permute-start | bytes 294920 | tf_op jit(solution)/shard_map/ppermute | solution.py:224
  110.1 14.6 %collective-permute-start.31 = (bf16[64,2048]{1,0:T(8,128)(2,1)S(1)}, bf16[64,2048]{1,0:T(8,128)(2,1)S(1)}, u32[]{:S(2)}, u32[]{:S(2)}) collective-permute-start(bf16[64,2048]{1,0:T(8,128)(2,1)S(1)} %get-tuple-element.178), channel_id=1, source_target_pairs={{0,8},{1,9},{2,10},{3,11},{4,12},{5,13},{6,14},{7,15},{8,0},{9,1},... | collective-permute-start | bytes 786440 | tf_op jit(solution)/shard_map/ppermute | solution.py:221
  111.9 7.0 %collective-permute-start.35 = (bf16[64,2048]{1,0:T(8,128)(2,1)S(1)}, bf16[64,2048]{1,0:T(8,128)(2,1)S(1)}, u32[]{:S(2)}, u32[]{:S(2)}) collective-permute-start(bf16[64,2048]{1,0:T(8,128)(2,1)S(1)} %get-tuple-element.185), channel_id=1, source_target_pairs={{0,2},{1,3},{2,0},{3,1},{4,6},{5,7},{6,4},{7,5},{8,10},{9,11},{10,... | collective-permute-start | bytes 786440 | tf_op jit(solution)/shard_map/ppermute | solution.py:221
  116.3 4.7 %collective-permute-start.34 = (bf16[64,768]{1,0:T(8,128)(2,1)S(1)}, bf16[64,768]{1,0:T(8,128)(2,1)S(1)}, u32[]{:S(2)}, u32[]{:S(2)}) collective-permute-start(bf16[64,768]{1,0:T(8,128)(2,1)S(1)} %get-tuple-element.183.refs_1_), channel_id=1, source_target_pairs={{0,16},{16,0},{1,17},{17,1},{2,18},{18,2},{3,19},{19,3},{4,20},{20... | collective-permute-start | bytes 294920 | tf_op jit(solution)/shard_map/ppermute | solution.py:224
  117.9 5.5 %collective-permute-start.36 = (bf16[64,2048]{1,0:T(8,128)(2,1)S(1)}, bf16[64,2048]{1,0:T(8,128)(2,1)S(1)}, u32[]{:S(2)}, u32[]{:S(2)}) collective-permute-start(bf16[64,2048]{1,0:T(8,128)(2,1)S(1)} %get-tuple-element.189), channel_id=1, source_target_pairs={{0,1},{1,0},{2,3},{3,2},{4,5},{5,4},{6,7},{7,6},{8,9},{9,8},{10,11... | collective-permute-start | bytes 786440 | tf_op jit(solution)/shard_map/ppermute | solution.py:221
  122.6 11.7 %collective-permute-start.37 = (bf16[64,2048]{1,0:T(8,128)(2,1)S(1)}, bf16[64,2048]{1,0:T(8,128)(2,1)S(1)}, u32[]{:S(2)}, u32[]{:S(2)}) collective-permute-start(bf16[64,2048]{1,0:T(8,128)(2,1)S(1)} %get-tuple-element.193), channel_id=1, source_target_pairs={{0,12},{1,13},{2,14},{3,15},{4,8},{5,9},{6,10},{7,11},{8,4},{9,5},... | collective-permute-start | bytes 786440 | tf_op jit(solution)/shard_map/ppermute | solution.py:221
  123.4 11.0 %collective-permute-start.38 = (bf16[64,2048]{1,0:T(8,128)(2,1)S(1)}, bf16[64,2048]{1,0:T(8,128)(2,1)S(1)}, u32[]{:S(2)}, u32[]{:S(2)}) collective-permute-start(bf16[64,2048]{1,0:T(8,128)(2,1)S(1)} %get-tuple-element.194), channel_id=1, source_target_pairs={{0,2},{1,3},{2,0},{3,1},{4,6},{5,7},{6,4},{7,5},{8,10},{9,11},{10,... | collective-permute-start | bytes 786440 | tf_op jit(solution)/shard_map/ppermute | solution.py:221
  (14 other events, 33.8 us)

commit v8 on v7

--- a/solution.py
+++ b/solution.py
@@ -214,8 +214,8 @@
     rows, width = tokens.shape
     sources = lax.axis_size("expert")
     half = gate_proj.shape[2] // 2
-    tile = 256 if half % 256 == 0 else half
-    out_tile = 512 if width % 512 == 0 else width
+    tile = half
+    out_tile = 1024 if width % 1024 == 0 else width
 
     def swap(value, r):
         return lax.ppermute(value, "expert", [(i, i ^ r) for i in range(sources)])

time: 135 us -> 134 us (level)
  Pallas kernels: 39.1 us -> 31.1 us
  waiting for transfers between devices: 57.9 us -> 64.6 us
    pallas_call x53, Pallas kernels: 39.1 us -> 31.1 us  [call(): pl.pallas_call(run, in_specs=[spec for _, spec in inputs] + [HERE] * len(...]
    ppermute x11, waiting for transfers between devices: 30.2 us -> 37.9 us  [cross(): return lax.ppermute(value, 'dp', [(0, 1), (1, 0)])]
  transfers between devices with their start and end apart: 39 -> 39, of which waited for: 18 -> 18; matrix products, arithmetic and copies ran while one was open for 0% -> 0% of each run, Pallas kernels for 28% -> 23%
where the time goes in v8:
time: 134 us
  waiting for transfers between devices  64.6 us (48%)
  starting transfers between devices  32.5 us (24%)
  Pallas kernels  31.1 us (23%)
  local copies, waits for them, and re-layouts  5.2 us (4%)
    ppermute x11, waiting for transfers between devices, cross(): return lax.ppermute(value, 'dp', [(0, 1), (1, 0)])  37.9 us
    pallas_call x53, Pallas kernels, call(): pl.pallas_call(run, in_specs=[spec for _, spec in inputs] + [HERE] * len(...  31.1 us
    ppermute x28, waiting for transfers between devices, swap(): return lax.ppermute(value, 'expert', [(i, i ^ r) for i in range(sources)])  26.7 us
    ppermute x28, starting transfers between devices, swap(): return lax.ppermute(value, 'expert', [(i, i ^ r) for i in range(sources)])  17.2 us
    ppermute x11, starting transfers between devices, cross(): return lax.ppermute(value, 'dp', [(0, 1), (1, 0)])  15.4 us
    unnamed x14, local copies, waits for them, and re-layouts  5.2 us
  transfers between devices with their start and end apart: 39, of which 18 were waited for; matrix products, arithmetic and copies ran while one was open for 0% of the time, Pallas kernels for 23%

profile of v8, /device:TPU:8, one launch (start us, length us, event | category | flops | bytes accessed | tf_op | source)
XLA Modules:
  0.0 134.0 jit_solution(1704917309219355783)
XLA Ops:
  5.1 1.8 %copy-done.1 = bf16[1,2048,1536]{2,1,0:T(8,128)(2,1)S(1)} copy-done((bf16[1,2048,1536]{2,1,0:T(8,128)(2,1)S(1)}, bf16[1,2048,1536]{2,1,0:T(8,128)(2,1)}, u32[]{:S(2)}) %copy-start.1) | copy-done | bytes 6291480
  8.0 2.7 %collective-permute-start.8 = (bf16[64,2176]{1,0:T(8,128)(2,1)S(1)}, bf16[64,2176]{1,0:T(8,128)(2,1)S(1)}, u32[]{:S(2)}, u32[]{:S(2)}) collective-permute-start(bf16[64,2176]{1,0:T(8,128)(2,1)S(1)} %get-tuple-element.101.refs_0_), channel_id=1, source_target_pairs={{0,8},{1,9},{2,10},{3,11},{4,12},{5,13},{6,14},{7,15},{8,0},{9,1},... | collective-permute-start | bytes 835592 | tf_op jit(solution)/shard_map/ppermute | solution.py:221
  12.3 1.6 %collective-permute-start.5 = (bf16[64,2176]{1,0:T(8,128)(2,1)S(1)}, bf16[64,2176]{1,0:T(8,128)(2,1)S(1)}, u32[]{:S(2)}, u32[]{:S(2)}) collective-permute-start(bf16[64,2176]{1,0:T(8,128)(2,1)S(1)} %get-tuple-element.105.refs_0_), channel_id=1, source_target_pairs={{0,2},{1,3},{2,0},{3,1},{4,6},{5,7},{6,4},{7,5},{8,10},{9,11},{10,... | collective-permute-start | bytes 835592 | tf_op jit(solution)/shard_map/ppermute | solution.py:221
  16.0 6.6 %collective-permute-done.1.refs_4_ = bf16[256,768]{1,0:T(8,128)(2,1)S(1)} collective-permute-done((bf16[256,768]{1,0:T(8,128)(2,1)S(1)}, bf16[256,768]{1,0:T(8,128)(2,1)S(1)}, u32[]{:S(2)}, u32[]{:S(2)}) %collective-permute-start.1) | collective-permute-done | bytes 393248 | tf_op jit(solution)/shard_map/ppermute | solution.py:224
  23.8 1.6 %collective-permute-start.10 = (bf16[64,2176]{1,0:T(8,128)(2,1)S(1)}, bf16[64,2176]{1,0:T(8,128)(2,1)S(1)}, u32[]{:S(2)}, u32[]{:S(2)}) collective-permute-start(bf16[64,2176]{1,0:T(8,128)(2,1)S(1)} %get-tuple-element.114.refs_0_), channel_id=1, source_target_pairs={{0,2},{1,3},{2,0},{3,1},{4,6},{5,7},{6,4},{7,5},{8,10},{9,11},{10,... | collective-permute-start | bytes 835592 | tf_op jit(solution)/shard_map/ppermute | solution.py:221
  26.4 1.5 %collective-permute-start.9 = (bf16[384,768]{1,0:T(8,128)(2,1)S(1)}, bf16[384,768]{1,0:T(8,128)(2,1)S(1)}, u32[]{:S(2)}, u32[]{:S(2)}) collective-permute-start(bf16[384,768]{1,0:T(8,128)(2,1)S(1)} %get-tuple-element.113), channel_id=1, source_target_pairs={{0,16},{16,0},{1,17},{17,1},{2,18},{18,2},{3,19},{19,3},{4,20},{20... | collective-permute-start | bytes 1769480 | tf_op jit(solution)/shard_map/ppermute | solution.py:224
  27.9 3.1 %collective-permute-done.11.refs_4_ = bf16[256,768]{1,0:T(8,128)(2,1)S(1)} collective-permute-done((bf16[256,768]{1,0:T(8,128)(2,1)S(1)}, bf16[256,768]{1,0:T(8,128)(2,1)S(1)}, u32[]{:S(2)}, u32[]{:S(2)}) %collective-permute-start.11) | collective-permute-done | bytes 393248 | tf_op jit(solution)/shard_map/ppermute | solution.py:224
  33.1 1.9 %collective-permute-done.12.refs_1_ = bf16[128,2176]{1,0:T(8,128)(2,1)S(1)} collective-permute-done((bf16[128,2176]{1,0:T(8,128)(2,1)S(1)}, bf16[128,2176]{1,0:T(8,128)(2,1)S(1)}, u32[]{:S(2)}, u32[]{:S(2)}) %collective-permute-start.12) | collective-permute-done | bytes 557088 | tf_op jit(solution)/shard_map/ppermute | solution.py:221
  35.0 1.8 %shard_map.78 = (bf16[640,768]{1,0:T(8,128)(2,1)S(1)}, f32[8,128]{1,0:T(8,128)S(1)}) custom-call(bf16[128,2176]{1,0:T(8,128)(2,1)S(1)} %get-tuple-element.119.refs_0_, bf16[128,2176]{1,0:T(8,128)(2,1)S(1)} %collective-permute-done.12.refs_1_, bf16[1,2048,1536]{2,1,0:T(8,128)(2,1)S(1)} %copy-done, bf16[1,2048,1536]{2,1,0:T(8,128)(2,1)S(1)} %copy-done.1, ...), custom_call_target="tpu_custom_call" | custom-call | flops 8000000000 | bytes 1 | tf_op jit(solution)/shard_map/pallas_call | solution.py:100
  38.4 1.6 %collective-permute-start.16 = (bf16[64,2176]{1,0:T(8,128)(2,1)S(1)}, bf16[64,2176]{1,0:T(8,128)(2,1)S(1)}, u32[]{:S(2)}, u32[]{:S(2)}) collective-permute-start(bf16[64,2176]{1,0:T(8,128)(2,1)S(1)} %get-tuple-element.132), channel_id=1, source_target_pairs={{0,2},{1,3},{2,0},{3,1},{4,6},{5,7},{6,4},{7,5},{8,10},{9,11},{10,... | collective-permute-start | bytes 835592 | tf_op jit(solution)/shard_map/ppermute | solution.py:221
  40.0 3.8 %collective-permute-done.9.refs_4_.refs_3_ = bf16[384,768]{1,0:T(8,128)(2,1)S(1)} collective-permute-done((bf16[384,768]{1,0:T(8,128)(2,1)S(1)}, bf16[384,768]{1,0:T(8,128)(2,1)S(1)}, u32[]{:S(2)}, u32[]{:S(2)}) %collective-permute-start.9) | collective-permute-done | bytes 589856 | tf_op jit(solution)/shard_map/ppermute | solution.py:224
  46.3 1.8 %collective-permute-done.14.refs_0_ = bf16[64,2176]{1,0:T(8,128)(2,1)S(1)} collective-permute-done((bf16[64,2176]{1,0:T(8,128)(2,1)S(1)}, bf16[64,2176]{1,0:T(8,128)(2,1)S(1)}, u32[]{:S(2)}, u32[]{:S(2)}) %collective-permute-start.14) | collective-permute-done | bytes 278560 | tf_op jit(solution)/shard_map/ppermute | solution.py:221
  48.1 1.6 %collective-permute-start.17 = (bf16[64,2176]{1,0:T(8,128)(2,1)S(1)}, bf16[64,2176]{1,0:T(8,128)(2,1)S(1)}, u32[]{:S(2)}, u32[]{:S(2)}) collective-permute-start(bf16[64,2176]{1,0:T(8,128)(2,1)S(1)} %get-tuple-element.133.refs_0_), channel_id=1, source_target_pairs={{0,2},{1,3},{2,0},{3,1},{4,6},{5,7},{6,4},{7,5},{8,10},{9,11},{10,... | collective-permute-start | bytes 835592 | tf_op jit(solution)/shard_map/ppermute | solution.py:221
  49.7 6.7 %collective-permute-done.17.refs_1_ = bf16[64,2176]{1,0:T(8,128)(2,1)S(1)} collective-permute-done((bf16[64,2176]{1,0:T(8,128)(2,1)S(1)}, bf16[64,2176]{1,0:T(8,128)(2,1)S(1)}, u32[]{:S(2)}, u32[]{:S(2)}) %collective-permute-start.17) | collective-permute-done | bytes 278560 | tf_op jit(solution)/shard_map/ppermute | solution.py:221
  56.5 1.9 %collective-permute-done.18.refs_1_ = bf16[128,2176]{1,0:T(8,128)(2,1)S(1)} collective-permute-done((bf16[128,2176]{1,0:T(8,128)(2,1)S(1)}, bf16[128,2176]{1,0:T(8,128)(2,1)S(1)}, u32[]{:S(2)}, u32[]{:S(2)}) %collective-permute-start.18) | collective-permute-done | bytes 557088 | tf_op jit(solution)/shard_map/ppermute | solution.py:221
  58.5 1.8 %shard_map.86 = (bf16[640,768]{1,0:T(8,128)(2,1)S(1)}, f32[8,128]{1,0:T(8,128)S(1)}) custom-call(bf16[128,2176]{1,0:T(8,128)(2,1)S(1)} %get-tuple-element.135.refs_0_, bf16[128,2176]{1,0:T(8,128)(2,1)S(1)} %collective-permute-done.18.refs_1_, bf16[1,2048,1536]{2,1,0:T(8,128)(2,1)S(1)} %copy-done, bf16[1,2048,1536]{2,1,0:T(8,128)(2,1)S(1)} %copy-done.1, ...), custom_call_target="tpu_custom_call" | custom-call | flops 8000000000 | bytes 1 | tf_op jit(solution)/shard_map/pallas_call | solution.py:100
  60.3 1.6 %collective-permute-start.21 = (bf16[640,768]{1,0:T(8,128)(2,1)S(1)}, bf16[640,768]{1,0:T(8,128)(2,1)S(1)}, u32[]{:S(2)}, u32[]{:S(2)}) collective-permute-start(bf16[640,768]{1,0:T(8,128)(2,1)S(1)} %get-tuple-element.145), channel_id=1, source_target_pairs={{0,16},{16,0},{1,17},{17,1},{2,18},{18,2},{3,19},{19,3},{4,20},{20... | collective-permute-start | bytes 2949128 | tf_op jit(solution)/shard_map/ppermute | solution.py:224
  62.0 2.8 %collective-permute-done.15.refs_4_.refs_3_ = bf16[640,768]{1,0:T(8,128)(2,1)S(1)} collective-permute-done((bf16[640,768]{1,0:T(8,128)(2,1)S(1)}, bf16[640,768]{1,0:T(8,128)(2,1)S(1)}, u32[]{:S(2)}, u32[]{:S(2)}) %collective-permute-start.15) | collective-permute-done | bytes 983072 | tf_op jit(solution)/shard_map/ppermute | solution.py:224
  64.8 1.8 %shard_map.88 = (bf16[256,768]{1,0:T(8,128)(2,1)S(1)}, f32[8,128]{1,0:T(8,128)S(1)}) custom-call(bf16[128,2176]{1,0:T(8,128)(2,1)S(1)} %get-tuple-element.119.refs_0_, bf16[128,2176]{1,0:T(8,128)(2,1)S(1)} %collective-permute-done.12.refs_1_, bf16[1,2048,1536]{2,1,0:T(8,128)(2,1)S(1)} %copy-done, bf16[1,2048,1536]{2,1,0:T(8,128)(2,1)S(1)} %copy-done.1, ...), custom_call_target="tpu_custom_call" | custom-call | flops 8000000000 | bytes 1 | tf_op jit(solution)/shard_map/pallas_call | solution.py:100
  68.0 1.6 %collective-permute-start.26 = (bf16[256,768]{1,0:T(8,128)(2,1)S(1)}, bf16[256,768]{1,0:T(8,128)(2,1)S(1)}, u32[]{:S(2)}, u32[]{:S(2)}) collective-permute-start(bf16[256,768]{1,0:T(8,128)(2,1)S(1)} %get-tuple-element.162.refs_2_), channel_id=1, source_target_pairs={{0,16},{16,0},{1,17},{17,1},{2,18},{18,2},{3,19},{19,3},{4,20},{20... | collective-permute-start | bytes 1179656 | tf_op jit(solution)/shard_map/ppermute | solution.py:224
  72.6 13.2 %collective-permute-done.21.refs_4_.refs_3_ = bf16[640,768]{1,0:T(8,128)(2,1)S(1)} collective-permute-done((bf16[640,768]{1,0:T(8,128)(2,1)S(1)}, bf16[640,768]{1,0:T(8,128)(2,1)S(1)}, u32[]{:S(2)}, u32[]{:S(2)}) %collective-permute-start.21) | collective-permute-done | bytes 983072 | tf_op jit(solution)/shard_map/ppermute | solution.py:224
  85.9 1.8 %shard_map.94 = (bf16[256,768]{1,0:T(8,128)(2,1)S(1)}, f32[8,128]{1,0:T(8,128)S(1)}) custom-call(bf16[128,2176]{1,0:T(8,128)(2,1)S(1)} %get-tuple-element.135.refs_0_, bf16[128,2176]{1,0:T(8,128)(2,1)S(1)} %collective-permute-done.18.refs_1_, bf16[1,2048,1536]{2,1,0:T(8,128)(2,1)S(1)} %copy-done, bf16[1,2048,1536]{2,1,0:T(8,128)(2,1)S(1)} %copy-done.1, ...), custom_call_target="tpu_custom_call" | custom-call | flops 8000000000 | bytes 1 | tf_op jit(solution)/shard_map/pallas_call | solution.py:100
  94.3 2.1 %shard_map.101 = (f32[128,2048]{1,0:T(8,128)S(1)}, bf16[128,2048]{1,0:T(8,128)(2,1)S(1)}, f32[8,128]{1,0:T(8,128)S(1)}) custom-call(bf16[128,2176]{1,0:T(8,128)(2,1)S(1)} %get-tuple-element.119.refs_0_, bf16[128,2176]{1,0:T(8,128)(2,1)S(1)} %collective-permute-done.12.refs_1_, bf16[256,768]{1,0:T(8,128)(2,1)S(1)} %get-tuple-element.162.refs_2_, ...), custom_call_target="tpu_custom_call" | custom-call | flops 8000000000 | bytes 1 | tf_op jit(solution)/shard_map/pallas_call | solution.py:100
  96.5 1.9 %collective-permute-done.27.refs_1_ = bf16[128,2048]{1,0:T(8,128)(2,1)S(1)} collective-permute-done((bf16[128,2048]{1,0:T(8,128)(2,1)S(1)}, bf16[128,2048]{1,0:T(8,128)(2,1)S(1)}, u32[]{:S(2)}, u32[]{:S(2)}) %collective-permute-start.27) | collective-permute-done | bytes 524320 | tf_op jit(solution)/shard_map/ppermute | solution.py:221
  98.5 1.6 %collective-permute-start.28 = (bf16[64,2048]{1,0:T(8,128)(2,1)S(1)}, bf16[64,2048]{1,0:T(8,128)(2,1)S(1)}, u32[]{:S(2)}, u32[]{:S(2)}) collective-permute-start(bf16[64,2048]{1,0:T(8,128)(2,1)S(1)} %get-tuple-element.171), channel_id=1, source_target_pairs={{0,2},{1,3},{2,0},{3,1},{4,6},{5,7},{6,4},{7,5},{8,10},{9,11},{10,... | collective-permute-start | bytes 786440 | tf_op jit(solution)/shard_map/ppermute | solution.py:221
  100.0 2.7 %collective-permute-done.25.refs_3_ = bf16[256,768]{1,0:T(8,128)(2,1)S(1)} collective-permute-done((bf16[256,768]{1,0:T(8,128)(2,1)S(1)}, bf16[256,768]{1,0:T(8,128)(2,1)S(1)}, u32[]{:S(2)}, u32[]{:S(2)}) %collective-permute-start.25) | collective-permute-done | bytes 393248 | tf_op jit(solution)/shard_map/ppermute | solution.py:224
  102.7 2.1 %shard_map.104 = (f32[128,2048]{1,0:T(8,128)S(1)}, bf16[128,2048]{1,0:T(8,128)(2,1)S(1)}, f32[8,128]{1,0:T(8,128)S(1)}) custom-call(bf16[128,2176]{1,0:T(8,128)(2,1)S(1)} %get-tuple-element.135.refs_0_, bf16[128,2176]{1,0:T(8,128)(2,1)S(1)} %collective-permute-done.18.refs_1_, bf16[256,768]{1,0:T(8,128)(2,1)S(1)} %get-tuple-element.161.refs_2_, ...), custom_call_target="tpu_custom_call" | custom-call | flops 8000000000 | bytes 1 | tf_op jit(solution)/shard_map/pallas_call | solution.py:100
  105.0 1.9 %collective-permute-done.30.refs_3_ = bf16[128,768]{1,0:T(8,128)(2,1)S(1)} collective-permute-done((bf16[128,768]{1,0:T(8,128)(2,1)S(1)}, bf16[128,768]{1,0:T(8,128)(2,1)S(1)}, u32[]{:S(2)}, u32[]{:S(2)}) %collective-permute-start.30) | collective-permute-done | bytes 196640 | tf_op jit(solution)/shard_map/ppermute | solution.py:224
  108.1 1.6 %collective-permute-start.33 = (bf16[64,768]{1,0:T(8,128)(2,1)S(1)}, bf16[64,768]{1,0:T(8,128)(2,1)S(1)}, u32[]{:S(2)}, u32[]{:S(2)}) collective-permute-start(bf16[64,768]{1,0:T(8,128)(2,1)S(1)} %get-tuple-element.180.refs_1_), channel_id=1, source_target_pairs={{0,16},{16,0},{1,17},{17,1},{2,18},{18,2},{3,19},{19,3},{4,20},{20... | collective-permute-start | bytes 294920 | tf_op jit(solution)/shard_map/ppermute | solution.py:224
  115.5 1.6 %collective-permute-start.34 = (bf16[64,768]{1,0:T(8,128)(2,1)S(1)}, bf16[64,768]{1,0:T(8,128)(2,1)S(1)}, u32[]{:S(2)}, u32[]{:S(2)}) collective-permute-start(bf16[64,768]{1,0:T(8,128)(2,1)S(1)} %get-tuple-element.183.refs_1_), channel_id=1, source_target_pairs={{0,16},{16,0},{1,17},{17,1},{2,18},{18,2},{3,19},{19,3},{4,20},{20... | collective-permute-start | bytes 294920 | tf_op jit(solution)/shard_map/ppermute | solution.py:224
  117.5 2.6 %collective-permute-done.34.refs_2_ = bf16[64,768]{1,0:T(8,128)(2,1)S(1)} collective-permute-done((bf16[64,768]{1,0:T(8,128)(2,1)S(1)}, bf16[64,768]{1,0:T(8,128)(2,1)S(1)}, u32[]{:S(2)}, u32[]{:S(2)}) %collective-permute-start.34) | collective-permute-done | bytes 98336 | tf_op jit(solution)/shard_map/ppermute | solution.py:224
  123.3 9.8 %collective-permute-done.37.refs_1_ = bf16[64,2048]{1,0:T(8,128)(2,1)S(1)} collective-permute-done((bf16[64,2048]{1,0:T(8,128)(2,1)S(1)}, bf16[64,2048]{1,0:T(8,128)(2,1)S(1)}, u32[]{:S(2)}, u32[]{:S(2)}) %collective-permute-start.37) | collective-permute-done | bytes 262176 | tf_op jit(solution)/shard_map/ppermute | solution.py:221
  (115 shorter events, 40.9 us)
Async XLA Ops:
  2.5 9.7 %collective-permute-start.2 = (bf16[64,2176]{1,0:T(8,128)(2,1)S(1)}, bf16[64,2176]{1,0:T(8,128)(2,1)S(1)}, u32[]{:S(2)}, u32[]{:S(2)}) collective-permute-start(bf16[64,2176]{1,0:T(8,128)(2,1)S(1)} %get-tuple-element.101.refs_0_), channel_id=1, source_target_pairs={{0,4},{1,5},{2,6},{3,7},{4,0},{5,1},{6,2},{7,3},{8,12},{9,13},{10,... | collective-permute-start | bytes 835592 | tf_op jit(solution)/shard_map/ppermute | solution.py:221
  8.0 4.2 %collective-permute-start.3 = (f32[8,128]{1,0:T(8,128)S(1)}, f32[8,128]{1,0:T(8,128)S(1)}, u32[]{:S(2)}, u32[]{:S(2)}) collective-permute-start(f32[8,128]{1,0:T(8,128)S(1)} %get-tuple-element.104.refs_1_), channel_id=1, source_target_pairs={{0,1},{1,0},{2,3},{3,2},{4,5},{5,4},{6,7},{7,6},{8,9},{9,8},{10,11... | collective-permute-start | bytes 12296 | tf_op jit(solution)/shard_map/ppermute | solution.py:221
  8.0 15.7 %collective-permute-start.8 = (bf16[64,2176]{1,0:T(8,128)(2,1)S(1)}, bf16[64,2176]{1,0:T(8,128)(2,1)S(1)}, u32[]{:S(2)}, u32[]{:S(2)}) collective-permute-start(bf16[64,2176]{1,0:T(8,128)(2,1)S(1)} %get-tuple-element.101.refs_0_), channel_id=1, source_target_pairs={{0,8},{1,9},{2,10},{3,11},{4,12},{5,13},{6,14},{7,15},{8,0},{9,1},... | collective-permute-start | bytes 835592 | tf_op jit(solution)/shard_map/ppermute | solution.py:221
  10.7 12.0 %collective-permute-start.1 = (bf16[256,768]{1,0:T(8,128)(2,1)S(1)}, bf16[256,768]{1,0:T(8,128)(2,1)S(1)}, u32[]{:S(2)}, u32[]{:S(2)}) collective-permute-start(bf16[256,768]{1,0:T(8,128)(2,1)S(1)} %get-tuple-element.103), channel_id=1, source_target_pairs={{0,16},{16,0},{1,17},{17,1},{2,18},{18,2},{3,19},{19,3},{4,20},{20... | collective-permute-start | bytes 1179656 | tf_op jit(solution)/shard_map/ppermute | solution.py:224
  12.3 11.4 %collective-permute-start.5 = (bf16[64,2176]{1,0:T(8,128)(2,1)S(1)}, bf16[64,2176]{1,0:T(8,128)(2,1)S(1)}, u32[]{:S(2)}, u32[]{:S(2)}) collective-permute-start(bf16[64,2176]{1,0:T(8,128)(2,1)S(1)} %get-tuple-element.105.refs_0_), channel_id=1, source_target_pairs={{0,2},{1,3},{2,0},{3,1},{4,6},{5,7},{6,4},{7,5},{8,10},{9,11},{10,... | collective-permute-start | bytes 835592 | tf_op jit(solution)/shard_map/ppermute | solution.py:221
  14.9 8.8 %collective-permute-start.6 = (f32[8,128]{1,0:T(8,128)S(1)}, f32[8,128]{1,0:T(8,128)S(1)}, u32[]{:S(2)}, u32[]{:S(2)}) collective-permute-start(f32[8,128]{1,0:T(8,128)S(1)} %get-tuple-element.107.refs_5_), channel_id=1, source_target_pairs={{0,1},{1,0},{2,3},{3,2},{4,5},{5,4},{6,7},{7,6},{8,9},{9,8},{10,11... | collective-permute-start | bytes 12296 | tf_op jit(solution)/shard_map/ppermute | solution.py:221
  15.1 16.0 %collective-permute-start.11 = (bf16[256,768]{1,0:T(8,128)(2,1)S(1)}, bf16[256,768]{1,0:T(8,128)(2,1)S(1)}, u32[]{:S(2)}, u32[]{:S(2)}) collective-permute-start(bf16[256,768]{1,0:T(8,128)(2,1)S(1)} %get-tuple-element.115), channel_id=1, source_target_pairs={{0,16},{16,0},{1,17},{17,1},{2,18},{18,2},{3,19},{19,3},{4,20},{20... | collective-permute-start | bytes 1179656 | tf_op jit(solution)/shard_map/ppermute | solution.py:224
  23.8 9.1 %collective-permute-start.10 = (bf16[64,2176]{1,0:T(8,128)(2,1)S(1)}, bf16[64,2176]{1,0:T(8,128)(2,1)S(1)}, u32[]{:S(2)}, u32[]{:S(2)}) collective-permute-start(bf16[64,2176]{1,0:T(8,128)(2,1)S(1)} %get-tuple-element.114.refs_0_), channel_id=1, source_target_pairs={{0,2},{1,3},{2,0},{3,1},{4,6},{5,7},{6,4},{7,5},{8,10},{9,11},{10,... | collective-permute-start | bytes 835592 | tf_op jit(solution)/shard_map/ppermute | solution.py:221
  26.4 17.3 %collective-permute-start.9 = (bf16[384,768]{1,0:T(8,128)(2,1)S(1)}, bf16[384,768]{1,0:T(8,128)(2,1)S(1)}, u32[]{:S(2)}, u32[]{:S(2)}) collective-permute-start(bf16[384,768]{1,0:T(8,128)(2,1)S(1)} %get-tuple-element.113), channel_id=1, source_target_pairs={{0,16},{16,0},{1,17},{17,1},{2,18},{18,2},{3,19},{19,3},{4,20},{20... | collective-permute-start | bytes 1769480 | tf_op jit(solution)/shard_map/ppermute | solution.py:224
  33.1 15.0 %collective-permute-start.14 = (bf16[64,2176]{1,0:T(8,128)(2,1)S(1)}, bf16[64,2176]{1,0:T(8,128)(2,1)S(1)}, u32[]{:S(2)}, u32[]{:S(2)}) collective-permute-start(bf16[64,2176]{1,0:T(8,128)(2,1)S(1)} %get-tuple-element.127), channel_id=1, source_target_pairs={{0,12},{1,13},{2,14},{3,15},{4,8},{5,9},{6,10},{7,11},{8,4},{9,5},... | collective-permute-start | bytes 835592 | tf_op jit(solution)/shard_map/ppermute | solution.py:221
  36.8 28.0 %collective-permute-start.15 = (bf16[640,768]{1,0:T(8,128)(2,1)S(1)}, bf16[640,768]{1,0:T(8,128)(2,1)S(1)}, u32[]{:S(2)}, u32[]{:S(2)}) collective-permute-start(bf16[640,768]{1,0:T(8,128)(2,1)S(1)} %get-tuple-element.131), channel_id=1, source_target_pairs={{0,16},{16,0},{1,17},{17,1},{2,18},{18,2},{3,19},{19,3},{4,20},{20... | collective-permute-start | bytes 2949128 | tf_op jit(solution)/shard_map/ppermute | solution.py:224
  38.4 23.5 %collective-permute-start.16 = (bf16[64,2176]{1,0:T(8,128)(2,1)S(1)}, bf16[64,2176]{1,0:T(8,128)(2,1)S(1)}, u32[]{:S(2)}, u32[]{:S(2)}) collective-permute-start(bf16[64,2176]{1,0:T(8,128)(2,1)S(1)} %get-tuple-element.132), channel_id=1, source_target_pairs={{0,2},{1,3},{2,0},{3,1},{4,6},{5,7},{6,4},{7,5},{8,10},{9,11},{10,... | collective-permute-start | bytes 835592 | tf_op jit(solution)/shard_map/ppermute | solution.py:221
  46.2 3.5 %collective-permute-start.13 = (bf16[64,2048]{1,0:T(8,128)(2,1)S(1)}, bf16[64,2048]{1,0:T(8,128)(2,1)S(1)}, u32[]{:S(2)}, u32[]{:S(2)}) collective-permute-start(bf16[64,2048]{1,0:T(8,128)(2,1)S(1)} %get-tuple-element.126), channel_id=1, source_target_pairs={{0,1},{1,0},{2,3},{3,2},{4,5},{5,4},{6,7},{7,6},{8,9},{9,8},{10,11... | collective-permute-start | bytes 786440 | tf_op jit(solution)/shard_map/ppermute | solution.py:221
  48.1 8.3 %collective-permute-start.17 = (bf16[64,2176]{1,0:T(8,128)(2,1)S(1)}, bf16[64,2176]{1,0:T(8,128)(2,1)S(1)}, u32[]{:S(2)}, u32[]{:S(2)}) collective-permute-start(bf16[64,2176]{1,0:T(8,128)(2,1)S(1)} %get-tuple-element.133.refs_0_), channel_id=1, source_target_pairs={{0,2},{1,3},{2,0},{3,1},{4,6},{5,7},{6,4},{7,5},{8,10},{9,11},{10,... | collective-permute-start | bytes 835592 | tf_op jit(solution)/shard_map/ppermute | solution.py:221
  60.3 25.6 %collective-permute-start.21 = (bf16[640,768]{1,0:T(8,128)(2,1)S(1)}, bf16[640,768]{1,0:T(8,128)(2,1)S(1)}, u32[]{:S(2)}, u32[]{:S(2)}) collective-permute-start(bf16[640,768]{1,0:T(8,128)(2,1)S(1)} %get-tuple-element.145), channel_id=1, source_target_pairs={{0,16},{16,0},{1,17},{17,1},{2,18},{18,2},{3,19},{19,3},{4,20},{20... | collective-permute-start | bytes 2949128 | tf_op jit(solution)/shard_map/ppermute | solution.py:224
  61.9 8.3 %collective-permute-start.22 = (bf16[64,2176]{1,0:T(8,128)(2,1)S(1)}, bf16[64,2176]{1,0:T(8,128)(2,1)S(1)}, u32[]{:S(2)}, u32[]{:S(2)}) collective-permute-start(bf16[64,2176]{1,0:T(8,128)(2,1)S(1)} %get-tuple-element.146.refs_0_), channel_id=1, source_target_pairs={{0,1},{1,0},{2,3},{3,2},{4,5},{5,4},{6,7},{7,6},{8,9},{9,8},{10,11... | collective-permute-start | bytes 835592 | tf_op jit(solution)/shard_map/ppermute | solution.py:221
  68.0 26.3 %collective-permute-start.26 = (bf16[256,768]{1,0:T(8,128)(2,1)S(1)}, bf16[256,768]{1,0:T(8,128)(2,1)S(1)}, u32[]{:S(2)}, u32[]{:S(2)}) collective-permute-start(bf16[256,768]{1,0:T(8,128)(2,1)S(1)} %get-tuple-element.162.refs_2_), channel_id=1, source_target_pairs={{0,16},{16,0},{1,17},{17,1},{2,18},{18,2},{3,19},{19,3},{4,20},{20... | collective-permute-start | bytes 1179656 | tf_op jit(solution)/shard_map/ppermute | solution.py:224
  69.7 19.5 %collective-permute-start.20 = (bf16[64,2048]{1,0:T(8,128)(2,1)S(1)}, bf16[64,2048]{1,0:T(8,128)(2,1)S(1)}, u32[]{:S(2)}, u32[]{:S(2)}) collective-permute-start(bf16[64,2048]{1,0:T(8,128)(2,1)S(1)} %get-tuple-element.144), channel_id=1, source_target_pairs={{0,4},{1,5},{2,6},{3,7},{4,0},{5,1},{6,2},{7,3},{8,12},{9,13},{10,... | collective-permute-start | bytes 786440 | tf_op jit(solution)/shard_map/ppermute | solution.py:221
  89.0 3.7 %collective-permute-start.23 = (bf16[64,2048]{1,0:T(8,128)(2,1)S(1)}, bf16[64,2048]{1,0:T(8,128)(2,1)S(1)}, u32[]{:S(2)}, u32[]{:S(2)}) collective-permute-start(bf16[64,2048]{1,0:T(8,128)(2,1)S(1)} %get-tuple-element.158), channel_id=1, source_target_pairs={{0,1},{1,0},{2,3},{3,2},{4,5},{5,4},{6,7},{7,6},{8,9},{9,8},{10,11... | collective-permute-start | bytes 786440 | tf_op jit(solution)/shard_map/ppermute | solution.py:221
  89.2 13.5 %collective-permute-start.25 = (bf16[256,768]{1,0:T(8,128)(2,1)S(1)}, bf16[256,768]{1,0:T(8,128)(2,1)S(1)}, u32[]{:S(2)}, u32[]{:S(2)}) collective-permute-start(bf16[256,768]{1,0:T(8,128)(2,1)S(1)} %get-tuple-element.161.refs_2_), channel_id=1, source_target_pairs={{0,16},{16,0},{1,17},{17,1},{2,18},{18,2},{3,19},{19,3},{4,20},{20... | collective-permute-start | bytes 1179656 | tf_op jit(solution)/shard_map/ppermute | solution.py:224
  90.7 16.2 %collective-permute-start.30 = (bf16[128,768]{1,0:T(8,128)(2,1)S(1)}, bf16[128,768]{1,0:T(8,128)(2,1)S(1)}, u32[]{:S(2)}, u32[]{:S(2)}) collective-permute-start(bf16[128,768]{1,0:T(8,128)(2,1)S(1)} %get-tuple-element.174), channel_id=1, source_target_pairs={{0,16},{16,0},{1,17},{17,1},{2,18},{18,2},{3,19},{19,3},{4,20},{20... | collective-permute-start | bytes 589832 | tf_op jit(solution)/shard_map/ppermute | solution.py:224
  91.3 22.9 %collective-permute-start.32 = (bf16[128,768]{1,0:T(8,128)(2,1)S(1)}, bf16[128,768]{1,0:T(8,128)(2,1)S(1)}, u32[]{:S(2)}, u32[]{:S(2)}) collective-permute-start(bf16[128,768]{1,0:T(8,128)(2,1)S(1)} %get-tuple-element.179), channel_id=1, source_target_pairs={{0,16},{16,0},{1,17},{17,1},{2,18},{18,2},{3,19},{19,3},{4,20},{20... | collective-permute-start | bytes 589832 | tf_op jit(solution)/shard_map/ppermute | solution.py:224
  92.8 12.1 %collective-permute-start.24 = (bf16[64,2048]{1,0:T(8,128)(2,1)S(1)}, bf16[64,2048]{1,0:T(8,128)(2,1)S(1)}, u32[]{:S(2)}, u32[]{:S(2)}) collective-permute-start(bf16[64,2048]{1,0:T(8,128)(2,1)S(1)} %get-tuple-element.160), channel_id=1, source_target_pairs={{0,6},{1,7},{2,4},{3,5},{4,2},{5,3},{6,0},{7,1},{8,14},{9,15},{10,... | collective-permute-start | bytes 786440 | tf_op jit(solution)/shard_map/ppermute | solution.py:221
  98.5 11.3 %collective-permute-start.28 = (bf16[64,2048]{1,0:T(8,128)(2,1)S(1)}, bf16[64,2048]{1,0:T(8,128)(2,1)S(1)}, u32[]{:S(2)}, u32[]{:S(2)}) collective-permute-start(bf16[64,2048]{1,0:T(8,128)(2,1)S(1)} %get-tuple-element.171), channel_id=1, source_target_pairs={{0,2},{1,3},{2,0},{3,1},{4,6},{5,7},{6,4},{7,5},{8,10},{9,11},{10,... | collective-permute-start | bytes 786440 | tf_op jit(solution)/shard_map/ppermute | solution.py:221
  104.8 4.9 %collective-permute-start.29 = (bf16[128,2048]{1,0:T(8,128)(2,1)S(1)}, bf16[128,2048]{1,0:T(8,128)(2,1)S(1)}, u32[]{:S(2)}, u32[]{:S(2)}) collective-permute-start(bf16[128,2048]{1,0:T(8,128)(2,1)S(1)} %get-tuple-element.173), channel_id=1, source_target_pairs={{0,1},{1,0},{2,3},{3,2},{4,5},{5,4},{6,7},{7,6},{8,9},{9,8},{10,11... | collective-permute-start | bytes 1572872 | tf_op jit(solution)/shard_map/ppermute | solution.py:221
  108.1 4.7 %collective-permute-start.33 = (bf16[64,768]{1,0:T(8,128)(2,1)S(1)}, bf16[64,768]{1,0:T(8,128)(2,1)S(1)}, u32[]{:S(2)}, u32[]{:S(2)}) collective-permute-start(bf16[64,768]{1,0:T(8,128)(2,1)S(1)} %get-tuple-element.180.refs_1_), channel_id=1, source_target_pairs={{0,16},{16,0},{1,17},{17,1},{2,18},{18,2},{3,19},{19,3},{4,20},{20... | collective-permute-start | bytes 294920 | tf_op jit(solution)/shard_map/ppermute | solution.py:224
  109.9 13.4 %collective-permute-start.31 = (bf16[64,2048]{1,0:T(8,128)(2,1)S(1)}, bf16[64,2048]{1,0:T(8,128)(2,1)S(1)}, u32[]{:S(2)}, u32[]{:S(2)}) collective-permute-start(bf16[64,2048]{1,0:T(8,128)(2,1)S(1)} %get-tuple-element.178), channel_id=1, source_target_pairs={{0,8},{1,9},{2,10},{3,11},{4,12},{5,13},{6,14},{7,15},{8,0},{9,1},... | collective-permute-start | bytes 786440 | tf_op jit(solution)/shard_map/ppermute | solution.py:221
  111.0 6.4 %collective-permute-start.35 = (bf16[64,2048]{1,0:T(8,128)(2,1)S(1)}, bf16[64,2048]{1,0:T(8,128)(2,1)S(1)}, u32[]{:S(2)}, u32[]{:S(2)}) collective-permute-start(bf16[64,2048]{1,0:T(8,128)(2,1)S(1)} %get-tuple-element.185), channel_id=1, source_target_pairs={{0,2},{1,3},{2,0},{3,1},{4,6},{5,7},{6,4},{7,5},{8,10},{9,11},{10,... | collective-permute-start | bytes 786440 | tf_op jit(solution)/shard_map/ppermute | solution.py:221
  115.5 4.7 %collective-permute-start.34 = (bf16[64,768]{1,0:T(8,128)(2,1)S(1)}, bf16[64,768]{1,0:T(8,128)(2,1)S(1)}, u32[]{:S(2)}, u32[]{:S(2)}) collective-permute-start(bf16[64,768]{1,0:T(8,128)(2,1)S(1)} %get-tuple-element.183.refs_1_), channel_id=1, source_target_pairs={{0,16},{16,0},{1,17},{17,1},{2,18},{18,2},{3,19},{19,3},{4,20},{20... | collective-permute-start | bytes 294920 | tf_op jit(solution)/shard_map/ppermute | solution.py:224
  117.0 5.1 %collective-permute-start.36 = (bf16[64,2048]{1,0:T(8,128)(2,1)S(1)}, bf16[64,2048]{1,0:T(8,128)(2,1)S(1)}, u32[]{:S(2)}, u32[]{:S(2)}) collective-permute-start(bf16[64,2048]{1,0:T(8,128)(2,1)S(1)} %get-tuple-element.189), channel_id=1, source_target_pairs={{0,1},{1,0},{2,3},{3,2},{4,5},{5,4},{6,7},{7,6},{8,9},{9,8},{10,11... | collective-permute-start | bytes 786440 | tf_op jit(solution)/shard_map/ppermute | solution.py:221
  121.6 11.6 %collective-permute-start.37 = (bf16[64,2048]{1,0:T(8,128)(2,1)S(1)}, bf16[64,2048]{1,0:T(8,128)(2,1)S(1)}, u32[]{:S(2)}, u32[]{:S(2)}) collective-permute-start(bf16[64,2048]{1,0:T(8,128)(2,1)S(1)} %get-tuple-element.193), channel_id=1, source_target_pairs={{0,12},{1,13},{2,14},{3,15},{4,8},{5,9},{6,10},{7,11},{8,4},{9,5},... | collective-permute-start | bytes 786440 | tf_op jit(solution)/shard_map/ppermute | solution.py:221
  122.2 10.9 %collective-permute-start.38 = (bf16[64,2048]{1,0:T(8,128)(2,1)S(1)}, bf16[64,2048]{1,0:T(8,128)(2,1)S(1)}, u32[]{:S(2)}, u32[]{:S(2)}) collective-permute-start(bf16[64,2048]{1,0:T(8,128)(2,1)S(1)} %get-tuple-element.194), channel_id=1, source_target_pairs={{0,2},{1,3},{2,0},{3,1},{4,6},{5,7},{6,4},{7,5},{8,10},{9,11},{10,... | collective-permute-start | bytes 786440 | tf_op jit(solution)/shard_map/ppermute | solution.py:221
  (14 other events, 35.1 us)

commit v9 on v8

--- a/solution.py
+++ b/solution.py
@@ -215,7 +215,7 @@
     sources = lax.axis_size("expert")
     half = gate_proj.shape[2] // 2
     tile = half
-    out_tile = 1024 if width % 1024 == 0 else width
+    out_tile = width
 
     def swap(value, r):
         return lax.ppermute(value, "expert", [(i, i ^ r) for i in range(sources)])

time: 134 us -> 134 us (level)
  Pallas kernels: 31.1 us -> 29.4 us
  waiting for transfers between devices: 64.6 us -> 66 us
    pallas_call x53, Pallas kernels: 31.1 us -> 29.4 us  [call(): pl.pallas_call(run, in_specs=[spec for _, spec in inputs] + [HERE] * len(...]
  transfers between devices with their start and end apart: 39 -> 39, of which waited for: 18 -> 19; matrix products, arithmetic and copies ran while one was open for 0% -> 0% of each run, Pallas kernels for 23% -> 21%
where the time goes in v9:
time: 134 us
  waiting for transfers between devices  66 us (49%)
  starting transfers between devices  32.8 us (24%)
  Pallas kernels  29.4 us (22%)
  local copies, waits for them, and re-layouts  5.2 us (4%)
    ppermute x11, waiting for transfers between devices, cross(): return lax.ppermute(value, 'dp', [(0, 1), (1, 0)])  38.1 us
    pallas_call x53, Pallas kernels, call(): pl.pallas_call(run, in_specs=[spec for _, spec in inputs] + [HERE] * len(...  29.4 us
    ppermute x28, waiting for transfers between devices, swap(): return lax.ppermute(value, 'expert', [(i, i ^ r) for i in range(sources)])  28 us
    ppermute x28, starting transfers between devices, swap(): return lax.ppermute(value, 'expert', [(i, i ^ r) for i in range(sources)])  17.4 us
    ppermute x11, starting transfers between devices, cross(): return lax.ppermute(value, 'dp', [(0, 1), (1, 0)])  15.4 us
    unnamed x14, local copies, waits for them, and re-layouts  5.2 us
  transfers between devices with their start and end apart: 39, of which 19 were waited for; matrix products, arithmetic and copies ran while one was open for 0% of the time, Pallas kernels for 21%

profile of v9, /device:TPU:8, one launch (start us, length us, event | category | flops | bytes accessed | tf_op | source)
XLA Modules:
  0.0 134.0 jit_solution(13299178847106683402)
XLA Ops:
  5.1 1.8 %copy-done.1 = bf16[1,2048,1536]{2,1,0:T(8,128)(2,1)S(1)} copy-done((bf16[1,2048,1536]{2,1,0:T(8,128)(2,1)S(1)}, bf16[1,2048,1536]{2,1,0:T(8,128)(2,1)}, u32[]{:S(2)}) %copy-start.1) | copy-done | bytes 6291480
  8.0 2.7 %collective-permute-start.8 = (bf16[64,2176]{1,0:T(8,128)(2,1)S(1)}, bf16[64,2176]{1,0:T(8,128)(2,1)S(1)}, u32[]{:S(2)}, u32[]{:S(2)}) collective-permute-start(bf16[64,2176]{1,0:T(8,128)(2,1)S(1)} %get-tuple-element.101.refs_0_), channel_id=1, source_target_pairs={{0,8},{1,9},{2,10},{3,11},{4,12},{5,13},{6,14},{7,15},{8,0},{9,1},... | collective-permute-start | bytes 835592 | tf_op jit(solution)/shard_map/ppermute | solution.py:221
  12.3 1.6 %collective-permute-start.5 = (bf16[64,2176]{1,0:T(8,128)(2,1)S(1)}, bf16[64,2176]{1,0:T(8,128)(2,1)S(1)}, u32[]{:S(2)}, u32[]{:S(2)}) collective-permute-start(bf16[64,2176]{1,0:T(8,128)(2,1)S(1)} %get-tuple-element.105.refs_0_), channel_id=1, source_target_pairs={{0,2},{1,3},{2,0},{3,1},{4,6},{5,7},{6,4},{7,5},{8,10},{9,11},{10,... | collective-permute-start | bytes 835592 | tf_op jit(solution)/shard_map/ppermute | solution.py:221
  16.0 6.6 %collective-permute-done.1.refs_4_ = bf16[256,768]{1,0:T(8,128)(2,1)S(1)} collective-permute-done((bf16[256,768]{1,0:T(8,128)(2,1)S(1)}, bf16[256,768]{1,0:T(8,128)(2,1)S(1)}, u32[]{:S(2)}, u32[]{:S(2)}) %collective-permute-start.1) | collective-permute-done | bytes 393248 | tf_op jit(solution)/shard_map/ppermute | solution.py:224
  23.8 1.6 %collective-permute-start.10 = (bf16[64,2176]{1,0:T(8,128)(2,1)S(1)}, bf16[64,2176]{1,0:T(8,128)(2,1)S(1)}, u32[]{:S(2)}, u32[]{:S(2)}) collective-permute-start(bf16[64,2176]{1,0:T(8,128)(2,1)S(1)} %get-tuple-element.114.refs_0_), channel_id=1, source_target_pairs={{0,2},{1,3},{2,0},{3,1},{4,6},{5,7},{6,4},{7,5},{8,10},{9,11},{10,... | collective-permute-start | bytes 835592 | tf_op jit(solution)/shard_map/ppermute | solution.py:221
  26.4 1.5 %collective-permute-start.9 = (bf16[384,768]{1,0:T(8,128)(2,1)S(1)}, bf16[384,768]{1,0:T(8,128)(2,1)S(1)}, u32[]{:S(2)}, u32[]{:S(2)}) collective-permute-start(bf16[384,768]{1,0:T(8,128)(2,1)S(1)} %get-tuple-element.113), channel_id=1, source_target_pairs={{0,16},{16,0},{1,17},{17,1},{2,18},{18,2},{3,19},{19,3},{4,20},{20... | collective-permute-start | bytes 1769480 | tf_op jit(solution)/shard_map/ppermute | solution.py:224
  27.9 3.1 %collective-permute-done.11.refs_4_ = bf16[256,768]{1,0:T(8,128)(2,1)S(1)} collective-permute-done((bf16[256,768]{1,0:T(8,128)(2,1)S(1)}, bf16[256,768]{1,0:T(8,128)(2,1)S(1)}, u32[]{:S(2)}, u32[]{:S(2)}) %collective-permute-start.11) | collective-permute-done | bytes 393248 | tf_op jit(solution)/shard_map/ppermute | solution.py:224
  33.1 1.9 %collective-permute-done.12.refs_1_ = bf16[128,2176]{1,0:T(8,128)(2,1)S(1)} collective-permute-done((bf16[128,2176]{1,0:T(8,128)(2,1)S(1)}, bf16[128,2176]{1,0:T(8,128)(2,1)S(1)}, u32[]{:S(2)}, u32[]{:S(2)}) %collective-permute-start.12) | collective-permute-done | bytes 557088 | tf_op jit(solution)/shard_map/ppermute | solution.py:221
  35.0 1.8 %shard_map.78 = (bf16[640,768]{1,0:T(8,128)(2,1)S(1)}, f32[8,128]{1,0:T(8,128)S(1)}) custom-call(bf16[128,2176]{1,0:T(8,128)(2,1)S(1)} %get-tuple-element.119.refs_0_, bf16[128,2176]{1,0:T(8,128)(2,1)S(1)} %collective-permute-done.12.refs_1_, bf16[1,2048,1536]{2,1,0:T(8,128)(2,1)S(1)} %copy-done, bf16[1,2048,1536]{2,1,0:T(8,128)(2,1)S(1)} %copy-done.1, ...), custom_call_target="tpu_custom_call" | custom-call | flops 8000000000 | bytes 1 | tf_op jit(solution)/shard_map/pallas_call | solution.py:100
  38.4 1.6 %collective-permute-start.16 = (bf16[64,2176]{1,0:T(8,128)(2,1)S(1)}, bf16[64,2176]{1,0:T(8,128)(2,1)S(1)}, u32[]{:S(2)}, u32[]{:S(2)}) collective-permute-start(bf16[64,2176]{1,0:T(8,128)(2,1)S(1)} %get-tuple-element.132), channel_id=1, source_target_pairs={{0,2},{1,3},{2,0},{3,1},{4,6},{5,7},{6,4},{7,5},{8,10},{9,11},{10,... | collective-permute-start | bytes 835592 | tf_op jit(solution)/shard_map/ppermute | solution.py:221
  40.0 3.8 %collective-permute-done.9.refs_4_.refs_3_ = bf16[384,768]{1,0:T(8,128)(2,1)S(1)} collective-permute-done((bf16[384,768]{1,0:T(8,128)(2,1)S(1)}, bf16[384,768]{1,0:T(8,128)(2,1)S(1)}, u32[]{:S(2)}, u32[]{:S(2)}) %collective-permute-start.9) | collective-permute-done | bytes 589856 | tf_op jit(solution)/shard_map/ppermute | solution.py:224
  45.9 2.2 %collective-permute-done.14.refs_0_ = bf16[64,2176]{1,0:T(8,128)(2,1)S(1)} collective-permute-done((bf16[64,2176]{1,0:T(8,128)(2,1)S(1)}, bf16[64,2176]{1,0:T(8,128)(2,1)S(1)}, u32[]{:S(2)}, u32[]{:S(2)}) %collective-permute-start.14) | collective-permute-done | bytes 278560 | tf_op jit(solution)/shard_map/ppermute | solution.py:221
  48.1 1.6 %collective-permute-start.17 = (bf16[64,2176]{1,0:T(8,128)(2,1)S(1)}, bf16[64,2176]{1,0:T(8,128)(2,1)S(1)}, u32[]{:S(2)}, u32[]{:S(2)}) collective-permute-start(bf16[64,2176]{1,0:T(8,128)(2,1)S(1)} %get-tuple-element.133.refs_0_), channel_id=1, source_target_pairs={{0,2},{1,3},{2,0},{3,1},{4,6},{5,7},{6,4},{7,5},{8,10},{9,11},{10,... | collective-permute-start | bytes 835592 | tf_op jit(solution)/shard_map/ppermute | solution.py:221
  49.7 6.7 %collective-permute-done.17.refs_1_ = bf16[64,2176]{1,0:T(8,128)(2,1)S(1)} collective-permute-done((bf16[64,2176]{1,0:T(8,128)(2,1)S(1)}, bf16[64,2176]{1,0:T(8,128)(2,1)S(1)}, u32[]{:S(2)}, u32[]{:S(2)}) %collective-permute-start.17) | collective-permute-done | bytes 278560 | tf_op jit(solution)/shard_map/ppermute | solution.py:221
  56.5 1.9 %collective-permute-done.18.refs_1_ = bf16[128,2176]{1,0:T(8,128)(2,1)S(1)} collective-permute-done((bf16[128,2176]{1,0:T(8,128)(2,1)S(1)}, bf16[128,2176]{1,0:T(8,128)(2,1)S(1)}, u32[]{:S(2)}, u32[]{:S(2)}) %collective-permute-start.18) | collective-permute-done | bytes 557088 | tf_op jit(solution)/shard_map/ppermute | solution.py:221
  58.5 1.8 %shard_map.86 = (bf16[640,768]{1,0:T(8,128)(2,1)S(1)}, f32[8,128]{1,0:T(8,128)S(1)}) custom-call(bf16[128,2176]{1,0:T(8,128)(2,1)S(1)} %get-tuple-element.135.refs_0_, bf16[128,2176]{1,0:T(8,128)(2,1)S(1)} %collective-permute-done.18.refs_1_, bf16[1,2048,1536]{2,1,0:T(8,128)(2,1)S(1)} %copy-done, bf16[1,2048,1536]{2,1,0:T(8,128)(2,1)S(1)} %copy-done.1, ...), custom_call_target="tpu_custom_call" | custom-call | flops 8000000000 | bytes 1 | tf_op jit(solution)/shard_map/pallas_call | solution.py:100
  60.3 1.6 %collective-permute-start.21 = (bf16[640,768]{1,0:T(8,128)(2,1)S(1)}, bf16[640,768]{1,0:T(8,128)(2,1)S(1)}, u32[]{:S(2)}, u32[]{:S(2)}) collective-permute-start(bf16[640,768]{1,0:T(8,128)(2,1)S(1)} %get-tuple-element.145), channel_id=1, source_target_pairs={{0,16},{16,0},{1,17},{17,1},{2,18},{18,2},{3,19},{19,3},{4,20},{20... | collective-permute-start | bytes 2949128 | tf_op jit(solution)/shard_map/ppermute | solution.py:224
  62.0 2.8 %collective-permute-done.15.refs_4_.refs_3_ = bf16[640,768]{1,0:T(8,128)(2,1)S(1)} collective-permute-done((bf16[640,768]{1,0:T(8,128)(2,1)S(1)}, bf16[640,768]{1,0:T(8,128)(2,1)S(1)}, u32[]{:S(2)}, u32[]{:S(2)}) %collective-permute-start.15) | collective-permute-done | bytes 983072 | tf_op jit(solution)/shard_map/ppermute | solution.py:224
  64.8 1.8 %shard_map.88 = (bf16[256,768]{1,0:T(8,128)(2,1)S(1)}, f32[8,128]{1,0:T(8,128)S(1)}) custom-call(bf16[128,2176]{1,0:T(8,128)(2,1)S(1)} %get-tuple-element.119.refs_0_, bf16[128,2176]{1,0:T(8,128)(2,1)S(1)} %collective-permute-done.12.refs_1_, bf16[1,2048,1536]{2,1,0:T(8,128)(2,1)S(1)} %copy-done, bf16[1,2048,1536]{2,1,0:T(8,128)(2,1)S(1)} %copy-done.1, ...), custom_call_target="tpu_custom_call" | custom-call | flops 8000000000 | bytes 1 | tf_op jit(solution)/shard_map/pallas_call | solution.py:100
  67.9 1.6 %collective-permute-start.26 = (bf16[256,768]{1,0:T(8,128)(2,1)S(1)}, bf16[256,768]{1,0:T(8,128)(2,1)S(1)}, u32[]{:S(2)}, u32[]{:S(2)}) collective-permute-start(bf16[256,768]{1,0:T(8,128)(2,1)S(1)} %get-tuple-element.162.refs_2_), channel_id=1, source_target_pairs={{0,16},{16,0},{1,17},{17,1},{2,18},{18,2},{3,19},{19,3},{4,20},{20... | collective-permute-start | bytes 1179656 | tf_op jit(solution)/shard_map/ppermute | solution.py:224
  72.6 13.3 %collective-permute-done.21.refs_4_.refs_3_ = bf16[640,768]{1,0:T(8,128)(2,1)S(1)} collective-permute-done((bf16[640,768]{1,0:T(8,128)(2,1)S(1)}, bf16[640,768]{1,0:T(8,128)(2,1)S(1)}, u32[]{:S(2)}, u32[]{:S(2)}) %collective-permute-start.21) | collective-permute-done | bytes 983072 | tf_op jit(solution)/shard_map/ppermute | solution.py:224
  85.9 1.8 %shard_map.94 = (bf16[256,768]{1,0:T(8,128)(2,1)S(1)}, f32[8,128]{1,0:T(8,128)S(1)}) custom-call(bf16[128,2176]{1,0:T(8,128)(2,1)S(1)} %get-tuple-element.135.refs_0_, bf16[128,2176]{1,0:T(8,128)(2,1)S(1)} %collective-permute-done.18.refs_1_, bf16[1,2048,1536]{2,1,0:T(8,128)(2,1)S(1)} %copy-done, bf16[1,2048,1536]{2,1,0:T(8,128)(2,1)S(1)} %copy-done.1, ...), custom_call_target="tpu_custom_call" | custom-call | flops 8000000000 | bytes 1 | tf_op jit(solution)/shard_map/pallas_call | solution.py:100
  94.3 1.8 %shard_map.101 = (f32[128,2048]{1,0:T(8,128)S(1)}, bf16[128,2048]{1,0:T(8,128)(2,1)S(1)}, f32[8,128]{1,0:T(8,128)S(1)}) custom-call(bf16[128,2176]{1,0:T(8,128)(2,1)S(1)} %get-tuple-element.119.refs_0_, bf16[128,2176]{1,0:T(8,128)(2,1)S(1)} %collective-permute-done.12.refs_1_, bf16[256,768]{1,0:T(8,128)(2,1)S(1)} %get-tuple-element.162.refs_2_, ...), custom_call_target="tpu_custom_call" | custom-call | flops 8000000000 | bytes 1 | tf_op jit(solution)/shard_map/pallas_call | solution.py:100
  96.2 1.9 %collective-permute-done.27.refs_1_ = bf16[128,2048]{1,0:T(8,128)(2,1)S(1)} collective-permute-done((bf16[128,2048]{1,0:T(8,128)(2,1)S(1)}, bf16[128,2048]{1,0:T(8,128)(2,1)S(1)}, u32[]{:S(2)}, u32[]{:S(2)}) %collective-permute-start.27) | collective-permute-done | bytes 524320 | tf_op jit(solution)/shard_map/ppermute | solution.py:221
  98.2 1.6 %collective-permute-start.28 = (bf16[64,2048]{1,0:T(8,128)(2,1)S(1)}, bf16[64,2048]{1,0:T(8,128)(2,1)S(1)}, u32[]{:S(2)}, u32[]{:S(2)}) collective-permute-start(bf16[64,2048]{1,0:T(8,128)(2,1)S(1)} %get-tuple-element.171), channel_id=1, source_target_pairs={{0,2},{1,3},{2,0},{3,1},{4,6},{5,7},{6,4},{7,5},{8,10},{9,11},{10,... | collective-permute-start | bytes 786440 | tf_op jit(solution)/shard_map/ppermute | solution.py:221
  99.7 3.0 %collective-permute-done.25.refs_3_ = bf16[256,768]{1,0:T(8,128)(2,1)S(1)} collective-permute-done((bf16[256,768]{1,0:T(8,128)(2,1)S(1)}, bf16[256,768]{1,0:T(8,128)(2,1)S(1)}, u32[]{:S(2)}, u32[]{:S(2)}) %collective-permute-start.25) | collective-permute-done | bytes 393248 | tf_op jit(solution)/shard_map/ppermute | solution.py:224
  102.7 1.8 %shard_map.104 = (f32[128,2048]{1,0:T(8,128)S(1)}, bf16[128,2048]{1,0:T(8,128)(2,1)S(1)}, f32[8,128]{1,0:T(8,128)S(1)}) custom-call(bf16[128,2176]{1,0:T(8,128)(2,1)S(1)} %get-tuple-element.135.refs_0_, bf16[128,2176]{1,0:T(8,128)(2,1)S(1)} %collective-permute-done.18.refs_1_, bf16[256,768]{1,0:T(8,128)(2,1)S(1)} %get-tuple-element.161.refs_2_, ...), custom_call_target="tpu_custom_call" | custom-call | flops 8000000000 | bytes 1 | tf_op jit(solution)/shard_map/pallas_call | solution.py:100
  104.7 2.2 %collective-permute-done.30.refs_3_ = bf16[128,768]{1,0:T(8,128)(2,1)S(1)} collective-permute-done((bf16[128,768]{1,0:T(8,128)(2,1)S(1)}, bf16[128,768]{1,0:T(8,128)(2,1)S(1)}, u32[]{:S(2)}, u32[]{:S(2)}) %collective-permute-start.30) | collective-permute-done | bytes 196640 | tf_op jit(solution)/shard_map/ppermute | solution.py:224
  108.1 1.6 %collective-permute-start.33 = (bf16[64,768]{1,0:T(8,128)(2,1)S(1)}, bf16[64,768]{1,0:T(8,128)(2,1)S(1)}, u32[]{:S(2)}, u32[]{:S(2)}) collective-permute-start(bf16[64,768]{1,0:T(8,128)(2,1)S(1)} %get-tuple-element.180.refs_1_), channel_id=1, source_target_pairs={{0,16},{16,0},{1,17},{17,1},{2,18},{18,2},{3,19},{19,3},{4,20},{20... | collective-permute-start | bytes 294920 | tf_op jit(solution)/shard_map/ppermute | solution.py:224
  115.3 1.6 %collective-permute-start.34 = (bf16[64,768]{1,0:T(8,128)(2,1)S(1)}, bf16[64,768]{1,0:T(8,128)(2,1)S(1)}, u32[]{:S(2)}, u32[]{:S(2)}) collective-permute-start(bf16[64,768]{1,0:T(8,128)(2,1)S(1)} %get-tuple-element.183.refs_1_), channel_id=1, source_target_pairs={{0,16},{16,0},{1,17},{17,1},{2,18},{18,2},{3,19},{19,3},{4,20},{20... | collective-permute-start | bytes 294920 | tf_op jit(solution)/shard_map/ppermute | solution.py:224
  117.7 2.2 %collective-permute-done.34.refs_2_ = bf16[64,768]{1,0:T(8,128)(2,1)S(1)} collective-permute-done((bf16[64,768]{1,0:T(8,128)(2,1)S(1)}, bf16[64,768]{1,0:T(8,128)(2,1)S(1)}, u32[]{:S(2)}, u32[]{:S(2)}) %collective-permute-start.34) | collective-permute-done | bytes 98336 | tf_op jit(solution)/shard_map/ppermute | solution.py:224
  122.9 10.2 %collective-permute-done.37.refs_1_ = bf16[64,2048]{1,0:T(8,128)(2,1)S(1)} collective-permute-done((bf16[64,2048]{1,0:T(8,128)(2,1)S(1)}, bf16[64,2048]{1,0:T(8,128)(2,1)S(1)}, u32[]{:S(2)}, u32[]{:S(2)}) %collective-permute-start.37) | collective-permute-done | bytes 262176 | tf_op jit(solution)/shard_map/ppermute | solution.py:221
  (115 shorter events, 40.5 us)
Async XLA Ops:
  2.5 9.7 %collective-permute-start.2 = (bf16[64,2176]{1,0:T(8,128)(2,1)S(1)}, bf16[64,2176]{1,0:T(8,128)(2,1)S(1)}, u32[]{:S(2)}, u32[]{:S(2)}) collective-permute-start(bf16[64,2176]{1,0:T(8,128)(2,1)S(1)} %get-tuple-element.101.refs_0_), channel_id=1, source_target_pairs={{0,4},{1,5},{2,6},{3,7},{4,0},{5,1},{6,2},{7,3},{8,12},{9,13},{10,... | collective-permute-start | bytes 835592 | tf_op jit(solution)/shard_map/ppermute | solution.py:221
  8.0 4.2 %collective-permute-start.3 = (f32[8,128]{1,0:T(8,128)S(1)}, f32[8,128]{1,0:T(8,128)S(1)}, u32[]{:S(2)}, u32[]{:S(2)}) collective-permute-start(f32[8,128]{1,0:T(8,128)S(1)} %get-tuple-element.104.refs_1_), channel_id=1, source_target_pairs={{0,1},{1,0},{2,3},{3,2},{4,5},{5,4},{6,7},{7,6},{8,9},{9,8},{10,11... | collective-permute-start | bytes 12296 | tf_op jit(solution)/shard_map/ppermute | solution.py:221
  8.0 15.7 %collective-permute-start.8 = (bf16[64,2176]{1,0:T(8,128)(2,1)S(1)}, bf16[64,2176]{1,0:T(8,128)(2,1)S(1)}, u32[]{:S(2)}, u32[]{:S(2)}) collective-permute-start(bf16[64,2176]{1,0:T(8,128)(2,1)S(1)} %get-tuple-element.101.refs_0_), channel_id=1, source_target_pairs={{0,8},{1,9},{2,10},{3,11},{4,12},{5,13},{6,14},{7,15},{8,0},{9,1},... | collective-permute-start | bytes 835592 | tf_op jit(solution)/shard_map/ppermute | solution.py:221
  10.7 12.0 %collective-permute-start.1 = (bf16[256,768]{1,0:T(8,128)(2,1)S(1)}, bf16[256,768]{1,0:T(8,128)(2,1)S(1)}, u32[]{:S(2)}, u32[]{:S(2)}) collective-permute-start(bf16[256,768]{1,0:T(8,128)(2,1)S(1)} %get-tuple-element.103), channel_id=1, source_target_pairs={{0,16},{16,0},{1,17},{17,1},{2,18},{18,2},{3,19},{19,3},{4,20},{20... | collective-permute-start | bytes 1179656 | tf_op jit(solution)/shard_map/ppermute | solution.py:224
  12.3 11.4 %collective-permute-start.5 = (bf16[64,2176]{1,0:T(8,128)(2,1)S(1)}, bf16[64,2176]{1,0:T(8,128)(2,1)S(1)}, u32[]{:S(2)}, u32[]{:S(2)}) collective-permute-start(bf16[64,2176]{1,0:T(8,128)(2,1)S(1)} %get-tuple-element.105.refs_0_), channel_id=1, source_target_pairs={{0,2},{1,3},{2,0},{3,1},{4,6},{5,7},{6,4},{7,5},{8,10},{9,11},{10,... | collective-permute-start | bytes 835592 | tf_op jit(solution)/shard_map/ppermute | solution.py:221
  14.9 8.8 %collective-permute-start.6 = (f32[8,128]{1,0:T(8,128)S(1)}, f32[8,128]{1,0:T(8,128)S(1)}, u32[]{:S(2)}, u32[]{:S(2)}) collective-permute-start(f32[8,128]{1,0:T(8,128)S(1)} %get-tuple-element.107.refs_5_), channel_id=1, source_target_pairs={{0,1},{1,0},{2,3},{3,2},{4,5},{5,4},{6,7},{7,6},{8,9},{9,8},{10,11... | collective-permute-start | bytes 12296 | tf_op jit(solution)/shard_map/ppermute | solution.py:221
  15.1 16.0 %collective-permute-start.11 = (bf16[256,768]{1,0:T(8,128)(2,1)S(1)}, bf16[256,768]{1,0:T(8,128)(2,1)S(1)}, u32[]{:S(2)}, u32[]{:S(2)}) collective-permute-start(bf16[256,768]{1,0:T(8,128)(2,1)S(1)} %get-tuple-element.115), channel_id=1, source_target_pairs={{0,16},{16,0},{1,17},{17,1},{2,18},{18,2},{3,19},{19,3},{4,20},{20... | collective-permute-start | bytes 1179656 | tf_op jit(solution)/shard_map/ppermute | solution.py:224
  23.8 9.1 %collective-permute-start.10 = (bf16[64,2176]{1,0:T(8,128)(2,1)S(1)}, bf16[64,2176]{1,0:T(8,128)(2,1)S(1)}, u32[]{:S(2)}, u32[]{:S(2)}) collective-permute-start(bf16[64,2176]{1,0:T(8,128)(2,1)S(1)} %get-tuple-element.114.refs_0_), channel_id=1, source_target_pairs={{0,2},{1,3},{2,0},{3,1},{4,6},{5,7},{6,4},{7,5},{8,10},{9,11},{10,... | collective-permute-start | bytes 835592 | tf_op jit(solution)/shard_map/ppermute | solution.py:221
  26.4 17.3 %collective-permute-start.9 = (bf16[384,768]{1,0:T(8,128)(2,1)S(1)}, bf16[384,768]{1,0:T(8,128)(2,1)S(1)}, u32[]{:S(2)}, u32[]{:S(2)}) collective-permute-start(bf16[384,768]{1,0:T(8,128)(2,1)S(1)} %get-tuple-element.113), channel_id=1, source_target_pairs={{0,16},{16,0},{1,17},{17,1},{2,18},{18,2},{3,19},{19,3},{4,20},{20... | collective-permute-start | bytes 1769480 | tf_op jit(solution)/shard_map/ppermute | solution.py:224
  33.1 15.0 %collective-permute-start.14 = (bf16[64,2176]{1,0:T(8,128)(2,1)S(1)}, bf16[64,2176]{1,0:T(8,128)(2,1)S(1)}, u32[]{:S(2)}, u32[]{:S(2)}) collective-permute-start(bf16[64,2176]{1,0:T(8,128)(2,1)S(1)} %get-tuple-element.127), channel_id=1, source_target_pairs={{0,12},{1,13},{2,14},{3,15},{4,8},{5,9},{6,10},{7,11},{8,4},{9,5},... | collective-permute-start | bytes 835592 | tf_op jit(solution)/shard_map/ppermute | solution.py:221
  36.8 28.0 %collective-permute-start.15 = (bf16[640,768]{1,0:T(8,128)(2,1)S(1)}, bf16[640,768]{1,0:T(8,128)(2,1)S(1)}, u32[]{:S(2)}, u32[]{:S(2)}) collective-permute-start(bf16[640,768]{1,0:T(8,128)(2,1)S(1)} %get-tuple-element.131), channel_id=1, source_target_pairs={{0,16},{16,0},{1,17},{17,1},{2,18},{18,2},{3,19},{19,3},{4,20},{20... | collective-permute-start | bytes 2949128 | tf_op jit(solution)/shard_map/ppermute | solution.py:224
  38.4 23.5 %collective-permute-start.16 = (bf16[64,2176]{1,0:T(8,128)(2,1)S(1)}, bf16[64,2176]{1,0:T(8,128)(2,1)S(1)}, u32[]{:S(2)}, u32[]{:S(2)}) collective-permute-start(bf16[64,2176]{1,0:T(8,128)(2,1)S(1)} %get-tuple-element.132), channel_id=1, source_target_pairs={{0,2},{1,3},{2,0},{3,1},{4,6},{5,7},{6,4},{7,5},{8,10},{9,11},{10,... | collective-permute-start | bytes 835592 | tf_op jit(solution)/shard_map/ppermute | solution.py:221
  45.8 3.9 %collective-permute-start.13 = (bf16[64,2048]{1,0:T(8,128)(2,1)S(1)}, bf16[64,2048]{1,0:T(8,128)(2,1)S(1)}, u32[]{:S(2)}, u32[]{:S(2)}) collective-permute-start(bf16[64,2048]{1,0:T(8,128)(2,1)S(1)} %get-tuple-element.126), channel_id=1, source_target_pairs={{0,1},{1,0},{2,3},{3,2},{4,5},{5,4},{6,7},{7,6},{8,9},{9,8},{10,11... | collective-permute-start | bytes 786440 | tf_op jit(solution)/shard_map/ppermute | solution.py:221
  48.1 8.3 %collective-permute-start.17 = (bf16[64,2176]{1,0:T(8,128)(2,1)S(1)}, bf16[64,2176]{1,0:T(8,128)(2,1)S(1)}, u32[]{:S(2)}, u32[]{:S(2)}) collective-permute-start(bf16[64,2176]{1,0:T(8,128)(2,1)S(1)} %get-tuple-element.133.refs_0_), channel_id=1, source_target_pairs={{0,2},{1,3},{2,0},{3,1},{4,6},{5,7},{6,4},{7,5},{8,10},{9,11},{10,... | collective-permute-start | bytes 835592 | tf_op jit(solution)/shard_map/ppermute | solution.py:221
  60.3 25.6 %collective-permute-start.21 = (bf16[640,768]{1,0:T(8,128)(2,1)S(1)}, bf16[640,768]{1,0:T(8,128)(2,1)S(1)}, u32[]{:S(2)}, u32[]{:S(2)}) collective-permute-start(bf16[640,768]{1,0:T(8,128)(2,1)S(1)} %get-tuple-element.145), channel_id=1, source_target_pairs={{0,16},{16,0},{1,17},{17,1},{2,18},{18,2},{3,19},{19,3},{4,20},{20... | collective-permute-start | bytes 2949128 | tf_op jit(solution)/shard_map/ppermute | solution.py:224
  61.9 8.2 %collective-permute-start.22 = (bf16[64,2176]{1,0:T(8,128)(2,1)S(1)}, bf16[64,2176]{1,0:T(8,128)(2,1)S(1)}, u32[]{:S(2)}, u32[]{:S(2)}) collective-permute-start(bf16[64,2176]{1,0:T(8,128)(2,1)S(1)} %get-tuple-element.146.refs_0_), channel_id=1, source_target_pairs={{0,1},{1,0},{2,3},{3,2},{4,5},{5,4},{6,7},{7,6},{8,9},{9,8},{10,11... | collective-permute-start | bytes 835592 | tf_op jit(solution)/shard_map/ppermute | solution.py:221
  67.9 26.3 %collective-permute-start.26 = (bf16[256,768]{1,0:T(8,128)(2,1)S(1)}, bf16[256,768]{1,0:T(8,128)(2,1)S(1)}, u32[]{:S(2)}, u32[]{:S(2)}) collective-permute-start(bf16[256,768]{1,0:T(8,128)(2,1)S(1)} %get-tuple-element.162.refs_2_), channel_id=1, source_target_pairs={{0,16},{16,0},{1,17},{17,1},{2,18},{18,2},{3,19},{19,3},{4,20},{20... | collective-permute-start | bytes 1179656 | tf_op jit(solution)/shard_map/ppermute | solution.py:224
  69.6 19.3 %collective-permute-start.20 = (bf16[64,2048]{1,0:T(8,128)(2,1)S(1)}, bf16[64,2048]{1,0:T(8,128)(2,1)S(1)}, u32[]{:S(2)}, u32[]{:S(2)}) collective-permute-start(bf16[64,2048]{1,0:T(8,128)(2,1)S(1)} %get-tuple-element.144), channel_id=1, source_target_pairs={{0,4},{1,5},{2,6},{3,7},{4,0},{5,1},{6,2},{7,3},{8,12},{9,13},{10,... | collective-permute-start | bytes 786440 | tf_op jit(solution)/shard_map/ppermute | solution.py:221
  88.8 3.7 %collective-permute-start.23 = (bf16[64,2048]{1,0:T(8,128)(2,1)S(1)}, bf16[64,2048]{1,0:T(8,128)(2,1)S(1)}, u32[]{:S(2)}, u32[]{:S(2)}) collective-permute-start(bf16[64,2048]{1,0:T(8,128)(2,1)S(1)} %get-tuple-element.158), channel_id=1, source_target_pairs={{0,1},{1,0},{2,3},{3,2},{4,5},{5,4},{6,7},{7,6},{8,9},{9,8},{10,11... | collective-permute-start | bytes 786440 | tf_op jit(solution)/shard_map/ppermute | solution.py:221
  88.9 13.8 %collective-permute-start.25 = (bf16[256,768]{1,0:T(8,128)(2,1)S(1)}, bf16[256,768]{1,0:T(8,128)(2,1)S(1)}, u32[]{:S(2)}, u32[]{:S(2)}) collective-permute-start(bf16[256,768]{1,0:T(8,128)(2,1)S(1)} %get-tuple-element.161.refs_2_), channel_id=1, source_target_pairs={{0,16},{16,0},{1,17},{17,1},{2,18},{18,2},{3,19},{19,3},{4,20},{20... | collective-permute-start | bytes 1179656 | tf_op jit(solution)/shard_map/ppermute | solution.py:224
  90.5 16.4 %collective-permute-start.30 = (bf16[128,768]{1,0:T(8,128)(2,1)S(1)}, bf16[128,768]{1,0:T(8,128)(2,1)S(1)}, u32[]{:S(2)}, u32[]{:S(2)}) collective-permute-start(bf16[128,768]{1,0:T(8,128)(2,1)S(1)} %get-tuple-element.174), channel_id=1, source_target_pairs={{0,16},{16,0},{1,17},{17,1},{2,18},{18,2},{3,19},{19,3},{4,20},{20... | collective-permute-start | bytes 589832 | tf_op jit(solution)/shard_map/ppermute | solution.py:224
  91.0 23.0 %collective-permute-start.32 = (bf16[128,768]{1,0:T(8,128)(2,1)S(1)}, bf16[128,768]{1,0:T(8,128)(2,1)S(1)}, u32[]{:S(2)}, u32[]{:S(2)}) collective-permute-start(bf16[128,768]{1,0:T(8,128)(2,1)S(1)} %get-tuple-element.179), channel_id=1, source_target_pairs={{0,16},{16,0},{1,17},{17,1},{2,18},{18,2},{3,19},{19,3},{4,20},{20... | collective-permute-start | bytes 589832 | tf_op jit(solution)/shard_map/ppermute | solution.py:224
  92.6 12.1 %collective-permute-start.24 = (bf16[64,2048]{1,0:T(8,128)(2,1)S(1)}, bf16[64,2048]{1,0:T(8,128)(2,1)S(1)}, u32[]{:S(2)}, u32[]{:S(2)}) collective-permute-start(bf16[64,2048]{1,0:T(8,128)(2,1)S(1)} %get-tuple-element.160), channel_id=1, source_target_pairs={{0,6},{1,7},{2,4},{3,5},{4,2},{5,3},{6,0},{7,1},{8,14},{9,15},{10,... | collective-permute-start | bytes 786440 | tf_op jit(solution)/shard_map/ppermute | solution.py:221
  98.2 11.6 %collective-permute-start.28 = (bf16[64,2048]{1,0:T(8,128)(2,1)S(1)}, bf16[64,2048]{1,0:T(8,128)(2,1)S(1)}, u32[]{:S(2)}, u32[]{:S(2)}) collective-permute-start(bf16[64,2048]{1,0:T(8,128)(2,1)S(1)} %get-tuple-element.171), channel_id=1, source_target_pairs={{0,2},{1,3},{2,0},{3,1},{4,6},{5,7},{6,4},{7,5},{8,10},{9,11},{10,... | collective-permute-start | bytes 786440 | tf_op jit(solution)/shard_map/ppermute | solution.py:221
  104.5 5.1 %collective-permute-start.29 = (bf16[128,2048]{1,0:T(8,128)(2,1)S(1)}, bf16[128,2048]{1,0:T(8,128)(2,1)S(1)}, u32[]{:S(2)}, u32[]{:S(2)}) collective-permute-start(bf16[128,2048]{1,0:T(8,128)(2,1)S(1)} %get-tuple-element.173), channel_id=1, source_target_pairs={{0,1},{1,0},{2,3},{3,2},{4,5},{5,4},{6,7},{7,6},{8,9},{9,8},{10,11... | collective-permute-start | bytes 1572872 | tf_op jit(solution)/shard_map/ppermute | solution.py:221
  108.1 4.7 %collective-permute-start.33 = (bf16[64,768]{1,0:T(8,128)(2,1)S(1)}, bf16[64,768]{1,0:T(8,128)(2,1)S(1)}, u32[]{:S(2)}, u32[]{:S(2)}) collective-permute-start(bf16[64,768]{1,0:T(8,128)(2,1)S(1)} %get-tuple-element.180.refs_1_), channel_id=1, source_target_pairs={{0,16},{16,0},{1,17},{17,1},{2,18},{18,2},{3,19},{19,3},{4,20},{20... | collective-permute-start | bytes 294920 | tf_op jit(solution)/shard_map/ppermute | solution.py:224
  109.9 13.0 %collective-permute-start.31 = (bf16[64,2048]{1,0:T(8,128)(2,1)S(1)}, bf16[64,2048]{1,0:T(8,128)(2,1)S(1)}, u32[]{:S(2)}, u32[]{:S(2)}) collective-permute-start(bf16[64,2048]{1,0:T(8,128)(2,1)S(1)} %get-tuple-element.178), channel_id=1, source_target_pairs={{0,8},{1,9},{2,10},{3,11},{4,12},{5,13},{6,14},{7,15},{8,0},{9,1},... | collective-permute-start | bytes 786440 | tf_op jit(solution)/shard_map/ppermute | solution.py:221
  111.3 6.4 %collective-permute-start.35 = (bf16[64,2048]{1,0:T(8,128)(2,1)S(1)}, bf16[64,2048]{1,0:T(8,128)(2,1)S(1)}, u32[]{:S(2)}, u32[]{:S(2)}) collective-permute-start(bf16[64,2048]{1,0:T(8,128)(2,1)S(1)} %get-tuple-element.185), channel_id=1, source_target_pairs={{0,2},{1,3},{2,0},{3,1},{4,6},{5,7},{6,4},{7,5},{8,10},{9,11},{10,... | collective-permute-start | bytes 786440 | tf_op jit(solution)/shard_map/ppermute | solution.py:221
  115.3 4.7 %collective-permute-start.34 = (bf16[64,768]{1,0:T(8,128)(2,1)S(1)}, bf16[64,768]{1,0:T(8,128)(2,1)S(1)}, u32[]{:S(2)}, u32[]{:S(2)}) collective-permute-start(bf16[64,768]{1,0:T(8,128)(2,1)S(1)} %get-tuple-element.183.refs_1_), channel_id=1, source_target_pairs={{0,16},{16,0},{1,17},{17,1},{2,18},{18,2},{3,19},{19,3},{4,20},{20... | collective-permute-start | bytes 294920 | tf_op jit(solution)/shard_map/ppermute | solution.py:224
  116.8 4.9 %collective-permute-start.36 = (bf16[64,2048]{1,0:T(8,128)(2,1)S(1)}, bf16[64,2048]{1,0:T(8,128)(2,1)S(1)}, u32[]{:S(2)}, u32[]{:S(2)}) collective-permute-start(bf16[64,2048]{1,0:T(8,128)(2,1)S(1)} %get-tuple-element.189), channel_id=1, source_target_pairs={{0,1},{1,0},{2,3},{3,2},{4,5},{5,4},{6,7},{7,6},{8,9},{9,8},{10,11... | collective-permute-start | bytes 786440 | tf_op jit(solution)/shard_map/ppermute | solution.py:221
  121.2 12.0 %collective-permute-start.37 = (bf16[64,2048]{1,0:T(8,128)(2,1)S(1)}, bf16[64,2048]{1,0:T(8,128)(2,1)S(1)}, u32[]{:S(2)}, u32[]{:S(2)}) collective-permute-start(bf16[64,2048]{1,0:T(8,128)(2,1)S(1)} %get-tuple-element.193), channel_id=1, source_target_pairs={{0,12},{1,13},{2,14},{3,15},{4,8},{5,9},{6,10},{7,11},{8,4},{9,5},... | collective-permute-start | bytes 786440 | tf_op jit(solution)/shard_map/ppermute | solution.py:221
  121.8 11.3 %collective-permute-start.38 = (bf16[64,2048]{1,0:T(8,128)(2,1)S(1)}, bf16[64,2048]{1,0:T(8,128)(2,1)S(1)}, u32[]{:S(2)}, u32[]{:S(2)}) collective-permute-start(bf16[64,2048]{1,0:T(8,128)(2,1)S(1)} %get-tuple-element.194), channel_id=1, source_target_pairs={{0,2},{1,3},{2,0},{3,1},{4,6},{5,7},{6,4},{7,5},{8,10},{9,11},{10,... | collective-permute-start | bytes 786440 | tf_op jit(solution)/shard_map/ppermute | solution.py:221
  (14 other events, 35.1 us)
